TPU v7x, 32 devices: a whole 2x2x4 slice. The times are simulated.
32 devices in a mesh: dp: 2 (over y), space: 16 (over z, x, core).
Axes of the slice: x: 2, y: 2, z: 4, core: 2. Of those that a mesh axis runs over, the one named last changes fastest.
Arguments:
- inputs: bfloat16 [28, 32, 32, 640], P('dp', 'space'), may hold values from -27 to 27
- norm_gain: float32 [640], replicated, may hold values from 0.1 to 1.9
- norm_bias: float32 [640], replicated, may hold values from -3 to 3
- conv_weight: bfloat16 [9, 640, 640], P(None, 'dp'), may hold values from -0.078125 to 0.078125
- upstream: bfloat16 [28, 32, 32, 640], P('dp', 'space'), may hold values from -6 to 6
Outputs:
- mixed: bfloat16 [28, 32, 32, 640], P('dp', 'space')
- input_grad: bfloat16 [28, 32, 32, 640], P('dp', 'space')
- weight_grad: float32 [9, 640, 640], P(None, 'dp', 'space')
- gain_grad: float32 [640], replicated
- bias_grad: float32 [640], replicated
All inputs are finite; a program needn't handle non-finite values.
Results may differ from a plain program's by a relative error of at most 0.0031.
Values may be sent and summed in bfloat16 or wider, within the bound.
No kernel may reach another device: no remote copies, remote signals or barrier semaphores. Data moves between devices by JAX's collectives and lax.ppermute only.
A program may use at most 128 MiB of HBM per device.

v0:
```python
import jax
import jax.numpy as jnp
from jax import lax
from jax.sharding import PartitionSpec as P

GSIZE = 40


EPS = 1e-05


def with_halo(array, sides, width):
    for axis, dim in sides:
        count, length = (lax.axis_size(axis), array.shape[dim])
        up = [(i, (i + 1) % count) for i in range(count - 1)]
        down = [(j, i) for i, j in up]
        last = lax.slice_in_dim(array, length - width, length, axis=dim)
        leading = lax.slice_in_dim(array, 0, width, axis=dim)
        before = lax.ppermute(last, axis, up)
        after = lax.ppermute(leading, axis, down)
        array = jnp.concatenate([before, array, after], axis=dim)
    return array


def member_table(channels, group_count):
    chan_index = lax.broadcasted_iota(jnp.int32, (channels, group_count), 0)
    group_index = lax.broadcasted_iota(jnp.int32, (channels, group_count), 1)
    return (chan_index // (channels // group_count) == group_index).astype(jnp.float32)


def to_groups(chan_sums, member):
    return jnp.dot(chan_sums, member, precision=lax.Precision.HIGHEST)


def to_chans(group_vals, member):
    return jnp.dot(group_vals, member.T, precision=lax.Precision.HIGHEST)[:, None, None, :]


def tap_windows(padded, row_count, col_count, flipped):
    pieces = []
    for tap_row in range(3):
        for tap_col in range(3):
            row_first = 2 - tap_row if flipped else tap_row
            col_first = 2 - tap_col if flipped else tap_col
            window = padded[
                :, row_first : row_first + row_count, col_first : col_first + col_count, :
            ]
            pieces.append(window.reshape(-1, padded.shape[3]))
    return jnp.stack(pieces)


def body(inputs, norm_gain, norm_bias, conv_weight, upstream):
    image_count, row_count, col_count, channels = inputs.shape
    group_count = channels // GSIZE
    member = member_table(channels, group_count)
    count_all = float(row_count * col_count * GSIZE * lax.axis_size("space"))
    x_float = inputs.astype(jnp.float32)
    chan_sum = jnp.sum(x_float, axis=(1, 2))
    chan_square = jnp.sum(x_float * x_float, axis=(1, 2))
    group_sum, group_square = lax.psum(
        (to_groups(chan_sum, member), to_groups(chan_square, member)), "space"
    )
    group_mean = group_sum / count_all
    group_rstd = lax.rsqrt(group_square / count_all - group_mean * group_mean + EPS)
    mean_chan = to_chans(group_mean, member)
    rstd_chan = to_chans(group_rstd, member)
    centred = (x_float - mean_chan) * rstd_chan
    normed = centred * norm_gain + norm_bias
    activated = jax.nn.silu(normed).astype(jnp.bfloat16)
    act_rim = with_halo(activated, (("space", 1),), 1)
    act_pad = jnp.pad(act_rim, ((0, 0), (0, 0), (1, 1), (0, 0)))
    act_taps = tap_windows(act_pad, row_count, col_count, False)
    pixels = act_taps.shape[1]
    conv_out = jnp.einsum(
        "tpk,tko->po",
        act_taps,
        lax.all_gather(conv_weight, "dp", axis=1, tiled=True),
        preferred_element_type=jnp.float32,
    )
    mixed = (x_float + conv_out.reshape(inputs.shape)).astype(jnp.bfloat16)
    grad_rim = with_halo(upstream, (("space", 1),), 1)
    grad_pad = jnp.pad(grad_rim, ((0, 0), (0, 0), (1, 1), (0, 0)))
    grad_taps = tap_windows(grad_pad, row_count, col_count, True)
    act_grad = jnp.einsum(
        "tpo,tko->pk",
        grad_taps,
        lax.all_gather(conv_weight, "dp", axis=1, tiled=True),
        preferred_element_type=jnp.float32,
    )
    upstream_flat = upstream.reshape(pixels, channels)
    weight_terms = jnp.einsum(
        "tpi,po->tio", act_taps, upstream_flat, preferred_element_type=jnp.float32
    )
    partial_grad = lax.psum_scatter(weight_terms, "space", scatter_dimension=2, tiled=True)
    weight_grad = lax.psum_scatter(partial_grad, "dp", scatter_dimension=1, tiled=True)
    sigmoid_n = jax.nn.sigmoid(normed)
    normed_grad = act_grad.reshape(inputs.shape) * sigmoid_n * (1.0 + normed * (1.0 - sigmoid_n))
    gain_part = jnp.sum(normed_grad * centred, axis=(0, 1, 2))
    bias_part = jnp.sum(normed_grad, axis=(0, 1, 2))
    centred_grad = normed_grad * norm_gain
    first_part = to_groups(jnp.sum(centred_grad, axis=(1, 2)), member)
    second_part = to_groups(jnp.sum(centred_grad * centred, axis=(1, 2)), member)
    first_sum, second_sum = lax.psum((first_part, second_part), "space")
    gain_grad, bias_grad = lax.psum((gain_part, bias_part), ("dp", "space"))
    first_mean = to_chans(first_sum / count_all, member)
    second_mean = to_chans(second_sum / count_all, member)
    input_grad = (
        upstream.astype(jnp.float32)
        + rstd_chan * (centred_grad - first_mean - centred * second_mean)
    ).astype(jnp.bfloat16)
    return (mixed, input_grad, weight_grad, gain_grad, bias_grad)


def solution(mesh):
    in_specs = (
        P("dp", "space", None, None),
        P(),
        P(),
        P(None, "dp", None),
        P("dp", "space", None, None),
    )
    out_specs = (
        P("dp", "space", None, None),
        P("dp", "space", None, None),
        P(None, "dp", "space"),
        P(),
        P(),
    )
    return jax.shard_map(body, mesh=mesh, in_specs=in_specs, out_specs=out_specs, check_vma=False)
```

profile of v0, /device:TPU:0, one launch (start us, length us, event | category | flops | bytes accessed | tf_op | source)
XLA Modules:
  0.0 352.5 jit_solution(10134031782386659920)
XLA Ops:
  7.2 0.0 all-gather.2.cloned.1.call-start
  7.2 0.7 all-gather.2.cloned.1.call-update
  7.9 0.0 reduce-scatter.5.cloned.1.call-start
  8.0 0.5 copy-done
  8.4 1.1 fusion.82
  9.5 2.4 collective-permute-start.2
  11.9 1.3 collective-permute-start.3
  13.3 0.4 convert_reduce_fusion
  13.7 0.5 fusion.32
  14.2 0.5 fusion.30
  14.7 65.2 %all-reduce.4 = (f32[14,16]{1,0:T(8,128)S(1)}, f32[14,16]{1,0:T(8,128)S(1)}) all-reduce(f32[14,16]{1,0:T(8,128)S(1)} %fusion.30, f32[14,16]{1,0:T(8,128)S(1)} %fusion.32), channel_id=1, replica_groups=mesh['dp'=2,'space'=16] {'space'}, use_global_device_ids=true, to_apply=%region_3.4 | all-reduce | flops 448 | bytes 3584 | tf_op jit(solution)/shard_map/psum | solution.py:60
  79.9 0.5 fusion.31
  80.4 0.5 fusion.29
  81.0 1.4 select_maximum_fusion
  82.3 1.4 fusion.80
  83.7 1.1 constant_dynamic-update-slice_fusion.17
  84.8 0.2 pad_maximum_fusion
  85.1 1.1 constant_dynamic-update-slice_fusion.16
  86.2 1.1 constant_dynamic-update-slice_fusion.15
  87.3 1.1 constant_dynamic-update-slice_fusion.14
  88.4 1.1 constant_dynamic-update-slice_fusion.13
  89.6 1.1 constant_dynamic-update-slice_fusion.12
  90.7 1.1 constant_dynamic-update-slice_fusion.11
  91.8 1.2 constant_dynamic-update-slice_fusion.10
  93.0 1.1 constant_dynamic-update-slice_fusion.9
  94.1 10.8 %all-gather.2.cloned.1.call-done = bf16[9,640,640]{2,1,0:T(8,128)(2,1)} async-done(((bf16[9,320,640]{2,1,0:T(8,128)(2,1)}), bf16[9,640,640]{2,1,0:T(8,128)(2,1)}) %all-gather.2.cloned.1.call-update) | async-done | bytes 7372816 | tf_op jit(solution)/shard_map/all_gather | solution.py:77
  104.9 13.2 %fusion.85 = f32[896,640,1]{1,0,2:T(8,128)S(1)} fusion(bf16[9,896,640]{2,1,0:T(8,128)(2,1)} %constant_dynamic-update-slice_fusion.9, bf16[9,640,640]{2,1,0:T(8,128)(2,1)} %all-gather.2.cloned.1.call-done), kind=kOutput, calls=%fused_computation.122 | convolution fusion | flops 6606028800 | bytes 19988480 | tf_op jit(solution)/shard_map/tpo,tko->pk/dot_general | solution.py:84
  118.1 2.9 fusion.22
  120.9 0.1 fusion.83
  121.0 1.8 collective-permute-start
  122.8 1.5 collective-permute-start.1
  124.3 0.1 collective-permute-done
  124.4 3.5 %collective-permute-done.1 = bf16[14,1,32,640]{3,2,1,0:T(8,128)(2,1)S(1)} collective-permute-done((bf16[14,1,32,640]{3,2,1,0:T(8,128)(2,1)S(1)}, bf16[14,1,32,640]{3,2,1,0:T(8,128)(2,1)S(1)}, u32[]{:S(2)}, u32[]{:S(2)}) %collective-permute-start.1) | collective-permute-done | bytes 573472 | tf_op jit(solution)/shard_map/ppermute | solution.py:20
  127.9 1.3 select_maximum_fusion.2
  129.3 1.4 fusion.81
  130.7 0.1 constant_dynamic-update-slice_fusion.8
  130.8 0.2 pad_maximum_fusion.2
  131.0 0.2 constant_dynamic-update-slice_fusion.7
  131.2 0.2 constant_dynamic-update-slice_fusion.6
  131.4 0.2 constant_dynamic-update-slice_fusion.5
  131.6 0.2 constant_dynamic-update-slice_fusion.4
  131.8 0.2 constant_dynamic-update-slice_fusion.3
  132.1 0.2 constant_dynamic-update-slice_fusion.2
  132.3 0.2 constant_dynamic-update-slice_fusion.1
  132.5 0.2 constant_dynamic-update-slice_fusion
  132.7 3.8 %copy-done.3 = bf16[9,896,640]{2,1,0:T(8,128)(2,1)} copy-done((bf16[9,896,640]{2,1,0:T(8,128)(2,1)}, bf16[9,896,640]{2,1,0:T(8,128)(2,1)S(1)}, u32[]{:S(2)}) %copy-start.3) | copy-done | bytes 10321944
  136.5 11.0 %fusion.86 = f32[9,640,640]{1,2,0:T(8,128)} fusion(bf16[9,896,640]{2,1,0:T(8,128)(2,1)S(1)} %constant_dynamic-update-slice_fusion, bf16[896,640,1]{1,0,2:T(8,128)(2,1)S(1)} %bitcast.42), kind=kOutput, calls=%fused_computation.123 | convolution fusion | flops 6606028800 | bytes 26214400 | tf_op jit(solution)/shard_map/tpi,po->tio/dot_general | solution.py:91
  147.4 0.0 reduce-scatter.5.cloned.1.call-update
  147.5 0.0 reduce-scatter.7.cloned.1.call-start
  147.5 0.5 fusion.26
  148.0 0.5 fusion.28
  148.5 69.1 %all-reduce.3 = (f32[14,16]{1,0:T(8,128)S(1)}, f32[14,16]{1,0:T(8,128)S(1)}) all-reduce(f32[14,16]{1,0:T(8,128)S(1)} %fusion.26, f32[14,16]{1,0:T(8,128)S(1)} %fusion.28), channel_id=1, replica_groups=mesh['dp'=2,'space'=16] {'space'}, use_global_device_ids=true, to_apply=%region_7.8 | all-reduce | flops 448 | bytes 3584 | tf_op jit(solution)/shard_map/psum | solution.py:103
  217.6 44.4 %all-reduce.2 = (f32[640]{0:T(1024)}, f32[640]{0:T(1024)}) all-reduce(f32[640]{0:T(1024)S(1)} %get-tuple-element.5, f32[640]{0:T(1024)S(1)} %get-tuple-element.8), channel_id=1, replica_groups=mesh['dp'=2,'space'=16] {'dp','space'}, use_global_device_ids=true, to_apply=%region_11.12 | all-reduce | flops 1280 | bytes 10240 | tf_op jit(solution)/shard_map/psum | solution.py:104
  262.0 0.5 fusion.25
  262.5 0.5 fusion.27
  263.0 47.5 %reduce-scatter.5.cloned.1.call-done = f32[9,640,40]{1,2,0:T(8,128)} async-done(((f32[9,640,640]{1,2,0:T(8,128)}), f32[9,640,40]{1,2,0:T(8,128)}) %reduce-scatter.5.cloned.1.call-update) | async-done | bytes 921616 | tf_op jit(solution)/shard_map/reduce_scatter | solution.py:94
  310.6 5.6 %copy.14 = f32[9,640,40]{2,0,1:T(8,128)} copy(f32[9,640,40]{1,2,0:T(8,128)} %reduce-scatter.5.cloned.1.call-done) | data formatting | bytes 1843200
  316.2 4.9 %reshape.31 = f32[640,360]{1,0:T(8,128)} reshape(f32[640,9,40]{2,1,0:T(8,128)} %bitcast.43) | data formatting | bytes 1843200
  321.1 0.0 reduce-scatter.7.cloned.1.call-update
  321.1 13.3 %fusion.84 = f32[896,640,1]{1,0,2:T(8,128)S(1)} fusion(bf16[9,896,640]{2,1,0:T(8,128)(2,1)} %copy-done.3, bf16[9,640,640]{2,1,0:T(8,128)(2,1)} %all-gather.2.cloned.1.call-done), kind=kOutput, calls=%fused_computation.121 | convolution fusion | flops 6606028800 | bytes 19988480 | tf_op jit(solution)/shard_map/tpk,tko->po/dot_general | solution.py:74
  334.4 2.6 fusion.21
  337.0 3.0 reduce-scatter.7.cloned.1.call-done
  339.9 3.2 reshape.32
  343.1 2.9 copy.15
  (14 shorter events, 0.1 us)
Async XLA Ops:
  7.2 1.3 copy-start
  7.2 6.1 %copy-start.1 = (bf16[14,2,32,640]{3,2,1,0:T(8,128)(2,1)S(1)}, bf16[14,2,32,640]{3,2,1,0:T(8,128)(2,1)}, u32[]{:S(2)}) copy-start(bf16[14,2,32,640]{3,2,1,0:T(8,128)(2,1)} %param.5) | copy-start | bytes 3440644
  7.2 97.7 %all-gather.2.cloned.1.call-start = ((), (), s32[]{:S(2)}) async-start(), calls=%async_computation.2 | async-start | bytes 11059200 | tf_op jit(solution)/shard_map/all_gather | solution.py:77
  7.9 302.7 %reduce-scatter.5.cloned.1.call-start = ((), (), s32[]{:S(2)}) async-start(), calls=%async_computation.3 | async-start | bytes 15667200 | tf_op jit(solution)/shard_map/reduce_scatter | solution.py:94
  9.5 71.4 %collective-permute-start.2 = (bf16[14,1,32,640]{3,2,1,0:T(8,128)(2,1)}, bf16[14,1,32,640]{3,2,1,0:T(8,128)(2,1)S(1)}, u32[]{:S(2)}, u32[]{:S(2)}) collective-permute-start(bf16[14,1,32,640]{3,2,1,0:T(8,128)(2,1)} %get-tuple-element.35), channel_id=1, source_target_pairs={{0,1},{1,2},{2,3},{3,4},{4,5},{5,6},{6,7},{7,8},{8,9},{9,10},{10,1... | collective-permute-start | bytes 1720328 | tf_op jit(solution)/shard_map/ppermute | solution.py:19
  11.9 69.0 %collective-permute-start.3 = (bf16[14,1,32,640]{3,2,1,0:T(8,128)(2,1)}, bf16[14,1,32,640]{3,2,1,0:T(8,128)(2,1)S(1)}, u32[]{:S(2)}, u32[]{:S(2)}) collective-permute-start(bf16[14,1,32,640]{3,2,1,0:T(8,128)(2,1)} %get-tuple-element.36), channel_id=1, source_target_pairs={{1,0},{2,1},{3,2},{4,3},{5,4},{6,5},{7,6},{8,7},{9,8},{10,9},{11,1... | collective-permute-start | bytes 1720328 | tf_op jit(solution)/shard_map/ppermute | solution.py:20
  94.1 24.0 %copy-start.4 = (f32[640]{0:T(1024)S(1)}, f32[640]{0:T(1024)}, u32[]{:S(2)}) copy-start(f32[640]{0:T(1024)} %param.6) | copy-start | bytes 7684
  94.1 24.0 %copy-start.5 = (f32[640]{0:T(1024)S(1)}, f32[640]{0:T(1024)}, u32[]{:S(2)}) copy-start(f32[640]{0:T(1024)} %param.7) | copy-start | bytes 7684
  121.0 3.3 collective-permute-start
  122.8 5.1 %collective-permute-start.1 = (bf16[14,1,32,640]{3,2,1,0:T(8,128)(2,1)S(1)}, bf16[14,1,32,640]{3,2,1,0:T(8,128)(2,1)S(1)}, u32[]{:S(2)}, u32[]{:S(2)}) collective-permute-start(bf16[14,1,32,640]{3,2,1,0:T(8,128)(2,1)S(1)} %get-tuple-element.40), channel_id=1, source_target_pairs={{1,0},{2,1},{3,2},{4,3},{5,4},{6,5},{7,6},{8,7},{9,8},{10,9},{11,1... | collective-permute-start | bytes 1720328 | tf_op jit(solution)/shard_map/ppermute | solution.py:20
  132.7 3.8 %copy-start.3 = (bf16[9,896,640]{2,1,0:T(8,128)(2,1)}, bf16[9,896,640]{2,1,0:T(8,128)(2,1)S(1)}, u32[]{:S(2)}) copy-start(bf16[9,896,640]{2,1,0:T(8,128)(2,1)S(1)} %constant_dynamic-update-slice_fusion) | copy-start | bytes 30965764
  147.5 192.5 %reduce-scatter.7.cloned.1.call-start = ((), (), s32[]{:S(2)}) async-start(), calls=%async_computation.4 | async-start | bytes 1474560
  321.1 13.3 %copy-start.2 = (f32[14,2,32,640]{3,2,1,0:T(8,128)S(1)}, f32[14,2,32,640]{3,2,1,0:T(8,128)}, u32[]{:S(2)}) copy-start(f32[14,2,32,640]{3,2,1,0:T(8,128)} %get-tuple-element.17) | copy-start | bytes 6881284
Sparse Core Ops, SparseCore 0:
  9.6 95.2 all-gather.1
  147.6 162.9 reduce-scatter.4
  321.2 18.6 reduce-scatter.6
where the time goes:
time: 353 us; the launch traced here: 352 us
  blocking collectives  179 us (51%)
  waiting for transfers between devices  65.6 us (19%)
  matrix products  41.5 us (12%)
  local copies, waits for them, and re-layouts  36.5 us (10%)
  between operations  14 us (4%)
  other arithmetic  9.05 us (3%)
  starting transfers between devices  7.04 us (2%)
    psum x1, blocking collectives, body(): first_sum, second_sum = lax.psum((first_part, second_part), 'space')  69.1 us
    psum x1, blocking collectives, body(): lax.psum((to_groups(chan_sum, member), to_groups(chan_square, member)), '...  65.2 us
    reduce_scatter x1, waiting for transfers between devices, body(): lax.psum_scatter(weight_terms, 'space', scatter_dimension=2, tiled=True)  47.5 us
    psum x1, blocking collectives, body(): gain_grad, bias_grad = lax.psum((gain_part, bias_part), ('dp', 'space'))  44.4 us
    unnamed x32, local copies, waits for them, and re-layouts  31.3 us
    dot_general x1, matrix products, body(): jnp.einsum('tpk,tko->po', act_taps, lax.all_gather(conv_weight, 'dp', axi...  13.3 us
    dot_general x1, matrix products, body(): jnp.einsum('tpo,tko->pk', grad_taps, lax.all_gather(conv_weight, 'dp', ax...  13.2 us
    dot_general x1, matrix products, body(): jnp.einsum('tpi,po->tio', act_taps, upstream_flat, preferred_element_type...  11 us
  transfers between devices with their start and end apart: 7, of which 5 were waited for; matrix products, arithmetic and copies ran while one was open for 10% of the time, Pallas kernels for 0%

commit v1 on v0

v1 whole, which is shorter than its diff:
```python
import functools

import jax
import jax.numpy as jnp
from jax import lax
from jax.experimental import pallas as pl
from jax.experimental.pallas import tpu as pltpu
from jax.sharding import PartitionSpec as P

GSIZE = 40
EPS = 1e-05
GROUP_A, GROUP_B = (0, 1, 2, 3, 4), (5, 6, 7, 8)
LANES = 128
F32 = jnp.float32
BF16 = jnp.bfloat16
HIGHEST = lax.Precision.HIGHEST
VMEM_SPEC = pl.BlockSpec(memory_space=pltpu.VMEM)
SMEM_SPEC = pl.BlockSpec(memory_space=pltpu.SMEM)
HBM_SPEC = pl.BlockSpec(memory_space=pltpu.HBM)
MIB = 1 << 20
V, S, H = VMEM_SPEC, SMEM_SPEC, HBM_SPEC


def kernel_call(body, mib, out_shape, in_specs, name, scratch=(), out_specs=None):
    return pl.pallas_call(
        body,
        out_shape=out_shape,
        in_specs=in_specs,
        out_specs=out_specs or jax.tree.map(lambda _: VMEM_SPEC, out_shape),
        scratch_shapes=scratch,
        compiler_params=pltpu.CompilerParams(vmem_limit_bytes=mib * MIB),
        name=name,
    )


def struct(shape, dtype):
    return jax.ShapeDtypeStruct(shape, dtype)


def swap(value, axis, bit):
    count = lax.axis_size(axis)
    return lax.ppermute(value, axis, [(i, i ^ bit) for i in range(count)])


def after(value, *others):
    return lax.optimization_barrier((value,) + others)[0]


def members(channels, groups):
    chan = lax.broadcasted_iota(jnp.int32, (groups, channels), 1)
    first = lax.broadcasted_iota(jnp.int32, (groups, channels), 0) * GSIZE
    return ((chan >= first) & (chan < first + GSIZE)).astype(F32)


def to_groups(sums, member):
    return lax.dot_general(
        sums, member, (((1,), (1,)), ((), ())), precision=HIGHEST, preferred_element_type=F32
    )


def to_chans(values, member):
    return jnp.dot(values, member, precision=HIGHEST, preferred_element_type=F32)


def shifted(block):
    columns = block.shape[0]
    col = lax.broadcasted_iota(jnp.int32, block.shape, 0)
    down = jnp.where(col == 0, 0.0, pltpu.roll(block, 1, axis=0))
    up = jnp.where(col == columns - 1, 0.0, pltpu.roll(block, columns - 1, axis=0))
    return down, up


def stats_kernel(info, x, u, *refs):
    if len(refs) == 7:
        w, out, edge_x, edge_u, w_first, w_last, sem = refs
    else:
        out, edge_x, edge_u, sem = refs
    images, _, _, channels = x.shape
    core = info[0]
    copies = [
        pltpu.make_async_copy(x.at[:, core], edge_x, sem.at[0]),
        pltpu.make_async_copy(u.at[:, core], edge_u, sem.at[1]),
    ]
    if len(refs) == 7:
        part, rows = w.shape[1] // 2, w_last.shape[1]
        for k, (start, dst) in enumerate(((info[4] * 3 * rows, w_first), (2 * rows, w_last))):
            at = pl.ds(pl.multiple_of(core * part + start, 32), dst.shape[1])
            copies.append(pltpu.make_async_copy(w.at[:, at, :], dst, sem.at[2 + k]))
    for c in copies:
        c.start()
    one, two = [], []
    for img in range(images):
        value = x[img].astype(F32).reshape(-1, channels)
        one.append(jnp.sum(value, axis=0, keepdims=True))
        two.append(jnp.sum(value * value, axis=0, keepdims=True))
    out[...] = to_groups(jnp.concatenate(one + two), members(channels, channels // GSIZE))
    for c in copies:
        c.wait()


def act_kernel(size, info, stats, x, x_mate, rim, rim_mate, gain, bias, mid, side, mean, rstd):
    images, _, columns, channels = x.shape
    core, own_ok, mate_ok = info[0], info[1], info[2]
    member = members(channels, channels // GSIZE)
    group_mean = stats[:images] / size
    group_rstd = lax.rsqrt(stats[images:] / size - group_mean * group_mean + EPS)
    mean[...] = to_chans(group_mean, member)
    rstd[...] = to_chans(group_rstd, member)

    def fill(load, row, keep):
        def step(img, carry):
            value = load(img).astype(F32)
            scale = rstd[pl.ds(img, 1), :] * gain[...]
            normed = (value - mean[pl.ds(img, 1), :]) * scale + bias[...]
            act = normed / (1.0 + jnp.exp(-normed))
            if keep is not None:
                act = jnp.where(keep > 0, act, 0.0)
            down, up = shifted(act)
            at = pl.ds(pl.multiple_of((row * images + img) * columns, columns), columns)
            mid[at, :] = act.astype(BF16)
            side[0, at, :] = down.astype(BF16)
            side[1, at, :] = up.astype(BF16)
            return carry

        lax.fori_loop(0, images, step, 0)

    fill(lambda img: x[img, 0], 1 + 2 * core, None)
    fill(lambda img: x[img, 1], 2 + 2 * core, None)
    fill(lambda img: x_mate[img, 0], 3 - 2 * core, None)
    fill(lambda img: x_mate[img, 1], 4 - 2 * core, None)
    fill(lambda img: rim[img], 5 * core, own_ok)
    fill(lambda img: rim_mate[img], 5 - 5 * core, mate_ok)


def turn_kernel(bits, info, u, u_mate, out, rows):
    images, _, columns, channels = u.shape
    core, me = info[0], info[5]
    block = images * columns
    for r in range(2):
        at = pl.multiple_of((r + 2 * core) * block, 64)
        rows[pl.ds(at, block), :] = u[:, r].reshape(block, channels)
        at = pl.multiple_of((r + 2 - 2 * core) * block, 64)
        rows[pl.ds(at, block), :] = u_mate[:, r].reshape(block, channels)
    width = channels >> bits
    row = lax.broadcasted_iota(jnp.int32, out.shape[:1] + (channels,), 0)
    chan = core * width + row
    for place in range(bits - 1):
        low = width << (bits - 2 - place)
        own = (me >> (place + 1)) & 1
        late = lax.rem(row, 2 * low) >= low
        chan = chan - jnp.where(late, low, 0)
        bit = jnp.where(late, own, 1 - own)
        chan = chan + bit * (width << (place + 1))
    index = lax.broadcasted_iota(jnp.int32, chan.shape, 1)
    table = (index == chan).astype(F32).astype(BF16)
    out[...] = lax.dot_general(
        table, rows[...], (((1,), (1,)), ((), ())), preferred_element_type=F32
    ).astype(BF16)


def tap_block(mid, side, t, start, rows):
    at = pl.ds(start, rows)
    return mid[at, :] if t % 3 == 1 else side[(t % 3) // 2, at, :]


def halves(value, part):
    taps = value.shape[1] // (2 * part)
    low = [value[:, 2 * t * part : (2 * t + 1) * part] for t in range(taps)]
    high = [value[:, (2 * t + 1) * part : (2 * t + 2) * part] for t in range(taps)]
    return jnp.concatenate(low, axis=1), jnp.concatenate(high, axis=1)


def grad_kernel(taps, block, by_dp, info, lhs, mid, side, sent, kept):
    channels = mid.shape[1]
    cut = lhs.shape[0] // 2
    for first in range(0, len(taps), 2):
        pair = taps[first : first + 2]
        rhs = [tap_block(mid, side, t, (t // 3) * block, lhs.shape[1]) for t in pair]
        rhs = rhs[0] if len(rhs) == 1 else jnp.concatenate(rhs, axis=1)
        got = jnp.dot(lhs[...], rhs, preferred_element_type=F32)
        if by_dp:
            low, high = halves(got, channels // 2)
            at = slice(first * channels // 2, first * channels // 2 + low.shape[1])
            sent[:, at] = jnp.where(info[3] == 0, high, low).astype(BF16)
            kept[:, at] = jnp.where(info[3] == 0, low, high)
        else:
            at = slice(first * channels, first * channels + rhs.shape[1])
            sent[:, at] = got[:cut].astype(BF16)
            kept[:, at] = got[cut:]


def fold_kernel(kept, got, sent_out, kept_out):
    cut = sent_out.shape[0]
    sent_out[...] = (kept[:cut] + got[:cut].astype(F32)).astype(BF16)
    kept_out[...] = kept[cut:] + got[cut:].astype(F32)


def part_kernel(part, info, kept, got, sent_out, kept_out):
    low, high = halves(kept[...] + got[...].astype(F32), part)
    sent_out[...] = jnp.where(info[3] == 0, high, low).astype(BF16)
    kept_out[...] = jnp.where(info[3] == 0, low, high)


def weights_kernel(places, *refs):
    parts, out = refs[:-1], refs[-1]
    for k, part in enumerate(parts):
        at = pl.ds(pl.multiple_of(places[k], 32), part.shape[1])
        for t in range(out.shape[0]):
            out[t, at, :] = part[t]


def conv_kernel(info, mid, w, x, out, side):
    images, _, columns, channels = x.shape
    block = images * columns
    first = pl.multiple_of(2 * info[0] * block, 64)
    taps = w.shape[0]

    def fill(k, carry):
        at = pl.multiple_of(k * columns, columns)
        down, up = shifted(mid[pl.ds(first + at, columns), :].astype(F32))
        side[0, pl.ds(at, columns), :] = down.astype(BF16)
        side[1, pl.ds(at, columns), :] = up.astype(BF16)
        return carry

    lax.fori_loop(0, 4 * images, fill, 0)
    rhs = w[...].reshape(taps * channels, channels)
    for r in range(2):
        lhs = []
        for t in range(taps):
            at = (r + t // 3) * block
            if t % 3 == 1:
                lhs.append(mid[pl.ds(pl.multiple_of(first + at, 64), block), :])
            else:
                lhs.append(side[(t % 3) // 2, at : at + block, :])
        lhs = jnp.concatenate(lhs, axis=1)
        value = jnp.dot(lhs, rhs, preferred_element_type=F32).reshape(images, columns, channels)
        out[:, r] = (x[:, r].astype(F32) + value).astype(BF16)


def back_kernel(info, u, u_mate, rim, w, x, mean, rstd, gain, bias, out, sums, part, one, two):
    images, _, columns, channels = x.shape
    block = images * columns
    taps = w.shape[0]
    core = info[0]

    def fill(load, row):
        def step(img, carry):
            value = load(img)
            down, up = shifted(value.astype(F32))
            at = pl.ds(pl.multiple_of((row * images + img) * columns, columns), columns)
            part[0, at, :] = down.astype(BF16)
            part[1, at, :] = value
            part[2, at, :] = up.astype(BF16)
            return carry

        lax.fori_loop(0, images, step, 0)

    fill(lambda img: u[img, 0], 1)
    fill(lambda img: u[img, 1], 2)
    fill(lambda img: u_mate[img, core], 3 - 3 * core)
    fill(lambda img: rim[img], 3 * core)

    rhs = jnp.concatenate([w[t] for t in range(taps)], axis=1)
    for r in range(2):
        lhs = jnp.concatenate([
            part[2 - t % 3, (r + 2 - t // 3) * block : (r + 3 - t // 3) * block, :]
            for t in range(taps)
        ], axis=1)
        out[:, r] = lax.dot_general(
            lhs, rhs, (((1,), (1,)), ((), ())), preferred_element_type=F32
        ).reshape(images, columns, channels)

    def finish(img, carry):
        first = jnp.zeros((1, channels), F32)
        second = jnp.zeros((1, channels), F32)
        for r in range(2):
            centred = (x[img, r].astype(F32) - mean[pl.ds(img, 1), :]) * rstd[pl.ds(img, 1), :]
            normed = centred * gain[...] + bias[...]
            s = 1.0 / (1.0 + jnp.exp(-normed))
            grad = out[img, r] * s * (1.0 + normed * (1.0 - s))
            out[img, r] = grad
            first = first + jnp.sum(grad, axis=0, keepdims=True)
            second = second + jnp.sum(grad * centred, axis=0, keepdims=True)
        one[pl.ds(img, 1), :] = first
        two[pl.ds(img, 1), :] = second
        return carry

    lax.fori_loop(0, images, finish, 0)
    groups = channels // GSIZE
    member = members(channels, groups)
    sums[...] = jnp.zeros_like(sums)
    sums[0:images, 0:groups] = to_groups(one[...] * gain[...], member)
    sums[0:images, groups : 2 * groups] = to_groups(two[...] * gain[...], member)
    base = images + images % 2
    rows = channels // LANES
    gain_part = jnp.sum(two[...], axis=0, keepdims=True)
    bias_part = jnp.sum(one[...], axis=0, keepdims=True)
    for k in range(rows):
        at = slice(k * LANES, (k + 1) * LANES)
        sums[base + k : base + k + 1, :] = gain_part[:, at]
        sums[base + rows + k : base + rows + k + 1, :] = bias_part[:, at]


def input_kernel(size, sums, grad, x, u, mean, rstd, gain, out):
    images, rows, columns, channels = x.shape
    groups = channels // GSIZE
    member = members(channels, groups)
    means = sums[...] / size
    first = to_chans(means[:images, :groups], member)
    second = to_chans(means[:images, groups : 2 * groups], member)
    for img in range(images):
        at = slice(img, img + 1)
        for r in range(rows):
            centred = (x[img, r].astype(F32) - mean[at]) * rstd[at]
            inner = grad[img, r] * gain[...] - first[at] - centred * second[at]
            out[img, r] = (u[img, r].astype(F32) + rstd[at] * inner).astype(BF16)


def body(inputs, norm_gain, norm_bias, conv_weight, upstream):
    images, rows, columns, channels = inputs.shape
    count, dps = lax.axis_size("space"), lax.axis_size("dp")
    me, half = lax.axis_index("space"), lax.axis_index("dp")
    core, mate, side_bit = me & 1, me ^ 1, (me >> 2) & 1
    groups = channels // GSIZE
    bits = count.bit_length() - 1
    size = float(rows * columns * GSIZE * count)
    block = images * columns
    two = dps == 2
    gain_row, bias_row = norm_gain[None], norm_bias[None]
    taps = conv_weight.shape[0]
    own_ok = jnp.where((me == 0) | (me == count - 1), 0, 1)
    mate_ok = jnp.where((mate == 0) | (mate == count - 1), 0, 1)
    info = jnp.stack(
        [core, own_ok, mate_ok, half if two else 0 * core, side_bit, me]
    ).astype(jnp.int32)

    pairs = []
    for i in range(1, count - 1, 2):
        pairs += [(i, i + 1), (i + 1, i)]
    x_mate = swap(inputs, "space", 1)
    u_mate = swap(upstream, "space", 1)

    part = conv_weight.shape[1] // 2
    fifth = part // 5
    row_shape = (images, columns, channels)
    out_shape = [struct((2 * images, groups), F32), struct(row_shape, BF16), struct(row_shape, BF16)]
    operands = [info, inputs, upstream]
    if two:
        out_shape += [
            struct((taps, 2 * fifth, channels), BF16), struct((taps, fifth, channels), BF16)
        ]
        operands.append(conv_weight)
    stats, edge_x, edge_u, *w_sent = kernel_call(
        stats_kernel, 16, tuple(out_shape), [S, V, H] + [H] * (len(operands) - 3), "stats",
        [pltpu.SemaphoreType.DMA((4,))], (V,) + (H,) * (len(out_shape) - 1),
    )(*operands)
    rim_x = lax.ppermute(edge_x, "space", pairs)
    for place in [0] + list(range(2, bits)) + [1]:
        if place == 1:
            stats, rim_x = lax.optimization_barrier((stats, rim_x))
        stats = stats + swap(stats, "space", 1 << place)
        if two and place == 2:
            w_first = swap(after(w_sent[0], stats), "dp", 1)
        if two and place == 3:
            w_last = swap(after(w_sent[1], stats), "dp", 1)
    rim_x_mate = swap(rim_x, "space", 1)
    rim_u = lax.ppermute(after(edge_u, stats), "space", pairs)
    if two:
        w_second = swap(after(w_first, stats), "space", 4)

    act_mid, act_side, mean, rstd = kernel_call(
        functools.partial(act_kernel, size), 24,
        (
            struct((6 * block, channels), BF16),
            struct((2, 6 * block, channels), BF16),
            struct((images, channels), F32),
            struct((images, channels), F32),
        ),
        [S] + [V] * 7, "activate",
    )(info, stats, inputs, x_mate, rim_x, rim_x_mate, gain_row, bias_row)

    lhs = kernel_call(
        functools.partial(turn_kernel, bits), 16, struct((channels // 2, 4 * block), BF16),
        [S, V, V], "turn", [pltpu.VMEM((4 * block, channels), BF16)],
    )(info, upstream, u_mate)

    def terms(group, by_dp, lhs):
        width = len(group) * channels
        shape = (channels // 2, width // 2) if by_dp else (channels // 4, width)
        return kernel_call(
            functools.partial(grad_kernel, group, block, by_dp), 28,
            (struct(shape, BF16), struct(shape, F32)), [S] + [V] * 3, "weight_terms",
        )(info, lhs, act_mid, act_side)

    def fold(kept, got):
        shape = (kept.shape[0] // 2, kept.shape[1])
        return kernel_call(
            fold_kernel, 8, (struct(shape, BF16), struct(shape, F32)), [V, V], "fold"
        )(kept, got)

    def split(kept, got):
        shape = (kept.shape[0], kept.shape[1] // 2)
        return kernel_call(
            functools.partial(part_kernel, channels // 2), 8,
            (struct(shape, BF16), struct(shape, F32)), [S, V, V], "split",
        )(info, kept, got)

    sent_a, kept_a = terms(GROUP_A, False, lhs)
    got_a = swap(sent_a, "space", 2)
    sent_b, kept_b = terms(GROUP_B, two, after(lhs, sent_a, rim_u))
    got_b = swap(sent_b, "dp", 1) if two else swap(sent_b, "space", 2)

    if two:
        w_parts = list(lax.optimization_barrier((w_first, w_second, w_last, sent_a))[:3])
        w_parts += [swap(value, "space", 1) for value in w_parts]
        other = (1 - half) * 2 * part
        spots = [half * 2 * part]
        for which in (core, 1 - core):
            spots += [
                other + which * part + side_bit * 3 * fifth,
                other + which * part + (1 - side_bit) * 3 * fifth,
                other + which * part + 2 * fifth,
            ]
        weights = kernel_call(
            weights_kernel, 20, struct((taps, channels, channels), BF16), [S] + [V] * 7, "weights",
        )(jnp.stack(spots).astype(jnp.int32), after(conv_weight, sent_b), *w_parts)
    else:
        weights = lax.all_gather(conv_weight, "dp", axis=1, tiled=True)

    grad, sums = kernel_call(
        back_kernel, 32,
        (struct(inputs.shape, F32), struct((40, LANES), F32)), [S] + [V] * 9, "conv_backward",
        [
            pltpu.VMEM((3, 4 * block, channels), BF16),
            pltpu.VMEM((images, channels), F32),
            pltpu.VMEM((images, channels), F32),
        ],
    )(info, upstream, u_mate, rim_u, weights, inputs, mean, rstd, gain_row, bias_row)

    sums = sums + swap(sums, "space", 1)
    step = swap(sums, "space", 4)
    if two:
        sent_b, kept_b = fold(kept_b, after(got_b, sums))
        got_b = swap(sent_b, "space", 2)
    else:
        sent_b, kept_b = fold(kept_b, after(got_b, sums))
        got_b = swap(sent_b, "space", 4)
    sent_a, kept_a = fold(kept_a, after(got_a, sent_b))
    got_a = swap(sent_a, "space", 4)

    mixed = kernel_call(
        conv_kernel, 28, struct(inputs.shape, BF16), [S] + [V] * 3, "conv_forward",
        [pltpu.VMEM((2, 4 * block, channels), BF16)],
    )(after(info, sent_a, sent_b), act_mid, weights, inputs)

    sums = sums + after(step, mixed)
    step = swap(sums, "space", 8)
    if two:
        sent_a, kept_a = split(kept_a, after(got_a, mixed))
        got_a = swap(sent_a, "dp", 1)
        sent_b, kept_b = fold(kept_b, after(got_b, sent_a))
        got_b = swap(sent_b, "space", 4)
    sums = sums + after(step, sent_b)
    sums = sums + swap(sums, "space", 2)
    input_grad = kernel_call(
        functools.partial(input_kernel, size), 16, struct(inputs.shape, BF16), [V] * 7, "input_grad"
    )(sums, grad, inputs, upstream, mean, rstd, gain_row)

    base = images + images % 2
    totals = sums[base : base + 2 * channels // LANES]
    totals = totals + swap(totals, "dp", 1) if two else lax.psum(totals, "dp")
    totals = totals.reshape(2, channels)

    sent_a, kept_a = fold(kept_a, after(got_a, input_grad))
    got_a = swap(sent_a, "space", 8)
    sent_b, kept_b = fold(kept_b, after(got_b, sent_a))
    got_b = swap(sent_b, "space", 8)
    weight_grad = jnp.concatenate(
        [kept_a + got_a.astype(F32), kept_b + got_b.astype(F32)], axis=1
    )
    weight_grad = weight_grad.reshape(weight_grad.shape[0], taps, -1)
    if not two:
        weight_grad = lax.psum_scatter(weight_grad, "dp", scatter_dimension=2, tiled=True)
    weight_grad = weight_grad.transpose(1, 2, 0)
    return (mixed, input_grad, weight_grad, totals[0], totals[1])


def solution(mesh):
    in_specs = (
        P("dp", "space", None, None),
        P(),
        P(),
        P(None, "dp", None),
        P("dp", "space", None, None),
    )
    out_specs = (
        P("dp", "space", None, None),
        P("dp", "space", None, None),
        P(None, "dp", "space"),
        P(),
        P(),
    )
    return jax.shard_map(body, mesh=mesh, in_specs=in_specs, out_specs=out_specs, check_vma=False)
```

time: 353 us -> 136 us (0.39)
  blocking collectives: 179 us -> 0 us
  Pallas kernels: 0 us -> 55.3 us
  matrix products: 41.5 us -> 0 us
  waiting for transfers between devices: 65.6 us -> 26.4 us
  starting transfers between devices: 7.04 us -> 42.7 us
  local copies, waits for them, and re-layouts: 36.5 us -> 9.81 us
  between operations: 14 us -> 0.9 us
  other arithmetic: 9.05 us -> 0.21 us
    psum x3 -> x0, blocking collectives: 179 us -> none  [the longest x1 69.1 us: body(): first_sum, second_sum = lax.psum((first_part, second_part), 'space')]
    pallas_call x0 -> x15, Pallas kernels: none -> 55.3 us  [the longest x1 13.3 us: body(): kernel_call(back_kernel, 32, (struct(inputs.shape, F32), struct((40, LANE...]
    reduce_scatter x1 -> x0, waiting for transfers between devices: 47.5 us -> none  [body(): lax.psum_scatter(weight_terms, 'space', scatter_dimension=2, tiled=True)]
    dot_general x11 -> x0, matrix products: 41.5 us -> none  [the longest x1 13.3 us: body(): jnp.einsum('tpk,tko->po', act_taps, lax.all_gather(conv_weight, 'dp', axi...]
    ppermute x4 -> x28, starting transfers between devices: 6.92 us -> 42.7 us  [the longest x26 41.3 us: swap(): return lax.ppermute(value, axis, [(i, i ^ bit) for i in range(count)])]
    ppermute x4 -> x28, waiting for transfers between devices: 3.62 us -> 26.4 us  [the longest x26 26.4 us: swap(): return lax.ppermute(value, axis, [(i, i ^ bit) for i in range(count)])]
    unnamed x32 -> x31, local copies, waits for them, and re-layouts: 31.3 us -> 8.84 us
    all_gather x1 -> x0, waiting for transfers between devices: 10.8 us -> none  [body(): lax.all_gather(conv_weight, 'dp', axis=1, tiled=True)]
  transfers between devices with their start and end apart: 7 -> 28, of which waited for: 5 -> 12; matrix products, arithmetic and copies ran while one was open for 10% -> 1% of each run, Pallas kernels for 0% -> 40%
where the time goes in v1:
time: 136 us; the launch traced here: 135 us
  Pallas kernels  55.3 us (41%)
  starting transfers between devices  42.7 us (31%)
  waiting for transfers between devices  26.4 us (19%)
  local copies, waits for them, and re-layouts  9.81 us (7%)
    ppermute x26, starting transfers between devices, swap(): return lax.ppermute(value, axis, [(i, i ^ bit) for i in range(count)])  41.3 us
    ppermute x26, waiting for transfers between devices, swap(): return lax.ppermute(value, axis, [(i, i ^ bit) for i in range(count)])  26.4 us
    pallas_call x1, Pallas kernels, body(): kernel_call(back_kernel, 32, (struct(inputs.shape, F32), struct((40, LANE...  13.3 us
    pallas_call x1, Pallas kernels, body(): kernel_call(conv_kernel, 28, struct(inputs.shape, BF16), [S] + [V] * 3, '...  11.8 us
    pallas_call x2, Pallas kernels, terms(): kernel_call(functools.partial(grad_kernel, group, block, by_dp), 28, (str...  10.3 us
    unnamed x31, local copies, waits for them, and re-layouts  8.84 us
    pallas_call x1, Pallas kernels, body(): kernel_call(functools.partial(act_kernel, size), 24, (struct((6 * block,...  6.06 us
    pallas_call x1, Pallas kernels, body(): kernel_call(functools.partial(input_kernel, size), 16, struct(inputs.shap...  3.34 us
  transfers between devices with their start and end apart: 28, of which 12 were waited for; matrix products, arithmetic and copies ran while one was open for 1% of the time, Pallas kernels for 40%

profile of v1, /device:TPU:0, one launch (start us, length us, event | category | flops | bytes accessed | tf_op | source)
XLA Modules:
  0.0 135.3 jit_solution(1113778064053652499)
XLA Ops:
  0.6 0.5 collective-permute-start
  1.1 0.1 stack.51.info
  1.2 1.3 copy-done
  2.5 2.0 %copy-done.3 = bf16[9,320,640]{2,1,0:T(8,128)(2,1)S(1)} copy-done((bf16[9,320,640]{2,1,0:T(8,128)(2,1)S(1)}, bf16[9,320,640]{2,1,0:T(8,128)(2,1)}, u32[]{:S(2)}) %copy-start.3) | copy-done | bytes 3686424
  4.5 2.1 %stats.1 = (f32[28,16]{1,0:T(8,128)S(1)}, bf16[14,32,640]{2,1,0:T(8,128)(2,1)S(1)}, bf16[14,32,640]{2,1,0:T(8,128)(2,1)S(1)}, bf16[9,64,640]{2,1,0:T(8,128)(2,1)S(1)}, bf16[9,32,640]{2,1,0:T(8,128)(2,1)S(1)}) custom-call(s32[6]{0:T(128)S(1)} %stack.51.info, bf16[14,2,32,640]{3,2,1,0:T(8,128)(2,1)} %x.9, bf16[14,2,32,640]{3,2,1,0:T(8,128)(2,1)S(1)} %copy-done, ...), custom_call_target="tpu_custom_call" | custom-call | tf_op jit(solution)/shard_map/stats/pallas_call | solution.py:353
  6.7 0.1 collective-permute-start.1
  6.8 1.1 collective-permute-done.1
  7.9 2.7 %collective-permute-start.2 = (f32[28,16]{1,0:T(8,128)S(1)}, f32[28,16]{1,0:T(8,128)S(1)}, u32[]{:S(2)}, u32[]{:S(2)}) collective-permute-start(f32[28,16]{1,0:T(8,128)S(1)} %add.61), channel_id=1, source_target_pairs={{0,4},{1,5},{2,6},{3,7},{4,0},{5,1},{6,2},{7,3},{8,12},{9,13},{10,... | collective-permute-start | bytes 5384 | tf_op jit(solution)/shard_map/ppermute | solution.py:42
  10.7 1.7 %collective-permute-done.2 = f32[28,16]{1,0:T(8,128)S(1)} collective-permute-done((f32[28,16]{1,0:T(8,128)S(1)}, f32[28,16]{1,0:T(8,128)S(1)}, u32[]{:S(2)}, u32[]{:S(2)}) %collective-permute-start.2) | collective-permute-done | bytes 1824 | tf_op jit(solution)/shard_map/ppermute | solution.py:42
  12.4 2.0 %collective-permute-start.11 = (bf16[9,64,640]{2,1,0:T(8,128)(2,1)S(1)}, bf16[9,64,640]{2,1,0:T(8,128)(2,1)}, u32[]{:S(2)}, u32[]{:S(2)}) collective-permute-start(bf16[9,64,640]{2,1,0:T(8,128)(2,1)S(1)} %get-tuple-element.67), channel_id=1, source_target_pairs={{0,16},{16,0},{1,17},{17,1},{2,18},{18,2},{3,19},{19,3},{4,20},{20... | collective-permute-start | bytes 2211848 | tf_op jit(solution)/shard_map/ppermute | solution.py:42
  14.4 0.7 collective-permute-start.4
  15.1 2.9 %collective-permute-start.6 = (bf16[14,2,32,640]{3,2,1,0:T(8,128)(2,1)}, bf16[14,2,32,640]{3,2,1,0:T(8,128)(2,1)S(1)}, u32[]{:S(2)}, u32[]{:S(2)}) collective-permute-start(bf16[14,2,32,640]{3,2,1,0:T(8,128)(2,1)} %x.9), channel_id=1, source_target_pairs={{0,1},{1,0},{2,3},{3,2},{4,5},{5,4},{6,7},{7,6},{8,9},{9,8},{10,11... | collective-permute-start | bytes 3440648 | tf_op jit(solution)/shard_map/ppermute | solution.py:42
  17.9 2.6 %collective-permute-start.3 = (f32[28,16]{1,0:T(8,128)S(1)}, f32[28,16]{1,0:T(8,128)S(1)}, u32[]{:S(2)}, u32[]{:S(2)}) collective-permute-start(f32[28,16]{1,0:T(8,128)S(1)} %add.62), channel_id=1, source_target_pairs={{0,8},{1,9},{2,10},{3,11},{4,12},{5,13},{6,14},{7,15},{8,0},{9,1},... | collective-permute-start | bytes 5384 | tf_op jit(solution)/shard_map/ppermute | solution.py:42
  20.5 6.6 %collective-permute-done.3 = f32[28,16]{1,0:T(8,128)S(1)} collective-permute-done((f32[28,16]{1,0:T(8,128)S(1)}, f32[28,16]{1,0:T(8,128)S(1)}, u32[]{:S(2)}, u32[]{:S(2)}) %collective-permute-start.3) | collective-permute-done | bytes 1824 | tf_op jit(solution)/shard_map/ppermute | solution.py:42
  27.1 3.5 %collective-permute-start.7 = (bf16[14,32,640]{2,1,0:T(8,128)(2,1)S(1)}, bf16[14,32,640]{2,1,0:T(8,128)(2,1)S(1)}, u32[]{:S(2)}, u32[]{:S(2)}) collective-permute-start(bf16[14,32,640]{2,1,0:T(8,128)(2,1)S(1)} %collective-permute-done.4.rim), channel_id=1, source_target_pairs={{0,1},{1,0},{2,3},{3,2},{4,5},{5,4},{6,7},{7,6},{8,9},{9,8},{10,11... | collective-permute-start | bytes 1720328 | tf_op jit(solution)/shard_map/ppermute | solution.py:42
  30.7 2.4 %collective-permute-start.5 = (f32[28,16]{1,0:T(8,128)S(1)}, f32[28,16]{1,0:T(8,128)S(1)}, u32[]{:S(2)}, u32[]{:S(2)}) collective-permute-start(f32[28,16]{1,0:T(8,128)S(1)} %add.63), channel_id=1, source_target_pairs={{0,2},{1,3},{2,0},{3,1},{4,6},{5,7},{6,4},{7,5},{8,10},{9,11},{10,... | collective-permute-start | bytes 5384 | tf_op jit(solution)/shard_map/ppermute | solution.py:42
  33.0 1.7 %collective-permute-done.5 = f32[28,16]{1,0:T(8,128)S(1)} collective-permute-done((f32[28,16]{1,0:T(8,128)S(1)}, f32[28,16]{1,0:T(8,128)S(1)}, u32[]{:S(2)}, u32[]{:S(2)}) %collective-permute-start.5) | collective-permute-done | bytes 1824 | tf_op jit(solution)/shard_map/ppermute | solution.py:42
  34.7 2.0 %collective-permute-start.12 = (bf16[9,64,640]{2,1,0:T(8,128)(2,1)}, bf16[9,64,640]{2,1,0:T(8,128)(2,1)}, u32[]{:S(2)}, u32[]{:S(2)}) collective-permute-start(bf16[9,64,640]{2,1,0:T(8,128)(2,1)} %collective-permute-done.11.refs_1_), channel_id=1, source_target_pairs={{0,4},{1,5},{2,6},{3,7},{4,0},{5,1},{6,2},{7,3},{8,12},{9,13},{10,... | collective-permute-start | bytes 2211848 | tf_op jit(solution)/shard_map/ppermute | solution.py:42
  36.8 0.7 collective-permute-start.9
  37.5 0.0 copy-start.5
  37.5 0.8 collective-permute-start.13
  38.4 1.9 %turn.1.lhs = bf16[320,1792]{1,0:T(8,128)(2,1)S(1)} custom-call(s32[6]{0:T(128)S(1)} %stack.51.info, bf16[14,2,32,640]{3,2,1,0:T(8,128)(2,1)S(1)} %copy-done.1, bf16[14,2,32,640]{3,2,1,0:T(8,128)(2,1)S(1)} %collective-permute-done.u_mate), custom_call_target="tpu_custom_call" | custom-call | tf_op jit(solution)/shard_map/turn/pallas_call | solution.py:382
  40.4 6.1 %activate.1 = (bf16[2688,640]{1,0:T(8,128)(2,1)S(1)}, bf16[2,2688,640]{2,1,0:T(8,128)(2,1)S(1)}, f32[14,640]{1,0:T(8,128)S(1)}, f32[14,640]{1,0:T(8,128)S(1)}) custom-call(s32[6]{0:T(128)S(1)} %stack.51.info, f32[28,16]{1,0:T(8,128)S(1)} %add.64.stats, bf16[14,2,32,640]{3,2,1,0:T(8,128)(2,1)} %x.9, ...), custom_call_target="tpu_custom_call" | custom-call | tf_op jit(solution)/shard_map/activate/pallas_call | solution.py:371
  46.4 5.6 %weight_terms.2 = (bf16[160,3200]{1,0:T(8,128)(2,1)}, f32[160,3200]{1,0:T(8,128)S(1)}) custom-call(s32[6]{0:T(128)S(1)} %stack.51.info, bf16[320,1792]{1,0:T(8,128)(2,1)S(1)} %turn.1.lhs, bf16[2688,640]{1,0:T(8,128)(2,1)S(1)} %get-tuple-element.56.mid, bf16[2,2688,640]{2,1,0:T(8,128)(2,1)S(1)} %get-tuple-element.57.side), custom_call_target="tpu_custom_call" | custom-call | tf_op jit(solution)/shard_map/weight_terms/pallas_call | solution.py:390
  52.0 1.3 copy-done.7
  53.3 2.6 %collective-permute-start.8 = (bf16[160,3200]{1,0:T(8,128)(2,1)}, bf16[160,3200]{1,0:T(8,128)(2,1)}, u32[]{:S(2)}, u32[]{:S(2)}) collective-permute-start(bf16[160,3200]{1,0:T(8,128)(2,1)} %get-tuple-element.59), channel_id=1, source_target_pairs={{0,2},{1,3},{2,0},{3,1},{4,6},{5,7},{6,4},{7,5},{8,10},{9,11},{10,... | collective-permute-start | bytes 3072008 | tf_op jit(solution)/shard_map/ppermute | solution.py:42
  55.9 4.8 %weight_terms.3 = (bf16[320,1280]{1,0:T(8,128)(2,1)}, f32[320,1280]{1,0:T(8,128)S(1)}) custom-call(s32[6]{0:T(128)S(1)} %stack.51.info, bf16[320,1792]{1,0:T(8,128)(2,1)S(1)} %turn.1.lhs, bf16[2688,640]{1,0:T(8,128)(2,1)S(1)} %get-tuple-element.56.mid, bf16[2,2688,640]{2,1,0:T(8,128)(2,1)S(1)} %get-tuple-element.57.side), custom_call_target="tpu_custom_call" | custom-call | tf_op jit(solution)/shard_map/weight_terms/pallas_call | solution.py:390
  60.7 1.2 copy-done.9
  61.8 1.5 %collective-permute-start.10 = (bf16[320,1280]{1,0:T(8,128)(2,1)}, bf16[320,1280]{1,0:T(8,128)(2,1)}, u32[]{:S(2)}, u32[]{:S(2)}) collective-permute-start(bf16[320,1280]{1,0:T(8,128)(2,1)} %get-tuple-element.64), channel_id=1, source_target_pairs={{0,16},{16,0},{1,17},{17,1},{2,18},{18,2},{3,19},{19,3},{4,20},{20... | collective-permute-start | bytes 2457608 | tf_op jit(solution)/shard_map/ppermute | solution.py:42
  63.4 0.5 collective-permute-start.15
  63.9 0.1 collective-permute-start.16
  63.9 0.1 stack.59.places
  64.0 3.5 %collective-permute-done.16.refs_6_ = bf16[9,32,640]{2,1,0:T(8,128)(2,1)} collective-permute-done((bf16[9,32,640]{2,1,0:T(8,128)(2,1)}, bf16[9,32,640]{2,1,0:T(8,128)(2,1)}, u32[]{:S(2)}, u32[]{:S(2)}) %collective-permute-start.16) | collective-permute-done | bytes 368672 | tf_op jit(solution)/shard_map/ppermute | solution.py:42
  67.5 2.0 %copy-done.4 = bf16[9,320,640]{2,1,0:T(8,128)(2,1)S(1)} copy-done((bf16[9,320,640]{2,1,0:T(8,128)(2,1)S(1)}, bf16[9,320,640]{2,1,0:T(8,128)(2,1)}, u32[]{:S(2)}) %copy-start.4) | copy-done | bytes 3686424
  69.6 2.7 %weights.1.w = bf16[9,640,640]{2,1,0:T(8,128)(2,1)S(1)} custom-call(s32[7]{0:T(128)S(1)} %stack.59.places, bf16[9,320,640]{2,1,0:T(8,128)(2,1)S(1)} %copy-done.4, bf16[9,64,640]{2,1,0:T(8,128)(2,1)} %collective-permute-done.11.refs_1_, bf16[9,64,640]{2,1,0:T(8,128)(2,1)} %collective-permute-done.12.refs_2_, ...), custom_call_target="tpu_custom_call" | custom-call | tf_op jit(solution)/shard_map/weights/pallas_call | solution.py:424
  72.3 13.3 %conv_backward.1 = (f32[14,2,32,640]{3,2,1,0:T(8,128)S(1)}, f32[40,128]{1,0:T(8,128)S(1)}) custom-call(s32[6]{0:T(128)S(1)} %stack.51.info, bf16[14,2,32,640]{3,2,1,0:T(8,128)(2,1)S(1)} %copy-done.2, bf16[14,2,32,640]{3,2,1,0:T(8,128)(2,1)S(1)} %copy-done.6, bf16[14,32,640]{2,1,0:T(8,128)(2,1)S(1)} %copy-done.12, bf16[9,640,640]{2,1,0:T(8,128)(2,1)S(1)} %weights.1.w, ...), custom_call_target="tpu_custom_call" | custom-call | tf_op jit(solution)/shard_map/conv_backward/pallas_call | solution.py:430
  85.6 0.2 collective-permute-start.17
  85.7 1.1 collective-permute-done.17
  86.8 1.3 fold.5
  88.1 1.4 %fold.6 = (bf16[80,3200]{1,0:T(8,128)(2,1)S(1)}, f32[80,3200]{1,0:T(8,128)S(1)}) custom-call(f32[160,3200]{1,0:T(8,128)S(1)} %copy-done.8, bf16[160,3200]{1,0:T(8,128)(2,1)} %collective-permute-done.8.got), custom_call_target="tpu_custom_call" | custom-call | tf_op jit(solution)/shard_map/fold/pallas_call | solution.py:397
  89.5 5.2 %collective-permute-start.21 = (bf16[80,3200]{1,0:T(8,128)(2,1)S(1)}, bf16[80,3200]{1,0:T(8,128)(2,1)S(1)}, u32[]{:S(2)}, u32[]{:S(2)}) collective-permute-start(bf16[80,3200]{1,0:T(8,128)(2,1)S(1)} %get-tuple-element.80), channel_id=1, source_target_pairs={{0,4},{1,5},{2,6},{3,7},{4,0},{5,1},{6,2},{7,3},{8,12},{9,13},{10,... | collective-permute-start | bytes 1536008 | tf_op jit(solution)/shard_map/ppermute | solution.py:42
  94.7 0.2 collective-permute-start.18
  94.9 11.8 %conv_forward.1 = bf16[14,2,32,640]{3,2,1,0:T(8,128)(2,1)} custom-call(s32[6]{0:T(128)S(1)} %stack.51.info, bf16[2688,640]{1,0:T(8,128)(2,1)S(1)} %get-tuple-element.56.mid, bf16[9,640,640]{2,1,0:T(8,128)(2,1)S(1)} %weights.1.w, bf16[14,2,32,640]{3,2,1,0:T(8,128)(2,1)} %x.9), custom_call_target="tpu_custom_call" | custom-call | tf_op jit(solution)/shard_map/conv_forward/pallas_call | solution.py:451
  106.7 0.4 collective-permute-done.18
  107.2 2.0 %collective-permute-start.19 = (f32[40,128]{1,0:T(8,128)S(1)}, f32[40,128]{1,0:T(8,128)S(1)}, u32[]{:S(2)}, u32[]{:S(2)}) collective-permute-start(f32[40,128]{1,0:T(8,128)S(1)} %add.74), channel_id=1, source_target_pairs={{0,8},{1,9},{2,10},{3,11},{4,12},{5,13},{6,14},{7,15},{8,0},{9,1},... | collective-permute-start | bytes 61448 | tf_op jit(solution)/shard_map/ppermute | solution.py:42
  109.2 0.8 split.1
  110.0 1.6 %collective-permute-start.23 = (bf16[80,1600]{1,0:T(8,128)(2,1)S(1)}, bf16[80,1600]{1,0:T(8,128)(2,1)S(1)}, u32[]{:S(2)}, u32[]{:S(2)}) collective-permute-start(bf16[80,1600]{1,0:T(8,128)(2,1)S(1)} %get-tuple-element.86), channel_id=1, source_target_pairs={{0,16},{16,0},{1,17},{17,1},{2,18},{18,2},{3,19},{19,3},{4,20},{20... | collective-permute-start | bytes 768008 | tf_op jit(solution)/shard_map/ppermute | solution.py:42
  111.6 0.1 fold.7
  111.6 0.2 collective-permute-done.19
  111.8 1.6 %collective-permute-start.22 = (f32[40,128]{1,0:T(8,128)S(1)}, f32[40,128]{1,0:T(8,128)S(1)}, u32[]{:S(2)}, u32[]{:S(2)}) collective-permute-start(f32[40,128]{1,0:T(8,128)S(1)} %add.75), channel_id=1, source_target_pairs={{0,2},{1,3},{2,0},{3,1},{4,6},{5,7},{6,4},{7,5},{8,10},{9,11},{10,... | collective-permute-start | bytes 61448 | tf_op jit(solution)/shard_map/ppermute | solution.py:42
  113.4 2.2 %collective-permute-done.22 = f32[40,128]{1,0:T(8,128)S(1)} collective-permute-done((f32[40,128]{1,0:T(8,128)S(1)}, f32[40,128]{1,0:T(8,128)S(1)}, u32[]{:S(2)}, u32[]{:S(2)}) %collective-permute-start.22) | collective-permute-done | bytes 20512 | tf_op jit(solution)/shard_map/ppermute | solution.py:42
  115.6 1.6 %collective-permute-start.27 = (f32[10,128]{1,0:T(8,128)S(1)}, f32[10,128]{1,0:T(8,128)S(1)}, u32[]{:S(2)}, u32[]{:S(2)}) collective-permute-start(f32[10,128]{1,0:T(8,128)S(1)} %slice.14), channel_id=1, source_target_pairs={{0,16},{16,0},{1,17},{17,1},{2,18},{18,2},{3,19},{19,3},{4,20},{20... | collective-permute-start | bytes 15368 | tf_op jit(solution)/shard_map/ppermute | solution.py:42
  117.2 1.7 %collective-permute-start.25 = (bf16[80,1280]{1,0:T(8,128)(2,1)S(1)}, bf16[80,1280]{1,0:T(8,128)(2,1)S(1)}, u32[]{:S(2)}, u32[]{:S(2)}) collective-permute-start(bf16[80,1280]{1,0:T(8,128)(2,1)S(1)} %get-tuple-element.88), channel_id=1, source_target_pairs={{0,4},{1,5},{2,6},{3,7},{4,0},{5,1},{6,2},{7,3},{8,12},{9,13},{10,... | collective-permute-start | bytes 614408 | tf_op jit(solution)/shard_map/ppermute | solution.py:42
  119.0 3.3 %input_grad.1 = bf16[14,2,32,640]{3,2,1,0:T(8,128)(2,1)} custom-call(f32[40,128]{1,0:T(8,128)S(1)} %add.76.sums, f32[14,2,32,640]{3,2,1,0:T(8,128)S(1)} %get-tuple-element.90.grad, bf16[14,2,32,640]{3,2,1,0:T(8,128)(2,1)} %x.9, bf16[14,2,32,640]{3,2,1,0:T(8,128)(2,1)S(1)} %copy-done.2, f32[14,640]{1,0:T(8,128)S(1)} %get-tuple-element.74.mean, ...), custom_call_target="tpu_custom_call" | custom-call | tf_op jit(solution)/shard_map/input_grad/pallas_call | solution.py:465
  122.3 0.1 fold.8
  122.4 1.7 %collective-permute-done.25.got = bf16[80,1280]{1,0:T(8,128)(2,1)S(1)} collective-permute-done((bf16[80,1280]{1,0:T(8,128)(2,1)S(1)}, bf16[80,1280]{1,0:T(8,128)(2,1)S(1)}, u32[]{:S(2)}, u32[]{:S(2)}) %collective-permute-start.25) | collective-permute-done | bytes 204832 | tf_op jit(solution)/shard_map/ppermute | solution.py:42
  124.1 2.0 %collective-permute-start.26 = (bf16[40,1280]{1,0:T(8,128)(2,1)S(1)}, bf16[40,1280]{1,0:T(8,128)(2,1)S(1)}, u32[]{:S(2)}, u32[]{:S(2)}) collective-permute-start(bf16[40,1280]{1,0:T(8,128)(2,1)S(1)} %get-tuple-element.98), channel_id=1, source_target_pairs={{0,8},{1,9},{2,10},{3,11},{4,12},{5,13},{6,14},{7,15},{8,0},{9,1},... | collective-permute-start | bytes 307208 | tf_op jit(solution)/shard_map/ppermute | solution.py:42
  126.1 0.6 slice_bitcast_fusion
  126.7 1.0 collective-permute-start.24
  127.7 2.0 %collective-permute-done.26 = bf16[40,1280]{1,0:T(8,128)(2,1)S(1)} collective-permute-done((bf16[40,1280]{1,0:T(8,128)(2,1)S(1)}, bf16[40,1280]{1,0:T(8,128)(2,1)S(1)}, u32[]{:S(2)}, u32[]{:S(2)}) %collective-permute-start.26) | collective-permute-done | bytes 102432 | tf_op jit(solution)/shard_map/ppermute | solution.py:42
  129.8 4.2 %collective-permute-done.24 = bf16[40,1600]{1,0:T(8,128)(2,1)S(1)} collective-permute-done((bf16[40,1600]{1,0:T(8,128)(2,1)S(1)}, bf16[40,1600]{1,0:T(8,128)(2,1)S(1)}, u32[]{:S(2)}, u32[]{:S(2)}) %collective-permute-start.24) | collective-permute-done | bytes 128032 | tf_op jit(solution)/shard_map/ppermute | solution.py:42
  134.0 0.1 pad_maximum_fusion
  134.2 0.2 reshape.18
  134.4 1.0 copy.11
  (57 shorter events, 0.2 us)
Async XLA Ops:
  0.6 36.9 %collective-permute-start = (bf16[14,2,32,640]{3,2,1,0:T(8,128)(2,1)}, bf16[14,2,32,640]{3,2,1,0:T(8,128)(2,1)S(1)}, u32[]{:S(2)}, u32[]{:S(2)}) collective-permute-start(bf16[14,2,32,640]{3,2,1,0:T(8,128)(2,1)} %u.7), channel_id=1, source_target_pairs={{0,1},{1,0},{2,3},{3,2},{4,5},{5,4},{6,7},{7,6},{8,9},{9,8},{10,11... | collective-permute-start | bytes 3440648 | tf_op jit(solution)/shard_map/ppermute | solution.py:42
  1.2 1.3 copy-start
  2.5 2.0 %copy-start.3 = (bf16[9,320,640]{2,1,0:T(8,128)(2,1)S(1)}, bf16[9,320,640]{2,1,0:T(8,128)(2,1)}, u32[]{:S(2)}) copy-start(bf16[9,320,640]{2,1,0:T(8,128)(2,1)} %refs_0_.2) | copy-start | bytes 11059204
  4.5 33.8 %copy-start.13 = (f32[640]{0:T(1024)S(1)}, f32[640]{0:T(1024)}, u32[]{:S(2)}) copy-start(f32[640]{0:T(1024)} %param.6) | copy-start | bytes 7684
  4.5 33.8 %copy-start.14 = (f32[640]{0:T(1024)S(1)}, f32[640]{0:T(1024)}, u32[]{:S(2)}) copy-start(f32[640]{0:T(1024)} %param.7) | copy-start | bytes 7684
  4.5 33.8 %copy-start.1 = (bf16[14,2,32,640]{3,2,1,0:T(8,128)(2,1)S(1)}, bf16[14,2,32,640]{3,2,1,0:T(8,128)(2,1)}, u32[]{:S(2)}) copy-start(bf16[14,2,32,640]{3,2,1,0:T(8,128)(2,1)} %u.7) | copy-start | bytes 3440644
  6.7 1.2 collective-permute-start.1
  7.9 4.5 %collective-permute-start.2 = (f32[28,16]{1,0:T(8,128)S(1)}, f32[28,16]{1,0:T(8,128)S(1)}, u32[]{:S(2)}, u32[]{:S(2)}) collective-permute-start(f32[28,16]{1,0:T(8,128)S(1)} %add.61), channel_id=1, source_target_pairs={{0,4},{1,5},{2,6},{3,7},{4,0},{5,1},{6,2},{7,3},{8,12},{9,13},{10,... | collective-permute-start | bytes 5384 | tf_op jit(solution)/shard_map/ppermute | solution.py:42
  12.4 22.3 %collective-permute-start.11 = (bf16[9,64,640]{2,1,0:T(8,128)(2,1)S(1)}, bf16[9,64,640]{2,1,0:T(8,128)(2,1)}, u32[]{:S(2)}, u32[]{:S(2)}) collective-permute-start(bf16[9,64,640]{2,1,0:T(8,128)(2,1)S(1)} %get-tuple-element.67), channel_id=1, source_target_pairs={{0,16},{16,0},{1,17},{17,1},{2,18},{18,2},{3,19},{19,3},{4,20},{20... | collective-permute-start | bytes 2211848 | tf_op jit(solution)/shard_map/ppermute | solution.py:42
  14.4 12.7 %collective-permute-start.4 = (bf16[14,32,640]{2,1,0:T(8,128)(2,1)S(1)}, bf16[14,32,640]{2,1,0:T(8,128)(2,1)S(1)}, u32[]{:S(2)}, u32[]{:S(2)}) collective-permute-start(bf16[14,32,640]{2,1,0:T(8,128)(2,1)S(1)} %get-tuple-element.53), channel_id=1, source_target_pairs={{1,2},{2,1},{3,4},{4,3},{5,6},{6,5},{7,8},{8,7},{9,10},{10,9},{11,... | collective-permute-start | bytes 1720328 | tf_op jit(solution)/shard_map/ppermute | solution.py:357
  15.1 25.3 %collective-permute-start.6 = (bf16[14,2,32,640]{3,2,1,0:T(8,128)(2,1)}, bf16[14,2,32,640]{3,2,1,0:T(8,128)(2,1)S(1)}, u32[]{:S(2)}, u32[]{:S(2)}) collective-permute-start(bf16[14,2,32,640]{3,2,1,0:T(8,128)(2,1)} %x.9), channel_id=1, source_target_pairs={{0,1},{1,0},{2,3},{3,2},{4,5},{5,4},{6,7},{7,6},{8,9},{9,8},{10,11... | collective-permute-start | bytes 3440648 | tf_op jit(solution)/shard_map/ppermute | solution.py:42
  17.9 9.2 %collective-permute-start.3 = (f32[28,16]{1,0:T(8,128)S(1)}, f32[28,16]{1,0:T(8,128)S(1)}, u32[]{:S(2)}, u32[]{:S(2)}) collective-permute-start(f32[28,16]{1,0:T(8,128)S(1)} %add.62), channel_id=1, source_target_pairs={{0,8},{1,9},{2,10},{3,11},{4,12},{5,13},{6,14},{7,15},{8,0},{9,1},... | collective-permute-start | bytes 5384 | tf_op jit(solution)/shard_map/ppermute | solution.py:42
  27.1 13.2 %collective-permute-start.7 = (bf16[14,32,640]{2,1,0:T(8,128)(2,1)S(1)}, bf16[14,32,640]{2,1,0:T(8,128)(2,1)S(1)}, u32[]{:S(2)}, u32[]{:S(2)}) collective-permute-start(bf16[14,32,640]{2,1,0:T(8,128)(2,1)S(1)} %collective-permute-done.4.rim), channel_id=1, source_target_pairs={{0,1},{1,0},{2,3},{3,2},{4,5},{5,4},{6,7},{7,6},{8,9},{9,8},{10,11... | collective-permute-start | bytes 1720328 | tf_op jit(solution)/shard_map/ppermute | solution.py:42
  30.7 4.1 %collective-permute-start.5 = (f32[28,16]{1,0:T(8,128)S(1)}, f32[28,16]{1,0:T(8,128)S(1)}, u32[]{:S(2)}, u32[]{:S(2)}) collective-permute-start(f32[28,16]{1,0:T(8,128)S(1)} %add.63), channel_id=1, source_target_pairs={{0,2},{1,3},{2,0},{3,1},{4,6},{5,7},{6,4},{7,5},{8,10},{9,11},{10,... | collective-permute-start | bytes 5384 | tf_op jit(solution)/shard_map/ppermute | solution.py:42
  34.7 28.6 %collective-permute-start.12 = (bf16[9,64,640]{2,1,0:T(8,128)(2,1)}, bf16[9,64,640]{2,1,0:T(8,128)(2,1)}, u32[]{:S(2)}, u32[]{:S(2)}) collective-permute-start(bf16[9,64,640]{2,1,0:T(8,128)(2,1)} %collective-permute-done.11.refs_1_), channel_id=1, source_target_pairs={{0,4},{1,5},{2,6},{3,7},{4,0},{5,1},{6,2},{7,3},{8,12},{9,13},{10,... | collective-permute-start | bytes 2211848 | tf_op jit(solution)/shard_map/ppermute | solution.py:42
  36.8 19.1 %collective-permute-start.9 = (bf16[14,32,640]{2,1,0:T(8,128)(2,1)S(1)}, bf16[14,32,640]{2,1,0:T(8,128)(2,1)S(1)}, u32[]{:S(2)}, u32[]{:S(2)}) collective-permute-start(bf16[14,32,640]{2,1,0:T(8,128)(2,1)S(1)} %get-tuple-element.61), channel_id=1, source_target_pairs={{1,2},{2,1},{3,4},{4,3},{5,6},{6,5},{7,8},{8,7},{9,10},{10,9},{11,... | collective-permute-start | bytes 1720328 | tf_op jit(solution)/shard_map/ppermute | solution.py:367
  37.5 2.8 %copy-start.5 = (bf16[14,2,32,640]{3,2,1,0:T(8,128)(2,1)}, bf16[14,2,32,640]{3,2,1,0:T(8,128)(2,1)S(1)}, u32[]{:S(2)}) copy-start(bf16[14,2,32,640]{3,2,1,0:T(8,128)(2,1)S(1)} %collective-permute-done.u_mate) | copy-start | bytes 3440644
  37.5 25.8 %collective-permute-start.13 = (bf16[9,32,640]{2,1,0:T(8,128)(2,1)S(1)}, bf16[9,32,640]{2,1,0:T(8,128)(2,1)}, u32[]{:S(2)}, u32[]{:S(2)}) collective-permute-start(bf16[9,32,640]{2,1,0:T(8,128)(2,1)S(1)} %get-tuple-element.70), channel_id=1, source_target_pairs={{0,16},{16,0},{1,17},{17,1},{2,18},{18,2},{3,19},{19,3},{4,20},{20... | collective-permute-start | bytes 1105928 | tf_op jit(solution)/shard_map/ppermute | solution.py:42
  52.0 1.3 copy-start.7
  53.3 34.8 %collective-permute-start.8 = (bf16[160,3200]{1,0:T(8,128)(2,1)}, bf16[160,3200]{1,0:T(8,128)(2,1)}, u32[]{:S(2)}, u32[]{:S(2)}) collective-permute-start(bf16[160,3200]{1,0:T(8,128)(2,1)} %get-tuple-element.59), channel_id=1, source_target_pairs={{0,2},{1,3},{2,0},{3,1},{4,6},{5,7},{6,4},{7,5},{8,10},{9,11},{10,... | collective-permute-start | bytes 3072008 | tf_op jit(solution)/shard_map/ppermute | solution.py:42
  55.9 4.8 %copy-start.11 = (bf16[14,32,640]{2,1,0:T(8,128)(2,1)}, bf16[14,32,640]{2,1,0:T(8,128)(2,1)S(1)}, u32[]{:S(2)}) copy-start(bf16[14,32,640]{2,1,0:T(8,128)(2,1)S(1)} %collective-permute-done.9.rim) | copy-start | bytes 1720324
  60.7 1.2 copy-start.9
  61.8 25.0 %collective-permute-start.10 = (bf16[320,1280]{1,0:T(8,128)(2,1)}, bf16[320,1280]{1,0:T(8,128)(2,1)}, u32[]{:S(2)}, u32[]{:S(2)}) collective-permute-start(bf16[320,1280]{1,0:T(8,128)(2,1)} %get-tuple-element.64), channel_id=1, source_target_pairs={{0,16},{16,0},{1,17},{17,1},{2,18},{18,2},{3,19},{19,3},{4,20},{20... | collective-permute-start | bytes 2457608 | tf_op jit(solution)/shard_map/ppermute | solution.py:42
  63.4 4.1 %collective-permute-start.14 = (bf16[9,64,640]{2,1,0:T(8,128)(2,1)}, bf16[9,64,640]{2,1,0:T(8,128)(2,1)}, u32[]{:S(2)}, u32[]{:S(2)}) collective-permute-start(bf16[9,64,640]{2,1,0:T(8,128)(2,1)} %collective-permute-done.11.refs_1_), channel_id=1, source_target_pairs={{0,1},{1,0},{2,3},{3,2},{4,5},{5,4},{6,7},{7,6},{8,9},{9,8},{10,11... | collective-permute-start | bytes 2211848 | tf_op jit(solution)/shard_map/ppermute | solution.py:42
  63.4 4.1 %collective-permute-start.15 = (bf16[9,64,640]{2,1,0:T(8,128)(2,1)}, bf16[9,64,640]{2,1,0:T(8,128)(2,1)}, u32[]{:S(2)}, u32[]{:S(2)}) collective-permute-start(bf16[9,64,640]{2,1,0:T(8,128)(2,1)} %collective-permute-done.12.refs_2_), channel_id=1, source_target_pairs={{0,1},{1,0},{2,3},{3,2},{4,5},{5,4},{6,7},{7,6},{8,9},{9,8},{10,11... | collective-permute-start | bytes 2211848 | tf_op jit(solution)/shard_map/ppermute | solution.py:42
  63.9 3.6 %collective-permute-start.16 = (bf16[9,32,640]{2,1,0:T(8,128)(2,1)}, bf16[9,32,640]{2,1,0:T(8,128)(2,1)}, u32[]{:S(2)}, u32[]{:S(2)}) collective-permute-start(bf16[9,32,640]{2,1,0:T(8,128)(2,1)} %collective-permute-done.13.refs_3_), channel_id=1, source_target_pairs={{0,1},{1,0},{2,3},{3,2},{4,5},{5,4},{6,7},{7,6},{8,9},{9,8},{10,11... | collective-permute-start | bytes 1105928 | tf_op jit(solution)/shard_map/ppermute | solution.py:42
  64.0 8.2 %copy-start.2 = (bf16[14,2,32,640]{3,2,1,0:T(8,128)(2,1)S(1)}, bf16[14,2,32,640]{3,2,1,0:T(8,128)(2,1)}, u32[]{:S(2)}) copy-start(bf16[14,2,32,640]{3,2,1,0:T(8,128)(2,1)} %u.7) | copy-start | bytes 3440644
  67.5 2.0 %copy-start.4 = (bf16[9,320,640]{2,1,0:T(8,128)(2,1)S(1)}, bf16[9,320,640]{2,1,0:T(8,128)(2,1)}, u32[]{:S(2)}) copy-start(bf16[9,320,640]{2,1,0:T(8,128)(2,1)} %refs_0_.2) | copy-start | bytes 11059204
  69.5 2.7 %copy-start.6 = (bf16[14,2,32,640]{3,2,1,0:T(8,128)(2,1)S(1)}, bf16[14,2,32,640]{3,2,1,0:T(8,128)(2,1)}, u32[]{:S(2)}) copy-start(bf16[14,2,32,640]{3,2,1,0:T(8,128)(2,1)} %copy-done.5) | copy-start | bytes 3440644
  69.5 2.7 %copy-start.12 = (bf16[14,32,640]{2,1,0:T(8,128)(2,1)S(1)}, bf16[14,32,640]{2,1,0:T(8,128)(2,1)}, u32[]{:S(2)}) copy-start(bf16[14,32,640]{2,1,0:T(8,128)(2,1)} %copy-done.11) | copy-start | bytes 1720324
  72.3 14.5 %copy-start.10 = (f32[320,1280]{1,0:T(8,128)S(1)}, f32[320,1280]{1,0:T(8,128)}, u32[]{:S(2)}) copy-start(f32[320,1280]{1,0:T(8,128)} %copy-done.9) | copy-start | bytes 4915204
  85.6 2.5 %copy-start.8 = (f32[160,3200]{1,0:T(8,128)S(1)}, f32[160,3200]{1,0:T(8,128)}, u32[]{:S(2)}) copy-start(f32[160,3200]{1,0:T(8,128)} %copy-done.7) | copy-start | bytes 6144004
  85.6 1.2 collective-permute-start.17
  89.5 19.7 %collective-permute-start.21 = (bf16[80,3200]{1,0:T(8,128)(2,1)S(1)}, bf16[80,3200]{1,0:T(8,128)(2,1)S(1)}, u32[]{:S(2)}, u32[]{:S(2)}) collective-permute-start(bf16[80,3200]{1,0:T(8,128)(2,1)S(1)} %get-tuple-element.80), channel_id=1, source_target_pairs={{0,4},{1,5},{2,6},{3,7},{4,0},{5,1},{6,2},{7,3},{8,12},{9,13},{10,... | collective-permute-start | bytes 1536008 | tf_op jit(solution)/shard_map/ppermute | solution.py:42
  94.7 16.8 %collective-permute-start.20 = (bf16[160,1280]{1,0:T(8,128)(2,1)S(1)}, bf16[160,1280]{1,0:T(8,128)(2,1)S(1)}, u32[]{:S(2)}, u32[]{:S(2)}) collective-permute-start(bf16[160,1280]{1,0:T(8,128)(2,1)S(1)} %get-tuple-element.78), channel_id=1, source_target_pairs={{0,2},{1,3},{2,0},{3,1},{4,6},{5,7},{6,4},{7,5},{8,10},{9,11},{10,... | collective-permute-start | bytes 1228808 | tf_op jit(solution)/shard_map/ppermute | solution.py:42
  94.7 12.4 %collective-permute-start.18 = (f32[40,128]{1,0:T(8,128)S(1)}, f32[40,128]{1,0:T(8,128)S(1)}, u32[]{:S(2)}, u32[]{:S(2)}) collective-permute-start(f32[40,128]{1,0:T(8,128)S(1)} %add.73), channel_id=1, source_target_pairs={{0,4},{1,5},{2,6},{3,7},{4,0},{5,1},{6,2},{7,3},{8,12},{9,13},{10,... | collective-permute-start | bytes 61448 | tf_op jit(solution)/shard_map/ppermute | solution.py:42
  107.2 4.7 %collective-permute-start.19 = (f32[40,128]{1,0:T(8,128)S(1)}, f32[40,128]{1,0:T(8,128)S(1)}, u32[]{:S(2)}, u32[]{:S(2)}) collective-permute-start(f32[40,128]{1,0:T(8,128)S(1)} %add.74), channel_id=1, source_target_pairs={{0,8},{1,9},{2,10},{3,11},{4,12},{5,13},{6,14},{7,15},{8,0},{9,1},... | collective-permute-start | bytes 61448 | tf_op jit(solution)/shard_map/ppermute | solution.py:42
  110.0 12.4 %collective-permute-start.23 = (bf16[80,1600]{1,0:T(8,128)(2,1)S(1)}, bf16[80,1600]{1,0:T(8,128)(2,1)S(1)}, u32[]{:S(2)}, u32[]{:S(2)}) collective-permute-start(bf16[80,1600]{1,0:T(8,128)(2,1)S(1)} %get-tuple-element.86), channel_id=1, source_target_pairs={{0,16},{16,0},{1,17},{17,1},{2,18},{18,2},{3,19},{19,3},{4,20},{20... | collective-permute-start | bytes 768008 | tf_op jit(solution)/shard_map/ppermute | solution.py:42
  111.8 3.8 %collective-permute-start.22 = (f32[40,128]{1,0:T(8,128)S(1)}, f32[40,128]{1,0:T(8,128)S(1)}, u32[]{:S(2)}, u32[]{:S(2)}) collective-permute-start(f32[40,128]{1,0:T(8,128)S(1)} %add.75), channel_id=1, source_target_pairs={{0,2},{1,3},{2,0},{3,1},{4,6},{5,7},{6,4},{7,5},{8,10},{9,11},{10,... | collective-permute-start | bytes 61448 | tf_op jit(solution)/shard_map/ppermute | solution.py:42
  115.6 6.7 %collective-permute-start.27 = (f32[10,128]{1,0:T(8,128)S(1)}, f32[10,128]{1,0:T(8,128)S(1)}, u32[]{:S(2)}, u32[]{:S(2)}) collective-permute-start(f32[10,128]{1,0:T(8,128)S(1)} %slice.14), channel_id=1, source_target_pairs={{0,16},{16,0},{1,17},{17,1},{2,18},{18,2},{3,19},{19,3},{4,20},{20... | collective-permute-start | bytes 15368 | tf_op jit(solution)/shard_map/ppermute | solution.py:42
  117.2 6.9 %collective-permute-start.25 = (bf16[80,1280]{1,0:T(8,128)(2,1)S(1)}, bf16[80,1280]{1,0:T(8,128)(2,1)S(1)}, u32[]{:S(2)}, u32[]{:S(2)}) collective-permute-start(bf16[80,1280]{1,0:T(8,128)(2,1)S(1)} %get-tuple-element.88), channel_id=1, source_target_pairs={{0,4},{1,5},{2,6},{3,7},{4,0},{5,1},{6,2},{7,3},{8,12},{9,13},{10,... | collective-permute-start | bytes 614408 | tf_op jit(solution)/shard_map/ppermute | solution.py:42
  124.1 5.6 %collective-permute-start.26 = (bf16[40,1280]{1,0:T(8,128)(2,1)S(1)}, bf16[40,1280]{1,0:T(8,128)(2,1)S(1)}, u32[]{:S(2)}, u32[]{:S(2)}) collective-permute-start(bf16[40,1280]{1,0:T(8,128)(2,1)S(1)} %get-tuple-element.98), channel_id=1, source_target_pairs={{0,8},{1,9},{2,10},{3,11},{4,12},{5,13},{6,14},{7,15},{8,0},{9,1},... | collective-permute-start | bytes 307208 | tf_op jit(solution)/shard_map/ppermute | solution.py:42
  126.7 7.3 %collective-permute-start.24 = (bf16[40,1600]{1,0:T(8,128)(2,1)S(1)}, bf16[40,1600]{1,0:T(8,128)(2,1)S(1)}, u32[]{:S(2)}, u32[]{:S(2)}) collective-permute-start(bf16[40,1600]{1,0:T(8,128)(2,1)S(1)} %get-tuple-element.94), channel_id=1, source_target_pairs={{0,8},{1,9},{2,10},{3,11},{4,12},{5,13},{6,14},{7,15},{8,0},{9,1},... | collective-permute-start | bytes 384008 | tf_op jit(solution)/shard_map/ppermute | solution.py:42

commit v2 on v1

--- a/solution.py
+++ b/solution.py
@@ -9,7 +9,7 @@
 
 GSIZE = 40
 EPS = 1e-05
-GROUP_A, GROUP_B = (0, 1, 2, 3, 4), (5, 6, 7, 8)
+GROUP_A, GROUP_B = (0, 1, 2, 3), (4, 5, 6, 7, 8)
 LANES = 128
 F32 = jnp.float32
 BF16 = jnp.bfloat16
@@ -42,6 +42,10 @@
     return lax.ppermute(value, axis, [(i, i ^ bit) for i in range(count)])
 
 
+def in_hbm(value):
+    return pltpu.with_memory_space_constraint(value, pltpu.HBM)
+
+
 def after(value, *others):
     return lax.optimization_barrier((value,) + others)[0]
 
@@ -71,8 +75,8 @@
 
 
 def stats_kernel(info, x, u, *refs):
-    if len(refs) == 7:
-        w, out, edge_x, edge_u, w_first, w_last, sem = refs
+    if len(refs) == 6:
+        w, out, edge_x, edge_u, w_sent, sem = refs
     else:
         out, edge_x, edge_u, sem = refs
     images, _, _, channels = x.shape
@@ -81,11 +85,10 @@
         pltpu.make_async_copy(x.at[:, core], edge_x, sem.at[0]),
         pltpu.make_async_copy(u.at[:, core], edge_u, sem.at[1]),
     ]
-    if len(refs) == 7:
-        part, rows = w.shape[1] // 2, w_last.shape[1]
-        for k, (start, dst) in enumerate(((info[4] * 3 * rows, w_first), (2 * rows, w_last))):
-            at = pl.ds(pl.multiple_of(core * part + start, 32), dst.shape[1])
-            copies.append(pltpu.make_async_copy(w.at[:, at, :], dst, sem.at[2 + k]))
+    if len(refs) == 6:
+        rows = w_sent.shape[1]
+        at = pl.ds(pl.multiple_of(core * rows, 32), rows)
+        copies.append(pltpu.make_async_copy(w.at[:, at, :], w_sent, sem.at[2]))
     for c in copies:
         c.start()
     one, two = [], []
@@ -134,7 +137,7 @@
 
 def turn_kernel(bits, info, u, u_mate, out, rows):
     images, _, columns, channels = u.shape
-    core, me = info[0], info[5]
+    core, me = info[0], info[4]
     block = images * columns
     for r in range(2):
         at = pl.multiple_of((r + 2 * core) * block, 64)
@@ -170,23 +173,41 @@
     return jnp.concatenate(low, axis=1), jnp.concatenate(high, axis=1)
 
 
-def grad_kernel(taps, block, by_dp, info, lhs, mid, side, sent, kept):
+def second_bit(value):
+    quarter = value.shape[0] // 4
+    one, two, three, four = [value[k * quarter : (k + 1) * quarter] for k in range(4)]
+    return jnp.concatenate([one, three]), jnp.concatenate([two, four])
+
+
+def grad_kernel(block, by_dp, info, lhs, mid, side, *refs):
+    outs, stages, sem = refs[:4], refs[4:8], refs[8]
     channels = mid.shape[1]
-    cut = lhs.shape[0] // 2
-    for first in range(0, len(taps), 2):
-        pair = taps[first : first + 2]
-        rhs = [tap_block(mid, side, t, (t // 3) * block, lhs.shape[1]) for t in pair]
-        rhs = rhs[0] if len(rhs) == 1 else jnp.concatenate(rhs, axis=1)
-        got = jnp.dot(lhs[...], rhs, preferred_element_type=F32)
-        if by_dp:
-            low, high = halves(got, channels // 2)
-            at = slice(first * channels // 2, first * channels // 2 + low.shape[1])
-            sent[:, at] = jnp.where(info[3] == 0, high, low).astype(BF16)
-            kept[:, at] = jnp.where(info[3] == 0, low, high)
-        else:
-            at = slice(first * channels, first * channels + rhs.shape[1])
-            sent[:, at] = got[:cut].astype(BF16)
-            kept[:, at] = got[cut:]
+    copies = []
+    for group, cut, base in ((GROUP_A, False, 0), (GROUP_B, by_dp, 2)):
+        for first in range(0, len(group), 2):
+            pair = group[first : first + 2]
+            rhs = [tap_block(mid, side, t, (t // 3) * block, lhs.shape[1]) for t in pair]
+            rhs = rhs[0] if len(rhs) == 1 else jnp.concatenate(rhs, axis=1)
+            got = jnp.dot(lhs[...], rhs, preferred_element_type=F32)
+            if cut:
+                low, high = halves(got, channels // 2)
+                sent = jnp.where(info[3] == 0, high, low)
+                kept = jnp.where(info[3] == 0, low, high)
+                start = first * channels // 2
+            else:
+                sent, kept = second_bit(got)
+                start = first * channels
+            at = slice(start, start + sent.shape[1])
+            stages[base][:, at] = sent.astype(BF16)
+            stages[base + 1][:, at] = kept
+            for k in (base, base + 1):
+                copy = pltpu.make_async_copy(
+                    stages[k].at[:, at], outs[k].at[:, at], sem.at[len(copies)]
+                )
+                copy.start()
+                copies.append(copy)
+    for copy in copies:
+        copy.wait()
 
 
 def fold_kernel(kept, got, sent_out, kept_out):
@@ -195,46 +216,70 @@
     kept_out[...] = kept[cut:] + got[cut:].astype(F32)
 
 
+def fold_second_kernel(kept, got, sent_out, kept_out):
+    sent, own = second_bit(kept[...] + got[...].astype(F32))
+    sent_out[...] = sent.astype(BF16)
+    kept_out[...] = own
+
+
 def part_kernel(part, info, kept, got, sent_out, kept_out):
     low, high = halves(kept[...] + got[...].astype(F32), part)
     sent_out[...] = jnp.where(info[3] == 0, high, low).astype(BF16)
     kept_out[...] = jnp.where(info[3] == 0, low, high)
 
 
-def weights_kernel(places, *refs):
-    parts, out = refs[:-1], refs[-1]
-    for k, part in enumerate(parts):
-        at = pl.ds(pl.multiple_of(places[k], 32), part.shape[1])
-        for t in range(out.shape[0]):
-            out[t, at, :] = part[t]
-
-
-def conv_kernel(info, mid, w, x, out, side):
+def conv_kernel(info, places, mid, *refs):
+    parts, (x, out, w, side, total, sem) = refs[:-6], refs[-6:]
     images, _, columns, channels = x.shape
     block = images * columns
-    first = pl.multiple_of(2 * info[0] * block, 64)
     taps = w.shape[0]
+    own = pl.multiple_of(2 * info[0] * block, 64)
+    copies = [
+        [
+            pltpu.make_async_copy(
+                part.at[t],
+                w.at[t, pl.ds(pl.multiple_of(places[k], 32), part.shape[1]), :],
+                sem.at[t, k],
+            )
+            for k, part in enumerate(parts)
+        ]
+        for t in range(taps)
+    ]
+    for tap in copies:
+        for c in tap:
+            c.start()
 
     def fill(k, carry):
         at = pl.multiple_of(k * columns, columns)
-        down, up = shifted(mid[pl.ds(first + at, columns), :].astype(F32))
+        down, up = shifted(mid[pl.ds(own + at, columns), :].astype(F32))
         side[0, pl.ds(at, columns), :] = down.astype(BF16)
         side[1, pl.ds(at, columns), :] = up.astype(BF16)
         return carry
 
     lax.fori_loop(0, 4 * images, fill, 0)
-    rhs = w[...].reshape(taps * channels, channels)
-    for r in range(2):
-        lhs = []
-        for t in range(taps):
-            at = (r + t // 3) * block
-            if t % 3 == 1:
-                lhs.append(mid[pl.ds(pl.multiple_of(first + at, 64), block), :])
+    for pair in (range(0, 2), range(2, 4), range(4, taps)):
+        first = pair[0]
+        for t in pair:
+            for c in copies[t]:
+                c.wait()
+        rhs = w[first : first + len(pair)].reshape(len(pair) * channels, channels)
+        for r in range(2):
+            lhs = []
+            for t in pair:
+                at = (r + t // 3) * block
+                if t % 3 == 1:
+                    lhs.append(mid[pl.ds(pl.multiple_of(own + at, 64), block), :])
+                else:
+                    lhs.append(side[(t % 3) // 2, at : at + block, :])
+            got = jnp.dot(jnp.concatenate(lhs, axis=1), rhs, preferred_element_type=F32)
+            at = slice(r * block, (r + 1) * block)
+            if first == 0:
+                total[at] = got
+            elif pair[-1] + 1 < taps:
+                total[at] += got
             else:
-                lhs.append(side[(t % 3) // 2, at : at + block, :])
-        lhs = jnp.concatenate(lhs, axis=1)
-        value = jnp.dot(lhs, rhs, preferred_element_type=F32).reshape(images, columns, channels)
-        out[:, r] = (x[:, r].astype(F32) + value).astype(BF16)
+                value = (total[at] + got).reshape(images, columns, channels)
+                out[:, r] = (x[:, r].astype(F32) + value).astype(BF16)
 
 
 def back_kernel(info, u, u_mate, rim, w, x, mean, rstd, gain, bias, out, sums, part, one, two):
@@ -320,7 +365,7 @@
     images, rows, columns, channels = inputs.shape
     count, dps = lax.axis_size("space"), lax.axis_size("dp")
     me, half = lax.axis_index("space"), lax.axis_index("dp")
-    core, mate, side_bit = me & 1, me ^ 1, (me >> 2) & 1
+    core, mate = me & 1, me ^ 1
     groups = channels // GSIZE
     bits = count.bit_length() - 1
     size = float(rows * columns * GSIZE * count)
@@ -331,7 +376,7 @@
     own_ok = jnp.where((me == 0) | (me == count - 1), 0, 1)
     mate_ok = jnp.where((mate == 0) | (mate == count - 1), 0, 1)
     info = jnp.stack(
-        [core, own_ok, mate_ok, half if two else 0 * core, side_bit, me]
+        [core, own_ok, mate_ok, half if two else 0 * core, me]
     ).astype(jnp.int32)
 
     pairs = []
@@ -341,32 +386,29 @@
     u_mate = swap(upstream, "space", 1)
 
     part = conv_weight.shape[1] // 2
-    fifth = part // 5
     row_shape = (images, columns, channels)
     out_shape = [struct((2 * images, groups), F32), struct(row_shape, BF16), struct(row_shape, BF16)]
-    operands = [info, inputs, upstream]
+    operands = [info, inputs, in_hbm(upstream)]
     if two:
-        out_shape += [
-            struct((taps, 2 * fifth, channels), BF16), struct((taps, fifth, channels), BF16)
-        ]
-        operands.append(conv_weight)
+        out_shape.append(struct((taps, part, channels), BF16))
+        operands.append(in_hbm(conv_weight))
     stats, edge_x, edge_u, *w_sent = kernel_call(
         stats_kernel, 16, tuple(out_shape), [S, V, H] + [H] * (len(operands) - 3), "stats",
-        [pltpu.SemaphoreType.DMA((4,))], (V,) + (H,) * (len(out_shape) - 1),
+        [pltpu.SemaphoreType.DMA((3,))],
     )(*operands)
+    if two:
+        w_low = swap(w_sent[0], "dp", 1)
     rim_x = lax.ppermute(edge_x, "space", pairs)
+    lhs = kernel_call(
+        functools.partial(turn_kernel, bits), 16, struct((channels // 2, 4 * block), BF16),
+        [S, V, V], "turn", [pltpu.VMEM((4 * block, channels), BF16)],
+    )(info, upstream, u_mate)
     for place in [0] + list(range(2, bits)) + [1]:
         if place == 1:
-            stats, rim_x = lax.optimization_barrier((stats, rim_x))
+            stats, rim_x, lhs = lax.optimization_barrier((stats, rim_x, lhs))
         stats = stats + swap(stats, "space", 1 << place)
-        if two and place == 2:
-            w_first = swap(after(w_sent[0], stats), "dp", 1)
-        if two and place == 3:
-            w_last = swap(after(w_sent[1], stats), "dp", 1)
     rim_x_mate = swap(rim_x, "space", 1)
     rim_u = lax.ppermute(after(edge_u, stats), "space", pairs)
-    if two:
-        w_second = swap(after(w_first, stats), "space", 4)
 
     act_mid, act_side, mean, rstd = kernel_call(
         functools.partial(act_kernel, size), 24,
@@ -379,23 +421,10 @@
         [S] + [V] * 7, "activate",
     )(info, stats, inputs, x_mate, rim_x, rim_x_mate, gain_row, bias_row)
 
-    lhs = kernel_call(
-        functools.partial(turn_kernel, bits), 16, struct((channels // 2, 4 * block), BF16),
-        [S, V, V], "turn", [pltpu.VMEM((4 * block, channels), BF16)],
-    )(info, upstream, u_mate)
-
-    def terms(group, by_dp, lhs):
-        width = len(group) * channels
-        shape = (channels // 2, width // 2) if by_dp else (channels // 4, width)
-        return kernel_call(
-            functools.partial(grad_kernel, group, block, by_dp), 28,
-            (struct(shape, BF16), struct(shape, F32)), [S] + [V] * 3, "weight_terms",
-        )(info, lhs, act_mid, act_side)
-
-    def fold(kept, got):
+    def fold(kept, got, kernel=fold_kernel):
         shape = (kept.shape[0] // 2, kept.shape[1])
         return kernel_call(
-            fold_kernel, 8, (struct(shape, BF16), struct(shape, F32)), [V, V], "fold"
+            kernel, 8, (struct(shape, BF16), struct(shape, F32)), [V, V], "fold"
         )(kept, got)
 
     def split(kept, got):
@@ -405,27 +434,45 @@
             (struct(shape, BF16), struct(shape, F32)), [S, V, V], "split",
         )(info, kept, got)
 
-    sent_a, kept_a = terms(GROUP_A, False, lhs)
+    width_a, width_b = len(GROUP_A) * channels, len(GROUP_B) * channels
+    shape_b = (channels // 2, width_b // 2) if two else (channels // 4, width_b)
+    shapes = [((channels // 4, width_a), BF16), ((channels // 4, width_a), F32)]
+    shapes += [(shape_b, BF16), (shape_b, F32)]
+    sent_a, kept_a, sent_b, kept_b = kernel_call(
+        functools.partial(grad_kernel, block, two), 28,
+        tuple(pltpu.HBM(*shape) for shape in shapes), [S] + [V] * 3, "weight_terms",
+        [pltpu.VMEM(*shape) for shape in shapes] + [pltpu.SemaphoreType.DMA((10,))], (H,) * 4,
+    )(info, lhs, act_mid, act_side)
+    got_a = swap(sent_a, "space", 4)
+    got_b = swap(sent_b, "dp", 1) if two else swap(sent_b, "space", 4)
+
+    if two:
+        w_low = after(w_low, sent_b)
+        other = (1 - half) * 2 * part
+        spots = jnp.stack([half * 2 * part, other + core * part, other + (1 - core) * part])
+        w_parts = [conv_weight, w_low, swap(w_low, "space", 1)]
+    else:
+        spots = jnp.zeros((1,), jnp.int32)
+        w_parts = [lax.all_gather(conv_weight, "dp", axis=1, tiled=True)]
+    mixed, weights = kernel_call(
+        conv_kernel, 32,
+        (struct(inputs.shape, BF16), struct((taps, channels, channels), BF16)),
+        [S, S, V] + [H] * len(w_parts) + [V], "conv_forward",
+        [
+            pltpu.VMEM((2, 4 * block, channels), BF16),
+            pltpu.VMEM((2 * block, channels), F32),
+            pltpu.SemaphoreType.DMA((taps, len(w_parts))),
+        ],
+    )(
+        after(info, sent_b), spots.astype(jnp.int32), act_mid,
+        *[in_hbm(value) for value in w_parts], inputs,
+    )
+
+    sent_a, kept_a = fold(kept_a, after(got_a, mixed))
     got_a = swap(sent_a, "space", 2)
-    sent_b, kept_b = terms(GROUP_B, two, after(lhs, sent_a, rim_u))
-    got_b = swap(sent_b, "dp", 1) if two else swap(sent_b, "space", 2)
-
-    if two:
-        w_parts = list(lax.optimization_barrier((w_first, w_second, w_last, sent_a))[:3])
-        w_parts += [swap(value, "space", 1) for value in w_parts]
-        other = (1 - half) * 2 * part
-        spots = [half * 2 * part]
-        for which in (core, 1 - core):
-            spots += [
-                other + which * part + side_bit * 3 * fifth,
-                other + which * part + (1 - side_bit) * 3 * fifth,
-                other + which * part + 2 * fifth,
-            ]
-        weights = kernel_call(
-            weights_kernel, 20, struct((taps, channels, channels), BF16), [S] + [V] * 7, "weights",
-        )(jnp.stack(spots).astype(jnp.int32), after(conv_weight, sent_b), *w_parts)
-    else:
-        weights = lax.all_gather(conv_weight, "dp", axis=1, tiled=True)
+    got_b = after(got_b, sent_a)
+    sent_b, kept_b = fold(kept_b, got_b, fold_second_kernel if two else fold_kernel)
+    got_b = swap(sent_b, "space", 4 if two else 2)
 
     grad, sums = kernel_call(
         back_kernel, 32,
@@ -435,46 +482,34 @@
             pltpu.VMEM((images, channels), F32),
             pltpu.VMEM((images, channels), F32),
         ],
-    )(info, upstream, u_mate, rim_u, weights, inputs, mean, rstd, gain_row, bias_row)
-
-    sums = sums + swap(sums, "space", 1)
-    step = swap(sums, "space", 4)
+    )(
+        after(info, sent_a, sent_b), upstream, u_mate, rim_u, weights, inputs, mean, rstd,
+        gain_row, bias_row,
+    )
+
     if two:
-        sent_b, kept_b = fold(kept_b, after(got_b, sums))
-        got_b = swap(sent_b, "space", 2)
-    else:
-        sent_b, kept_b = fold(kept_b, after(got_b, sums))
-        got_b = swap(sent_b, "space", 4)
-    sent_a, kept_a = fold(kept_a, after(got_a, sent_b))
-    got_a = swap(sent_a, "space", 4)
-
-    mixed = kernel_call(
-        conv_kernel, 28, struct(inputs.shape, BF16), [S] + [V] * 3, "conv_forward",
-        [pltpu.VMEM((2, 4 * block, channels), BF16)],
-    )(after(info, sent_a, sent_b), act_mid, weights, inputs)
-
-    sums = sums + after(step, mixed)
-    step = swap(sums, "space", 8)
-    if two:
-        sent_a, kept_a = split(kept_a, after(got_a, mixed))
+        sent_a, kept_a = split(kept_a, after(got_a, sums))
         got_a = swap(sent_a, "dp", 1)
         sent_b, kept_b = fold(kept_b, after(got_b, sent_a))
-        got_b = swap(sent_b, "space", 4)
-    sums = sums + after(step, sent_b)
-    sums = sums + swap(sums, "space", 2)
+        got_b = swap(sent_b, "space", 2)
+        sums = after(sums, sent_b)
+    for place in [0] + list(range(2, bits)) + [1]:
+        sums = sums + swap(sums, "space", 1 << place)
+    sent_a, kept_a = fold(kept_a, after(got_a, sums))
+    got_a = swap(sent_a, "space", 8)
+    sent_b, kept_b = fold(kept_b, after(got_b, sent_a))
+    got_b = swap(sent_b, "space", 8)
+    sums = after(sums, sent_b)
     input_grad = kernel_call(
         functools.partial(input_kernel, size), 16, struct(inputs.shape, BF16), [V] * 7, "input_grad"
     )(sums, grad, inputs, upstream, mean, rstd, gain_row)
 
     base = images + images % 2
     totals = sums[base : base + 2 * channels // LANES]
-    totals = totals + swap(totals, "dp", 1) if two else lax.psum(totals, "dp")
+    totals = totals + after(swap(totals, "dp", 1), input_grad) if two else lax.psum(totals, "dp")
     totals = totals.reshape(2, channels)
 
-    sent_a, kept_a = fold(kept_a, after(got_a, input_grad))
-    got_a = swap(sent_a, "space", 8)
-    sent_b, kept_b = fold(kept_b, after(got_b, sent_a))
-    got_b = swap(sent_b, "space", 8)
+    got_a = after(got_a, input_grad)
     weight_grad = jnp.concatenate(
         [kept_a + got_a.astype(F32), kept_b + got_b.astype(F32)], axis=1
     )

time: 136 us -> 122 us (0.90)
  starting transfers between devices: 42.7 us -> 29.5 us
  waiting for transfers between devices: 26.4 us -> 35.3 us
  local copies, waits for them, and re-layouts: 9.81 us -> 3.85 us
  Pallas kernels: 55.3 us -> 51.5 us
    ppermute x26 -> x22, starting transfers between devices: 41.3 us -> 27.9 us  [swap(): return lax.ppermute(value, axis, [(i, i ^ bit) for i in range(count)])]
    ppermute x26 -> x22, waiting for transfers between devices: 26.4 us -> 35.3 us  [swap(): return lax.ppermute(value, axis, [(i, i ^ bit) for i in range(count)])]
    unnamed x31 -> x17, local copies, waits for them, and re-layouts: 8.84 us -> 2.98 us
    pallas_call x9 -> x7, Pallas kernels: 27.7 us -> 23.3 us  [the longest x1 12.8 us: body(): kernel_call(conv_kernel, 32, (struct(inputs.shape, BF16), struct((taps, c...]
  transfers between devices with their start and end apart: 28 -> 24, of which waited for: 12 -> 13; matrix products, arithmetic and copies ran while one was open for 1% -> 1% of each run, Pallas kernels for 40% -> 40%
where the time goes in v2:
time: 122 us; the launch traced here: 121 us
  Pallas kernels  51.5 us (42%)
  waiting for transfers between devices  35.3 us (29%)
  starting transfers between devices  29.5 us (24%)
  local copies, waits for them, and re-layouts  3.85 us (3%)
    ppermute x22, waiting for transfers between devices, swap(): return lax.ppermute(value, axis, [(i, i ^ bit) for i in range(count)])  35.3 us
    ppermute x22, starting transfers between devices, swap(): return lax.ppermute(value, axis, [(i, i ^ bit) for i in range(count)])  27.9 us
    pallas_call x1, Pallas kernels, body(): kernel_call(back_kernel, 32, (struct(inputs.shape, F32), struct((40, LANE...  13.1 us
    pallas_call x1, Pallas kernels, body(): kernel_call(conv_kernel, 32, (struct(inputs.shape, BF16), struct((taps, c...  12.8 us
    pallas_call x1, Pallas kernels, body(): kernel_call(functools.partial(grad_kernel, block, two), 28, tuple((pltpu....  8.8 us
    pallas_call x1, Pallas kernels, body(): kernel_call(functools.partial(act_kernel, size), 24, (struct((6 * block,...  5.93 us
    pallas_call x1, Pallas kernels, body(): kernel_call(functools.partial(input_kernel, size), 16, struct(inputs.shap...  3.29 us
    pallas_call x1, Pallas kernels, body(): kernel_call(stats_kernel, 16, tuple(out_shape), [S, V, H] + [H] * (len(op...  3.15 us
  transfers between devices with their start and end apart: 24, of which 13 were waited for; matrix products, arithmetic and copies ran while one was open for 1% of the time, Pallas kernels for 40%

profile of v2, /device:TPU:0, one launch (start us, length us, event | category | flops | bytes accessed | tf_op | source)
XLA Modules:
  0.0 121.3 jit_solution(5462917479206951413)
XLA Ops:
  0.7 0.1 stack.35.info
  0.7 3.1 %stats.1 = (f32[28,16]{1,0:T(8,128)S(1)}, bf16[14,32,640]{2,1,0:T(8,128)(2,1)S(1)}, bf16[14,32,640]{2,1,0:T(8,128)(2,1)S(1)}, bf16[9,160,640]{2,1,0:T(8,128)(2,1)S(1)}) custom-call(s32[5]{0:T(128)S(1)} %stack.35.info, bf16[14,2,32,640]{3,2,1,0:T(8,128)(2,1)} %x.7, bf16[14,2,32,640]{3,2,1,0:T(8,128)(2,1)} %u.7, bf16[9,320,640]{2,1,0:T(8,128)(2,1)} %refs_0_.3), custom_call_target="tpu_custom_call" | custom-call | tf_op jit(solution)/shard_map/stats/pallas_call | solution.py:395
  3.9 3.0 %collective-permute-start.8 = (bf16[9,160,640]{2,1,0:T(8,128)(2,1)S(1)}, bf16[9,160,640]{2,1,0:T(8,128)(2,1)}, u32[]{:S(2)}, u32[]{:S(2)}) collective-permute-start(bf16[9,160,640]{2,1,0:T(8,128)(2,1)S(1)} %get-tuple-element.59), channel_id=1, source_target_pairs={{0,16},{16,0},{1,17},{17,1},{2,18},{18,2},{3,19},{19,3},{4,20},{20... | collective-permute-start | bytes 5529608 | tf_op jit(solution)/shard_map/ppermute | solution.py:42
  6.9 0.0 collective-permute-start.4
  6.9 0.7 collective-permute-start.3
  7.6 2.9 %collective-permute-start.6 = (bf16[14,2,32,640]{3,2,1,0:T(8,128)(2,1)}, bf16[14,2,32,640]{3,2,1,0:T(8,128)(2,1)S(1)}, u32[]{:S(2)}, u32[]{:S(2)}) collective-permute-start(bf16[14,2,32,640]{3,2,1,0:T(8,128)(2,1)} %x.7), channel_id=1, source_target_pairs={{0,1},{1,0},{2,3},{3,2},{4,5},{5,4},{6,7},{7,6},{8,9},{9,8},{10,11... | collective-permute-start | bytes 3440648 | tf_op jit(solution)/shard_map/ppermute | solution.py:42
  10.5 0.1 collective-permute-start
  10.6 2.2 %collective-permute-done = f32[28,16]{1,0:T(8,128)S(1)} collective-permute-done((f32[28,16]{1,0:T(8,128)S(1)}, f32[28,16]{1,0:T(8,128)S(1)}, u32[]{:S(2)}, u32[]{:S(2)}) %collective-permute-start) | collective-permute-done | bytes 1824 | tf_op jit(solution)/shard_map/ppermute | solution.py:42
  12.8 1.7 %collective-permute-start.1 = (f32[28,16]{1,0:T(8,128)S(1)}, f32[28,16]{1,0:T(8,128)S(1)}, u32[]{:S(2)}, u32[]{:S(2)}) collective-permute-start(f32[28,16]{1,0:T(8,128)S(1)} %add.39), channel_id=1, source_target_pairs={{0,4},{1,5},{2,6},{3,7},{4,0},{5,1},{6,2},{7,3},{8,12},{9,13},{10,... | collective-permute-start | bytes 5384 | tf_op jit(solution)/shard_map/ppermute | solution.py:42
  14.6 5.4 %collective-permute-done.1 = f32[28,16]{1,0:T(8,128)S(1)} collective-permute-done((f32[28,16]{1,0:T(8,128)S(1)}, f32[28,16]{1,0:T(8,128)S(1)}, u32[]{:S(2)}, u32[]{:S(2)}) %collective-permute-start.1) | collective-permute-done | bytes 1824 | tf_op jit(solution)/shard_map/ppermute | solution.py:42
  20.0 2.8 %collective-permute-start.2 = (f32[28,16]{1,0:T(8,128)S(1)}, f32[28,16]{1,0:T(8,128)S(1)}, u32[]{:S(2)}, u32[]{:S(2)}) collective-permute-start(f32[28,16]{1,0:T(8,128)S(1)} %add.40), channel_id=1, source_target_pairs={{0,8},{1,9},{2,10},{3,11},{4,12},{5,13},{6,14},{7,15},{8,0},{9,1},... | collective-permute-start | bytes 5384 | tf_op jit(solution)/shard_map/ppermute | solution.py:42
  22.7 1.9 %collective-permute-done.2 = f32[28,16]{1,0:T(8,128)S(1)} collective-permute-done((f32[28,16]{1,0:T(8,128)S(1)}, f32[28,16]{1,0:T(8,128)S(1)}, u32[]{:S(2)}, u32[]{:S(2)}) %collective-permute-start.2) | collective-permute-done | bytes 1824 | tf_op jit(solution)/shard_map/ppermute | solution.py:42
  24.6 0.0 collective-permute-done.4.u_mate
  24.6 1.9 %turn.1.lhs = bf16[320,1792]{1,0:T(8,128)(2,1)S(1)} custom-call(s32[5]{0:T(128)S(1)} %stack.35.info, bf16[14,2,32,640]{3,2,1,0:T(8,128)(2,1)S(1)} %copy-done, bf16[14,2,32,640]{3,2,1,0:T(8,128)(2,1)S(1)} %collective-permute-done.4.u_mate), custom_call_target="tpu_custom_call" | custom-call | tf_op jit(solution)/shard_map/turn/pallas_call | solution.py:402
  26.6 0.0 collective-permute-done.3.rim
  26.6 0.1 collective-permute-start.7
  26.7 0.1 collective-permute-start.5
  26.8 3.7 %collective-permute-done.5 = f32[28,16]{1,0:T(8,128)S(1)} collective-permute-done((f32[28,16]{1,0:T(8,128)S(1)}, f32[28,16]{1,0:T(8,128)S(1)}, u32[]{:S(2)}, u32[]{:S(2)}) %collective-permute-start.5) | collective-permute-done | bytes 1824 | tf_op jit(solution)/shard_map/ppermute | solution.py:42
  30.5 0.0 collective-permute-done.6.x_mate
  30.5 0.0 collective-permute-done.7.rim_mate
  30.5 5.9 %activate.1 = (bf16[2688,640]{1,0:T(8,128)(2,1)S(1)}, bf16[2,2688,640]{2,1,0:T(8,128)(2,1)S(1)}, f32[14,640]{1,0:T(8,128)S(1)}, f32[14,640]{1,0:T(8,128)S(1)}) custom-call(s32[5]{0:T(128)S(1)} %stack.35.info, f32[28,16]{1,0:T(8,128)S(1)} %add.42.stats, bf16[14,2,32,640]{3,2,1,0:T(8,128)(2,1)} %x.7, ...), custom_call_target="tpu_custom_call" | custom-call | tf_op jit(solution)/shard_map/activate/pallas_call | solution.py:413
  36.4 8.8 %weight_terms.1 = (bf16[160,2560]{1,0:T(8,128)(2,1)}, f32[160,2560]{1,0:T(8,128)}, bf16[320,1600]{1,0:T(8,128)(2,1)}, f32[320,1600]{1,0:T(8,128)}) custom-call(s32[5]{0:T(128)S(1)} %stack.35.info, bf16[320,1792]{1,0:T(8,128)(2,1)S(1)} %turn.1.lhs, bf16[2688,640]{1,0:T(8,128)(2,1)S(1)} %get-tuple-element.55.mid, bf16[2,2688,640]{2,1,0:T(8,128)(2,1)S(1)} %get-tuple-element.56.side), custom_call_target="tpu_custom_call" | custom-call | tf_op jit(solution)/shard_map/weight_terms/pallas_call | solution.py:441
  45.3 2.0 %collective-permute-done.8.refs_1_ = bf16[9,160,640]{2,1,0:T(8,128)(2,1)} collective-permute-done((bf16[9,160,640]{2,1,0:T(8,128)(2,1)S(1)}, bf16[9,160,640]{2,1,0:T(8,128)(2,1)}, u32[]{:S(2)}, u32[]{:S(2)}) %collective-permute-start.8) | collective-permute-done | bytes 1843232 | tf_op jit(solution)/shard_map/ppermute | solution.py:42
  47.2 0.0 collective-permute-start.9
  47.2 1.7 %collective-permute-start.11 = (bf16[320,1600]{1,0:T(8,128)(2,1)}, bf16[320,1600]{1,0:T(8,128)(2,1)S(1)}, u32[]{:S(2)}, u32[]{:S(2)}) collective-permute-start(bf16[320,1600]{1,0:T(8,128)(2,1)} %get-tuple-element.57), channel_id=1, source_target_pairs={{0,16},{16,0},{1,17},{17,1},{2,18},{18,2},{3,19},{19,3},{4,20},{20... | collective-permute-start | bytes 3072008 | tf_op jit(solution)/shard_map/ppermute | solution.py:42
  49.0 1.6 %collective-permute-start.10 = (bf16[160,2560]{1,0:T(8,128)(2,1)}, bf16[160,2560]{1,0:T(8,128)(2,1)}, u32[]{:S(2)}, u32[]{:S(2)}) collective-permute-start(bf16[160,2560]{1,0:T(8,128)(2,1)} %get-tuple-element.63), channel_id=1, source_target_pairs={{0,4},{1,5},{2,6},{3,7},{4,0},{5,1},{6,2},{7,3},{8,12},{9,13},{10,... | collective-permute-start | bytes 2457608 | tf_op jit(solution)/shard_map/ppermute | solution.py:42
  50.5 0.9 collective-permute-start.12
  51.4 0.1 pad_add_fusion.places
  51.5 0.0 collective-permute-done.9.refs_2_
  51.5 2.0 %copy-done.2 = bf16[2688,640]{1,0:T(8,128)(2,1)S(1)} copy-done((bf16[2688,640]{1,0:T(8,128)(2,1)S(1)}, bf16[2688,640]{1,0:T(8,128)(2,1)}, u32[]{:S(2)}) %copy-start.2) | copy-done | bytes 3440664
  53.5 12.8 %conv_forward.1 = (bf16[14,2,32,640]{3,2,1,0:T(8,128)(2,1)}, bf16[9,640,640]{2,1,0:T(8,128)(2,1)S(1)}) custom-call(s32[5]{0:T(128)S(1)} %stack.35.info, s32[3]{0:T(128)S(1)} %pad_add_fusion.places, bf16[2688,640]{1,0:T(8,128)(2,1)S(1)} %copy-done.2, bf16[9,320,640]{2,1,0:T(8,128)(2,1)} %refs_0_.3, bf16[9,160,640]{2,1,0:T(8,128)(2,1)} %collective-permute-done.8.refs_1_, ...), custom_call_target="tpu_custom_call" | custom-call | tf_op jit(solution)/shard_map/conv_forward/pallas_call | solution.py:457
  66.3 3.4 %collective-permute-done.10.got = bf16[160,2560]{1,0:T(8,128)(2,1)} collective-permute-done((bf16[160,2560]{1,0:T(8,128)(2,1)}, bf16[160,2560]{1,0:T(8,128)(2,1)}, u32[]{:S(2)}, u32[]{:S(2)}) %collective-permute-start.10) | collective-permute-done | bytes 819232 | tf_op jit(solution)/shard_map/ppermute | solution.py:42
  69.7 1.3 %fold.5 = (bf16[80,2560]{1,0:T(8,128)(2,1)S(1)}, f32[80,2560]{1,0:T(8,128)S(1)}) custom-call(f32[160,2560]{1,0:T(8,128)S(1)} %copy-done.4, bf16[160,2560]{1,0:T(8,128)(2,1)} %collective-permute-done.10.got), custom_call_target="tpu_custom_call" | custom-call | tf_op jit(solution)/shard_map/fold/pallas_call | solution.py:426
  71.0 2.4 %collective-permute-done.11.got = bf16[320,1600]{1,0:T(8,128)(2,1)S(1)} collective-permute-done((bf16[320,1600]{1,0:T(8,128)(2,1)}, bf16[320,1600]{1,0:T(8,128)(2,1)S(1)}, u32[]{:S(2)}, u32[]{:S(2)}) %collective-permute-start.11) | collective-permute-done | bytes 1024032 | tf_op jit(solution)/shard_map/ppermute | solution.py:42
  73.4 0.2 fold.6
  73.6 1.9 %collective-permute-start.13 = (bf16[160,1600]{1,0:T(8,128)(2,1)S(1)}, bf16[160,1600]{1,0:T(8,128)(2,1)S(1)}, u32[]{:S(2)}, u32[]{:S(2)}) collective-permute-start(bf16[160,1600]{1,0:T(8,128)(2,1)S(1)} %get-tuple-element.68), channel_id=1, source_target_pairs={{0,4},{1,5},{2,6},{3,7},{4,0},{5,1},{6,2},{7,3},{8,12},{9,13},{10,... | collective-permute-start | bytes 1536008 | tf_op jit(solution)/shard_map/ppermute | solution.py:42
  75.5 1.5 %collective-permute-start.14 = (bf16[80,2560]{1,0:T(8,128)(2,1)S(1)}, bf16[80,2560]{1,0:T(8,128)(2,1)S(1)}, u32[]{:S(2)}, u32[]{:S(2)}) collective-permute-start(bf16[80,2560]{1,0:T(8,128)(2,1)S(1)} %get-tuple-element.65), channel_id=1, source_target_pairs={{0,2},{1,3},{2,0},{3,1},{4,6},{5,7},{6,4},{7,5},{8,10},{9,11},{10,... | collective-permute-start | bytes 1228808 | tf_op jit(solution)/shard_map/ppermute | solution.py:42
  76.9 13.1 %conv_backward.1 = (f32[14,2,32,640]{3,2,1,0:T(8,128)S(1)}, f32[40,128]{1,0:T(8,128)S(1)}) custom-call(s32[5]{0:T(128)S(1)} %stack.35.info, bf16[14,2,32,640]{3,2,1,0:T(8,128)(2,1)S(1)} %copy-done, bf16[14,2,32,640]{3,2,1,0:T(8,128)(2,1)S(1)} %collective-permute-done.4.u_mate, bf16[14,32,640]{2,1,0:T(8,128)(2,1)S(1)} %collective-permute-done.12.rim, ...), custom_call_target="tpu_custom_call" | custom-call | tf_op jit(solution)/shard_map/conv_backward/pallas_call | solution.py:477
  90.1 0.0 collective-permute-done.14.got
  90.1 0.7 split.1
  90.9 1.6 %collective-permute-start.20 = (bf16[80,1280]{1,0:T(8,128)(2,1)S(1)}, bf16[80,1280]{1,0:T(8,128)(2,1)S(1)}, u32[]{:S(2)}, u32[]{:S(2)}) collective-permute-start(bf16[80,1280]{1,0:T(8,128)(2,1)S(1)} %get-tuple-element.79), channel_id=1, source_target_pairs={{0,16},{16,0},{1,17},{17,1},{2,18},{18,2},{3,19},{19,3},{4,20},{20... | collective-permute-start | bytes 614408 | tf_op jit(solution)/shard_map/ppermute | solution.py:42
  92.4 0.0 collective-permute-done.13.got
  92.4 0.1 fold.7
  92.5 0.6 collective-permute-start.19
  93.1 0.0 collective-permute-start.15
  93.1 1.2 collective-permute-done.15
  94.3 0.5 collective-permute-start.16
  94.8 3.3 %collective-permute-done.16 = f32[40,128]{1,0:T(8,128)S(1)} collective-permute-done((f32[40,128]{1,0:T(8,128)S(1)}, f32[40,128]{1,0:T(8,128)S(1)}, u32[]{:S(2)}, u32[]{:S(2)}) %collective-permute-start.16) | collective-permute-done | bytes 20512 | tf_op jit(solution)/shard_map/ppermute | solution.py:42
  98.1 2.6 %collective-permute-start.17 = (f32[40,128]{1,0:T(8,128)S(1)}, f32[40,128]{1,0:T(8,128)S(1)}, u32[]{:S(2)}, u32[]{:S(2)}) collective-permute-start(f32[40,128]{1,0:T(8,128)S(1)} %add.46), channel_id=1, source_target_pairs={{0,8},{1,9},{2,10},{3,11},{4,12},{5,13},{6,14},{7,15},{8,0},{9,1},... | collective-permute-start | bytes 61448 | tf_op jit(solution)/shard_map/ppermute | solution.py:42
  100.7 2.2 %collective-permute-done.17 = f32[40,128]{1,0:T(8,128)S(1)} collective-permute-done((f32[40,128]{1,0:T(8,128)S(1)}, f32[40,128]{1,0:T(8,128)S(1)}, u32[]{:S(2)}, u32[]{:S(2)}) %collective-permute-start.17) | collective-permute-done | bytes 20512 | tf_op jit(solution)/shard_map/ppermute | solution.py:42
  102.9 1.5 %collective-permute-start.18 = (f32[40,128]{1,0:T(8,128)S(1)}, f32[40,128]{1,0:T(8,128)S(1)}, u32[]{:S(2)}, u32[]{:S(2)}) collective-permute-start(f32[40,128]{1,0:T(8,128)S(1)} %add.47), channel_id=1, source_target_pairs={{0,2},{1,3},{2,0},{3,1},{4,6},{5,7},{6,4},{7,5},{8,10},{9,11},{10,... | collective-permute-start | bytes 61448 | tf_op jit(solution)/shard_map/ppermute | solution.py:42
  104.4 2.3 %collective-permute-done.18 = f32[40,128]{1,0:T(8,128)S(1)} collective-permute-done((f32[40,128]{1,0:T(8,128)S(1)}, f32[40,128]{1,0:T(8,128)S(1)}, u32[]{:S(2)}, u32[]{:S(2)}) %collective-permute-start.18) | collective-permute-done | bytes 20512 | tf_op jit(solution)/shard_map/ppermute | solution.py:42
  106.7 0.0 collective-permute-done.20.got
  106.7 2.5 %collective-permute-start.21 = (bf16[40,1280]{1,0:T(8,128)(2,1)S(1)}, bf16[40,1280]{1,0:T(8,128)(2,1)S(1)}, u32[]{:S(2)}, u32[]{:S(2)}) collective-permute-start(bf16[40,1280]{1,0:T(8,128)(2,1)S(1)} %get-tuple-element.86), channel_id=1, source_target_pairs={{0,8},{1,9},{2,10},{3,11},{4,12},{5,13},{6,14},{7,15},{8,0},{9,1},... | collective-permute-start | bytes 307208 | tf_op jit(solution)/shard_map/ppermute | solution.py:42
  109.3 0.1 fold.9
  109.4 0.5 collective-permute-start.22
  109.9 3.3 %input_grad.1 = bf16[14,2,32,640]{3,2,1,0:T(8,128)(2,1)} custom-call(f32[40,128]{1,0:T(8,128)S(1)} %add.48.sums, f32[14,2,32,640]{3,2,1,0:T(8,128)S(1)} %get-tuple-element.90.grad, bf16[14,2,32,640]{3,2,1,0:T(8,128)(2,1)} %x.7, bf16[14,2,32,640]{3,2,1,0:T(8,128)(2,1)S(1)} %copy-done, f32[14,640]{1,0:T(8,128)S(1)} %get-tuple-element.73.mean, ...), custom_call_target="tpu_custom_call" | custom-call | tf_op jit(solution)/shard_map/input_grad/pallas_call | solution.py:503
  113.2 2.6 %collective-permute-done.21 = bf16[40,1280]{1,0:T(8,128)(2,1)S(1)} collective-permute-done((bf16[40,1280]{1,0:T(8,128)(2,1)S(1)}, bf16[40,1280]{1,0:T(8,128)(2,1)S(1)}, u32[]{:S(2)}, u32[]{:S(2)}) %collective-permute-start.21) | collective-permute-done | bytes 102432 | tf_op jit(solution)/shard_map/ppermute | solution.py:42
  115.8 0.9 collective-permute-start.23
  116.7 2.8 %collective-permute-done.23 = f32[10,128]{1,0:T(8,128)S(1)} collective-permute-done((f32[10,128]{1,0:T(8,128)S(1)}, f32[10,128]{1,0:T(8,128)S(1)}, u32[]{:S(2)}, u32[]{:S(2)}) %collective-permute-start.23) | collective-permute-done | bytes 5152 | tf_op jit(solution)/shard_map/ppermute | solution.py:42
  119.4 0.6 slice_bitcast_fusion
  120.0 0.0 collective-permute-done.22
  120.1 0.2 reshape.18
  120.3 1.0 copy.11
  (33 shorter events, 0.2 us)
Async XLA Ops:
  0.7 6.2 %copy-start = (bf16[14,2,32,640]{3,2,1,0:T(8,128)(2,1)S(1)}, bf16[14,2,32,640]{3,2,1,0:T(8,128)(2,1)}, u32[]{:S(2)}) copy-start(bf16[14,2,32,640]{3,2,1,0:T(8,128)(2,1)} %u.7) | copy-start | bytes 3440644
  3.9 22.7 %copy-start.5 = (bf16[14,32,640]{2,1,0:T(8,128)(2,1)}, bf16[14,32,640]{2,1,0:T(8,128)(2,1)S(1)}, u32[]{:S(2)}) copy-start(bf16[14,32,640]{2,1,0:T(8,128)(2,1)S(1)} %get-tuple-element.71) | copy-start | bytes 1720324
  3.9 43.3 %collective-permute-start.8 = (bf16[9,160,640]{2,1,0:T(8,128)(2,1)S(1)}, bf16[9,160,640]{2,1,0:T(8,128)(2,1)}, u32[]{:S(2)}, u32[]{:S(2)}) collective-permute-start(bf16[9,160,640]{2,1,0:T(8,128)(2,1)S(1)} %get-tuple-element.59), channel_id=1, source_target_pairs={{0,16},{16,0},{1,17},{17,1},{2,18},{18,2},{3,19},{19,3},{4,20},{20... | collective-permute-start | bytes 5529608 | tf_op jit(solution)/shard_map/ppermute | solution.py:42
  6.9 17.7 %collective-permute-start.4 = (bf16[14,2,32,640]{3,2,1,0:T(8,128)(2,1)S(1)}, bf16[14,2,32,640]{3,2,1,0:T(8,128)(2,1)S(1)}, u32[]{:S(2)}, u32[]{:S(2)}) collective-permute-start(bf16[14,2,32,640]{3,2,1,0:T(8,128)(2,1)S(1)} %copy-done), channel_id=1, source_target_pairs={{0,1},{1,0},{2,3},{3,2},{4,5},{5,4},{6,7},{7,6},{8,9},{9,8},{10,11... | collective-permute-start | bytes 3440648 | tf_op jit(solution)/shard_map/ppermute | solution.py:42
  6.9 19.6 %collective-permute-start.3 = (bf16[14,32,640]{2,1,0:T(8,128)(2,1)S(1)}, bf16[14,32,640]{2,1,0:T(8,128)(2,1)S(1)}, u32[]{:S(2)}, u32[]{:S(2)}) collective-permute-start(bf16[14,32,640]{2,1,0:T(8,128)(2,1)S(1)} %get-tuple-element.51), channel_id=1, source_target_pairs={{1,2},{2,1},{3,4},{4,3},{5,6},{6,5},{7,8},{8,7},{9,10},{10,9},{11,... | collective-permute-start | bytes 1720328 | tf_op jit(solution)/shard_map/ppermute | solution.py:401
  7.6 22.9 %collective-permute-start.6 = (bf16[14,2,32,640]{3,2,1,0:T(8,128)(2,1)}, bf16[14,2,32,640]{3,2,1,0:T(8,128)(2,1)S(1)}, u32[]{:S(2)}, u32[]{:S(2)}) collective-permute-start(bf16[14,2,32,640]{3,2,1,0:T(8,128)(2,1)} %x.7), channel_id=1, source_target_pairs={{0,1},{1,0},{2,3},{3,2},{4,5},{5,4},{6,7},{7,6},{8,9},{9,8},{10,11... | collective-permute-start | bytes 3440648 | tf_op jit(solution)/shard_map/ppermute | solution.py:42
  10.5 2.3 %collective-permute-start = (f32[28,16]{1,0:T(8,128)S(1)}, f32[28,16]{1,0:T(8,128)S(1)}, u32[]{:S(2)}, u32[]{:S(2)}) collective-permute-start(f32[28,16]{1,0:T(8,128)S(1)} %get-tuple-element.50), channel_id=1, source_target_pairs={{0,1},{1,0},{2,3},{3,2},{4,5},{5,4},{6,7},{7,6},{8,9},{9,8},{10,11... | collective-permute-start | bytes 5384 | tf_op jit(solution)/shard_map/ppermute | solution.py:42
  12.8 7.1 %collective-permute-start.1 = (f32[28,16]{1,0:T(8,128)S(1)}, f32[28,16]{1,0:T(8,128)S(1)}, u32[]{:S(2)}, u32[]{:S(2)}) collective-permute-start(f32[28,16]{1,0:T(8,128)S(1)} %add.39), channel_id=1, source_target_pairs={{0,4},{1,5},{2,6},{3,7},{4,0},{5,1},{6,2},{7,3},{8,12},{9,13},{10,... | collective-permute-start | bytes 5384 | tf_op jit(solution)/shard_map/ppermute | solution.py:42
  20.0 4.6 %collective-permute-start.2 = (f32[28,16]{1,0:T(8,128)S(1)}, f32[28,16]{1,0:T(8,128)S(1)}, u32[]{:S(2)}, u32[]{:S(2)}) collective-permute-start(f32[28,16]{1,0:T(8,128)S(1)} %add.40), channel_id=1, source_target_pairs={{0,8},{1,9},{2,10},{3,11},{4,12},{5,13},{6,14},{7,15},{8,0},{9,1},... | collective-permute-start | bytes 5384 | tf_op jit(solution)/shard_map/ppermute | solution.py:42
  24.6 2.1 %copy-start.6 = (f32[640]{0:T(1024)S(1)}, f32[640]{0:T(1024)}, u32[]{:S(2)}) copy-start(f32[640]{0:T(1024)} %param.6) | copy-start | bytes 7684
  24.6 2.2 %copy-start.7 = (f32[640]{0:T(1024)S(1)}, f32[640]{0:T(1024)}, u32[]{:S(2)}) copy-start(f32[640]{0:T(1024)} %param.7) | copy-start | bytes 7684
  26.6 3.9 %collective-permute-start.7 = (bf16[14,32,640]{2,1,0:T(8,128)(2,1)S(1)}, bf16[14,32,640]{2,1,0:T(8,128)(2,1)S(1)}, u32[]{:S(2)}, u32[]{:S(2)}) collective-permute-start(bf16[14,32,640]{2,1,0:T(8,128)(2,1)S(1)} %collective-permute-done.3.rim), channel_id=1, source_target_pairs={{0,1},{1,0},{2,3},{3,2},{4,5},{5,4},{6,7},{7,6},{8,9},{9,8},{10,11... | collective-permute-start | bytes 1720328 | tf_op jit(solution)/shard_map/ppermute | solution.py:42
  26.7 3.8 %collective-permute-start.5 = (f32[28,16]{1,0:T(8,128)S(1)}, f32[28,16]{1,0:T(8,128)S(1)}, u32[]{:S(2)}, u32[]{:S(2)}) collective-permute-start(f32[28,16]{1,0:T(8,128)S(1)} %add.41), channel_id=1, source_target_pairs={{0,2},{1,3},{2,0},{3,1},{4,6},{5,7},{6,4},{7,5},{8,10},{9,11},{10,... | collective-permute-start | bytes 5384 | tf_op jit(solution)/shard_map/ppermute | solution.py:42
  36.4 8.8 %copy-start.1 = (bf16[2688,640]{1,0:T(8,128)(2,1)}, bf16[2688,640]{1,0:T(8,128)(2,1)S(1)}, u32[]{:S(2)}) copy-start(bf16[2688,640]{1,0:T(8,128)(2,1)S(1)} %get-tuple-element.55.mid) | copy-start | bytes 10321924
  47.2 4.3 %collective-permute-start.9 = (bf16[9,160,640]{2,1,0:T(8,128)(2,1)}, bf16[9,160,640]{2,1,0:T(8,128)(2,1)}, u32[]{:S(2)}, u32[]{:S(2)}) collective-permute-start(bf16[9,160,640]{2,1,0:T(8,128)(2,1)} %collective-permute-done.8.refs_1_), channel_id=1, source_target_pairs={{0,1},{1,0},{2,3},{3,2},{4,5},{5,4},{6,7},{7,6},{8,9},{9,8},{10,11... | collective-permute-start | bytes 5529608 | tf_op jit(solution)/shard_map/ppermute | solution.py:42
  47.2 26.1 %collective-permute-start.11 = (bf16[320,1600]{1,0:T(8,128)(2,1)}, bf16[320,1600]{1,0:T(8,128)(2,1)S(1)}, u32[]{:S(2)}, u32[]{:S(2)}) collective-permute-start(bf16[320,1600]{1,0:T(8,128)(2,1)} %get-tuple-element.57), channel_id=1, source_target_pairs={{0,16},{16,0},{1,17},{17,1},{2,18},{18,2},{3,19},{19,3},{4,20},{20... | collective-permute-start | bytes 3072008 | tf_op jit(solution)/shard_map/ppermute | solution.py:42
  49.0 20.7 %collective-permute-start.10 = (bf16[160,2560]{1,0:T(8,128)(2,1)}, bf16[160,2560]{1,0:T(8,128)(2,1)}, u32[]{:S(2)}, u32[]{:S(2)}) collective-permute-start(bf16[160,2560]{1,0:T(8,128)(2,1)} %get-tuple-element.63), channel_id=1, source_target_pairs={{0,4},{1,5},{2,6},{3,7},{4,0},{5,1},{6,2},{7,3},{8,12},{9,13},{10,... | collective-permute-start | bytes 2457608 | tf_op jit(solution)/shard_map/ppermute | solution.py:42
  50.5 26.4 %collective-permute-start.12 = (bf16[14,32,640]{2,1,0:T(8,128)(2,1)}, bf16[14,32,640]{2,1,0:T(8,128)(2,1)S(1)}, u32[]{:S(2)}, u32[]{:S(2)}) collective-permute-start(bf16[14,32,640]{2,1,0:T(8,128)(2,1)} %copy-done.5), channel_id=1, source_target_pairs={{1,2},{2,1},{3,4},{4,3},{5,6},{6,5},{7,8},{8,7},{9,10},{10,9},{11,... | collective-permute-start | bytes 1720328 | tf_op jit(solution)/shard_map/ppermute | solution.py:411
  51.5 2.0 %copy-start.2 = (bf16[2688,640]{1,0:T(8,128)(2,1)S(1)}, bf16[2688,640]{1,0:T(8,128)(2,1)}, u32[]{:S(2)}) copy-start(bf16[2688,640]{1,0:T(8,128)(2,1)} %copy-done.1) | copy-start | bytes 10321924
  53.5 16.2 %copy-start.4 = (f32[160,2560]{1,0:T(8,128)S(1)}, f32[160,2560]{1,0:T(8,128)}, u32[]{:S(2)}) copy-start(f32[160,2560]{1,0:T(8,128)} %get-tuple-element.62.kept) | copy-start | bytes 4915204
  66.3 7.1 %copy-start.3 = (f32[320,1600]{1,0:T(8,128)S(1)}, f32[320,1600]{1,0:T(8,128)}, u32[]{:S(2)}) copy-start(f32[320,1600]{1,0:T(8,128)} %get-tuple-element.66.kept) | copy-start | bytes 6144004
  73.6 18.9 %collective-permute-start.13 = (bf16[160,1600]{1,0:T(8,128)(2,1)S(1)}, bf16[160,1600]{1,0:T(8,128)(2,1)S(1)}, u32[]{:S(2)}, u32[]{:S(2)}) collective-permute-start(bf16[160,1600]{1,0:T(8,128)(2,1)S(1)} %get-tuple-element.68), channel_id=1, source_target_pairs={{0,4},{1,5},{2,6},{3,7},{4,0},{5,1},{6,2},{7,3},{8,12},{9,13},{10,... | collective-permute-start | bytes 1536008 | tf_op jit(solution)/shard_map/ppermute | solution.py:42
  75.5 14.6 %collective-permute-start.14 = (bf16[80,2560]{1,0:T(8,128)(2,1)S(1)}, bf16[80,2560]{1,0:T(8,128)(2,1)S(1)}, u32[]{:S(2)}, u32[]{:S(2)}) collective-permute-start(bf16[80,2560]{1,0:T(8,128)(2,1)S(1)} %get-tuple-element.65), channel_id=1, source_target_pairs={{0,2},{1,3},{2,0},{3,1},{4,6},{5,7},{6,4},{7,5},{8,10},{9,11},{10,... | collective-permute-start | bytes 1228808 | tf_op jit(solution)/shard_map/ppermute | solution.py:42
  90.9 15.8 %collective-permute-start.20 = (bf16[80,1280]{1,0:T(8,128)(2,1)S(1)}, bf16[80,1280]{1,0:T(8,128)(2,1)S(1)}, u32[]{:S(2)}, u32[]{:S(2)}) collective-permute-start(bf16[80,1280]{1,0:T(8,128)(2,1)S(1)} %get-tuple-element.79), channel_id=1, source_target_pairs={{0,16},{16,0},{1,17},{17,1},{2,18},{18,2},{3,19},{19,3},{4,20},{20... | collective-permute-start | bytes 614408 | tf_op jit(solution)/shard_map/ppermute | solution.py:42
  92.5 16.8 %collective-permute-start.19 = (bf16[80,1600]{1,0:T(8,128)(2,1)S(1)}, bf16[80,1600]{1,0:T(8,128)(2,1)S(1)}, u32[]{:S(2)}, u32[]{:S(2)}) collective-permute-start(bf16[80,1600]{1,0:T(8,128)(2,1)S(1)} %get-tuple-element.81), channel_id=1, source_target_pairs={{0,2},{1,3},{2,0},{3,1},{4,6},{5,7},{6,4},{7,5},{8,10},{9,11},{10,... | collective-permute-start | bytes 768008 | tf_op jit(solution)/shard_map/ppermute | solution.py:42
  93.1 1.2 collective-permute-start.15
  94.3 3.8 %collective-permute-start.16 = (f32[40,128]{1,0:T(8,128)S(1)}, f32[40,128]{1,0:T(8,128)S(1)}, u32[]{:S(2)}, u32[]{:S(2)}) collective-permute-start(f32[40,128]{1,0:T(8,128)S(1)} %add.45), channel_id=1, source_target_pairs={{0,4},{1,5},{2,6},{3,7},{4,0},{5,1},{6,2},{7,3},{8,12},{9,13},{10,... | collective-permute-start | bytes 61448 | tf_op jit(solution)/shard_map/ppermute | solution.py:42
  98.1 4.8 %collective-permute-start.17 = (f32[40,128]{1,0:T(8,128)S(1)}, f32[40,128]{1,0:T(8,128)S(1)}, u32[]{:S(2)}, u32[]{:S(2)}) collective-permute-start(f32[40,128]{1,0:T(8,128)S(1)} %add.46), channel_id=1, source_target_pairs={{0,8},{1,9},{2,10},{3,11},{4,12},{5,13},{6,14},{7,15},{8,0},{9,1},... | collective-permute-start | bytes 61448 | tf_op jit(solution)/shard_map/ppermute | solution.py:42
  102.9 3.8 %collective-permute-start.18 = (f32[40,128]{1,0:T(8,128)S(1)}, f32[40,128]{1,0:T(8,128)S(1)}, u32[]{:S(2)}, u32[]{:S(2)}) collective-permute-start(f32[40,128]{1,0:T(8,128)S(1)} %add.47), channel_id=1, source_target_pairs={{0,2},{1,3},{2,0},{3,1},{4,6},{5,7},{6,4},{7,5},{8,10},{9,11},{10,... | collective-permute-start | bytes 61448 | tf_op jit(solution)/shard_map/ppermute | solution.py:42
  106.7 9.0 %collective-permute-start.21 = (bf16[40,1280]{1,0:T(8,128)(2,1)S(1)}, bf16[40,1280]{1,0:T(8,128)(2,1)S(1)}, u32[]{:S(2)}, u32[]{:S(2)}) collective-permute-start(bf16[40,1280]{1,0:T(8,128)(2,1)S(1)} %get-tuple-element.86), channel_id=1, source_target_pairs={{0,8},{1,9},{2,10},{3,11},{4,12},{5,13},{6,14},{7,15},{8,0},{9,1},... | collective-permute-start | bytes 307208 | tf_op jit(solution)/shard_map/ppermute | solution.py:42
  109.4 10.7 %collective-permute-start.22 = (bf16[40,1600]{1,0:T(8,128)(2,1)S(1)}, bf16[40,1600]{1,0:T(8,128)(2,1)S(1)}, u32[]{:S(2)}, u32[]{:S(2)}) collective-permute-start(bf16[40,1600]{1,0:T(8,128)(2,1)S(1)} %get-tuple-element.88), channel_id=1, source_target_pairs={{0,8},{1,9},{2,10},{3,11},{4,12},{5,13},{6,14},{7,15},{8,0},{9,1},... | collective-permute-start | bytes 384008 | tf_op jit(solution)/shard_map/ppermute | solution.py:42
  115.8 3.7 %collective-permute-start.23 = (f32[10,128]{1,0:T(8,128)S(1)}, f32[10,128]{1,0:T(8,128)S(1)}, u32[]{:S(2)}, u32[]{:S(2)}) collective-permute-start(f32[10,128]{1,0:T(8,128)S(1)} %slice.11), channel_id=1, source_target_pairs={{0,16},{16,0},{1,17},{17,1},{2,18},{18,2},{3,19},{19,3},{4,20},{20... | collective-permute-start | bytes 15368 | tf_op jit(solution)/shard_map/ppermute | solution.py:42

commit v3 on v2

--- a/solution.py
+++ b/solution.py
@@ -216,77 +216,61 @@
     kept_out[...] = kept[cut:] + got[cut:].astype(F32)
 
 
-def fold_second_kernel(kept, got, sent_out, kept_out):
-    sent, own = second_bit(kept[...] + got[...].astype(F32))
-    sent_out[...] = sent.astype(BF16)
-    kept_out[...] = own
-
-
 def part_kernel(part, info, kept, got, sent_out, kept_out):
     low, high = halves(kept[...] + got[...].astype(F32), part)
     sent_out[...] = jnp.where(info[3] == 0, high, low).astype(BF16)
     kept_out[...] = jnp.where(info[3] == 0, low, high)
 
 
-def conv_kernel(info, places, mid, *refs):
-    parts, (x, out, w, side, total, sem) = refs[:-6], refs[-6:]
+def conv_kernel(info, mid, w, x, out, side):
+    images, _, columns, channels = x.shape
+    block = images * columns
+    first = pl.multiple_of(2 * info[0] * block, 64)
+    taps = w.shape[0]
+
+    def fill(k, carry):
+        at = pl.multiple_of(k * columns, columns)
+        down, up = shifted(mid[pl.ds(first + at, columns), :].astype(F32))
+        side[0, pl.ds(at, columns), :] = down.astype(BF16)
+        side[1, pl.ds(at, columns), :] = up.astype(BF16)
+        return carry
+
+    lax.fori_loop(0, 4 * images, fill, 0)
+    rhs = w[...].reshape(taps * channels, channels)
+    for r in range(2):
+        lhs = []
+        for t in range(taps):
+            at = (r + t // 3) * block
+            if t % 3 == 1:
+                lhs.append(mid[pl.ds(pl.multiple_of(first + at, 64), block), :])
+            else:
+                lhs.append(side[(t % 3) // 2, at : at + block, :])
+        value = jnp.dot(jnp.concatenate(lhs, axis=1), rhs, preferred_element_type=F32)
+        value = value.reshape(images, columns, channels)
+        out[:, r] = (x[:, r].astype(F32) + value).astype(BF16)
+
+
+def back_kernel(info, places, *refs):
+    u, u_mate, rim, x, mean, rstd, gain, bias, out, sums, w, part, one, two, sem = refs[-15:]
+    pieces = refs[:-15]
     images, _, columns, channels = x.shape
     block = images * columns
     taps = w.shape[0]
-    own = pl.multiple_of(2 * info[0] * block, 64)
+    core = info[0]
     copies = [
         [
             pltpu.make_async_copy(
-                part.at[t],
-                w.at[t, pl.ds(pl.multiple_of(places[k], 32), part.shape[1]), :],
+                piece.at[t],
+                w.at[t, pl.ds(pl.multiple_of(places[k], 32), piece.shape[1]), :],
                 sem.at[t, k],
             )
-            for k, part in enumerate(parts)
+            for k, piece in enumerate(pieces)
         ]
         for t in range(taps)
     ]
     for tap in copies:
         for c in tap:
             c.start()
-
-    def fill(k, carry):
-        at = pl.multiple_of(k * columns, columns)
-        down, up = shifted(mid[pl.ds(own + at, columns), :].astype(F32))
-        side[0, pl.ds(at, columns), :] = down.astype(BF16)
-        side[1, pl.ds(at, columns), :] = up.astype(BF16)
-        return carry
-
-    lax.fori_loop(0, 4 * images, fill, 0)
-    for pair in (range(0, 2), range(2, 4), range(4, taps)):
-        first = pair[0]
-        for t in pair:
-            for c in copies[t]:
-                c.wait()
-        rhs = w[first : first + len(pair)].reshape(len(pair) * channels, channels)
-        for r in range(2):
-            lhs = []
-            for t in pair:
-                at = (r + t // 3) * block
-                if t % 3 == 1:
-                    lhs.append(mid[pl.ds(pl.multiple_of(own + at, 64), block), :])
-                else:
-                    lhs.append(side[(t % 3) // 2, at : at + block, :])
-            got = jnp.dot(jnp.concatenate(lhs, axis=1), rhs, preferred_element_type=F32)
-            at = slice(r * block, (r + 1) * block)
-            if first == 0:
-                total[at] = got
-            elif pair[-1] + 1 < taps:
-                total[at] += got
-            else:
-                value = (total[at] + got).reshape(images, columns, channels)
-                out[:, r] = (x[:, r].astype(F32) + value).astype(BF16)
-
-
-def back_kernel(info, u, u_mate, rim, w, x, mean, rstd, gain, bias, out, sums, part, one, two):
-    images, _, columns, channels = x.shape
-    block = images * columns
-    taps = w.shape[0]
-    core = info[0]
 
     def fill(load, row):
         def step(img, carry):
@@ -305,15 +289,23 @@
     fill(lambda img: u_mate[img, core], 3 - 3 * core)
     fill(lambda img: rim[img], 3 * core)
 
-    rhs = jnp.concatenate([w[t] for t in range(taps)], axis=1)
-    for r in range(2):
-        lhs = jnp.concatenate([
-            part[2 - t % 3, (r + 2 - t // 3) * block : (r + 3 - t // 3) * block, :]
-            for t in range(taps)
-        ], axis=1)
-        out[:, r] = lax.dot_general(
-            lhs, rhs, (((1,), (1,)), ((), ())), preferred_element_type=F32
-        ).reshape(images, columns, channels)
+    for group in (range(0, 4), range(4, taps)):
+        for t in group:
+            for c in copies[t]:
+                c.wait()
+        rhs = jnp.concatenate([w[t] for t in group], axis=1)
+        for r in range(2):
+            lhs = jnp.concatenate([
+                part[2 - t % 3, (r + 2 - t // 3) * block : (r + 3 - t // 3) * block, :]
+                for t in group
+            ], axis=1)
+            value = lax.dot_general(
+                lhs, rhs, (((1,), (1,)), ((), ())), preferred_element_type=F32
+            ).reshape(images, columns, channels)
+            if group[0] == 0:
+                out[:, r] = value
+            else:
+                out[:, r] += value
 
     def finish(img, carry):
         first = jnp.zeros((1, channels), F32)
@@ -421,10 +413,10 @@
         [S] + [V] * 7, "activate",
     )(info, stats, inputs, x_mate, rim_x, rim_x_mate, gain_row, bias_row)
 
-    def fold(kept, got, kernel=fold_kernel):
+    def fold(kept, got):
         shape = (kept.shape[0] // 2, kept.shape[1])
         return kernel_call(
-            kernel, 8, (struct(shape, BF16), struct(shape, F32)), [V, V], "fold"
+            fold_kernel, 8, (struct(shape, BF16), struct(shape, F32)), [V, V], "fold"
         )(kept, got)
 
     def split(kept, got):
@@ -443,6 +435,7 @@
         tuple(pltpu.HBM(*shape) for shape in shapes), [S] + [V] * 3, "weight_terms",
         [pltpu.VMEM(*shape) for shape in shapes] + [pltpu.SemaphoreType.DMA((10,))], (H,) * 4,
     )(info, lhs, act_mid, act_side)
+    sent_a, sent_b, rim_u = lax.optimization_barrier((sent_a, sent_b, rim_u))
     got_a = swap(sent_a, "space", 4)
     got_b = swap(sent_b, "dp", 1) if two else swap(sent_b, "space", 4)
 
@@ -454,62 +447,58 @@
     else:
         spots = jnp.zeros((1,), jnp.int32)
         w_parts = [lax.all_gather(conv_weight, "dp", axis=1, tiled=True)]
-    mixed, weights = kernel_call(
-        conv_kernel, 32,
-        (struct(inputs.shape, BF16), struct((taps, channels, channels), BF16)),
-        [S, S, V] + [H] * len(w_parts) + [V], "conv_forward",
-        [
-            pltpu.VMEM((2, 4 * block, channels), BF16),
-            pltpu.VMEM((2 * block, channels), F32),
-            pltpu.SemaphoreType.DMA((taps, len(w_parts))),
-        ],
-    )(
-        after(info, sent_b), spots.astype(jnp.int32), act_mid,
-        *[in_hbm(value) for value in w_parts], inputs,
-    )
-
-    sent_a, kept_a = fold(kept_a, after(got_a, mixed))
-    got_a = swap(sent_a, "space", 2)
-    got_b = after(got_b, sent_a)
-    sent_b, kept_b = fold(kept_b, got_b, fold_second_kernel if two else fold_kernel)
-    got_b = swap(sent_b, "space", 4 if two else 2)
-
-    grad, sums = kernel_call(
+    grad, sums, weights = kernel_call(
         back_kernel, 32,
-        (struct(inputs.shape, F32), struct((40, LANES), F32)), [S] + [V] * 9, "conv_backward",
+        (
+            struct(inputs.shape, F32),
+            struct((40, LANES), F32),
+            struct((taps, channels, channels), BF16),
+        ),
+        [S, S] + [H] * len(w_parts) + [V] * 8, "conv_backward",
         [
             pltpu.VMEM((3, 4 * block, channels), BF16),
             pltpu.VMEM((images, channels), F32),
             pltpu.VMEM((images, channels), F32),
+            pltpu.SemaphoreType.DMA((taps, len(w_parts))),
         ],
     )(
-        after(info, sent_a, sent_b), upstream, u_mate, rim_u, weights, inputs, mean, rstd,
-        gain_row, bias_row,
+        after(info, sent_b), spots.astype(jnp.int32), *[in_hbm(value) for value in w_parts],
+        upstream, u_mate, rim_u, inputs, mean, rstd, gain_row, bias_row,
     )
 
+    base = images + images % 2
+    last = base + 2 * channels // LANES
+    totals = sums[base:last]
     if two:
         sent_a, kept_a = split(kept_a, after(got_a, sums))
         got_a = swap(sent_a, "dp", 1)
         sent_b, kept_b = fold(kept_b, after(got_b, sent_a))
         got_b = swap(sent_b, "space", 2)
-        sums = after(sums, sent_b)
-    for place in [0] + list(range(2, bits)) + [1]:
+        totals = totals + after(swap(totals, "dp", 1), sent_b)
+    else:
+        totals = lax.psum(totals, "dp")
+    sums = jnp.concatenate([sums[:base], totals, sums[last:]])
+    for place in [0] + list(range(2, bits)):
         sums = sums + swap(sums, "space", 1 << place)
     sent_a, kept_a = fold(kept_a, after(got_a, sums))
+    got_a = swap(sent_a, "space", 2)
+    sent_b, kept_b = fold(kept_b, after(got_b, sent_a))
+    got_b = swap(sent_b, "space", 4 if two else 2)
+    sums = after(sums, sent_b)
+    sums = sums + swap(sums, "space", 2)
+    input_grad = kernel_call(
+        functools.partial(input_kernel, size), 16, struct(inputs.shape, BF16), [V] * 7, "input_grad"
+    )(sums, grad, inputs, upstream, mean, rstd, gain_row)
+    totals = sums[base:last].reshape(2, channels)
+    sent_a, kept_a = fold(kept_a, after(got_a, input_grad))
     got_a = swap(sent_a, "space", 8)
     sent_b, kept_b = fold(kept_b, after(got_b, sent_a))
     got_b = swap(sent_b, "space", 8)
-    sums = after(sums, sent_b)
-    input_grad = kernel_call(
-        functools.partial(input_kernel, size), 16, struct(inputs.shape, BF16), [V] * 7, "input_grad"
-    )(sums, grad, inputs, upstream, mean, rstd, gain_row)
-
-    base = images + images % 2
-    totals = sums[base : base + 2 * channels // LANES]
-    totals = totals + after(swap(totals, "dp", 1), input_grad) if two else lax.psum(totals, "dp")
-    totals = totals.reshape(2, channels)
-
-    got_a = after(got_a, input_grad)
+    mixed = kernel_call(
+        conv_kernel, 32, struct(inputs.shape, BF16), [S] + [V] * 3, "conv_forward",
+        [pltpu.VMEM((2, 4 * block, channels), BF16)],
+    )(after(info, sent_b), act_mid, weights, inputs)
+    got_a = after(got_a, mixed)
     weight_grad = jnp.concatenate(
         [kept_a + got_a.astype(F32), kept_b + got_b.astype(F32)], axis=1
     )

time: 122 us -> 116 us (0.951)
  waiting for transfers between devices: 35.3 us -> 27.3 us
  starting transfers between devices: 29.5 us -> 31.8 us
    ppermute x22, waiting for transfers between devices: 35.3 us -> 27.3 us  [swap(): return lax.ppermute(value, axis, [(i, i ^ bit) for i in range(count)])]
    ppermute x22, starting transfers between devices: 27.9 us -> 30.2 us  [swap(): return lax.ppermute(value, axis, [(i, i ^ bit) for i in range(count)])]
    pallas_call x6, Pallas kernels: 14.5 us -> 12.4 us  [the longest x1 11.9 us: body(): kernel_call(conv_kernel, 32, struct(inputs.shape, BF16), [S] + [V] * 3, '...]
    pallas_call x1, Pallas kernels: 13.1 us -> 14.4 us  [body(): kernel_call(back_kernel, 32, (struct(inputs.shape, F32), struct((40, LANE...]
    unnamed x17 -> x19, local copies, waits for them, and re-layouts: 2.98 us -> 2.87 us
  transfers between devices with their start and end apart: 24 -> 24, of which waited for: 13 -> 12; matrix products, arithmetic and copies ran while one was open for 1% -> 1% of each run, Pallas kernels for 40% -> 42%
where the time goes in v3:
time: 116 us
  Pallas kernels  51.8 us (45%)
  starting transfers between devices  31.8 us (27%)
  waiting for transfers between devices  27.3 us (24%)
  local copies, waits for them, and re-layouts  3.75 us (3%)
    ppermute x22, starting transfers between devices, swap(): return lax.ppermute(value, axis, [(i, i ^ bit) for i in range(count)])  30.2 us
    ppermute x22, waiting for transfers between devices, swap(): return lax.ppermute(value, axis, [(i, i ^ bit) for i in range(count)])  27.3 us
    pallas_call x1, Pallas kernels, body(): kernel_call(back_kernel, 32, (struct(inputs.shape, F32), struct((40, LANE...  14.4 us
    pallas_call x1, Pallas kernels, body(): kernel_call(conv_kernel, 32, struct(inputs.shape, BF16), [S] + [V] * 3, '...  11.9 us
    pallas_call x1, Pallas kernels, body(): kernel_call(functools.partial(grad_kernel, block, two), 28, tuple((pltpu....  9.03 us
    pallas_call x1, Pallas kernels, body(): kernel_call(functools.partial(act_kernel, size), 24, (struct((6 * block,...  5.93 us
    pallas_call x1, Pallas kernels, body(): kernel_call(functools.partial(input_kernel, size), 16, struct(inputs.shap...  3.45 us
    pallas_call x1, Pallas kernels, body(): kernel_call(stats_kernel, 16, tuple(out_shape), [S, V, H] + [H] * (len(op...  3.15 us
  transfers between devices with their start and end apart: 24, of which 12 were waited for; matrix products, arithmetic and copies ran while one was open for 1% of the time, Pallas kernels for 42%

profile of v3, /device:TPU:0, one launch (start us, length us, event | category | flops | bytes accessed | tf_op | source)
XLA Modules:
  0.0 115.8 jit_solution(1488623626798912436)
XLA Ops:
  0.7 0.1 stack.35.info
  0.7 3.1 %stats.1 = (f32[28,16]{1,0:T(8,128)S(1)}, bf16[14,32,640]{2,1,0:T(8,128)(2,1)S(1)}, bf16[14,32,640]{2,1,0:T(8,128)(2,1)S(1)}, bf16[9,160,640]{2,1,0:T(8,128)(2,1)S(1)}) custom-call(s32[5]{0:T(128)S(1)} %stack.35.info, bf16[14,2,32,640]{3,2,1,0:T(8,128)(2,1)} %x.7, bf16[14,2,32,640]{3,2,1,0:T(8,128)(2,1)} %u.5, bf16[9,320,640]{2,1,0:T(8,128)(2,1)} %refs_0_.3), custom_call_target="tpu_custom_call" | custom-call | tf_op jit(solution)/shard_map/stats/pallas_call | solution.py:387
  3.9 3.0 %collective-permute-start.11 = (bf16[9,160,640]{2,1,0:T(8,128)(2,1)S(1)}, bf16[9,160,640]{2,1,0:T(8,128)(2,1)}, u32[]{:S(2)}, u32[]{:S(2)}) collective-permute-start(bf16[9,160,640]{2,1,0:T(8,128)(2,1)S(1)} %get-tuple-element.67), channel_id=1, source_target_pairs={{0,16},{16,0},{1,17},{17,1},{2,18},{18,2},{3,19},{19,3},{4,20},{20... | collective-permute-start | bytes 5529608 | tf_op jit(solution)/shard_map/ppermute | solution.py:42
  6.9 0.0 collective-permute-start.4
  6.9 0.7 collective-permute-start.3
  7.6 2.9 %collective-permute-start.6 = (bf16[14,2,32,640]{3,2,1,0:T(8,128)(2,1)}, bf16[14,2,32,640]{3,2,1,0:T(8,128)(2,1)S(1)}, u32[]{:S(2)}, u32[]{:S(2)}) collective-permute-start(bf16[14,2,32,640]{3,2,1,0:T(8,128)(2,1)} %x.7), channel_id=1, source_target_pairs={{0,1},{1,0},{2,3},{3,2},{4,5},{5,4},{6,7},{7,6},{8,9},{9,8},{10,11... | collective-permute-start | bytes 3440648 | tf_op jit(solution)/shard_map/ppermute | solution.py:42
  10.5 0.1 collective-permute-start
  10.6 2.2 %collective-permute-done = f32[28,16]{1,0:T(8,128)S(1)} collective-permute-done((f32[28,16]{1,0:T(8,128)S(1)}, f32[28,16]{1,0:T(8,128)S(1)}, u32[]{:S(2)}, u32[]{:S(2)}) %collective-permute-start) | collective-permute-done | bytes 1824 | tf_op jit(solution)/shard_map/ppermute | solution.py:42
  12.8 1.7 %collective-permute-start.1 = (f32[28,16]{1,0:T(8,128)S(1)}, f32[28,16]{1,0:T(8,128)S(1)}, u32[]{:S(2)}, u32[]{:S(2)}) collective-permute-start(f32[28,16]{1,0:T(8,128)S(1)} %add.39), channel_id=1, source_target_pairs={{0,4},{1,5},{2,6},{3,7},{4,0},{5,1},{6,2},{7,3},{8,12},{9,13},{10,... | collective-permute-start | bytes 5384 | tf_op jit(solution)/shard_map/ppermute | solution.py:42
  14.6 5.4 %collective-permute-done.1 = f32[28,16]{1,0:T(8,128)S(1)} collective-permute-done((f32[28,16]{1,0:T(8,128)S(1)}, f32[28,16]{1,0:T(8,128)S(1)}, u32[]{:S(2)}, u32[]{:S(2)}) %collective-permute-start.1) | collective-permute-done | bytes 1824 | tf_op jit(solution)/shard_map/ppermute | solution.py:42
  20.0 2.8 %collective-permute-start.2 = (f32[28,16]{1,0:T(8,128)S(1)}, f32[28,16]{1,0:T(8,128)S(1)}, u32[]{:S(2)}, u32[]{:S(2)}) collective-permute-start(f32[28,16]{1,0:T(8,128)S(1)} %add.40), channel_id=1, source_target_pairs={{0,8},{1,9},{2,10},{3,11},{4,12},{5,13},{6,14},{7,15},{8,0},{9,1},... | collective-permute-start | bytes 5384 | tf_op jit(solution)/shard_map/ppermute | solution.py:42
  22.7 1.9 %collective-permute-done.2 = f32[28,16]{1,0:T(8,128)S(1)} collective-permute-done((f32[28,16]{1,0:T(8,128)S(1)}, f32[28,16]{1,0:T(8,128)S(1)}, u32[]{:S(2)}, u32[]{:S(2)}) %collective-permute-start.2) | collective-permute-done | bytes 1824 | tf_op jit(solution)/shard_map/ppermute | solution.py:42
  24.6 0.0 collective-permute-done.4.u_mate.refs_4_
  24.6 1.9 %turn.1.lhs = bf16[320,1792]{1,0:T(8,128)(2,1)S(1)} custom-call(s32[5]{0:T(128)S(1)} %stack.35.info, bf16[14,2,32,640]{3,2,1,0:T(8,128)(2,1)S(1)} %copy-done, bf16[14,2,32,640]{3,2,1,0:T(8,128)(2,1)S(1)} %collective-permute-done.4.u_mate.refs_4_), custom_call_target="tpu_custom_call" | custom-call | tf_op jit(solution)/shard_map/turn/pallas_call | solution.py:394
  26.6 0.0 collective-permute-done.3.rim
  26.6 0.1 collective-permute-start.5
  26.7 0.1 collective-permute-start.7
  26.7 3.6 %collective-permute-done.5 = f32[28,16]{1,0:T(8,128)S(1)} collective-permute-done((f32[28,16]{1,0:T(8,128)S(1)}, f32[28,16]{1,0:T(8,128)S(1)}, u32[]{:S(2)}, u32[]{:S(2)}) %collective-permute-start.5) | collective-permute-done | bytes 1824 | tf_op jit(solution)/shard_map/ppermute | solution.py:42
  30.4 0.9 collective-permute-start.8
  31.3 0.0 collective-permute-done.6.x_mate
  31.3 0.0 collective-permute-done.7.rim_mate
  31.3 5.9 %activate.1 = (bf16[2688,640]{1,0:T(8,128)(2,1)S(1)}, bf16[2,2688,640]{2,1,0:T(8,128)(2,1)S(1)}, f32[14,640]{1,0:T(8,128)S(1)}, f32[14,640]{1,0:T(8,128)S(1)}) custom-call(s32[5]{0:T(128)S(1)} %stack.35.info, f32[28,16]{1,0:T(8,128)S(1)} %add.42.stats, bf16[14,2,32,640]{3,2,1,0:T(8,128)(2,1)} %x.7, ...), custom_call_target="tpu_custom_call" | custom-call | tf_op jit(solution)/shard_map/activate/pallas_call | solution.py:405
  37.3 9.0 %weight_terms.1 = (bf16[160,2560]{1,0:T(8,128)(2,1)}, f32[160,2560]{1,0:T(8,128)}, bf16[320,1600]{1,0:T(8,128)(2,1)}, f32[320,1600]{1,0:T(8,128)}) custom-call(s32[5]{0:T(128)S(1)} %stack.35.info, bf16[320,1792]{1,0:T(8,128)(2,1)S(1)} %turn.1.lhs, bf16[2688,640]{1,0:T(8,128)(2,1)S(1)} %get-tuple-element.56.mid, bf16[2,2688,640]{2,1,0:T(8,128)(2,1)S(1)} %get-tuple-element.57.side), custom_call_target="tpu_custom_call" | custom-call | tf_op jit(solution)/shard_map/weight_terms/pallas_call | solution.py:433
  46.3 0.8 copy-done.5
  47.1 0.1 collective-permute-done.11.refs_1_
  47.2 1.3 %collective-permute-start.12 = (bf16[9,160,640]{2,1,0:T(8,128)(2,1)}, bf16[9,160,640]{2,1,0:T(8,128)(2,1)}, u32[]{:S(2)}, u32[]{:S(2)}) collective-permute-start(bf16[9,160,640]{2,1,0:T(8,128)(2,1)} %collective-permute-done.11.refs_1_), channel_id=1, source_target_pairs={{0,1},{1,0},{2,3},{3,2},{4,5},{5,4},{6,7},{7,6},{8,9},{9,8},{10,11... | collective-permute-start | bytes 5529608 | tf_op jit(solution)/shard_map/ppermute | solution.py:42
  48.5 0.5 collective-permute-start.9
  49.0 1.5 %collective-permute-start.10 = (bf16[160,2560]{1,0:T(8,128)(2,1)}, bf16[160,2560]{1,0:T(8,128)(2,1)}, u32[]{:S(2)}, u32[]{:S(2)}) collective-permute-start(bf16[160,2560]{1,0:T(8,128)(2,1)} %get-tuple-element.65), channel_id=1, source_target_pairs={{0,4},{1,5},{2,6},{3,7},{4,0},{5,1},{6,2},{7,3},{8,12},{9,13},{10,... | collective-permute-start | bytes 2457608 | tf_op jit(solution)/shard_map/ppermute | solution.py:42
  50.5 0.1 pad_add_fusion.places
  50.6 1.6 %collective-permute-done.12.refs_2_ = bf16[9,160,640]{2,1,0:T(8,128)(2,1)} collective-permute-done((bf16[9,160,640]{2,1,0:T(8,128)(2,1)}, bf16[9,160,640]{2,1,0:T(8,128)(2,1)}, u32[]{:S(2)}, u32[]{:S(2)}) %collective-permute-start.12) | collective-permute-done | bytes 1843232 | tf_op jit(solution)/shard_map/ppermute | solution.py:42
  52.3 1.1 copy-done.6
  53.3 14.4 %conv_backward.1 = (f32[14,2,32,640]{3,2,1,0:T(8,128)S(1)}, f32[40,128]{1,0:T(8,128)S(1)}, bf16[9,640,640]{2,1,0:T(8,128)(2,1)S(1)}) custom-call(s32[5]{0:T(128)S(1)} %stack.35.info, s32[3]{0:T(128)S(1)} %pad_add_fusion.places, bf16[9,320,640]{2,1,0:T(8,128)(2,1)} %refs_0_.3, bf16[9,160,640]{2,1,0:T(8,128)(2,1)} %collective-permute-done.11.refs_1_, ...), custom_call_target="tpu_custom_call" | custom-call | tf_op jit(solution)/shard_map/conv_backward/pallas_call | solution.py:450
  67.8 0.9 collective-permute-start.15
  68.7 1.0 collective-permute-done.10.got
  69.7 1.5 %split.1 = (bf16[160,1280]{1,0:T(8,128)(2,1)S(1)}, f32[160,1280]{1,0:T(8,128)S(1)}) custom-call(s32[5]{0:T(128)S(1)} %stack.35.info, f32[160,2560]{1,0:T(8,128)S(1)} %copy-done.4, bf16[160,2560]{1,0:T(8,128)(2,1)} %collective-permute-done.10.got), custom_call_target="tpu_custom_call" | custom-call | tf_op jit(solution)/shard_map/split/pallas_call | solution.py:424
  71.1 1.1 collective-permute-start.14
  72.3 2.8 %collective-permute-done.9.got = bf16[320,1600]{1,0:T(8,128)(2,1)S(1)} collective-permute-done((bf16[320,1600]{1,0:T(8,128)(2,1)}, bf16[320,1600]{1,0:T(8,128)(2,1)S(1)}, u32[]{:S(2)}, u32[]{:S(2)}) %collective-permute-start.9) | collective-permute-done | bytes 1024032 | tf_op jit(solution)/shard_map/ppermute | solution.py:42
  75.1 0.2 fold.5
  75.3 0.3 collective-permute-start.13
  75.6 0.0 collective-permute-done.15
  75.6 0.1 collective-permute-start.16
  75.7 1.2 %collective-permute-done.16 = f32[40,128]{1,0:T(8,128)S(1)} collective-permute-done((f32[40,128]{1,0:T(8,128)S(1)}, f32[40,128]{1,0:T(8,128)S(1)}, u32[]{:S(2)}, u32[]{:S(2)}) %collective-permute-start.16) | collective-permute-done | bytes 20512 | tf_op jit(solution)/shard_map/ppermute | solution.py:42
  76.9 4.6 %collective-permute-start.17 = (f32[40,128]{1,0:T(8,128)S(1)}, f32[40,128]{1,0:T(8,128)S(1)}, u32[]{:S(2)}, u32[]{:S(2)}) collective-permute-start(f32[40,128]{1,0:T(8,128)S(1)} %fusion), channel_id=1, source_target_pairs={{0,4},{1,5},{2,6},{3,7},{4,0},{5,1},{6,2},{7,3},{8,12},{9,13},{10,... | collective-permute-start | bytes 61448 | tf_op jit(solution)/shard_map/ppermute | solution.py:42
  81.5 1.8 %collective-permute-done.17 = f32[40,128]{1,0:T(8,128)S(1)} collective-permute-done((f32[40,128]{1,0:T(8,128)S(1)}, f32[40,128]{1,0:T(8,128)S(1)}, u32[]{:S(2)}, u32[]{:S(2)}) %collective-permute-start.17) | collective-permute-done | bytes 20512 | tf_op jit(solution)/shard_map/ppermute | solution.py:42
  83.3 0.8 collective-permute-start.18
  84.0 3.9 %collective-permute-done.18 = f32[40,128]{1,0:T(8,128)S(1)} collective-permute-done((f32[40,128]{1,0:T(8,128)S(1)}, f32[40,128]{1,0:T(8,128)S(1)}, u32[]{:S(2)}, u32[]{:S(2)}) %collective-permute-start.18) | collective-permute-done | bytes 20512 | tf_op jit(solution)/shard_map/ppermute | solution.py:42
  88.0 0.1 fold.6
  88.1 0.1 collective-permute-start.20
  88.2 0.1 fold.7
  88.3 2.9 %collective-permute-start.19 = (bf16[80,1600]{1,0:T(8,128)(2,1)S(1)}, bf16[80,1600]{1,0:T(8,128)(2,1)S(1)}, u32[]{:S(2)}, u32[]{:S(2)}) collective-permute-start(bf16[80,1600]{1,0:T(8,128)(2,1)S(1)} %get-tuple-element.84), channel_id=1, source_target_pairs={{0,4},{1,5},{2,6},{3,7},{4,0},{5,1},{6,2},{7,3},{8,12},{9,13},{10,... | collective-permute-start | bytes 768008 | tf_op jit(solution)/shard_map/ppermute | solution.py:42
  91.1 2.5 %collective-permute-start.21 = (f32[40,128]{1,0:T(8,128)S(1)}, f32[40,128]{1,0:T(8,128)S(1)}, u32[]{:S(2)}, u32[]{:S(2)}) collective-permute-start(f32[40,128]{1,0:T(8,128)S(1)} %add.48), channel_id=1, source_target_pairs={{0,2},{1,3},{2,0},{3,1},{4,6},{5,7},{6,4},{7,5},{8,10},{9,11},{10,... | collective-permute-start | bytes 61448 | tf_op jit(solution)/shard_map/ppermute | solution.py:42
  93.6 1.8 %collective-permute-done.21 = f32[40,128]{1,0:T(8,128)S(1)} collective-permute-done((f32[40,128]{1,0:T(8,128)S(1)}, f32[40,128]{1,0:T(8,128)S(1)}, u32[]{:S(2)}, u32[]{:S(2)}) %collective-permute-start.21) | collective-permute-done | bytes 20512 | tf_op jit(solution)/shard_map/ppermute | solution.py:42
  95.4 3.4 %input_grad.1 = bf16[14,2,32,640]{3,2,1,0:T(8,128)(2,1)} custom-call(f32[40,128]{1,0:T(8,128)S(1)} %add.49.sums, f32[14,2,32,640]{3,2,1,0:T(8,128)S(1)} %get-tuple-element.87.grad, bf16[14,2,32,640]{3,2,1,0:T(8,128)(2,1)} %x.7, bf16[14,2,32,640]{3,2,1,0:T(8,128)(2,1)S(1)} %copy-done, f32[14,640]{1,0:T(8,128)S(1)} %get-tuple-element.70.refs_7_.mean, ...), custom_call_target="tpu_custom_call" | custom-call | tf_op jit(solution)/shard_map/input_grad/pallas_call | solution.py:489
  98.8 0.0 collective-permute-done.20.got
  98.9 1.5 %collective-permute-start.22 = (bf16[40,1280]{1,0:T(8,128)(2,1)S(1)}, bf16[40,1280]{1,0:T(8,128)(2,1)S(1)}, u32[]{:S(2)}, u32[]{:S(2)}) collective-permute-start(bf16[40,1280]{1,0:T(8,128)(2,1)S(1)} %get-tuple-element.89), channel_id=1, source_target_pairs={{0,8},{1,9},{2,10},{3,11},{4,12},{5,13},{6,14},{7,15},{8,0},{9,1},... | collective-permute-start | bytes 307208 | tf_op jit(solution)/shard_map/ppermute | solution.py:42
  100.4 0.6 slice_bitcast_fusion
  101.0 0.0 collective-permute-done.19.got
  101.0 0.1 fold.9
  101.0 1.6 %collective-permute-start.23 = (bf16[40,1600]{1,0:T(8,128)(2,1)S(1)}, bf16[40,1600]{1,0:T(8,128)(2,1)S(1)}, u32[]{:S(2)}, u32[]{:S(2)}) collective-permute-start(bf16[40,1600]{1,0:T(8,128)(2,1)S(1)} %get-tuple-element.91), channel_id=1, source_target_pairs={{0,8},{1,9},{2,10},{3,11},{4,12},{5,13},{6,14},{7,15},{8,0},{9,1},... | collective-permute-start | bytes 384008 | tf_op jit(solution)/shard_map/ppermute | solution.py:42
  102.6 11.9 %conv_forward.1 = bf16[14,2,32,640]{3,2,1,0:T(8,128)(2,1)} custom-call(s32[5]{0:T(128)S(1)} %stack.35.info, bf16[2688,640]{1,0:T(8,128)(2,1)S(1)} %copy-done.2, bf16[9,640,640]{2,1,0:T(8,128)(2,1)S(1)} %get-tuple-element.93.w, bf16[14,2,32,640]{3,2,1,0:T(8,128)(2,1)} %x.7), custom_call_target="tpu_custom_call" | custom-call | tf_op jit(solution)/shard_map/conv_forward/pallas_call | solution.py:497
  114.5 0.0 collective-permute-done.22
  114.5 0.0 collective-permute-done.23
  114.6 0.2 reshape.18
  114.8 1.0 copy.11
  (38 shorter events, 0.2 us)
Async XLA Ops:
  0.7 6.2 %copy-start = (bf16[14,2,32,640]{3,2,1,0:T(8,128)(2,1)S(1)}, bf16[14,2,32,640]{3,2,1,0:T(8,128)(2,1)}, u32[]{:S(2)}) copy-start(bf16[14,2,32,640]{3,2,1,0:T(8,128)(2,1)} %u.5) | copy-start | bytes 3440644
  3.9 43.3 %collective-permute-start.11 = (bf16[9,160,640]{2,1,0:T(8,128)(2,1)S(1)}, bf16[9,160,640]{2,1,0:T(8,128)(2,1)}, u32[]{:S(2)}, u32[]{:S(2)}) collective-permute-start(bf16[9,160,640]{2,1,0:T(8,128)(2,1)S(1)} %get-tuple-element.67), channel_id=1, source_target_pairs={{0,16},{16,0},{1,17},{17,1},{2,18},{18,2},{3,19},{19,3},{4,20},{20... | collective-permute-start | bytes 5529608 | tf_op jit(solution)/shard_map/ppermute | solution.py:42
  6.9 17.7 %collective-permute-start.4 = (bf16[14,2,32,640]{3,2,1,0:T(8,128)(2,1)S(1)}, bf16[14,2,32,640]{3,2,1,0:T(8,128)(2,1)S(1)}, u32[]{:S(2)}, u32[]{:S(2)}) collective-permute-start(bf16[14,2,32,640]{3,2,1,0:T(8,128)(2,1)S(1)} %copy-done), channel_id=1, source_target_pairs={{0,1},{1,0},{2,3},{3,2},{4,5},{5,4},{6,7},{7,6},{8,9},{9,8},{10,11... | collective-permute-start | bytes 3440648 | tf_op jit(solution)/shard_map/ppermute | solution.py:42
  6.9 19.6 %collective-permute-start.3 = (bf16[14,32,640]{2,1,0:T(8,128)(2,1)S(1)}, bf16[14,32,640]{2,1,0:T(8,128)(2,1)S(1)}, u32[]{:S(2)}, u32[]{:S(2)}) collective-permute-start(bf16[14,32,640]{2,1,0:T(8,128)(2,1)S(1)} %get-tuple-element.52), channel_id=1, source_target_pairs={{1,2},{2,1},{3,4},{4,3},{5,6},{6,5},{7,8},{8,7},{9,10},{10,9},{11,... | collective-permute-start | bytes 1720328 | tf_op jit(solution)/shard_map/ppermute | solution.py:393
  7.6 23.7 %collective-permute-start.6 = (bf16[14,2,32,640]{3,2,1,0:T(8,128)(2,1)}, bf16[14,2,32,640]{3,2,1,0:T(8,128)(2,1)S(1)}, u32[]{:S(2)}, u32[]{:S(2)}) collective-permute-start(bf16[14,2,32,640]{3,2,1,0:T(8,128)(2,1)} %x.7), channel_id=1, source_target_pairs={{0,1},{1,0},{2,3},{3,2},{4,5},{5,4},{6,7},{7,6},{8,9},{9,8},{10,11... | collective-permute-start | bytes 3440648 | tf_op jit(solution)/shard_map/ppermute | solution.py:42
  10.5 2.3 %collective-permute-start = (f32[28,16]{1,0:T(8,128)S(1)}, f32[28,16]{1,0:T(8,128)S(1)}, u32[]{:S(2)}, u32[]{:S(2)}) collective-permute-start(f32[28,16]{1,0:T(8,128)S(1)} %get-tuple-element.51), channel_id=1, source_target_pairs={{0,1},{1,0},{2,3},{3,2},{4,5},{5,4},{6,7},{7,6},{8,9},{9,8},{10,11... | collective-permute-start | bytes 5384 | tf_op jit(solution)/shard_map/ppermute | solution.py:42
  12.8 7.1 %collective-permute-start.1 = (f32[28,16]{1,0:T(8,128)S(1)}, f32[28,16]{1,0:T(8,128)S(1)}, u32[]{:S(2)}, u32[]{:S(2)}) collective-permute-start(f32[28,16]{1,0:T(8,128)S(1)} %add.39), channel_id=1, source_target_pairs={{0,4},{1,5},{2,6},{3,7},{4,0},{5,1},{6,2},{7,3},{8,12},{9,13},{10,... | collective-permute-start | bytes 5384 | tf_op jit(solution)/shard_map/ppermute | solution.py:42
  20.0 4.6 %collective-permute-start.2 = (f32[28,16]{1,0:T(8,128)S(1)}, f32[28,16]{1,0:T(8,128)S(1)}, u32[]{:S(2)}, u32[]{:S(2)}) collective-permute-start(f32[28,16]{1,0:T(8,128)S(1)} %add.40), channel_id=1, source_target_pairs={{0,8},{1,9},{2,10},{3,11},{4,12},{5,13},{6,14},{7,15},{8,0},{9,1},... | collective-permute-start | bytes 5384 | tf_op jit(solution)/shard_map/ppermute | solution.py:42
  24.6 6.7 %copy-start.7 = (f32[640]{0:T(1024)S(1)}, f32[640]{0:T(1024)}, u32[]{:S(2)}) copy-start(f32[640]{0:T(1024)} %param.6) | copy-start | bytes 7684
  24.6 6.7 %copy-start.8 = (f32[640]{0:T(1024)S(1)}, f32[640]{0:T(1024)}, u32[]{:S(2)}) copy-start(f32[640]{0:T(1024)} %param.7) | copy-start | bytes 7684
  26.6 3.8 %collective-permute-start.5 = (f32[28,16]{1,0:T(8,128)S(1)}, f32[28,16]{1,0:T(8,128)S(1)}, u32[]{:S(2)}, u32[]{:S(2)}) collective-permute-start(f32[28,16]{1,0:T(8,128)S(1)} %add.41), channel_id=1, source_target_pairs={{0,2},{1,3},{2,0},{3,1},{4,6},{5,7},{6,4},{7,5},{8,10},{9,11},{10,... | collective-permute-start | bytes 5384 | tf_op jit(solution)/shard_map/ppermute | solution.py:42
  26.7 4.7 %collective-permute-start.7 = (bf16[14,32,640]{2,1,0:T(8,128)(2,1)S(1)}, bf16[14,32,640]{2,1,0:T(8,128)(2,1)S(1)}, u32[]{:S(2)}, u32[]{:S(2)}) collective-permute-start(bf16[14,32,640]{2,1,0:T(8,128)(2,1)S(1)} %collective-permute-done.3.rim), channel_id=1, source_target_pairs={{0,1},{1,0},{2,3},{3,2},{4,5},{5,4},{6,7},{7,6},{8,9},{9,8},{10,11... | collective-permute-start | bytes 1720328 | tf_op jit(solution)/shard_map/ppermute | solution.py:42
  30.4 15.9 %collective-permute-start.8 = (bf16[14,32,640]{2,1,0:T(8,128)(2,1)S(1)}, bf16[14,32,640]{2,1,0:T(8,128)(2,1)S(1)}, u32[]{:S(2)}, u32[]{:S(2)}) collective-permute-start(bf16[14,32,640]{2,1,0:T(8,128)(2,1)S(1)} %get-tuple-element.62), channel_id=1, source_target_pairs={{1,2},{2,1},{3,4},{4,3},{5,6},{6,5},{7,8},{8,7},{9,10},{10,9},{11,... | collective-permute-start | bytes 1720328 | tf_op jit(solution)/shard_map/ppermute | solution.py:403
  37.3 9.1 %copy-start.1 = (bf16[2688,640]{1,0:T(8,128)(2,1)}, bf16[2688,640]{1,0:T(8,128)(2,1)S(1)}, u32[]{:S(2)}) copy-start(bf16[2688,640]{1,0:T(8,128)(2,1)S(1)} %get-tuple-element.56.mid) | copy-start | bytes 10321924
  46.3 0.8 copy-start.5
  47.2 5.0 %collective-permute-start.12 = (bf16[9,160,640]{2,1,0:T(8,128)(2,1)}, bf16[9,160,640]{2,1,0:T(8,128)(2,1)}, u32[]{:S(2)}, u32[]{:S(2)}) collective-permute-start(bf16[9,160,640]{2,1,0:T(8,128)(2,1)} %collective-permute-done.11.refs_1_), channel_id=1, source_target_pairs={{0,1},{1,0},{2,3},{3,2},{4,5},{5,4},{6,7},{7,6},{8,9},{9,8},{10,11... | collective-permute-start | bytes 5529608 | tf_op jit(solution)/shard_map/ppermute | solution.py:42
  48.5 26.6 %collective-permute-start.9 = (bf16[320,1600]{1,0:T(8,128)(2,1)}, bf16[320,1600]{1,0:T(8,128)(2,1)S(1)}, u32[]{:S(2)}, u32[]{:S(2)}) collective-permute-start(bf16[320,1600]{1,0:T(8,128)(2,1)} %get-tuple-element.63), channel_id=1, source_target_pairs={{0,16},{16,0},{1,17},{17,1},{2,18},{18,2},{3,19},{19,3},{4,20},{20... | collective-permute-start | bytes 3072008 | tf_op jit(solution)/shard_map/ppermute | solution.py:42
  49.0 20.7 %collective-permute-start.10 = (bf16[160,2560]{1,0:T(8,128)(2,1)}, bf16[160,2560]{1,0:T(8,128)(2,1)}, u32[]{:S(2)}, u32[]{:S(2)}) collective-permute-start(bf16[160,2560]{1,0:T(8,128)(2,1)} %get-tuple-element.65), channel_id=1, source_target_pairs={{0,4},{1,5},{2,6},{3,7},{4,0},{5,1},{6,2},{7,3},{8,12},{9,13},{10,... | collective-permute-start | bytes 2457608 | tf_op jit(solution)/shard_map/ppermute | solution.py:42
  52.3 1.1 copy-start.6
  53.3 16.3 %copy-start.4 = (f32[160,2560]{1,0:T(8,128)S(1)}, f32[160,2560]{1,0:T(8,128)}, u32[]{:S(2)}) copy-start(f32[160,2560]{1,0:T(8,128)} %get-tuple-element.64.kept) | copy-start | bytes 4915204
  67.7 7.3 %copy-start.3 = (f32[320,1600]{1,0:T(8,128)S(1)}, f32[320,1600]{1,0:T(8,128)}, u32[]{:S(2)}) copy-start(f32[320,1600]{1,0:T(8,128)} %get-tuple-element.58.kept) | copy-start | bytes 6144004
  67.8 7.8 %collective-permute-start.15 = (f32[10,128]{1,0:T(8,128)S(1)}, f32[10,128]{1,0:T(8,128)S(1)}, u32[]{:S(2)}, u32[]{:S(2)}) collective-permute-start(f32[10,128]{1,0:T(8,128)S(1)} %slice.21), channel_id=1, source_target_pairs={{0,16},{16,0},{1,17},{17,1},{2,18},{18,2},{3,19},{19,3},{4,20},{20... | collective-permute-start | bytes 15368 | tf_op jit(solution)/shard_map/ppermute | solution.py:42
  71.1 16.8 %collective-permute-start.14 = (bf16[160,1280]{1,0:T(8,128)(2,1)S(1)}, bf16[160,1280]{1,0:T(8,128)(2,1)S(1)}, u32[]{:S(2)}, u32[]{:S(2)}) collective-permute-start(bf16[160,1280]{1,0:T(8,128)(2,1)S(1)} %get-tuple-element.74), channel_id=1, source_target_pairs={{0,16},{16,0},{1,17},{17,1},{2,18},{18,2},{3,19},{19,3},{4,20},{20... | collective-permute-start | bytes 1228808 | tf_op jit(solution)/shard_map/ppermute | solution.py:42
  75.3 12.9 %collective-permute-start.13 = (bf16[160,1600]{1,0:T(8,128)(2,1)S(1)}, bf16[160,1600]{1,0:T(8,128)(2,1)S(1)}, u32[]{:S(2)}, u32[]{:S(2)}) collective-permute-start(bf16[160,1600]{1,0:T(8,128)(2,1)S(1)} %get-tuple-element.77), channel_id=1, source_target_pairs={{0,2},{1,3},{2,0},{3,1},{4,6},{5,7},{6,4},{7,5},{8,10},{9,11},{10,... | collective-permute-start | bytes 1536008 | tf_op jit(solution)/shard_map/ppermute | solution.py:42
  75.6 1.3 %collective-permute-start.16 = (f32[40,128]{1,0:T(8,128)S(1)}, f32[40,128]{1,0:T(8,128)S(1)}, u32[]{:S(2)}, u32[]{:S(2)}) collective-permute-start(f32[40,128]{1,0:T(8,128)S(1)} %pad_maximum_fusion.1), channel_id=1, source_target_pairs={{0,1},{1,0},{2,3},{3,2},{4,5},{5,4},{6,7},{7,6},{8,9},{9,8},{10,11... | collective-permute-start | bytes 61448 | tf_op jit(solution)/shard_map/ppermute | solution.py:42
  76.9 6.4 %collective-permute-start.17 = (f32[40,128]{1,0:T(8,128)S(1)}, f32[40,128]{1,0:T(8,128)S(1)}, u32[]{:S(2)}, u32[]{:S(2)}) collective-permute-start(f32[40,128]{1,0:T(8,128)S(1)} %fusion), channel_id=1, source_target_pairs={{0,4},{1,5},{2,6},{3,7},{4,0},{5,1},{6,2},{7,3},{8,12},{9,13},{10,... | collective-permute-start | bytes 61448 | tf_op jit(solution)/shard_map/ppermute | solution.py:42
  83.3 4.7 %collective-permute-start.18 = (f32[40,128]{1,0:T(8,128)S(1)}, f32[40,128]{1,0:T(8,128)S(1)}, u32[]{:S(2)}, u32[]{:S(2)}) collective-permute-start(f32[40,128]{1,0:T(8,128)S(1)} %add.47), channel_id=1, source_target_pairs={{0,8},{1,9},{2,10},{3,11},{4,12},{5,13},{6,14},{7,15},{8,0},{9,1},... | collective-permute-start | bytes 61448 | tf_op jit(solution)/shard_map/ppermute | solution.py:42
  88.1 10.8 %collective-permute-start.20 = (bf16[80,1280]{1,0:T(8,128)(2,1)S(1)}, bf16[80,1280]{1,0:T(8,128)(2,1)S(1)}, u32[]{:S(2)}, u32[]{:S(2)}) collective-permute-start(bf16[80,1280]{1,0:T(8,128)(2,1)S(1)} %get-tuple-element.81), channel_id=1, source_target_pairs={{0,2},{1,3},{2,0},{3,1},{4,6},{5,7},{6,4},{7,5},{8,10},{9,11},{10,... | collective-permute-start | bytes 614408 | tf_op jit(solution)/shard_map/ppermute | solution.py:42
  88.3 12.7 %collective-permute-start.19 = (bf16[80,1600]{1,0:T(8,128)(2,1)S(1)}, bf16[80,1600]{1,0:T(8,128)(2,1)S(1)}, u32[]{:S(2)}, u32[]{:S(2)}) collective-permute-start(bf16[80,1600]{1,0:T(8,128)(2,1)S(1)} %get-tuple-element.84), channel_id=1, source_target_pairs={{0,4},{1,5},{2,6},{3,7},{4,0},{5,1},{6,2},{7,3},{8,12},{9,13},{10,... | collective-permute-start | bytes 768008 | tf_op jit(solution)/shard_map/ppermute | solution.py:42
  91.1 4.2 %collective-permute-start.21 = (f32[40,128]{1,0:T(8,128)S(1)}, f32[40,128]{1,0:T(8,128)S(1)}, u32[]{:S(2)}, u32[]{:S(2)}) collective-permute-start(f32[40,128]{1,0:T(8,128)S(1)} %add.48), channel_id=1, source_target_pairs={{0,2},{1,3},{2,0},{3,1},{4,6},{5,7},{6,4},{7,5},{8,10},{9,11},{10,... | collective-permute-start | bytes 61448 | tf_op jit(solution)/shard_map/ppermute | solution.py:42
  95.4 7.2 %copy-start.2 = (bf16[2688,640]{1,0:T(8,128)(2,1)S(1)}, bf16[2688,640]{1,0:T(8,128)(2,1)}, u32[]{:S(2)}) copy-start(bf16[2688,640]{1,0:T(8,128)(2,1)} %copy-done.1) | copy-start | bytes 10321924
  98.9 15.6 %collective-permute-start.22 = (bf16[40,1280]{1,0:T(8,128)(2,1)S(1)}, bf16[40,1280]{1,0:T(8,128)(2,1)S(1)}, u32[]{:S(2)}, u32[]{:S(2)}) collective-permute-start(bf16[40,1280]{1,0:T(8,128)(2,1)S(1)} %get-tuple-element.89), channel_id=1, source_target_pairs={{0,8},{1,9},{2,10},{3,11},{4,12},{5,13},{6,14},{7,15},{8,0},{9,1},... | collective-permute-start | bytes 307208 | tf_op jit(solution)/shard_map/ppermute | solution.py:42
  101.0 13.5 %collective-permute-start.23 = (bf16[40,1600]{1,0:T(8,128)(2,1)S(1)}, bf16[40,1600]{1,0:T(8,128)(2,1)S(1)}, u32[]{:S(2)}, u32[]{:S(2)}) collective-permute-start(bf16[40,1600]{1,0:T(8,128)(2,1)S(1)} %get-tuple-element.91), channel_id=1, source_target_pairs={{0,8},{1,9},{2,10},{3,11},{4,12},{5,13},{6,14},{7,15},{8,0},{9,1},... | collective-permute-start | bytes 384008 | tf_op jit(solution)/shard_map/ppermute | solution.py:42

commit v4 on v3

--- a/solution.py
+++ b/solution.py
@@ -9,7 +9,7 @@
 
 GSIZE = 40
 EPS = 1e-05
-GROUP_A, GROUP_B = (0, 1, 2, 3), (4, 5, 6, 7, 8)
+GROUP_A, GROUP_B = (0, 1, 2, 3, 4), (5, 6, 7, 8)
 LANES = 128
 F32 = jnp.float32
 BF16 = jnp.bfloat16
@@ -222,6 +222,17 @@
     kept_out[...] = jnp.where(info[3] == 0, low, high)
 
 
+def last_kernel(kept_a, got_a, kept_b, got_b, out):
+    part = out.shape[2]
+    first = 0
+    for kept, got in ((kept_a, got_a), (kept_b, got_b)):
+        value = kept[...] + got[...].astype(F32)
+        count = value.shape[1] // part
+        for t in range(count):
+            out[first + t] = value[:, t * part : (t + 1) * part]
+        first += count
+
+
 def conv_kernel(info, mid, w, x, out, side):
     images, _, columns, channels = x.shape
     block = images * columns
@@ -251,8 +262,9 @@
 
 
 def back_kernel(info, places, *refs):
-    u, u_mate, rim, x, mean, rstd, gain, bias, out, sums, w, part, one, two, sem = refs[-15:]
-    pieces = refs[:-15]
+    pieces, refs = refs[:-17], refs[-17:]
+    u, u_mate, rim_there, x, mean, rstd, gain, bias, out, sums, w = refs[:11]
+    part, rim, one, two, sem, rim_sem = refs[11:]
     images, _, columns, channels = x.shape
     block = images * columns
     taps = w.shape[0]
@@ -268,7 +280,9 @@
         ]
         for t in range(taps)
     ]
-    for tap in copies:
+    rim_copy = pltpu.make_async_copy(rim_there, rim, rim_sem)
+    rim_copy.start()
+    for tap in copies[:4]:
         for c in tap:
             c.start()
 
@@ -287,6 +301,10 @@
     fill(lambda img: u[img, 0], 1)
     fill(lambda img: u[img, 1], 2)
     fill(lambda img: u_mate[img, core], 3 - 3 * core)
+    rim_copy.wait()
+    for tap in copies[4:]:
+        for c in tap:
+            c.start()
     fill(lambda img: rim[img], 3 * core)
 
     for group in (range(0, 4), range(4, taps)):
@@ -397,8 +415,11 @@
     )(info, upstream, u_mate)
     for place in [0] + list(range(2, bits)) + [1]:
         if place == 1:
-            stats, rim_x, lhs = lax.optimization_barrier((stats, rim_x, lhs))
-        stats = stats + swap(stats, "space", 1 << place)
+            stats, rim_x = lax.optimization_barrier((stats, rim_x))
+        step = swap(stats, "space", 1 << place)
+        if place == 2:
+            step, lhs = lax.optimization_barrier((step, lhs))
+        stats = stats + step
     rim_x_mate = swap(rim_x, "space", 1)
     rim_u = lax.ppermute(after(edge_u, stats), "space", pairs)
 
@@ -454,38 +475,42 @@
             struct((40, LANES), F32),
             struct((taps, channels, channels), BF16),
         ),
-        [S, S] + [H] * len(w_parts) + [V] * 8, "conv_backward",
+        [S, S] + [H] * len(w_parts) + [V, V, H] + [V] * 5, "conv_backward",
         [
             pltpu.VMEM((3, 4 * block, channels), BF16),
+            pltpu.VMEM(row_shape, BF16),
             pltpu.VMEM((images, channels), F32),
             pltpu.VMEM((images, channels), F32),
             pltpu.SemaphoreType.DMA((taps, len(w_parts))),
+            pltpu.SemaphoreType.DMA,
         ],
     )(
         after(info, sent_b), spots.astype(jnp.int32), *[in_hbm(value) for value in w_parts],
-        upstream, u_mate, rim_u, inputs, mean, rstd, gain_row, bias_row,
+        upstream, u_mate, in_hbm(rim_u), inputs, mean, rstd, gain_row, bias_row,
     )
 
     base = images + images % 2
     last = base + 2 * channels // LANES
+    for place in range(2):
+        sums = sums + swap(sums, "space", 1 << place)
     totals = sums[base:last]
     if two:
+        more = swap(totals, "dp", 1)
         sent_a, kept_a = split(kept_a, after(got_a, sums))
         got_a = swap(sent_a, "dp", 1)
         sent_b, kept_b = fold(kept_b, after(got_b, sent_a))
         got_b = swap(sent_b, "space", 2)
-        totals = totals + after(swap(totals, "dp", 1), sent_b)
+        totals = totals + after(more, sent_b)
     else:
         totals = lax.psum(totals, "dp")
     sums = jnp.concatenate([sums[:base], totals, sums[last:]])
-    for place in [0] + list(range(2, bits)):
+    for place in range(2, bits):
         sums = sums + swap(sums, "space", 1 << place)
     sent_a, kept_a = fold(kept_a, after(got_a, sums))
     got_a = swap(sent_a, "space", 2)
     sent_b, kept_b = fold(kept_b, after(got_b, sent_a))
     got_b = swap(sent_b, "space", 4 if two else 2)
     sums = after(sums, sent_b)
-    sums = sums + swap(sums, "space", 2)
     input_grad = kernel_call(
         functools.partial(input_kernel, size), 16, struct(inputs.shape, BF16), [V] * 7, "input_grad"
     )(sums, grad, inputs, upstream, mean, rstd, gain_row)
@@ -499,13 +524,13 @@
         [pltpu.VMEM((2, 4 * block, channels), BF16)],
     )(after(info, sent_b), act_mid, weights, inputs)
     got_a = after(got_a, mixed)
-    weight_grad = jnp.concatenate(
-        [kept_a + got_a.astype(F32), kept_b + got_b.astype(F32)], axis=1
-    )
-    weight_grad = weight_grad.reshape(weight_grad.shape[0], taps, -1)
+    wide = channels // 2 if two else channels
+    weight_grad = kernel_call(
+        last_kernel, 16, struct((taps, kept_a.shape[0], wide), F32), [V] * 4, "last"
+    )(kept_a, got_a, kept_b, got_b)
     if not two:
         weight_grad = lax.psum_scatter(weight_grad, "dp", scatter_dimension=2, tiled=True)
-    weight_grad = weight_grad.transpose(1, 2, 0)
+    weight_grad = weight_grad.transpose(0, 2, 1)
     return (mixed, input_grad, weight_grad, totals[0], totals[1])
 
 

time: 116 us -> 112 us (0.966)
  waiting for transfers between devices: 27.3 us -> 21.9 us
  local copies, waits for them, and re-layouts: 3.75 us -> 0.74 us
  starting transfers between devices: 31.8 us -> 34.5 us
  Pallas kernels: 51.8 us -> 53.8 us
    ppermute x22, waiting for transfers between devices: 27.3 us -> 21.9 us  [swap(): return lax.ppermute(value, axis, [(i, i ^ bit) for i in range(count)])]
    unnamed x19 -> x16, local copies, waits for them, and re-layouts: 2.87 us -> 0.04 us
    ppermute x22, starting transfers between devices: 30.2 us -> 32.9 us  [swap(): return lax.ppermute(value, axis, [(i, i ^ bit) for i in range(count)])]
  transfers between devices with their start and end apart: 24 -> 24, of which waited for: 12 -> 11; matrix products, arithmetic and copies ran while one was open for 1% -> 1% of each run, Pallas kernels for 42% -> 44%
where the time goes in v4:
time: 112 us
  Pallas kernels  53.8 us (48%)
  starting transfers between devices  34.5 us (31%)
  waiting for transfers between devices  21.9 us (20%)
    ppermute x22, starting transfers between devices, swap(): return lax.ppermute(value, axis, [(i, i ^ bit) for i in range(count)])  32.9 us
    ppermute x22, waiting for transfers between devices, swap(): return lax.ppermute(value, axis, [(i, i ^ bit) for i in range(count)])  21.9 us
    pallas_call x1, Pallas kernels, body(): kernel_call(back_kernel, 32, (struct(inputs.shape, F32), struct((40, LANE...  14.9 us
    pallas_call x1, Pallas kernels, body(): kernel_call(conv_kernel, 32, struct(inputs.shape, BF16), [S] + [V] * 3, '...  11.9 us
    pallas_call x1, Pallas kernels, body(): kernel_call(functools.partial(grad_kernel, block, two), 28, tuple((pltpu....  9 us
    pallas_call x1, Pallas kernels, body(): kernel_call(functools.partial(act_kernel, size), 24, (struct((6 * block,...  5.93 us
    pallas_call x1, Pallas kernels, body(): kernel_call(functools.partial(input_kernel, size), 16, struct(inputs.shap...  3.44 us
    pallas_call x1, Pallas kernels, body(): kernel_call(stats_kernel, 16, tuple(out_shape), [S, V, H] + [H] * (len(op...  3.15 us
  transfers between devices with their start and end apart: 24, of which 11 were waited for; matrix products, arithmetic and copies ran while one was open for 1% of the time, Pallas kernels for 44%

profile of v4, /device:TPU:0, one launch (start us, length us, event | category | flops | bytes accessed | tf_op | source)
XLA Modules:
  0.0 111.9 jit_solution(16577783138807102670)
XLA Ops:
  0.7 0.1 stack.35.info
  0.7 3.1 %stats.1 = (f32[28,16]{1,0:T(8,128)S(1)}, bf16[14,32,640]{2,1,0:T(8,128)(2,1)S(1)}, bf16[14,32,640]{2,1,0:T(8,128)(2,1)S(1)}, bf16[9,160,640]{2,1,0:T(8,128)(2,1)S(1)}) custom-call(s32[5]{0:T(128)S(1)} %stack.35.info, bf16[14,2,32,640]{3,2,1,0:T(8,128)(2,1)} %x.7, bf16[14,2,32,640]{3,2,1,0:T(8,128)(2,1)} %u.5, bf16[9,320,640]{2,1,0:T(8,128)(2,1)} %refs_0_.3), custom_call_target="tpu_custom_call" | custom-call | tf_op jit(solution)/shard_map/stats/pallas_call | solution.py:405
  3.9 0.0 copy-start.6
  3.9 0.0 copy-start.7
  3.9 3.0 %collective-permute-start.11 = (bf16[9,160,640]{2,1,0:T(8,128)(2,1)S(1)}, bf16[9,160,640]{2,1,0:T(8,128)(2,1)}, u32[]{:S(2)}, u32[]{:S(2)}) collective-permute-start(bf16[9,160,640]{2,1,0:T(8,128)(2,1)S(1)} %get-tuple-element.69), channel_id=1, source_target_pairs={{0,16},{16,0},{1,17},{17,1},{2,18},{18,2},{3,19},{19,3},{4,20},{20... | collective-permute-start | bytes 5529608 | tf_op jit(solution)/shard_map/ppermute | solution.py:42
  7.0 0.0 collective-permute-start.2
  7.0 0.7 collective-permute-start.4
  7.6 2.9 %collective-permute-start.6 = (bf16[14,2,32,640]{3,2,1,0:T(8,128)(2,1)}, bf16[14,2,32,640]{3,2,1,0:T(8,128)(2,1)S(1)}, u32[]{:S(2)}, u32[]{:S(2)}) collective-permute-start(bf16[14,2,32,640]{3,2,1,0:T(8,128)(2,1)} %x.7), channel_id=1, source_target_pairs={{0,1},{1,0},{2,3},{3,2},{4,5},{5,4},{6,7},{7,6},{8,9},{9,8},{10,11... | collective-permute-start | bytes 3440648 | tf_op jit(solution)/shard_map/ppermute | solution.py:42
  10.5 0.1 collective-permute-start
  10.6 2.2 %collective-permute-done = f32[28,16]{1,0:T(8,128)S(1)} collective-permute-done((f32[28,16]{1,0:T(8,128)S(1)}, f32[28,16]{1,0:T(8,128)S(1)}, u32[]{:S(2)}, u32[]{:S(2)}) %collective-permute-start) | collective-permute-done | bytes 1824 | tf_op jit(solution)/shard_map/ppermute | solution.py:42
  12.9 1.7 %collective-permute-start.1 = (f32[28,16]{1,0:T(8,128)S(1)}, f32[28,16]{1,0:T(8,128)S(1)}, u32[]{:S(2)}, u32[]{:S(2)}) collective-permute-start(f32[28,16]{1,0:T(8,128)S(1)} %add.33), channel_id=1, source_target_pairs={{0,4},{1,5},{2,6},{3,7},{4,0},{5,1},{6,2},{7,3},{8,12},{9,13},{10,... | collective-permute-start | bytes 5384 | tf_op jit(solution)/shard_map/ppermute | solution.py:42
  14.6 0.0 collective-permute-done.2.u_mate.refs_4_
  14.6 1.9 %turn.1.lhs = bf16[320,1792]{1,0:T(8,128)(2,1)S(1)} custom-call(s32[5]{0:T(128)S(1)} %stack.35.info, bf16[14,2,32,640]{3,2,1,0:T(8,128)(2,1)S(1)} %copy-done, bf16[14,2,32,640]{3,2,1,0:T(8,128)(2,1)S(1)} %collective-permute-done.2.u_mate.refs_4_), custom_call_target="tpu_custom_call" | custom-call | tf_op jit(solution)/shard_map/turn/pallas_call | solution.py:412
  16.5 3.5 %collective-permute-done.1 = f32[28,16]{1,0:T(8,128)S(1)} collective-permute-done((f32[28,16]{1,0:T(8,128)S(1)}, f32[28,16]{1,0:T(8,128)S(1)}, u32[]{:S(2)}, u32[]{:S(2)}) %collective-permute-start.1) | collective-permute-done | bytes 1824 | tf_op jit(solution)/shard_map/ppermute | solution.py:42
  20.0 2.8 %collective-permute-start.3 = (f32[28,16]{1,0:T(8,128)S(1)}, f32[28,16]{1,0:T(8,128)S(1)}, u32[]{:S(2)}, u32[]{:S(2)}) collective-permute-start(f32[28,16]{1,0:T(8,128)S(1)} %add.34), channel_id=1, source_target_pairs={{0,8},{1,9},{2,10},{3,11},{4,12},{5,13},{6,14},{7,15},{8,0},{9,1},... | collective-permute-start | bytes 5384 | tf_op jit(solution)/shard_map/ppermute | solution.py:42
  22.7 1.9 %collective-permute-done.3 = f32[28,16]{1,0:T(8,128)S(1)} collective-permute-done((f32[28,16]{1,0:T(8,128)S(1)}, f32[28,16]{1,0:T(8,128)S(1)}, u32[]{:S(2)}, u32[]{:S(2)}) %collective-permute-start.3) | collective-permute-done | bytes 1824 | tf_op jit(solution)/shard_map/ppermute | solution.py:42
  24.6 0.0 collective-permute-done.4.rim
  24.6 1.0 collective-permute-start.5
  25.6 0.0 collective-permute-start.7
  25.6 2.8 %collective-permute-done.5 = f32[28,16]{1,0:T(8,128)S(1)} collective-permute-done((f32[28,16]{1,0:T(8,128)S(1)}, f32[28,16]{1,0:T(8,128)S(1)}, u32[]{:S(2)}, u32[]{:S(2)}) %collective-permute-start.5) | collective-permute-done | bytes 1824 | tf_op jit(solution)/shard_map/ppermute | solution.py:42
  28.4 0.9 collective-permute-start.8
  29.4 0.0 collective-permute-done.6.x_mate
  29.4 0.0 collective-permute-done.7.rim_mate
  29.4 5.9 %activate.1 = (bf16[2688,640]{1,0:T(8,128)(2,1)S(1)}, bf16[2,2688,640]{2,1,0:T(8,128)(2,1)S(1)}, f32[14,640]{1,0:T(8,128)S(1)}, f32[14,640]{1,0:T(8,128)S(1)}) custom-call(s32[5]{0:T(128)S(1)} %stack.35.info, f32[28,16]{1,0:T(8,128)S(1)} %add.36.stats, bf16[14,2,32,640]{3,2,1,0:T(8,128)(2,1)} %x.7, ...), custom_call_target="tpu_custom_call" | custom-call | tf_op jit(solution)/shard_map/activate/pallas_call | solution.py:426
  35.3 9.0 %weight_terms.1 = (bf16[160,3200]{1,0:T(8,128)(2,1)}, f32[160,3200]{1,0:T(8,128)}, bf16[320,1280]{1,0:T(8,128)(2,1)}, f32[320,1280]{1,0:T(8,128)}) custom-call(s32[5]{0:T(128)S(1)} %stack.35.info, bf16[320,1792]{1,0:T(8,128)(2,1)S(1)} %turn.1.lhs, bf16[2688,640]{1,0:T(8,128)(2,1)S(1)} %get-tuple-element.58.mid, bf16[2,2688,640]{2,1,0:T(8,128)(2,1)S(1)} %get-tuple-element.59.side), custom_call_target="tpu_custom_call" | custom-call | tf_op jit(solution)/shard_map/weight_terms/pallas_call | solution.py:454
  44.3 0.0 collective-permute-done.8.refs_5_
  44.4 2.9 %collective-permute-done.11.refs_1_ = bf16[9,160,640]{2,1,0:T(8,128)(2,1)} collective-permute-done((bf16[9,160,640]{2,1,0:T(8,128)(2,1)S(1)}, bf16[9,160,640]{2,1,0:T(8,128)(2,1)}, u32[]{:S(2)}, u32[]{:S(2)}) %collective-permute-start.11) | collective-permute-done | bytes 1843232 | tf_op jit(solution)/shard_map/ppermute | solution.py:42
  47.2 0.2 collective-permute-start.12
  47.4 1.6 %collective-permute-start.10 = (bf16[160,3200]{1,0:T(8,128)(2,1)}, bf16[160,3200]{1,0:T(8,128)(2,1)S(1)}, u32[]{:S(2)}, u32[]{:S(2)}) collective-permute-start(bf16[160,3200]{1,0:T(8,128)(2,1)} %get-tuple-element.67), channel_id=1, source_target_pairs={{0,4},{1,5},{2,6},{3,7},{4,0},{5,1},{6,2},{7,3},{8,12},{9,13},{10,... | collective-permute-start | bytes 3072008 | tf_op jit(solution)/shard_map/ppermute | solution.py:42
  49.0 1.5 %collective-permute-start.9 = (bf16[320,1280]{1,0:T(8,128)(2,1)}, bf16[320,1280]{1,0:T(8,128)(2,1)}, u32[]{:S(2)}, u32[]{:S(2)}) collective-permute-start(bf16[320,1280]{1,0:T(8,128)(2,1)} %get-tuple-element.65), channel_id=1, source_target_pairs={{0,16},{16,0},{1,17},{17,1},{2,18},{18,2},{3,19},{19,3},{4,20},{20... | collective-permute-start | bytes 2457608 | tf_op jit(solution)/shard_map/ppermute | solution.py:42
  50.6 0.1 pad_add_fusion.places
  50.6 0.7 collective-permute-done.12.refs_2_
  51.4 14.9 %conv_backward.1 = (f32[14,2,32,640]{3,2,1,0:T(8,128)S(1)}, f32[40,128]{1,0:T(8,128)S(1)}, bf16[9,640,640]{2,1,0:T(8,128)(2,1)S(1)}) custom-call(s32[5]{0:T(128)S(1)} %stack.35.info, s32[3]{0:T(128)S(1)} %pad_add_fusion.places, bf16[9,320,640]{2,1,0:T(8,128)(2,1)} %refs_0_.3, bf16[9,160,640]{2,1,0:T(8,128)(2,1)} %collective-permute-done.11.refs_1_, ...), custom_call_target="tpu_custom_call" | custom-call | tf_op jit(solution)/shard_map/conv_backward/pallas_call | solution.py:471
  66.4 0.2 collective-permute-start.13
  66.6 1.0 collective-permute-done.13
  67.6 1.7 %collective-permute-start.14 = (f32[40,128]{1,0:T(8,128)S(1)}, f32[40,128]{1,0:T(8,128)S(1)}, u32[]{:S(2)}, u32[]{:S(2)}) collective-permute-start(f32[40,128]{1,0:T(8,128)S(1)} %add.39), channel_id=1, source_target_pairs={{0,2},{1,3},{2,0},{3,1},{4,6},{5,7},{6,4},{7,5},{8,10},{9,11},{10,... | collective-permute-start | bytes 61448 | tf_op jit(solution)/shard_map/ppermute | solution.py:42
  69.3 2.1 %collective-permute-done.14 = f32[40,128]{1,0:T(8,128)S(1)} collective-permute-done((f32[40,128]{1,0:T(8,128)S(1)}, f32[40,128]{1,0:T(8,128)S(1)}, u32[]{:S(2)}, u32[]{:S(2)}) %collective-permute-start.14) | collective-permute-done | bytes 20512 | tf_op jit(solution)/shard_map/ppermute | solution.py:42
  71.4 1.8 %collective-permute-start.17 = (f32[10,128]{1,0:T(8,128)S(1)}, f32[10,128]{1,0:T(8,128)S(1)}, u32[]{:S(2)}, u32[]{:S(2)}) collective-permute-start(f32[10,128]{1,0:T(8,128)S(1)} %slice.26), channel_id=1, source_target_pairs={{0,16},{16,0},{1,17},{17,1},{2,18},{18,2},{3,19},{19,3},{4,20},{20... | collective-permute-start | bytes 15368 | tf_op jit(solution)/shard_map/ppermute | solution.py:42
  73.2 0.0 collective-permute-done.10.got
  73.2 0.9 split.1
  74.2 1.1 collective-permute-start.16
  75.2 0.0 collective-permute-done.9.got
  75.2 1.3 %fold.5 = (bf16[160,1280]{1,0:T(8,128)(2,1)S(1)}, f32[160,1280]{1,0:T(8,128)S(1)}) custom-call(f32[320,1280]{1,0:T(8,128)S(1)} %copy-done.4, bf16[320,1280]{1,0:T(8,128)(2,1)} %collective-permute-done.9.got), custom_call_target="tpu_custom_call" | custom-call | tf_op jit(solution)/shard_map/fold/pallas_call | solution.py:439
  76.6 1.6 %collective-permute-start.15 = (bf16[160,1280]{1,0:T(8,128)(2,1)S(1)}, bf16[160,1280]{1,0:T(8,128)(2,1)S(1)}, u32[]{:S(2)}, u32[]{:S(2)}) collective-permute-start(bf16[160,1280]{1,0:T(8,128)(2,1)S(1)} %get-tuple-element.79), channel_id=1, source_target_pairs={{0,2},{1,3},{2,0},{3,1},{4,6},{5,7},{6,4},{7,5},{8,10},{9,11},{10,... | collective-permute-start | bytes 1228808 | tf_op jit(solution)/shard_map/ppermute | solution.py:42
  78.2 0.0 collective-permute-done.17
  78.2 1.6 %collective-permute-start.18 = (f32[40,128]{1,0:T(8,128)S(1)}, f32[40,128]{1,0:T(8,128)S(1)}, u32[]{:S(2)}, u32[]{:S(2)}) collective-permute-start(f32[40,128]{1,0:T(8,128)S(1)} %pad_maximum_fusion), channel_id=1, source_target_pairs={{0,4},{1,5},{2,6},{3,7},{4,0},{5,1},{6,2},{7,3},{8,12},{9,13},{10,... | collective-permute-start | bytes 61448 | tf_op jit(solution)/shard_map/ppermute | solution.py:42
  79.8 2.2 %collective-permute-done.18 = f32[40,128]{1,0:T(8,128)S(1)} collective-permute-done((f32[40,128]{1,0:T(8,128)S(1)}, f32[40,128]{1,0:T(8,128)S(1)}, u32[]{:S(2)}, u32[]{:S(2)}) %collective-permute-start.18) | collective-permute-done | bytes 20512 | tf_op jit(solution)/shard_map/ppermute | solution.py:42
  82.0 2.7 %collective-permute-start.19 = (f32[40,128]{1,0:T(8,128)S(1)}, f32[40,128]{1,0:T(8,128)S(1)}, u32[]{:S(2)}, u32[]{:S(2)}) collective-permute-start(f32[40,128]{1,0:T(8,128)S(1)} %fusion), channel_id=1, source_target_pairs={{0,8},{1,9},{2,10},{3,11},{4,12},{5,13},{6,14},{7,15},{8,0},{9,1},... | collective-permute-start | bytes 61448 | tf_op jit(solution)/shard_map/ppermute | solution.py:42
  84.7 2.1 %collective-permute-done.19 = f32[40,128]{1,0:T(8,128)S(1)} collective-permute-done((f32[40,128]{1,0:T(8,128)S(1)}, f32[40,128]{1,0:T(8,128)S(1)}, u32[]{:S(2)}, u32[]{:S(2)}) %collective-permute-start.19) | collective-permute-done | bytes 20512 | tf_op jit(solution)/shard_map/ppermute | solution.py:42
  86.8 0.5 collective-permute-done.16.got
  87.3 0.1 fold.6
  87.4 1.6 %collective-permute-start.21 = (bf16[80,1600]{1,0:T(8,128)(2,1)S(1)}, bf16[80,1600]{1,0:T(8,128)(2,1)S(1)}, u32[]{:S(2)}, u32[]{:S(2)}) collective-permute-start(bf16[80,1600]{1,0:T(8,128)(2,1)S(1)} %get-tuple-element.83), channel_id=1, source_target_pairs={{0,2},{1,3},{2,0},{3,1},{4,6},{5,7},{6,4},{7,5},{8,10},{9,11},{10,... | collective-permute-start | bytes 768008 | tf_op jit(solution)/shard_map/ppermute | solution.py:42
  89.0 0.0 collective-permute-done.15.got
  89.0 0.1 fold.7
  89.0 1.6 %collective-permute-start.20 = (bf16[80,1280]{1,0:T(8,128)(2,1)S(1)}, bf16[80,1280]{1,0:T(8,128)(2,1)S(1)}, u32[]{:S(2)}, u32[]{:S(2)}) collective-permute-start(bf16[80,1280]{1,0:T(8,128)(2,1)S(1)} %get-tuple-element.86), channel_id=1, source_target_pairs={{0,4},{1,5},{2,6},{3,7},{4,0},{5,1},{6,2},{7,3},{8,12},{9,13},{10,... | collective-permute-start | bytes 614408 | tf_op jit(solution)/shard_map/ppermute | solution.py:42
  90.7 3.4 %input_grad.1 = bf16[14,2,32,640]{3,2,1,0:T(8,128)(2,1)} custom-call(f32[40,128]{1,0:T(8,128)S(1)} %add.43.sums, f32[14,2,32,640]{3,2,1,0:T(8,128)S(1)} %get-tuple-element.89.grad, bf16[14,2,32,640]{3,2,1,0:T(8,128)(2,1)} %x.7, bf16[14,2,32,640]{3,2,1,0:T(8,128)(2,1)S(1)} %copy-done, f32[14,640]{1,0:T(8,128)S(1)} %get-tuple-element.72.refs_7_.mean, ...), custom_call_target="tpu_custom_call" | custom-call | tf_op jit(solution)/shard_map/input_grad/pallas_call | solution.py:514
  94.1 0.0 collective-permute-done.21.got
  94.1 0.1 fold.8
  94.2 2.8 %collective-permute-start.22 = (bf16[40,1600]{1,0:T(8,128)(2,1)S(1)}, bf16[40,1600]{1,0:T(8,128)(2,1)S(1)}, u32[]{:S(2)}, u32[]{:S(2)}) collective-permute-start(bf16[40,1600]{1,0:T(8,128)(2,1)S(1)} %get-tuple-element.91), channel_id=1, source_target_pairs={{0,8},{1,9},{2,10},{3,11},{4,12},{5,13},{6,14},{7,15},{8,0},{9,1},... | collective-permute-start | bytes 384008 | tf_op jit(solution)/shard_map/ppermute | solution.py:42
  97.0 1.4 %collective-permute-start.23 = (bf16[40,1280]{1,0:T(8,128)(2,1)S(1)}, bf16[40,1280]{1,0:T(8,128)(2,1)S(1)}, u32[]{:S(2)}, u32[]{:S(2)}) collective-permute-start(bf16[40,1280]{1,0:T(8,128)(2,1)S(1)} %get-tuple-element.93), channel_id=1, source_target_pairs={{0,8},{1,9},{2,10},{3,11},{4,12},{5,13},{6,14},{7,15},{8,0},{9,1},... | collective-permute-start | bytes 307208 | tf_op jit(solution)/shard_map/ppermute | solution.py:42
  98.5 0.6 slice_bitcast_fusion
  99.1 11.9 %conv_forward.1 = bf16[14,2,32,640]{3,2,1,0:T(8,128)(2,1)} custom-call(s32[5]{0:T(128)S(1)} %stack.35.info, bf16[2688,640]{1,0:T(8,128)(2,1)S(1)} %copy-done.2, bf16[9,640,640]{2,1,0:T(8,128)(2,1)S(1)} %get-tuple-element.95.w, bf16[14,2,32,640]{3,2,1,0:T(8,128)(2,1)} %x.7), custom_call_target="tpu_custom_call" | custom-call | tf_op jit(solution)/shard_map/conv_forward/pallas_call | solution.py:522
  111.0 0.0 collective-permute-done.23.got_b
  111.0 0.9 last.1
  (32 shorter events, 0.1 us)
Async XLA Ops:
  0.7 6.2 %copy-start = (bf16[14,2,32,640]{3,2,1,0:T(8,128)(2,1)S(1)}, bf16[14,2,32,640]{3,2,1,0:T(8,128)(2,1)}, u32[]{:S(2)}) copy-start(bf16[14,2,32,640]{3,2,1,0:T(8,128)(2,1)} %u.5) | copy-start | bytes 3440644
  3.9 25.4 %copy-start.6 = (f32[640]{0:T(1024)S(1)}, f32[640]{0:T(1024)}, u32[]{:S(2)}) copy-start(f32[640]{0:T(1024)} %param.6) | copy-start | bytes 7684
  3.9 25.4 %copy-start.7 = (f32[640]{0:T(1024)S(1)}, f32[640]{0:T(1024)}, u32[]{:S(2)}) copy-start(f32[640]{0:T(1024)} %param.7) | copy-start | bytes 7684
  3.9 43.3 %collective-permute-start.11 = (bf16[9,160,640]{2,1,0:T(8,128)(2,1)S(1)}, bf16[9,160,640]{2,1,0:T(8,128)(2,1)}, u32[]{:S(2)}, u32[]{:S(2)}) collective-permute-start(bf16[9,160,640]{2,1,0:T(8,128)(2,1)S(1)} %get-tuple-element.69), channel_id=1, source_target_pairs={{0,16},{16,0},{1,17},{17,1},{2,18},{18,2},{3,19},{19,3},{4,20},{20... | collective-permute-start | bytes 5529608 | tf_op jit(solution)/shard_map/ppermute | solution.py:42
  7.0 7.6 %collective-permute-start.2 = (bf16[14,2,32,640]{3,2,1,0:T(8,128)(2,1)S(1)}, bf16[14,2,32,640]{3,2,1,0:T(8,128)(2,1)S(1)}, u32[]{:S(2)}, u32[]{:S(2)}) collective-permute-start(bf16[14,2,32,640]{3,2,1,0:T(8,128)(2,1)S(1)} %copy-done), channel_id=1, source_target_pairs={{0,1},{1,0},{2,3},{3,2},{4,5},{5,4},{6,7},{7,6},{8,9},{9,8},{10,11... | collective-permute-start | bytes 3440648 | tf_op jit(solution)/shard_map/ppermute | solution.py:42
  7.0 17.7 %collective-permute-start.4 = (bf16[14,32,640]{2,1,0:T(8,128)(2,1)S(1)}, bf16[14,32,640]{2,1,0:T(8,128)(2,1)S(1)}, u32[]{:S(2)}, u32[]{:S(2)}) collective-permute-start(bf16[14,32,640]{2,1,0:T(8,128)(2,1)S(1)} %get-tuple-element.55), channel_id=1, source_target_pairs={{1,2},{2,1},{3,4},{4,3},{5,6},{6,5},{7,8},{8,7},{9,10},{10,9},{11,... | collective-permute-start | bytes 1720328 | tf_op jit(solution)/shard_map/ppermute | solution.py:411
  7.6 21.7 %collective-permute-start.6 = (bf16[14,2,32,640]{3,2,1,0:T(8,128)(2,1)}, bf16[14,2,32,640]{3,2,1,0:T(8,128)(2,1)S(1)}, u32[]{:S(2)}, u32[]{:S(2)}) collective-permute-start(bf16[14,2,32,640]{3,2,1,0:T(8,128)(2,1)} %x.7), channel_id=1, source_target_pairs={{0,1},{1,0},{2,3},{3,2},{4,5},{5,4},{6,7},{7,6},{8,9},{9,8},{10,11... | collective-permute-start | bytes 3440648 | tf_op jit(solution)/shard_map/ppermute | solution.py:42
  10.5 2.3 %collective-permute-start = (f32[28,16]{1,0:T(8,128)S(1)}, f32[28,16]{1,0:T(8,128)S(1)}, u32[]{:S(2)}, u32[]{:S(2)}) collective-permute-start(f32[28,16]{1,0:T(8,128)S(1)} %get-tuple-element.52), channel_id=1, source_target_pairs={{0,1},{1,0},{2,3},{3,2},{4,5},{5,4},{6,7},{7,6},{8,9},{9,8},{10,11... | collective-permute-start | bytes 5384 | tf_op jit(solution)/shard_map/ppermute | solution.py:42
  12.9 7.1 %collective-permute-start.1 = (f32[28,16]{1,0:T(8,128)S(1)}, f32[28,16]{1,0:T(8,128)S(1)}, u32[]{:S(2)}, u32[]{:S(2)}) collective-permute-start(f32[28,16]{1,0:T(8,128)S(1)} %add.33), channel_id=1, source_target_pairs={{0,4},{1,5},{2,6},{3,7},{4,0},{5,1},{6,2},{7,3},{8,12},{9,13},{10,... | collective-permute-start | bytes 5384 | tf_op jit(solution)/shard_map/ppermute | solution.py:42
  20.0 4.6 %collective-permute-start.3 = (f32[28,16]{1,0:T(8,128)S(1)}, f32[28,16]{1,0:T(8,128)S(1)}, u32[]{:S(2)}, u32[]{:S(2)}) collective-permute-start(f32[28,16]{1,0:T(8,128)S(1)} %add.34), channel_id=1, source_target_pairs={{0,8},{1,9},{2,10},{3,11},{4,12},{5,13},{6,14},{7,15},{8,0},{9,1},... | collective-permute-start | bytes 5384 | tf_op jit(solution)/shard_map/ppermute | solution.py:42
  24.6 3.8 %collective-permute-start.5 = (f32[28,16]{1,0:T(8,128)S(1)}, f32[28,16]{1,0:T(8,128)S(1)}, u32[]{:S(2)}, u32[]{:S(2)}) collective-permute-start(f32[28,16]{1,0:T(8,128)S(1)} %add.35), channel_id=1, source_target_pairs={{0,2},{1,3},{2,0},{3,1},{4,6},{5,7},{6,4},{7,5},{8,10},{9,11},{10,... | collective-permute-start | bytes 5384 | tf_op jit(solution)/shard_map/ppermute | solution.py:42
  25.6 3.8 %collective-permute-start.7 = (bf16[14,32,640]{2,1,0:T(8,128)(2,1)S(1)}, bf16[14,32,640]{2,1,0:T(8,128)(2,1)S(1)}, u32[]{:S(2)}, u32[]{:S(2)}) collective-permute-start(bf16[14,32,640]{2,1,0:T(8,128)(2,1)S(1)} %collective-permute-done.4.rim), channel_id=1, source_target_pairs={{0,1},{1,0},{2,3},{3,2},{4,5},{5,4},{6,7},{7,6},{8,9},{9,8},{10,11... | collective-permute-start | bytes 1720328 | tf_op jit(solution)/shard_map/ppermute | solution.py:42
  28.4 15.9 %collective-permute-start.8 = (bf16[14,32,640]{2,1,0:T(8,128)(2,1)S(1)}, bf16[14,32,640]{2,1,0:T(8,128)(2,1)S(1)}, u32[]{:S(2)}, u32[]{:S(2)}) collective-permute-start(bf16[14,32,640]{2,1,0:T(8,128)(2,1)S(1)} %get-tuple-element.64), channel_id=1, source_target_pairs={{1,2},{2,1},{3,4},{4,3},{5,6},{6,5},{7,8},{8,7},{9,10},{10,9},{11,... | collective-permute-start | bytes 1720328 | tf_op jit(solution)/shard_map/ppermute | solution.py:424
  35.3 9.0 %copy-start.1 = (bf16[2688,640]{1,0:T(8,128)(2,1)}, bf16[2688,640]{1,0:T(8,128)(2,1)S(1)}, u32[]{:S(2)}) copy-start(bf16[2688,640]{1,0:T(8,128)(2,1)S(1)} %get-tuple-element.58.mid) | copy-start | bytes 10321924
  44.4 2.9 %copy-start.5 = (bf16[14,32,640]{2,1,0:T(8,128)(2,1)}, bf16[14,32,640]{2,1,0:T(8,128)(2,1)S(1)}, u32[]{:S(2)}) copy-start(bf16[14,32,640]{2,1,0:T(8,128)(2,1)S(1)} %collective-permute-done.8.refs_5_) | copy-start | bytes 1720324
  47.2 4.1 %collective-permute-start.12 = (bf16[9,160,640]{2,1,0:T(8,128)(2,1)}, bf16[9,160,640]{2,1,0:T(8,128)(2,1)}, u32[]{:S(2)}, u32[]{:S(2)}) collective-permute-start(bf16[9,160,640]{2,1,0:T(8,128)(2,1)} %collective-permute-done.11.refs_1_), channel_id=1, source_target_pairs={{0,1},{1,0},{2,3},{3,2},{4,5},{5,4},{6,7},{7,6},{8,9},{9,8},{10,11... | collective-permute-start | bytes 5529608 | tf_op jit(solution)/shard_map/ppermute | solution.py:42
  47.4 25.8 %collective-permute-start.10 = (bf16[160,3200]{1,0:T(8,128)(2,1)}, bf16[160,3200]{1,0:T(8,128)(2,1)S(1)}, u32[]{:S(2)}, u32[]{:S(2)}) collective-permute-start(bf16[160,3200]{1,0:T(8,128)(2,1)} %get-tuple-element.67), channel_id=1, source_target_pairs={{0,4},{1,5},{2,6},{3,7},{4,0},{5,1},{6,2},{7,3},{8,12},{9,13},{10,... | collective-permute-start | bytes 3072008 | tf_op jit(solution)/shard_map/ppermute | solution.py:42
  49.0 26.2 %collective-permute-start.9 = (bf16[320,1280]{1,0:T(8,128)(2,1)}, bf16[320,1280]{1,0:T(8,128)(2,1)}, u32[]{:S(2)}, u32[]{:S(2)}) collective-permute-start(bf16[320,1280]{1,0:T(8,128)(2,1)} %get-tuple-element.65), channel_id=1, source_target_pairs={{0,16},{16,0},{1,17},{17,1},{2,18},{18,2},{3,19},{19,3},{4,20},{20... | collective-permute-start | bytes 2457608 | tf_op jit(solution)/shard_map/ppermute | solution.py:42
  51.4 21.8 %copy-start.3 = (f32[160,3200]{1,0:T(8,128)S(1)}, f32[160,3200]{1,0:T(8,128)}, u32[]{:S(2)}) copy-start(f32[160,3200]{1,0:T(8,128)} %get-tuple-element.66.kept) | copy-start | bytes 6144004
  66.3 8.9 %copy-start.4 = (f32[320,1280]{1,0:T(8,128)S(1)}, f32[320,1280]{1,0:T(8,128)}, u32[]{:S(2)}) copy-start(f32[320,1280]{1,0:T(8,128)} %get-tuple-element.60.kept) | copy-start | bytes 4915204
  66.4 1.3 %collective-permute-start.13 = (f32[40,128]{1,0:T(8,128)S(1)}, f32[40,128]{1,0:T(8,128)S(1)}, u32[]{:S(2)}, u32[]{:S(2)}) collective-permute-start(f32[40,128]{1,0:T(8,128)S(1)} %get-tuple-element.74), channel_id=1, source_target_pairs={{0,1},{1,0},{2,3},{3,2},{4,5},{5,4},{6,7},{7,6},{8,9},{9,8},{10,11... | collective-permute-start | bytes 61448 | tf_op jit(solution)/shard_map/ppermute | solution.py:42
  67.6 3.8 %collective-permute-start.14 = (f32[40,128]{1,0:T(8,128)S(1)}, f32[40,128]{1,0:T(8,128)S(1)}, u32[]{:S(2)}, u32[]{:S(2)}) collective-permute-start(f32[40,128]{1,0:T(8,128)S(1)} %add.39), channel_id=1, source_target_pairs={{0,2},{1,3},{2,0},{3,1},{4,6},{5,7},{6,4},{7,5},{8,10},{9,11},{10,... | collective-permute-start | bytes 61448 | tf_op jit(solution)/shard_map/ppermute | solution.py:42
  71.4 6.7 %collective-permute-start.17 = (f32[10,128]{1,0:T(8,128)S(1)}, f32[10,128]{1,0:T(8,128)S(1)}, u32[]{:S(2)}, u32[]{:S(2)}) collective-permute-start(f32[10,128]{1,0:T(8,128)S(1)} %slice.26), channel_id=1, source_target_pairs={{0,16},{16,0},{1,17},{17,1},{2,18},{18,2},{3,19},{19,3},{4,20},{20... | collective-permute-start | bytes 15368 | tf_op jit(solution)/shard_map/ppermute | solution.py:42
  74.2 13.1 %collective-permute-start.16 = (bf16[160,1600]{1,0:T(8,128)(2,1)S(1)}, bf16[160,1600]{1,0:T(8,128)(2,1)S(1)}, u32[]{:S(2)}, u32[]{:S(2)}) collective-permute-start(bf16[160,1600]{1,0:T(8,128)(2,1)S(1)} %get-tuple-element.76), channel_id=1, source_target_pairs={{0,16},{16,0},{1,17},{17,1},{2,18},{18,2},{3,19},{19,3},{4,20},{20... | collective-permute-start | bytes 1536008 | tf_op jit(solution)/shard_map/ppermute | solution.py:42
  76.6 12.4 %collective-permute-start.15 = (bf16[160,1280]{1,0:T(8,128)(2,1)S(1)}, bf16[160,1280]{1,0:T(8,128)(2,1)S(1)}, u32[]{:S(2)}, u32[]{:S(2)}) collective-permute-start(bf16[160,1280]{1,0:T(8,128)(2,1)S(1)} %get-tuple-element.79), channel_id=1, source_target_pairs={{0,2},{1,3},{2,0},{3,1},{4,6},{5,7},{6,4},{7,5},{8,10},{9,11},{10,... | collective-permute-start | bytes 1228808 | tf_op jit(solution)/shard_map/ppermute | solution.py:42
  78.2 3.8 %collective-permute-start.18 = (f32[40,128]{1,0:T(8,128)S(1)}, f32[40,128]{1,0:T(8,128)S(1)}, u32[]{:S(2)}, u32[]{:S(2)}) collective-permute-start(f32[40,128]{1,0:T(8,128)S(1)} %pad_maximum_fusion), channel_id=1, source_target_pairs={{0,4},{1,5},{2,6},{3,7},{4,0},{5,1},{6,2},{7,3},{8,12},{9,13},{10,... | collective-permute-start | bytes 61448 | tf_op jit(solution)/shard_map/ppermute | solution.py:42
  82.0 4.7 %collective-permute-start.19 = (f32[40,128]{1,0:T(8,128)S(1)}, f32[40,128]{1,0:T(8,128)S(1)}, u32[]{:S(2)}, u32[]{:S(2)}) collective-permute-start(f32[40,128]{1,0:T(8,128)S(1)} %fusion), channel_id=1, source_target_pairs={{0,8},{1,9},{2,10},{3,11},{4,12},{5,13},{6,14},{7,15},{8,0},{9,1},... | collective-permute-start | bytes 61448 | tf_op jit(solution)/shard_map/ppermute | solution.py:42
  87.4 6.7 %collective-permute-start.21 = (bf16[80,1600]{1,0:T(8,128)(2,1)S(1)}, bf16[80,1600]{1,0:T(8,128)(2,1)S(1)}, u32[]{:S(2)}, u32[]{:S(2)}) collective-permute-start(bf16[80,1600]{1,0:T(8,128)(2,1)S(1)} %get-tuple-element.83), channel_id=1, source_target_pairs={{0,2},{1,3},{2,0},{3,1},{4,6},{5,7},{6,4},{7,5},{8,10},{9,11},{10,... | collective-permute-start | bytes 768008 | tf_op jit(solution)/shard_map/ppermute | solution.py:42
  89.0 8.0 %collective-permute-start.20 = (bf16[80,1280]{1,0:T(8,128)(2,1)S(1)}, bf16[80,1280]{1,0:T(8,128)(2,1)S(1)}, u32[]{:S(2)}, u32[]{:S(2)}) collective-permute-start(bf16[80,1280]{1,0:T(8,128)(2,1)S(1)} %get-tuple-element.86), channel_id=1, source_target_pairs={{0,4},{1,5},{2,6},{3,7},{4,0},{5,1},{6,2},{7,3},{8,12},{9,13},{10,... | collective-permute-start | bytes 614408 | tf_op jit(solution)/shard_map/ppermute | solution.py:42
  90.7 8.4 %copy-start.2 = (bf16[2688,640]{1,0:T(8,128)(2,1)S(1)}, bf16[2688,640]{1,0:T(8,128)(2,1)}, u32[]{:S(2)}) copy-start(bf16[2688,640]{1,0:T(8,128)(2,1)} %copy-done.1) | copy-start | bytes 10321924
  94.2 16.8 %collective-permute-start.22 = (bf16[40,1600]{1,0:T(8,128)(2,1)S(1)}, bf16[40,1600]{1,0:T(8,128)(2,1)S(1)}, u32[]{:S(2)}, u32[]{:S(2)}) collective-permute-start(bf16[40,1600]{1,0:T(8,128)(2,1)S(1)} %get-tuple-element.91), channel_id=1, source_target_pairs={{0,8},{1,9},{2,10},{3,11},{4,12},{5,13},{6,14},{7,15},{8,0},{9,1},... | collective-permute-start | bytes 384008 | tf_op jit(solution)/shard_map/ppermute | solution.py:42
  97.0 13.9 %collective-permute-start.23 = (bf16[40,1280]{1,0:T(8,128)(2,1)S(1)}, bf16[40,1280]{1,0:T(8,128)(2,1)S(1)}, u32[]{:S(2)}, u32[]{:S(2)}) collective-permute-start(bf16[40,1280]{1,0:T(8,128)(2,1)S(1)} %get-tuple-element.93), channel_id=1, source_target_pairs={{0,8},{1,9},{2,10},{3,11},{4,12},{5,13},{6,14},{7,15},{8,0},{9,1},... | collective-permute-start | bytes 307208 | tf_op jit(solution)/shard_map/ppermute | solution.py:42

commit v5 on v4

--- a/solution.py
+++ b/solution.py
@@ -74,21 +74,21 @@
     return down, up
 
 
-def stats_kernel(info, x, u, *refs):
-    if len(refs) == 6:
-        w, out, edge_x, edge_u, w_sent, sem = refs
-    else:
-        out, edge_x, edge_u, sem = refs
+def slice_kernel(info, w, out, sem):
+    rows = out.shape[1]
+    at = pl.ds(pl.multiple_of(info[0] * rows, 32), rows)
+    copy = pltpu.make_async_copy(w.at[:, at, :], out, sem)
+    copy.start()
+    copy.wait()
+
+
+def stats_kernel(info, x, u, out, edge_x, edge_u, sem):
     images, _, _, channels = x.shape
     core = info[0]
     copies = [
         pltpu.make_async_copy(x.at[:, core], edge_x, sem.at[0]),
         pltpu.make_async_copy(u.at[:, core], edge_u, sem.at[1]),
     ]
-    if len(refs) == 6:
-        rows = w_sent.shape[1]
-        at = pl.ds(pl.multiple_of(core * rows, 32), rows)
-        copies.append(pltpu.make_async_copy(w.at[:, at, :], w_sent, sem.at[2]))
     for c in copies:
         c.start()
     one, two = [], []
@@ -233,30 +233,30 @@
         first += count
 
 
-def conv_kernel(info, mid, w, x, out, side):
+def own_kernel(columns, info, mid, out):
+    def fill(k, carry):
+        at = pl.ds(pl.multiple_of(k * columns, columns), columns)
+        first = pl.multiple_of(2 * info[0] * (out.shape[1] // 4), 64)
+        value = mid[pl.ds(first + pl.multiple_of(k * columns, columns), columns), :]
+        down, up = shifted(value.astype(F32))
+        out[0, at, :] = down.astype(BF16)
+        out[1, at, :] = value
+        out[2, at, :] = up.astype(BF16)
+        return carry
+
+    lax.fori_loop(0, out.shape[1] // columns, fill, 0)
+
+
+def conv_kernel(own, w, x, out):
     images, _, columns, channels = x.shape
     block = images * columns
-    first = pl.multiple_of(2 * info[0] * block, 64)
     taps = w.shape[0]
-
-    def fill(k, carry):
-        at = pl.multiple_of(k * columns, columns)
-        down, up = shifted(mid[pl.ds(first + at, columns), :].astype(F32))
-        side[0, pl.ds(at, columns), :] = down.astype(BF16)
-        side[1, pl.ds(at, columns), :] = up.astype(BF16)
-        return carry
-
-    lax.fori_loop(0, 4 * images, fill, 0)
     rhs = w[...].reshape(taps * channels, channels)
     for r in range(2):
-        lhs = []
-        for t in range(taps):
-            at = (r + t // 3) * block
-            if t % 3 == 1:
-                lhs.append(mid[pl.ds(pl.multiple_of(first + at, 64), block), :])
-            else:
-                lhs.append(side[(t % 3) // 2, at : at + block, :])
-        value = jnp.dot(jnp.concatenate(lhs, axis=1), rhs, preferred_element_type=F32)
+        lhs = jnp.concatenate([
+            own[t % 3, (r + t // 3) * block : (r + t // 3 + 1) * block, :] for t in range(taps)
+        ], axis=1)
+        value = jnp.dot(lhs, rhs, preferred_element_type=F32)
         value = value.reshape(images, columns, channels)
         out[:, r] = (x[:, r].astype(F32) + value).astype(BF16)
 
@@ -397,17 +397,19 @@
 
     part = conv_weight.shape[1] // 2
     row_shape = (images, columns, channels)
-    out_shape = [struct((2 * images, groups), F32), struct(row_shape, BF16), struct(row_shape, BF16)]
-    operands = [info, inputs, in_hbm(upstream)]
+    first_info = info
     if two:
-        out_shape.append(struct((taps, part, channels), BF16))
-        operands.append(in_hbm(conv_weight))
-    stats, edge_x, edge_u, *w_sent = kernel_call(
-        stats_kernel, 16, tuple(out_shape), [S, V, H] + [H] * (len(operands) - 3), "stats",
-        [pltpu.SemaphoreType.DMA((3,))],
-    )(*operands)
-    if two:
-        w_low = swap(w_sent[0], "dp", 1)
+        w_sent = kernel_call(
+            slice_kernel, 8, struct((taps, part, channels), BF16), [S, H], "slice",
+            [pltpu.SemaphoreType.DMA],
+        )(info, in_hbm(conv_weight))
+        w_low = swap(w_sent, "dp", 1)
+        first_info = after(info, w_sent)
+    stats, edge_x, edge_u = kernel_call(
+        stats_kernel, 16,
+        (struct((2 * images, groups), F32), struct(row_shape, BF16), struct(row_shape, BF16)),
+        [S, V, H], "stats", [pltpu.SemaphoreType.DMA((2,))],
+    )(first_info, inputs, in_hbm(upstream))
     rim_x = lax.ppermute(edge_x, "space", pairs)
     lhs = kernel_call(
         functools.partial(turn_kernel, bits), 16, struct((channels // 2, 4 * block), BF16),
@@ -504,8 +506,15 @@
     else:
         totals = lax.psum(totals, "dp")
     sums = jnp.concatenate([sums[:base], totals, sums[last:]])
+    own = kernel_call(
+        functools.partial(own_kernel, columns), 16, struct((3, 4 * block, channels), BF16),
+        [S, V], "own",
+    )(after(info, sent_b), act_mid)
     for place in range(2, bits):
-        sums = sums + swap(sums, "space", 1 << place)
+        step = swap(sums, "space", 1 << place)
+        if place == 2:
+            step, own = lax.optimization_barrier((step, own))
+        sums = sums + step
     sent_a, kept_a = fold(kept_a, after(got_a, sums))
     got_a = swap(sent_a, "space", 2)
     sent_b, kept_b = fold(kept_b, after(got_b, sent_a))
@@ -520,9 +529,8 @@
     sent_b, kept_b = fold(kept_b, after(got_b, sent_a))
     got_b = swap(sent_b, "space", 8)
     mixed = kernel_call(
-        conv_kernel, 32, struct(inputs.shape, BF16), [S] + [V] * 3, "conv_forward",
-        [pltpu.VMEM((2, 4 * block, channels), BF16)],
-    )(after(info, sent_b), act_mid, weights, inputs)
+        conv_kernel, 32, struct(inputs.shape, BF16), [V] * 3, "conv_forward"
+    )(after(own, sent_b), weights, inputs)
     got_a = after(got_a, mixed)
     wide = channels // 2 if two else channels
     weight_grad = kernel_call(

time: 112 us -> 110 us (0.982)
  starting transfers between devices: 34.5 us -> 32.7 us
  Pallas kernels: 53.8 us -> 52.2 us
    ppermute x22, starting transfers between devices: 32.9 us -> 31.1 us  [swap(): return lax.ppermute(value, axis, [(i, i ^ bit) for i in range(count)])]
    pallas_call x1, Pallas kernels: 3.44 us -> 2.04 us  [body(): kernel_call(functools.partial(input_kernel, size), 16, struct(inputs.shap...]
    pallas_call x2 -> x4, Pallas kernels: 15.1 us -> 15.5 us  [the longest x1 9.26 us: body(): kernel_call(conv_kernel, 32, struct(inputs.shape, BF16), [V] * 3, 'conv_f...]
  transfers between devices with their start and end apart: 24 -> 24, of which waited for: 11 -> 12; matrix products, arithmetic and copies ran while one was open for 1% -> 1% of each run, Pallas kernels for 44% -> 45%
where the time goes in v5:
time: 110 us; the launch traced here: 109 us
  Pallas kernels  52.2 us (47%)
  starting transfers between devices  32.7 us (30%)
  waiting for transfers between devices  22.7 us (21%)
    ppermute x22, starting transfers between devices, swap(): return lax.ppermute(value, axis, [(i, i ^ bit) for i in range(count)])  31.1 us
    ppermute x22, waiting for transfers between devices, swap(): return lax.ppermute(value, axis, [(i, i ^ bit) for i in range(count)])  22.7 us
    pallas_call x1, Pallas kernels, body(): kernel_call(back_kernel, 32, (struct(inputs.shape, F32), struct((40, LANE...  14.1 us
    pallas_call x1, Pallas kernels, body(): kernel_call(conv_kernel, 32, struct(inputs.shape, BF16), [V] * 3, 'conv_f...  9.26 us
    pallas_call x1, Pallas kernels, body(): kernel_call(functools.partial(grad_kernel, block, two), 28, tuple((pltpu....  9.01 us
    pallas_call x1, Pallas kernels, body(): kernel_call(functools.partial(act_kernel, size), 24, (struct((6 * block,...  5.2 us
  transfers between devices with their start and end apart: 24, of which 12 were waited for; matrix products, arithmetic and copies ran while one was open for 1% of the time, Pallas kernels for 45%

profile of v5, /device:TPU:0, one launch (start us, length us, event | category | flops | bytes accessed | tf_op | source)
XLA Modules:
  0.0 109.4 jit_solution(11138929935259856846)
XLA Ops:
  0.7 0.1 stack.35.info
  0.7 2.2 %slice.32 = bf16[9,160,640]{2,1,0:T(8,128)(2,1)S(1)} custom-call(s32[5]{0:T(128)S(1)} %stack.35.info, bf16[9,320,640]{2,1,0:T(8,128)(2,1)} %refs_0_.1), custom_call_target="tpu_custom_call" | custom-call | tf_op jit(solution)/shard_map/slice/pallas_call | solution.py:402
  2.9 0.0 copy-start.2
  3.0 3.0 %collective-permute-start.9 = (bf16[9,160,640]{2,1,0:T(8,128)(2,1)S(1)}, bf16[9,160,640]{2,1,0:T(8,128)(2,1)}, u32[]{:S(2)}, u32[]{:S(2)}) collective-permute-start(bf16[9,160,640]{2,1,0:T(8,128)(2,1)S(1)} %slice.32), channel_id=1, source_target_pairs={{0,16},{16,0},{1,17},{17,1},{2,18},{18,2},{3,19},{19,3},{4,20},{20... | collective-permute-start | bytes 5529608 | tf_op jit(solution)/shard_map/ppermute | solution.py:42
  6.0 2.0 %stats.1 = (f32[28,16]{1,0:T(8,128)S(1)}, bf16[14,32,640]{2,1,0:T(8,128)(2,1)S(1)}, bf16[14,32,640]{2,1,0:T(8,128)(2,1)S(1)}) custom-call(s32[5]{0:T(128)S(1)} %stack.35.info, bf16[14,2,32,640]{3,2,1,0:T(8,128)(2,1)S(1)} %copy-done, bf16[14,2,32,640]{3,2,1,0:T(8,128)(2,1)} %u.5), custom_call_target="tpu_custom_call" | custom-call | tf_op jit(solution)/shard_map/stats/pallas_call | solution.py:408
  8.0 0.0 copy-start.10
  8.0 0.0 copy-start.11
  8.0 0.7 collective-permute-start.4
  8.8 2.9 %collective-permute-start.6 = (bf16[14,2,32,640]{3,2,1,0:T(8,128)(2,1)S(1)}, bf16[14,2,32,640]{3,2,1,0:T(8,128)(2,1)S(1)}, u32[]{:S(2)}, u32[]{:S(2)}) collective-permute-start(bf16[14,2,32,640]{3,2,1,0:T(8,128)(2,1)S(1)} %copy-done), channel_id=1, source_target_pairs={{0,1},{1,0},{2,3},{3,2},{4,5},{5,4},{6,7},{7,6},{8,9},{9,8},{10,11... | collective-permute-start | bytes 3440648 | tf_op jit(solution)/shard_map/ppermute | solution.py:42
  11.6 0.1 collective-permute-start
  11.7 2.4 %collective-permute-done = f32[28,16]{1,0:T(8,128)S(1)} collective-permute-done((f32[28,16]{1,0:T(8,128)S(1)}, f32[28,16]{1,0:T(8,128)S(1)}, u32[]{:S(2)}, u32[]{:S(2)}) %collective-permute-start) | collective-permute-done | bytes 1824 | tf_op jit(solution)/shard_map/ppermute | solution.py:42
  14.1 1.8 %collective-permute-start.1 = (f32[28,16]{1,0:T(8,128)S(1)}, f32[28,16]{1,0:T(8,128)S(1)}, u32[]{:S(2)}, u32[]{:S(2)}) collective-permute-start(f32[28,16]{1,0:T(8,128)S(1)} %add.33), channel_id=1, source_target_pairs={{0,4},{1,5},{2,6},{3,7},{4,0},{5,1},{6,2},{7,3},{8,12},{9,13},{10,... | collective-permute-start | bytes 5384 | tf_op jit(solution)/shard_map/ppermute | solution.py:42
  15.9 0.0 collective-permute-done.2.u_mate.refs_4_
  15.9 1.9 %turn.1.lhs = bf16[320,1792]{1,0:T(8,128)(2,1)S(1)} custom-call(s32[5]{0:T(128)S(1)} %stack.35.info, bf16[14,2,32,640]{3,2,1,0:T(8,128)(2,1)S(1)} %copy-done.2, bf16[14,2,32,640]{3,2,1,0:T(8,128)(2,1)S(1)} %collective-permute-done.2.u_mate.refs_4_), custom_call_target="tpu_custom_call" | custom-call | tf_op jit(solution)/shard_map/turn/pallas_call | solution.py:414
  17.9 3.2 %collective-permute-done.1 = f32[28,16]{1,0:T(8,128)S(1)} collective-permute-done((f32[28,16]{1,0:T(8,128)S(1)}, f32[28,16]{1,0:T(8,128)S(1)}, u32[]{:S(2)}, u32[]{:S(2)}) %collective-permute-start.1) | collective-permute-done | bytes 1824 | tf_op jit(solution)/shard_map/ppermute | solution.py:42
  21.1 2.8 %collective-permute-start.3 = (f32[28,16]{1,0:T(8,128)S(1)}, f32[28,16]{1,0:T(8,128)S(1)}, u32[]{:S(2)}, u32[]{:S(2)}) collective-permute-start(f32[28,16]{1,0:T(8,128)S(1)} %add.34), channel_id=1, source_target_pairs={{0,8},{1,9},{2,10},{3,11},{4,12},{5,13},{6,14},{7,15},{8,0},{9,1},... | collective-permute-start | bytes 5384 | tf_op jit(solution)/shard_map/ppermute | solution.py:42
  23.8 1.9 %collective-permute-done.3 = f32[28,16]{1,0:T(8,128)S(1)} collective-permute-done((f32[28,16]{1,0:T(8,128)S(1)}, f32[28,16]{1,0:T(8,128)S(1)}, u32[]{:S(2)}, u32[]{:S(2)}) %collective-permute-start.3) | collective-permute-done | bytes 1824 | tf_op jit(solution)/shard_map/ppermute | solution.py:42
  25.7 0.0 collective-permute-done.4.rim
  25.7 1.0 collective-permute-start.5
  26.7 0.0 collective-permute-start.7
  26.7 2.8 %collective-permute-done.5 = f32[28,16]{1,0:T(8,128)S(1)} collective-permute-done((f32[28,16]{1,0:T(8,128)S(1)}, f32[28,16]{1,0:T(8,128)S(1)}, u32[]{:S(2)}, u32[]{:S(2)}) %collective-permute-start.5) | collective-permute-done | bytes 1824 | tf_op jit(solution)/shard_map/ppermute | solution.py:42
  29.5 0.9 collective-permute-start.8
  30.5 0.0 collective-permute-done.6.x_mate
  30.5 0.0 collective-permute-done.7.rim_mate
  30.5 5.2 %activate.1 = (bf16[2688,640]{1,0:T(8,128)(2,1)S(1)}, bf16[2,2688,640]{2,1,0:T(8,128)(2,1)S(1)}, f32[14,640]{1,0:T(8,128)S(1)}, f32[14,640]{1,0:T(8,128)S(1)}) custom-call(s32[5]{0:T(128)S(1)} %stack.35.info, f32[28,16]{1,0:T(8,128)S(1)} %add.36.stats, bf16[14,2,32,640]{3,2,1,0:T(8,128)(2,1)S(1)} %copy-done, ...), custom_call_target="tpu_custom_call" | custom-call | tf_op jit(solution)/shard_map/activate/pallas_call | solution.py:428
  35.7 0.0 copy-start.6
  35.7 9.0 %weight_terms.1 = (bf16[160,3200]{1,0:T(8,128)(2,1)}, f32[160,3200]{1,0:T(8,128)}, bf16[320,1280]{1,0:T(8,128)(2,1)}, f32[320,1280]{1,0:T(8,128)}) custom-call(s32[5]{0:T(128)S(1)} %stack.35.info, bf16[320,1792]{1,0:T(8,128)(2,1)S(1)} %turn.1.lhs, bf16[2688,640]{1,0:T(8,128)(2,1)S(1)} %get-tuple-element.62.mid, bf16[2,2688,640]{2,1,0:T(8,128)(2,1)S(1)} %get-tuple-element.63.side), custom_call_target="tpu_custom_call" | custom-call | tf_op jit(solution)/shard_map/weight_terms/pallas_call | solution.py:456
  44.8 1.5 %collective-permute-done.9.refs_1_ = bf16[9,160,640]{2,1,0:T(8,128)(2,1)} collective-permute-done((bf16[9,160,640]{2,1,0:T(8,128)(2,1)S(1)}, bf16[9,160,640]{2,1,0:T(8,128)(2,1)}, u32[]{:S(2)}, u32[]{:S(2)}) %collective-permute-start.9) | collective-permute-done | bytes 1843232 | tf_op jit(solution)/shard_map/ppermute | solution.py:42
  46.3 1.5 %collective-permute-start.10 = (bf16[9,160,640]{2,1,0:T(8,128)(2,1)}, bf16[9,160,640]{2,1,0:T(8,128)(2,1)}, u32[]{:S(2)}, u32[]{:S(2)}) collective-permute-start(bf16[9,160,640]{2,1,0:T(8,128)(2,1)} %collective-permute-done.9.refs_1_), channel_id=1, source_target_pairs={{0,1},{1,0},{2,3},{3,2},{4,5},{5,4},{6,7},{7,6},{8,9},{9,8},{10,11... | collective-permute-start | bytes 5529608 | tf_op jit(solution)/shard_map/ppermute | solution.py:42
  47.8 1.6 %collective-permute-start.15 = (bf16[160,3200]{1,0:T(8,128)(2,1)}, bf16[160,3200]{1,0:T(8,128)(2,1)}, u32[]{:S(2)}, u32[]{:S(2)}) collective-permute-start(bf16[160,3200]{1,0:T(8,128)(2,1)} %get-tuple-element.77), channel_id=1, source_target_pairs={{0,4},{1,5},{2,6},{3,7},{4,0},{5,1},{6,2},{7,3},{8,12},{9,13},{10,... | collective-permute-start | bytes 3072008 | tf_op jit(solution)/shard_map/ppermute | solution.py:42
  49.4 0.5 collective-permute-start.14
  49.9 0.1 pad_add_fusion.places
  50.0 1.6 %collective-permute-done.10.refs_2_ = bf16[9,160,640]{2,1,0:T(8,128)(2,1)} collective-permute-done((bf16[9,160,640]{2,1,0:T(8,128)(2,1)}, bf16[9,160,640]{2,1,0:T(8,128)(2,1)}, u32[]{:S(2)}, u32[]{:S(2)}) %collective-permute-start.10) | collective-permute-done | bytes 1843232 | tf_op jit(solution)/shard_map/ppermute | solution.py:42
  51.6 14.1 %conv_backward.1 = (f32[14,2,32,640]{3,2,1,0:T(8,128)S(1)}, f32[40,128]{1,0:T(8,128)S(1)}, bf16[9,640,640]{2,1,0:T(8,128)(2,1)S(1)}) custom-call(s32[5]{0:T(128)S(1)} %stack.35.info, s32[3]{0:T(128)S(1)} %pad_add_fusion.places, bf16[9,320,640]{2,1,0:T(8,128)(2,1)} %refs_0_.1, bf16[9,160,640]{2,1,0:T(8,128)(2,1)} %collective-permute-done.9.refs_1_, ...), custom_call_target="tpu_custom_call" | custom-call | tf_op jit(solution)/shard_map/conv_backward/pallas_call | solution.py:473
  65.7 0.4 collective-permute-start.11
  66.1 0.8 collective-permute-done.11
  66.9 1.0 collective-permute-start.12
  68.0 2.8 %collective-permute-done.12 = f32[40,128]{1,0:T(8,128)S(1)} collective-permute-done((f32[40,128]{1,0:T(8,128)S(1)}, f32[40,128]{1,0:T(8,128)S(1)}, u32[]{:S(2)}, u32[]{:S(2)}) %collective-permute-start.12) | collective-permute-done | bytes 20512 | tf_op jit(solution)/shard_map/ppermute | solution.py:42
  70.7 0.7 collective-permute-start.13
  71.4 1.2 %collective-permute-done.15.got = bf16[160,3200]{1,0:T(8,128)(2,1)} collective-permute-done((bf16[160,3200]{1,0:T(8,128)(2,1)}, bf16[160,3200]{1,0:T(8,128)(2,1)}, u32[]{:S(2)}, u32[]{:S(2)}) %collective-permute-start.15) | collective-permute-done | bytes 1024032 | tf_op jit(solution)/shard_map/ppermute | solution.py:42
  72.6 1.8 %split.1 = (bf16[160,1600]{1,0:T(8,128)(2,1)S(1)}, f32[160,1600]{1,0:T(8,128)S(1)}) custom-call(s32[5]{0:T(128)S(1)} %stack.35.info, f32[160,3200]{1,0:T(8,128)S(1)} %copy-done.7, bf16[160,3200]{1,0:T(8,128)(2,1)} %collective-permute-done.15.got), custom_call_target="tpu_custom_call" | custom-call | tf_op jit(solution)/shard_map/split/pallas_call | solution.py:447
  74.5 0.8 collective-permute-start.18
  75.3 1.3 %fold.5 = (bf16[160,1280]{1,0:T(8,128)(2,1)S(1)}, f32[160,1280]{1,0:T(8,128)S(1)}) custom-call(f32[320,1280]{1,0:T(8,128)S(1)} %copy-done.8, bf16[320,1280]{1,0:T(8,128)(2,1)} %collective-permute-done.14.got), custom_call_target="tpu_custom_call" | custom-call | tf_op jit(solution)/shard_map/fold/pallas_call | solution.py:441
  76.6 2.0 %collective-permute-start.17 = (bf16[160,1280]{1,0:T(8,128)(2,1)S(1)}, bf16[160,1280]{1,0:T(8,128)(2,1)S(1)}, u32[]{:S(2)}, u32[]{:S(2)}) collective-permute-start(bf16[160,1280]{1,0:T(8,128)(2,1)S(1)} %get-tuple-element.81), channel_id=1, source_target_pairs={{0,2},{1,3},{2,0},{3,1},{4,6},{5,7},{6,4},{7,5},{8,10},{9,11},{10,... | collective-permute-start | bytes 1228808 | tf_op jit(solution)/shard_map/ppermute | solution.py:42
  78.6 0.0 collective-permute-done.13
  78.6 1.8 %collective-permute-start.16 = (f32[40,128]{1,0:T(8,128)S(1)}, f32[40,128]{1,0:T(8,128)S(1)}, u32[]{:S(2)}, u32[]{:S(2)}) collective-permute-start(f32[40,128]{1,0:T(8,128)S(1)} %pad_maximum_fusion), channel_id=1, source_target_pairs={{0,4},{1,5},{2,6},{3,7},{4,0},{5,1},{6,2},{7,3},{8,12},{9,13},{10,... | collective-permute-start | bytes 61448 | tf_op jit(solution)/shard_map/ppermute | solution.py:42
  80.4 2.0 %own.1 = bf16[3,1792,640]{2,1,0:T(8,128)(2,1)S(1)} custom-call(s32[5]{0:T(128)S(1)} %stack.35.info, bf16[2688,640]{1,0:T(8,128)(2,1)S(1)} %copy-done.4), custom_call_target="tpu_custom_call" | custom-call | tf_op jit(solution)/shard_map/own/pallas_call | solution.py:509
  82.5 0.0 collective-permute-done.16
  82.5 2.2 %collective-permute-start.19 = (f32[40,128]{1,0:T(8,128)S(1)}, f32[40,128]{1,0:T(8,128)S(1)}, u32[]{:S(2)}, u32[]{:S(2)}) collective-permute-start(f32[40,128]{1,0:T(8,128)S(1)} %fusion), channel_id=1, source_target_pairs={{0,8},{1,9},{2,10},{3,11},{4,12},{5,13},{6,14},{7,15},{8,0},{9,1},... | collective-permute-start | bytes 61448 | tf_op jit(solution)/shard_map/ppermute | solution.py:42
  84.7 2.5 %collective-permute-done.19 = f32[40,128]{1,0:T(8,128)S(1)} collective-permute-done((f32[40,128]{1,0:T(8,128)S(1)}, f32[40,128]{1,0:T(8,128)S(1)}, u32[]{:S(2)}, u32[]{:S(2)}) %collective-permute-start.19) | collective-permute-done | bytes 20512 | tf_op jit(solution)/shard_map/ppermute | solution.py:42
  87.3 0.4 collective-permute-done.18.got
  87.7 0.1 fold.6
  87.8 2.5 %collective-permute-start.21 = (bf16[80,1600]{1,0:T(8,128)(2,1)S(1)}, bf16[80,1600]{1,0:T(8,128)(2,1)S(1)}, u32[]{:S(2)}, u32[]{:S(2)}) collective-permute-start(bf16[80,1600]{1,0:T(8,128)(2,1)S(1)} %get-tuple-element.89), channel_id=1, source_target_pairs={{0,2},{1,3},{2,0},{3,1},{4,6},{5,7},{6,4},{7,5},{8,10},{9,11},{10,... | collective-permute-start | bytes 768008 | tf_op jit(solution)/shard_map/ppermute | solution.py:42
  90.3 0.0 collective-permute-done.17.got
  90.3 0.1 fold.7
  90.4 1.5 %collective-permute-start.20 = (bf16[80,1280]{1,0:T(8,128)(2,1)S(1)}, bf16[80,1280]{1,0:T(8,128)(2,1)S(1)}, u32[]{:S(2)}, u32[]{:S(2)}) collective-permute-start(bf16[80,1280]{1,0:T(8,128)(2,1)S(1)} %get-tuple-element.92), channel_id=1, source_target_pairs={{0,4},{1,5},{2,6},{3,7},{4,0},{5,1},{6,2},{7,3},{8,12},{9,13},{10,... | collective-permute-start | bytes 614408 | tf_op jit(solution)/shard_map/ppermute | solution.py:42
  91.9 2.0 %input_grad.1 = bf16[14,2,32,640]{3,2,1,0:T(8,128)(2,1)} custom-call(f32[40,128]{1,0:T(8,128)S(1)} %add.43.sums, f32[14,2,32,640]{3,2,1,0:T(8,128)S(1)} %get-tuple-element.95.grad, bf16[14,2,32,640]{3,2,1,0:T(8,128)(2,1)S(1)} %copy-done, bf16[14,2,32,640]{3,2,1,0:T(8,128)(2,1)S(1)} %copy-done.2, f32[14,640]{1,0:T(8,128)S(1)} %get-tuple-element.72.refs_7_.mean, ...), custom_call_target="tpu_custom_call" | custom-call | tf_op jit(solution)/shard_map/input_grad/pallas_call | solution.py:523
  93.9 1.5 %collective-permute-done.21.got = bf16[80,1600]{1,0:T(8,128)(2,1)S(1)} collective-permute-done((bf16[80,1600]{1,0:T(8,128)(2,1)S(1)}, bf16[80,1600]{1,0:T(8,128)(2,1)S(1)}, u32[]{:S(2)}, u32[]{:S(2)}) %collective-permute-start.21) | collective-permute-done | bytes 256032 | tf_op jit(solution)/shard_map/ppermute | solution.py:42
  95.4 0.1 fold.8
  95.5 2.2 %collective-permute-start.22 = (bf16[40,1600]{1,0:T(8,128)(2,1)S(1)}, bf16[40,1600]{1,0:T(8,128)(2,1)S(1)}, u32[]{:S(2)}, u32[]{:S(2)}) collective-permute-start(bf16[40,1600]{1,0:T(8,128)(2,1)S(1)} %get-tuple-element.97), channel_id=1, source_target_pairs={{0,8},{1,9},{2,10},{3,11},{4,12},{5,13},{6,14},{7,15},{8,0},{9,1},... | collective-permute-start | bytes 384008 | tf_op jit(solution)/shard_map/ppermute | solution.py:42
  97.7 0.9 collective-permute-start.23
  98.6 0.6 slice_bitcast_fusion
  99.2 9.3 %conv_forward.1 = bf16[14,2,32,640]{3,2,1,0:T(8,128)(2,1)} custom-call(bf16[3,1792,640]{2,1,0:T(8,128)(2,1)S(1)} %own.1, bf16[9,640,640]{2,1,0:T(8,128)(2,1)S(1)} %get-tuple-element.101.w, bf16[14,2,32,640]{3,2,1,0:T(8,128)(2,1)S(1)} %copy-done), custom_call_target="tpu_custom_call" | custom-call | tf_op jit(solution)/shard_map/conv_forward/pallas_call | solution.py:531
  108.5 0.9 last.1
  (42 shorter events, 0.2 us)
Async XLA Ops:
  0.7 5.3 %copy-start.1 = (bf16[14,2,32,640]{3,2,1,0:T(8,128)(2,1)S(1)}, bf16[14,2,32,640]{3,2,1,0:T(8,128)(2,1)}, u32[]{:S(2)}) copy-start(bf16[14,2,32,640]{3,2,1,0:T(8,128)(2,1)} %u.5) | copy-start | bytes 3440644
  0.7 5.3 %copy-start = (bf16[14,2,32,640]{3,2,1,0:T(8,128)(2,1)S(1)}, bf16[14,2,32,640]{3,2,1,0:T(8,128)(2,1)}, u32[]{:S(2)}) copy-start(bf16[14,2,32,640]{3,2,1,0:T(8,128)(2,1)} %x.7) | copy-start | bytes 3440644
  2.9 13.0 %copy-start.2 = (bf16[14,2,32,640]{3,2,1,0:T(8,128)(2,1)S(1)}, bf16[14,2,32,640]{3,2,1,0:T(8,128)(2,1)}, u32[]{:S(2)}) copy-start(bf16[14,2,32,640]{3,2,1,0:T(8,128)(2,1)} %u.5) | copy-start | bytes 3440644
  3.0 43.3 %collective-permute-start.9 = (bf16[9,160,640]{2,1,0:T(8,128)(2,1)S(1)}, bf16[9,160,640]{2,1,0:T(8,128)(2,1)}, u32[]{:S(2)}, u32[]{:S(2)}) collective-permute-start(bf16[9,160,640]{2,1,0:T(8,128)(2,1)S(1)} %slice.32), channel_id=1, source_target_pairs={{0,16},{16,0},{1,17},{17,1},{2,18},{18,2},{3,19},{19,3},{4,20},{20... | collective-permute-start | bytes 5529608 | tf_op jit(solution)/shard_map/ppermute | solution.py:42
  6.0 9.9 %collective-permute-start.2 = (bf16[14,2,32,640]{3,2,1,0:T(8,128)(2,1)S(1)}, bf16[14,2,32,640]{3,2,1,0:T(8,128)(2,1)S(1)}, u32[]{:S(2)}, u32[]{:S(2)}) collective-permute-start(bf16[14,2,32,640]{3,2,1,0:T(8,128)(2,1)S(1)} %copy-done.1), channel_id=1, source_target_pairs={{0,1},{1,0},{2,3},{3,2},{4,5},{5,4},{6,7},{7,6},{8,9},{9,8},{10,11... | collective-permute-start | bytes 3440648 | tf_op jit(solution)/shard_map/ppermute | solution.py:42
  8.0 22.4 %copy-start.10 = (f32[640]{0:T(1024)S(1)}, f32[640]{0:T(1024)}, u32[]{:S(2)}) copy-start(f32[640]{0:T(1024)} %param.6) | copy-start | bytes 7684
  8.0 22.4 %copy-start.11 = (f32[640]{0:T(1024)S(1)}, f32[640]{0:T(1024)}, u32[]{:S(2)}) copy-start(f32[640]{0:T(1024)} %param.7) | copy-start | bytes 7684
  8.0 17.7 %collective-permute-start.4 = (bf16[14,32,640]{2,1,0:T(8,128)(2,1)S(1)}, bf16[14,32,640]{2,1,0:T(8,128)(2,1)S(1)}, u32[]{:S(2)}, u32[]{:S(2)}) collective-permute-start(bf16[14,32,640]{2,1,0:T(8,128)(2,1)S(1)} %get-tuple-element.59), channel_id=1, source_target_pairs={{1,2},{2,1},{3,4},{4,3},{5,6},{6,5},{7,8},{8,7},{9,10},{10,9},{11,... | collective-permute-start | bytes 1720328 | tf_op jit(solution)/shard_map/ppermute | solution.py:413
  8.8 21.7 %collective-permute-start.6 = (bf16[14,2,32,640]{3,2,1,0:T(8,128)(2,1)S(1)}, bf16[14,2,32,640]{3,2,1,0:T(8,128)(2,1)S(1)}, u32[]{:S(2)}, u32[]{:S(2)}) collective-permute-start(bf16[14,2,32,640]{3,2,1,0:T(8,128)(2,1)S(1)} %copy-done), channel_id=1, source_target_pairs={{0,1},{1,0},{2,3},{3,2},{4,5},{5,4},{6,7},{7,6},{8,9},{9,8},{10,11... | collective-permute-start | bytes 3440648 | tf_op jit(solution)/shard_map/ppermute | solution.py:42
  11.6 2.5 %collective-permute-start = (f32[28,16]{1,0:T(8,128)S(1)}, f32[28,16]{1,0:T(8,128)S(1)}, u32[]{:S(2)}, u32[]{:S(2)}) collective-permute-start(f32[28,16]{1,0:T(8,128)S(1)} %get-tuple-element.56), channel_id=1, source_target_pairs={{0,1},{1,0},{2,3},{3,2},{4,5},{5,4},{6,7},{7,6},{8,9},{9,8},{10,11... | collective-permute-start | bytes 5384 | tf_op jit(solution)/shard_map/ppermute | solution.py:42
  14.1 7.0 %collective-permute-start.1 = (f32[28,16]{1,0:T(8,128)S(1)}, f32[28,16]{1,0:T(8,128)S(1)}, u32[]{:S(2)}, u32[]{:S(2)}) collective-permute-start(f32[28,16]{1,0:T(8,128)S(1)} %add.33), channel_id=1, source_target_pairs={{0,4},{1,5},{2,6},{3,7},{4,0},{5,1},{6,2},{7,3},{8,12},{9,13},{10,... | collective-permute-start | bytes 5384 | tf_op jit(solution)/shard_map/ppermute | solution.py:42
  15.9 14.6 %copy-start.5 = (bf16[14,2,32,640]{3,2,1,0:T(8,128)(2,1)}, bf16[14,2,32,640]{3,2,1,0:T(8,128)(2,1)S(1)}, u32[]{:S(2)}) copy-start(bf16[14,2,32,640]{3,2,1,0:T(8,128)(2,1)S(1)} %collective-permute-done.2.u_mate.refs_4_) | copy-start | bytes 3440644
  21.1 4.6 %collective-permute-start.3 = (f32[28,16]{1,0:T(8,128)S(1)}, f32[28,16]{1,0:T(8,128)S(1)}, u32[]{:S(2)}, u32[]{:S(2)}) collective-permute-start(f32[28,16]{1,0:T(8,128)S(1)} %add.34), channel_id=1, source_target_pairs={{0,8},{1,9},{2,10},{3,11},{4,12},{5,13},{6,14},{7,15},{8,0},{9,1},... | collective-permute-start | bytes 5384 | tf_op jit(solution)/shard_map/ppermute | solution.py:42
  25.7 3.8 %collective-permute-start.5 = (f32[28,16]{1,0:T(8,128)S(1)}, f32[28,16]{1,0:T(8,128)S(1)}, u32[]{:S(2)}, u32[]{:S(2)}) collective-permute-start(f32[28,16]{1,0:T(8,128)S(1)} %add.35), channel_id=1, source_target_pairs={{0,2},{1,3},{2,0},{3,1},{4,6},{5,7},{6,4},{7,5},{8,10},{9,11},{10,... | collective-permute-start | bytes 5384 | tf_op jit(solution)/shard_map/ppermute | solution.py:42
  26.7 3.8 %collective-permute-start.7 = (bf16[14,32,640]{2,1,0:T(8,128)(2,1)S(1)}, bf16[14,32,640]{2,1,0:T(8,128)(2,1)S(1)}, u32[]{:S(2)}, u32[]{:S(2)}) collective-permute-start(bf16[14,32,640]{2,1,0:T(8,128)(2,1)S(1)} %collective-permute-done.4.rim), channel_id=1, source_target_pairs={{0,1},{1,0},{2,3},{3,2},{4,5},{5,4},{6,7},{7,6},{8,9},{9,8},{10,11... | collective-permute-start | bytes 1720328 | tf_op jit(solution)/shard_map/ppermute | solution.py:42
  29.5 15.2 %collective-permute-start.8 = (bf16[14,32,640]{2,1,0:T(8,128)(2,1)S(1)}, bf16[14,32,640]{2,1,0:T(8,128)(2,1)S(1)}, u32[]{:S(2)}, u32[]{:S(2)}) collective-permute-start(bf16[14,32,640]{2,1,0:T(8,128)(2,1)S(1)} %get-tuple-element.67), channel_id=1, source_target_pairs={{1,2},{2,1},{3,4},{4,3},{5,6},{6,5},{7,8},{8,7},{9,10},{10,9},{11,... | collective-permute-start | bytes 1720328 | tf_op jit(solution)/shard_map/ppermute | solution.py:426
  35.7 9.0 %copy-start.3 = (bf16[2688,640]{1,0:T(8,128)(2,1)}, bf16[2688,640]{1,0:T(8,128)(2,1)S(1)}, u32[]{:S(2)}) copy-start(bf16[2688,640]{1,0:T(8,128)(2,1)S(1)} %get-tuple-element.62.mid) | copy-start | bytes 10321924
  35.7 15.8 %copy-start.6 = (bf16[14,2,32,640]{3,2,1,0:T(8,128)(2,1)S(1)}, bf16[14,2,32,640]{3,2,1,0:T(8,128)(2,1)}, u32[]{:S(2)}) copy-start(bf16[14,2,32,640]{3,2,1,0:T(8,128)(2,1)} %copy-done.5) | copy-start | bytes 3440644
  44.8 1.5 %copy-start.9 = (bf16[14,32,640]{2,1,0:T(8,128)(2,1)}, bf16[14,32,640]{2,1,0:T(8,128)(2,1)S(1)}, u32[]{:S(2)}) copy-start(bf16[14,32,640]{2,1,0:T(8,128)(2,1)S(1)} %collective-permute-done.8.refs_5_) | copy-start | bytes 1720324
  46.3 5.3 %collective-permute-start.10 = (bf16[9,160,640]{2,1,0:T(8,128)(2,1)}, bf16[9,160,640]{2,1,0:T(8,128)(2,1)}, u32[]{:S(2)}, u32[]{:S(2)}) collective-permute-start(bf16[9,160,640]{2,1,0:T(8,128)(2,1)} %collective-permute-done.9.refs_1_), channel_id=1, source_target_pairs={{0,1},{1,0},{2,3},{3,2},{4,5},{5,4},{6,7},{7,6},{8,9},{9,8},{10,11... | collective-permute-start | bytes 5529608 | tf_op jit(solution)/shard_map/ppermute | solution.py:42
  47.8 24.9 %collective-permute-start.15 = (bf16[160,3200]{1,0:T(8,128)(2,1)}, bf16[160,3200]{1,0:T(8,128)(2,1)}, u32[]{:S(2)}, u32[]{:S(2)}) collective-permute-start(bf16[160,3200]{1,0:T(8,128)(2,1)} %get-tuple-element.77), channel_id=1, source_target_pairs={{0,4},{1,5},{2,6},{3,7},{4,0},{5,1},{6,2},{7,3},{8,12},{9,13},{10,... | collective-permute-start | bytes 3072008 | tf_op jit(solution)/shard_map/ppermute | solution.py:42
  49.4 25.9 %collective-permute-start.14 = (bf16[320,1280]{1,0:T(8,128)(2,1)}, bf16[320,1280]{1,0:T(8,128)(2,1)}, u32[]{:S(2)}, u32[]{:S(2)}) collective-permute-start(bf16[320,1280]{1,0:T(8,128)(2,1)} %get-tuple-element.68), channel_id=1, source_target_pairs={{0,16},{16,0},{1,17},{17,1},{2,18},{18,2},{3,19},{19,3},{4,20},{20... | collective-permute-start | bytes 2457608 | tf_op jit(solution)/shard_map/ppermute | solution.py:42
  51.6 21.1 %copy-start.7 = (f32[160,3200]{1,0:T(8,128)S(1)}, f32[160,3200]{1,0:T(8,128)}, u32[]{:S(2)}) copy-start(f32[160,3200]{1,0:T(8,128)} %get-tuple-element.76.kept) | copy-start | bytes 6144004
  65.6 9.6 %copy-start.8 = (f32[320,1280]{1,0:T(8,128)S(1)}, f32[320,1280]{1,0:T(8,128)}, u32[]{:S(2)}) copy-start(f32[320,1280]{1,0:T(8,128)} %get-tuple-element.75.kept) | copy-start | bytes 4915204
  65.7 1.3 %collective-permute-start.11 = (f32[40,128]{1,0:T(8,128)S(1)}, f32[40,128]{1,0:T(8,128)S(1)}, u32[]{:S(2)}, u32[]{:S(2)}) collective-permute-start(f32[40,128]{1,0:T(8,128)S(1)} %get-tuple-element.74), channel_id=1, source_target_pairs={{0,1},{1,0},{2,3},{3,2},{4,5},{5,4},{6,7},{7,6},{8,9},{9,8},{10,11... | collective-permute-start | bytes 61448 | tf_op jit(solution)/shard_map/ppermute | solution.py:42
  66.9 3.8 %collective-permute-start.12 = (f32[40,128]{1,0:T(8,128)S(1)}, f32[40,128]{1,0:T(8,128)S(1)}, u32[]{:S(2)}, u32[]{:S(2)}) collective-permute-start(f32[40,128]{1,0:T(8,128)S(1)} %add.39), channel_id=1, source_target_pairs={{0,2},{1,3},{2,0},{3,1},{4,6},{5,7},{6,4},{7,5},{8,10},{9,11},{10,... | collective-permute-start | bytes 61448 | tf_op jit(solution)/shard_map/ppermute | solution.py:42
  70.7 7.9 %collective-permute-start.13 = (f32[10,128]{1,0:T(8,128)S(1)}, f32[10,128]{1,0:T(8,128)S(1)}, u32[]{:S(2)}, u32[]{:S(2)}) collective-permute-start(f32[10,128]{1,0:T(8,128)S(1)} %slice.27), channel_id=1, source_target_pairs={{0,16},{16,0},{1,17},{17,1},{2,18},{18,2},{3,19},{19,3},{4,20},{20... | collective-permute-start | bytes 15368 | tf_op jit(solution)/shard_map/ppermute | solution.py:42
  72.6 7.8 %copy-start.4 = (bf16[2688,640]{1,0:T(8,128)(2,1)S(1)}, bf16[2688,640]{1,0:T(8,128)(2,1)}, u32[]{:S(2)}) copy-start(bf16[2688,640]{1,0:T(8,128)(2,1)} %copy-done.3) | copy-start | bytes 10321924
  74.5 13.2 %collective-permute-start.18 = (bf16[160,1600]{1,0:T(8,128)(2,1)S(1)}, bf16[160,1600]{1,0:T(8,128)(2,1)S(1)}, u32[]{:S(2)}, u32[]{:S(2)}) collective-permute-start(bf16[160,1600]{1,0:T(8,128)(2,1)S(1)} %get-tuple-element.79), channel_id=1, source_target_pairs={{0,16},{16,0},{1,17},{17,1},{2,18},{18,2},{3,19},{19,3},{4,20},{20... | collective-permute-start | bytes 1536008 | tf_op jit(solution)/shard_map/ppermute | solution.py:42
  76.6 13.7 %collective-permute-start.17 = (bf16[160,1280]{1,0:T(8,128)(2,1)S(1)}, bf16[160,1280]{1,0:T(8,128)(2,1)S(1)}, u32[]{:S(2)}, u32[]{:S(2)}) collective-permute-start(bf16[160,1280]{1,0:T(8,128)(2,1)S(1)} %get-tuple-element.81), channel_id=1, source_target_pairs={{0,2},{1,3},{2,0},{3,1},{4,6},{5,7},{6,4},{7,5},{8,10},{9,11},{10,... | collective-permute-start | bytes 1228808 | tf_op jit(solution)/shard_map/ppermute | solution.py:42
  78.6 3.9 %collective-permute-start.16 = (f32[40,128]{1,0:T(8,128)S(1)}, f32[40,128]{1,0:T(8,128)S(1)}, u32[]{:S(2)}, u32[]{:S(2)}) collective-permute-start(f32[40,128]{1,0:T(8,128)S(1)} %pad_maximum_fusion), channel_id=1, source_target_pairs={{0,4},{1,5},{2,6},{3,7},{4,0},{5,1},{6,2},{7,3},{8,12},{9,13},{10,... | collective-permute-start | bytes 61448 | tf_op jit(solution)/shard_map/ppermute | solution.py:42
  82.5 4.7 %collective-permute-start.19 = (f32[40,128]{1,0:T(8,128)S(1)}, f32[40,128]{1,0:T(8,128)S(1)}, u32[]{:S(2)}, u32[]{:S(2)}) collective-permute-start(f32[40,128]{1,0:T(8,128)S(1)} %fusion), channel_id=1, source_target_pairs={{0,8},{1,9},{2,10},{3,11},{4,12},{5,13},{6,14},{7,15},{8,0},{9,1},... | collective-permute-start | bytes 61448 | tf_op jit(solution)/shard_map/ppermute | solution.py:42
  87.8 7.6 %collective-permute-start.21 = (bf16[80,1600]{1,0:T(8,128)(2,1)S(1)}, bf16[80,1600]{1,0:T(8,128)(2,1)S(1)}, u32[]{:S(2)}, u32[]{:S(2)}) collective-permute-start(bf16[80,1600]{1,0:T(8,128)(2,1)S(1)} %get-tuple-element.89), channel_id=1, source_target_pairs={{0,2},{1,3},{2,0},{3,1},{4,6},{5,7},{6,4},{7,5},{8,10},{9,11},{10,... | collective-permute-start | bytes 768008 | tf_op jit(solution)/shard_map/ppermute | solution.py:42
  90.4 7.3 %collective-permute-start.20 = (bf16[80,1280]{1,0:T(8,128)(2,1)S(1)}, bf16[80,1280]{1,0:T(8,128)(2,1)S(1)}, u32[]{:S(2)}, u32[]{:S(2)}) collective-permute-start(bf16[80,1280]{1,0:T(8,128)(2,1)S(1)} %get-tuple-element.92), channel_id=1, source_target_pairs={{0,4},{1,5},{2,6},{3,7},{4,0},{5,1},{6,2},{7,3},{8,12},{9,13},{10,... | collective-permute-start | bytes 614408 | tf_op jit(solution)/shard_map/ppermute | solution.py:42
  95.5 13.0 %collective-permute-start.22 = (bf16[40,1600]{1,0:T(8,128)(2,1)S(1)}, bf16[40,1600]{1,0:T(8,128)(2,1)S(1)}, u32[]{:S(2)}, u32[]{:S(2)}) collective-permute-start(bf16[40,1600]{1,0:T(8,128)(2,1)S(1)} %get-tuple-element.97), channel_id=1, source_target_pairs={{0,8},{1,9},{2,10},{3,11},{4,12},{5,13},{6,14},{7,15},{8,0},{9,1},... | collective-permute-start | bytes 384008 | tf_op jit(solution)/shard_map/ppermute | solution.py:42
  97.7 10.7 %collective-permute-start.23 = (bf16[40,1280]{1,0:T(8,128)(2,1)S(1)}, bf16[40,1280]{1,0:T(8,128)(2,1)S(1)}, u32[]{:S(2)}, u32[]{:S(2)}) collective-permute-start(bf16[40,1280]{1,0:T(8,128)(2,1)S(1)} %get-tuple-element.99), channel_id=1, source_target_pairs={{0,8},{1,9},{2,10},{3,11},{4,12},{5,13},{6,14},{7,15},{8,0},{9,1},... | collective-permute-start | bytes 307208 | tf_op jit(solution)/shard_map/ppermute | solution.py:42

commit v6 on v5

--- a/solution.py
+++ b/solution.py
@@ -9,7 +9,7 @@
 
 GSIZE = 40
 EPS = 1e-05
-GROUP_A, GROUP_B = (0, 1, 2, 3, 4), (5, 6, 7, 8)
+GROUP_A, GROUP_B = (0, 1, 2, 3), (4, 5, 6, 7, 8)
 LANES = 128
 F32 = jnp.float32
 BF16 = jnp.bfloat16
@@ -247,18 +247,24 @@
     lax.fori_loop(0, out.shape[1] // columns, fill, 0)
 
 
-def conv_kernel(own, w, x, out):
+def conv_row(row, own, w, x):
     images, _, columns, channels = x.shape
     block = images * columns
     taps = w.shape[0]
-    rhs = w[...].reshape(taps * channels, channels)
-    for r in range(2):
-        lhs = jnp.concatenate([
-            own[t % 3, (r + t // 3) * block : (r + t // 3 + 1) * block, :] for t in range(taps)
-        ], axis=1)
-        value = jnp.dot(lhs, rhs, preferred_element_type=F32)
-        value = value.reshape(images, columns, channels)
-        out[:, r] = (x[:, r].astype(F32) + value).astype(BF16)
+    lhs = jnp.concatenate([
+        own[t % 3, (row + t // 3) * block : (row + t // 3 + 1) * block, :] for t in range(taps)
+    ], axis=1)
+    value = jnp.dot(lhs, w[...].reshape(taps * channels, channels), preferred_element_type=F32)
+    return (x[:, row].astype(F32) + value.reshape(images, columns, channels)).astype(BF16)
+
+
+def conv_first_kernel(own, w, x, out):
+    out[...] = conv_row(0, own, w, x)
+
+
+def conv_kernel(own, w, x, first, out):
+    out[:, 0] = first[...]
+    out[:, 1] = conv_row(1, own, w, x)
 
 
 def back_kernel(info, places, *refs):
@@ -495,17 +501,11 @@
     last = base + 2 * channels // LANES
     for place in range(2):
         sums = sums + swap(sums, "space", 1 << place)
-    totals = sums[base:last]
     if two:
-        more = swap(totals, "dp", 1)
         sent_a, kept_a = split(kept_a, after(got_a, sums))
         got_a = swap(sent_a, "dp", 1)
         sent_b, kept_b = fold(kept_b, after(got_b, sent_a))
         got_b = swap(sent_b, "space", 2)
-        totals = totals + after(more, sent_b)
-    else:
-        totals = lax.psum(totals, "dp")
-    sums = jnp.concatenate([sums[:base], totals, sums[last:]])
     own = kernel_call(
         functools.partial(own_kernel, columns), 16, struct((3, 4 * block, channels), BF16),
         [S, V], "own",
@@ -514,6 +514,11 @@
         step = swap(sums, "space", 1 << place)
         if place == 2:
             step, own = lax.optimization_barrier((step, own))
+        if place == 3:
+            first_row = kernel_call(
+                conv_first_kernel, 32, struct(row_shape, BF16), [V] * 3, "conv_forward"
+            )(after(own, sums), weights, inputs)
+            step, first_row = lax.optimization_barrier((step, first_row))
         sums = sums + step
     sent_a, kept_a = fold(kept_a, after(got_a, sums))
     got_a = swap(sent_a, "space", 2)
@@ -523,15 +528,17 @@
     input_grad = kernel_call(
         functools.partial(input_kernel, size), 16, struct(inputs.shape, BF16), [V] * 7, "input_grad"
     )(sums, grad, inputs, upstream, mean, rstd, gain_row)
-    totals = sums[base:last].reshape(2, channels)
+    totals = sums[base:last]
+    more = swap(totals, "dp", 1) if two else lax.psum(totals, "dp")
     sent_a, kept_a = fold(kept_a, after(got_a, input_grad))
     got_a = swap(sent_a, "space", 8)
     sent_b, kept_b = fold(kept_b, after(got_b, sent_a))
     got_b = swap(sent_b, "space", 8)
     mixed = kernel_call(
-        conv_kernel, 32, struct(inputs.shape, BF16), [V] * 3, "conv_forward"
-    )(after(own, sent_b), weights, inputs)
-    got_a = after(got_a, mixed)
+        conv_kernel, 32, struct(inputs.shape, BF16), [V] * 4, "conv_forward"
+    )(after(own, sent_b), weights, inputs, first_row)
+    got_a, more = lax.optimization_barrier((got_a, more, mixed))[:2]
+    totals = (totals + more if two else more).reshape(2, channels)
     wide = channels // 2 if two else channels
     weight_grad = kernel_call(
         last_kernel, 16, struct((taps, kept_a.shape[0], wide), F32), [V] * 4, "last"

time: 110 us -> 107 us (0.973)
  waiting for transfers between devices: 22.7 us -> 19.6 us
    ppermute x22, waiting for transfers between devices: 22.7 us -> 19.6 us  [swap(): return lax.ppermute(value, axis, [(i, i ^ bit) for i in range(count)])]
    pallas_call x1 -> x2, Pallas kernels: 9.26 us -> 9.52 us  [the longest x1 5.26 us: body(): kernel_call(conv_kernel, 32, struct(inputs.shape, BF16), [V] * 4, 'conv_f...]
  transfers between devices with their start and end apart: 24 -> 24, of which waited for: 12 -> 11; matrix products, arithmetic and copies ran while one was open for 1% -> 1% of each run, Pallas kernels for 45% -> 45%
where the time goes in v6:
time: 107 us; the launch traced here: 106 us
  Pallas kernels  52.3 us (49%)
  starting transfers between devices  32.8 us (31%)
  waiting for transfers between devices  19.6 us (18%)
    ppermute x22, starting transfers between devices, swap(): return lax.ppermute(value, axis, [(i, i ^ bit) for i in range(count)])  31.2 us
    ppermute x22, waiting for transfers between devices, swap(): return lax.ppermute(value, axis, [(i, i ^ bit) for i in range(count)])  19.6 us
    pallas_call x1, Pallas kernels, body(): kernel_call(back_kernel, 32, (struct(inputs.shape, F32), struct((40, LANE...  14.1 us
    pallas_call x1, Pallas kernels, body(): kernel_call(functools.partial(grad_kernel, block, two), 28, tuple((pltpu....  9.04 us
    pallas_call x1, Pallas kernels, body(): kernel_call(conv_kernel, 32, struct(inputs.shape, BF16), [V] * 4, 'conv_f...  5.26 us
    pallas_call x1, Pallas kernels, body(): kernel_call(functools.partial(act_kernel, size), 24, (struct((6 * block,...  5.2 us
    pallas_call x1, Pallas kernels, body(): kernel_call(conv_first_kernel, 32, struct(row_shape, BF16), [V] * 3, 'con...  4.26 us
    pallas_call x1, Pallas kernels, body(): kernel_call(slice_kernel, 8, struct((taps, part, channels), BF16), [S, H]...  2.2 us
  transfers between devices with their start and end apart: 24, of which 11 were waited for; matrix products, arithmetic and copies ran while one was open for 1% of the time, Pallas kernels for 45%

profile of v6, /device:TPU:0, one launch (start us, length us, event | category | flops | bytes accessed | tf_op | source)
XLA Modules:
  0.0 106.5 jit_solution(8356166773222381390)
XLA Ops:
  0.7 0.1 stack.35.info
  0.7 2.2 %slice.20 = bf16[9,160,640]{2,1,0:T(8,128)(2,1)S(1)} custom-call(s32[5]{0:T(128)S(1)} %stack.35.info, bf16[9,320,640]{2,1,0:T(8,128)(2,1)} %refs_0_.1), custom_call_target="tpu_custom_call" | custom-call | tf_op jit(solution)/shard_map/slice/pallas_call | solution.py:408
  2.9 0.0 copy-start.2
  3.0 3.0 %collective-permute-start.9 = (bf16[9,160,640]{2,1,0:T(8,128)(2,1)S(1)}, bf16[9,160,640]{2,1,0:T(8,128)(2,1)}, u32[]{:S(2)}, u32[]{:S(2)}) collective-permute-start(bf16[9,160,640]{2,1,0:T(8,128)(2,1)S(1)} %slice.20), channel_id=1, source_target_pairs={{0,16},{16,0},{1,17},{17,1},{2,18},{18,2},{3,19},{19,3},{4,20},{20... | collective-permute-start | bytes 5529608 | tf_op jit(solution)/shard_map/ppermute | solution.py:42
  6.0 0.0 collective-permute-start.2
  6.0 2.0 %stats.1 = (f32[28,16]{1,0:T(8,128)S(1)}, bf16[14,32,640]{2,1,0:T(8,128)(2,1)S(1)}, bf16[14,32,640]{2,1,0:T(8,128)(2,1)S(1)}) custom-call(s32[5]{0:T(128)S(1)} %stack.35.info, bf16[14,2,32,640]{3,2,1,0:T(8,128)(2,1)S(1)} %copy-done, bf16[14,2,32,640]{3,2,1,0:T(8,128)(2,1)} %u.5), custom_call_target="tpu_custom_call" | custom-call | tf_op jit(solution)/shard_map/stats/pallas_call | solution.py:414
  8.0 0.7 collective-permute-start.4
  8.7 2.9 %collective-permute-start.6 = (bf16[14,2,32,640]{3,2,1,0:T(8,128)(2,1)S(1)}, bf16[14,2,32,640]{3,2,1,0:T(8,128)(2,1)S(1)}, u32[]{:S(2)}, u32[]{:S(2)}) collective-permute-start(bf16[14,2,32,640]{3,2,1,0:T(8,128)(2,1)S(1)} %copy-done), channel_id=1, source_target_pairs={{0,1},{1,0},{2,3},{3,2},{4,5},{5,4},{6,7},{7,6},{8,9},{9,8},{10,11... | collective-permute-start | bytes 3440648 | tf_op jit(solution)/shard_map/ppermute | solution.py:42
  11.6 0.1 collective-permute-start
  11.7 2.4 %collective-permute-done = f32[28,16]{1,0:T(8,128)S(1)} collective-permute-done((f32[28,16]{1,0:T(8,128)S(1)}, f32[28,16]{1,0:T(8,128)S(1)}, u32[]{:S(2)}, u32[]{:S(2)}) %collective-permute-start) | collective-permute-done | bytes 1824 | tf_op jit(solution)/shard_map/ppermute | solution.py:42
  14.1 1.9 %collective-permute-start.1 = (f32[28,16]{1,0:T(8,128)S(1)}, f32[28,16]{1,0:T(8,128)S(1)}, u32[]{:S(2)}, u32[]{:S(2)}) collective-permute-start(f32[28,16]{1,0:T(8,128)S(1)} %add.33), channel_id=1, source_target_pairs={{0,4},{1,5},{2,6},{3,7},{4,0},{5,1},{6,2},{7,3},{8,12},{9,13},{10,... | collective-permute-start | bytes 5384 | tf_op jit(solution)/shard_map/ppermute | solution.py:42
  16.0 0.0 collective-permute-done.2.u_mate.refs_4_
  16.0 1.9 %turn.1.lhs = bf16[320,1792]{1,0:T(8,128)(2,1)S(1)} custom-call(s32[5]{0:T(128)S(1)} %stack.35.info, bf16[14,2,32,640]{3,2,1,0:T(8,128)(2,1)S(1)} %copy-done.2, bf16[14,2,32,640]{3,2,1,0:T(8,128)(2,1)S(1)} %collective-permute-done.2.u_mate.refs_4_), custom_call_target="tpu_custom_call" | custom-call | tf_op jit(solution)/shard_map/turn/pallas_call | solution.py:420
  17.9 3.1 %collective-permute-done.1 = f32[28,16]{1,0:T(8,128)S(1)} collective-permute-done((f32[28,16]{1,0:T(8,128)S(1)}, f32[28,16]{1,0:T(8,128)S(1)}, u32[]{:S(2)}, u32[]{:S(2)}) %collective-permute-start.1) | collective-permute-done | bytes 1824 | tf_op jit(solution)/shard_map/ppermute | solution.py:42
  21.1 2.8 %collective-permute-start.3 = (f32[28,16]{1,0:T(8,128)S(1)}, f32[28,16]{1,0:T(8,128)S(1)}, u32[]{:S(2)}, u32[]{:S(2)}) collective-permute-start(f32[28,16]{1,0:T(8,128)S(1)} %add.34), channel_id=1, source_target_pairs={{0,8},{1,9},{2,10},{3,11},{4,12},{5,13},{6,14},{7,15},{8,0},{9,1},... | collective-permute-start | bytes 5384 | tf_op jit(solution)/shard_map/ppermute | solution.py:42
  23.8 1.9 %collective-permute-done.3 = f32[28,16]{1,0:T(8,128)S(1)} collective-permute-done((f32[28,16]{1,0:T(8,128)S(1)}, f32[28,16]{1,0:T(8,128)S(1)}, u32[]{:S(2)}, u32[]{:S(2)}) %collective-permute-start.3) | collective-permute-done | bytes 1824 | tf_op jit(solution)/shard_map/ppermute | solution.py:42
  25.7 0.0 collective-permute-done.4.rim
  25.7 1.0 collective-permute-start.5
  26.7 0.0 collective-permute-start.7
  26.7 2.8 %collective-permute-done.5 = f32[28,16]{1,0:T(8,128)S(1)} collective-permute-done((f32[28,16]{1,0:T(8,128)S(1)}, f32[28,16]{1,0:T(8,128)S(1)}, u32[]{:S(2)}, u32[]{:S(2)}) %collective-permute-start.5) | collective-permute-done | bytes 1824 | tf_op jit(solution)/shard_map/ppermute | solution.py:42
  29.5 0.9 collective-permute-start.8
  30.4 0.0 collective-permute-done.6.x_mate
  30.5 0.0 collective-permute-done.7.rim_mate
  30.5 5.2 %activate.1 = (bf16[2688,640]{1,0:T(8,128)(2,1)S(1)}, bf16[2,2688,640]{2,1,0:T(8,128)(2,1)S(1)}, f32[14,640]{1,0:T(8,128)S(1)}, f32[14,640]{1,0:T(8,128)S(1)}) custom-call(s32[5]{0:T(128)S(1)} %stack.35.info, f32[28,16]{1,0:T(8,128)S(1)} %add.36.stats, bf16[14,2,32,640]{3,2,1,0:T(8,128)(2,1)S(1)} %copy-done, ...), custom_call_target="tpu_custom_call" | custom-call | tf_op jit(solution)/shard_map/activate/pallas_call | solution.py:434
  35.7 0.0 copy-start.6
  35.7 9.0 %weight_terms.1 = (bf16[160,2560]{1,0:T(8,128)(2,1)}, f32[160,2560]{1,0:T(8,128)}, bf16[320,1600]{1,0:T(8,128)(2,1)}, f32[320,1600]{1,0:T(8,128)}) custom-call(s32[5]{0:T(128)S(1)} %stack.35.info, bf16[320,1792]{1,0:T(8,128)(2,1)S(1)} %turn.1.lhs, bf16[2688,640]{1,0:T(8,128)(2,1)S(1)} %get-tuple-element.65.mid, bf16[2,2688,640]{2,1,0:T(8,128)(2,1)S(1)} %get-tuple-element.66.side), custom_call_target="tpu_custom_call" | custom-call | tf_op jit(solution)/shard_map/weight_terms/pallas_call | solution.py:462
  44.7 0.0 collective-permute-done.8.refs_5_
  44.8 1.5 %collective-permute-done.9.refs_1_ = bf16[9,160,640]{2,1,0:T(8,128)(2,1)} collective-permute-done((bf16[9,160,640]{2,1,0:T(8,128)(2,1)S(1)}, bf16[9,160,640]{2,1,0:T(8,128)(2,1)}, u32[]{:S(2)}, u32[]{:S(2)}) %collective-permute-start.9) | collective-permute-done | bytes 1843232 | tf_op jit(solution)/shard_map/ppermute | solution.py:42
  46.3 1.5 %collective-permute-start.10 = (bf16[9,160,640]{2,1,0:T(8,128)(2,1)}, bf16[9,160,640]{2,1,0:T(8,128)(2,1)}, u32[]{:S(2)}, u32[]{:S(2)}) collective-permute-start(bf16[9,160,640]{2,1,0:T(8,128)(2,1)} %collective-permute-done.9.refs_1_), channel_id=1, source_target_pairs={{0,1},{1,0},{2,3},{3,2},{4,5},{5,4},{6,7},{7,6},{8,9},{9,8},{10,11... | collective-permute-start | bytes 5529608 | tf_op jit(solution)/shard_map/ppermute | solution.py:42
  47.8 0.5 collective-permute-start.14
  48.3 1.6 %collective-permute-start.15 = (bf16[160,2560]{1,0:T(8,128)(2,1)}, bf16[160,2560]{1,0:T(8,128)(2,1)}, u32[]{:S(2)}, u32[]{:S(2)}) collective-permute-start(bf16[160,2560]{1,0:T(8,128)(2,1)} %get-tuple-element.80), channel_id=1, source_target_pairs={{0,4},{1,5},{2,6},{3,7},{4,0},{5,1},{6,2},{7,3},{8,12},{9,13},{10,... | collective-permute-start | bytes 2457608 | tf_op jit(solution)/shard_map/ppermute | solution.py:42
  49.9 0.1 pad_add_fusion.places
  50.0 1.6 %collective-permute-done.10.refs_2_ = bf16[9,160,640]{2,1,0:T(8,128)(2,1)} collective-permute-done((bf16[9,160,640]{2,1,0:T(8,128)(2,1)}, bf16[9,160,640]{2,1,0:T(8,128)(2,1)}, u32[]{:S(2)}, u32[]{:S(2)}) %collective-permute-start.10) | collective-permute-done | bytes 1843232 | tf_op jit(solution)/shard_map/ppermute | solution.py:42
  51.6 14.1 %conv_backward.1 = (f32[14,2,32,640]{3,2,1,0:T(8,128)S(1)}, f32[40,128]{1,0:T(8,128)S(1)}, bf16[9,640,640]{2,1,0:T(8,128)(2,1)S(1)}) custom-call(s32[5]{0:T(128)S(1)} %stack.35.info, s32[3]{0:T(128)S(1)} %pad_add_fusion.places, bf16[9,320,640]{2,1,0:T(8,128)(2,1)} %refs_0_.1, bf16[9,160,640]{2,1,0:T(8,128)(2,1)} %collective-permute-done.9.refs_1_, ...), custom_call_target="tpu_custom_call" | custom-call | tf_op jit(solution)/shard_map/conv_backward/pallas_call | solution.py:479
  65.6 0.4 collective-permute-start.11
  66.1 0.8 collective-permute-done.11
  66.9 1.0 collective-permute-start.12
  67.9 2.8 %collective-permute-done.12 = f32[40,128]{1,0:T(8,128)S(1)} collective-permute-done((f32[40,128]{1,0:T(8,128)S(1)}, f32[40,128]{1,0:T(8,128)S(1)}, u32[]{:S(2)}, u32[]{:S(2)}) %collective-permute-start.12) | collective-permute-done | bytes 20512 | tf_op jit(solution)/shard_map/ppermute | solution.py:42
  70.7 1.6 %split.1 = (bf16[160,1280]{1,0:T(8,128)(2,1)S(1)}, f32[160,1280]{1,0:T(8,128)S(1)}) custom-call(s32[5]{0:T(128)S(1)} %stack.35.info, f32[160,2560]{1,0:T(8,128)S(1)} %copy-done.8, bf16[160,2560]{1,0:T(8,128)(2,1)} %collective-permute-done.15.got), custom_call_target="tpu_custom_call" | custom-call | tf_op jit(solution)/shard_map/split/pallas_call | solution.py:453
  72.4 1.2 %collective-permute-done.14.got = bf16[320,1600]{1,0:T(8,128)(2,1)} collective-permute-done((bf16[320,1600]{1,0:T(8,128)(2,1)}, bf16[320,1600]{1,0:T(8,128)(2,1)}, u32[]{:S(2)}, u32[]{:S(2)}) %collective-permute-start.14) | collective-permute-done | bytes 1024032 | tf_op jit(solution)/shard_map/ppermute | solution.py:42
  73.5 1.4 %fold.5 = (bf16[160,1600]{1,0:T(8,128)(2,1)S(1)}, f32[160,1600]{1,0:T(8,128)S(1)}) custom-call(f32[320,1600]{1,0:T(8,128)S(1)} %copy-done.7, bf16[320,1600]{1,0:T(8,128)(2,1)} %collective-permute-done.14.got), custom_call_target="tpu_custom_call" | custom-call | tf_op jit(solution)/shard_map/fold/pallas_call | solution.py:447
  75.0 1.1 %collective-permute-start.16 = (bf16[160,1600]{1,0:T(8,128)(2,1)S(1)}, bf16[160,1600]{1,0:T(8,128)(2,1)S(1)}, u32[]{:S(2)}, u32[]{:S(2)}) collective-permute-start(bf16[160,1600]{1,0:T(8,128)(2,1)S(1)} %get-tuple-element.84), channel_id=1, source_target_pairs={{0,2},{1,3},{2,0},{3,1},{4,6},{5,7},{6,4},{7,5},{8,10},{9,11},{10,... | collective-permute-start | bytes 1536008 | tf_op jit(solution)/shard_map/ppermute | solution.py:42
  76.1 1.2 %collective-permute-start.17 = (bf16[160,1280]{1,0:T(8,128)(2,1)S(1)}, bf16[160,1280]{1,0:T(8,128)(2,1)S(1)}, u32[]{:S(2)}, u32[]{:S(2)}) collective-permute-start(bf16[160,1280]{1,0:T(8,128)(2,1)S(1)} %get-tuple-element.82), channel_id=1, source_target_pairs={{0,16},{16,0},{1,17},{17,1},{2,18},{18,2},{3,19},{19,3},{4,20},{20... | collective-permute-start | bytes 1228808 | tf_op jit(solution)/shard_map/ppermute | solution.py:42
  77.3 2.2 %collective-permute-start.13 = (f32[40,128]{1,0:T(8,128)S(1)}, f32[40,128]{1,0:T(8,128)S(1)}, u32[]{:S(2)}, u32[]{:S(2)}) collective-permute-start(f32[40,128]{1,0:T(8,128)S(1)} %add.40), channel_id=1, source_target_pairs={{0,4},{1,5},{2,6},{3,7},{4,0},{5,1},{6,2},{7,3},{8,12},{9,13},{10,... | collective-permute-start | bytes 61448 | tf_op jit(solution)/shard_map/ppermute | solution.py:42
  79.4 2.0 %own.1 = bf16[3,1792,640]{2,1,0:T(8,128)(2,1)S(1)} custom-call(s32[5]{0:T(128)S(1)} %stack.35.info, bf16[2688,640]{1,0:T(8,128)(2,1)S(1)} %copy-done.4), custom_call_target="tpu_custom_call" | custom-call | tf_op jit(solution)/shard_map/own/pallas_call | solution.py:509
  81.5 2.1 %collective-permute-start.18 = (f32[40,128]{1,0:T(8,128)S(1)}, f32[40,128]{1,0:T(8,128)S(1)}, u32[]{:S(2)}, u32[]{:S(2)}) collective-permute-start(f32[40,128]{1,0:T(8,128)S(1)} %add.41), channel_id=1, source_target_pairs={{0,8},{1,9},{2,10},{3,11},{4,12},{5,13},{6,14},{7,15},{8,0},{9,1},... | collective-permute-start | bytes 61448 | tf_op jit(solution)/shard_map/ppermute | solution.py:42
  83.6 4.3 %conv_forward.2.first = bf16[14,32,640]{2,1,0:T(8,128)(2,1)S(1)} custom-call(bf16[3,1792,640]{2,1,0:T(8,128)(2,1)S(1)} %own.1, bf16[9,640,640]{2,1,0:T(8,128)(2,1)S(1)} %get-tuple-element.91.w, bf16[14,2,32,640]{3,2,1,0:T(8,128)(2,1)S(1)} %copy-done), custom_call_target="tpu_custom_call" | custom-call | tf_op jit(solution)/shard_map/conv_forward/pallas_call | solution.py:518
  87.9 0.0 collective-permute-done.17.got
  87.9 0.1 fold.6
  88.0 0.6 collective-permute-start.20
  88.6 0.1 fold.7
  88.7 2.2 %collective-permute-start.19 = (bf16[80,1600]{1,0:T(8,128)(2,1)S(1)}, bf16[80,1600]{1,0:T(8,128)(2,1)S(1)}, u32[]{:S(2)}, u32[]{:S(2)}) collective-permute-start(bf16[80,1600]{1,0:T(8,128)(2,1)S(1)} %get-tuple-element.97), channel_id=1, source_target_pairs={{0,4},{1,5},{2,6},{3,7},{4,0},{5,1},{6,2},{7,3},{8,12},{9,13},{10,... | collective-permute-start | bytes 768008 | tf_op jit(solution)/shard_map/ppermute | solution.py:42
  91.0 2.0 %input_grad.1 = bf16[14,2,32,640]{3,2,1,0:T(8,128)(2,1)} custom-call(f32[40,128]{1,0:T(8,128)S(1)} %add.42.sums, f32[14,2,32,640]{3,2,1,0:T(8,128)S(1)} %get-tuple-element.100.grad, bf16[14,2,32,640]{3,2,1,0:T(8,128)(2,1)S(1)} %copy-done, bf16[14,2,32,640]{3,2,1,0:T(8,128)(2,1)S(1)} %copy-done.2, f32[14,640]{1,0:T(8,128)S(1)} %get-tuple-element.75.refs_7_.mean, ...), custom_call_target="tpu_custom_call" | custom-call | tf_op jit(solution)/shard_map/input_grad/pallas_call | solution.py:528
  93.0 0.8 collective-permute-done.20.got
  93.9 1.7 %collective-permute-start.21 = (bf16[40,1280]{1,0:T(8,128)(2,1)S(1)}, bf16[40,1280]{1,0:T(8,128)(2,1)S(1)}, u32[]{:S(2)}, u32[]{:S(2)}) collective-permute-start(bf16[40,1280]{1,0:T(8,128)(2,1)S(1)} %get-tuple-element.102), channel_id=1, source_target_pairs={{0,8},{1,9},{2,10},{3,11},{4,12},{5,13},{6,14},{7,15},{8,0},{9,1},... | collective-permute-start | bytes 307208 | tf_op jit(solution)/shard_map/ppermute | solution.py:42
  95.6 1.1 %collective-permute-start.22 = (f32[10,128]{1,0:T(8,128)S(1)}, f32[10,128]{1,0:T(8,128)S(1)}, u32[]{:S(2)}, u32[]{:S(2)}) collective-permute-start(f32[10,128]{1,0:T(8,128)S(1)} %slice.12), channel_id=1, source_target_pairs={{0,16},{16,0},{1,17},{17,1},{2,18},{18,2},{3,19},{19,3},{4,20},{20... | collective-permute-start | bytes 15368 | tf_op jit(solution)/shard_map/ppermute | solution.py:42
  96.7 0.1 fold.9
  96.7 2.3 %collective-permute-start.23 = (bf16[40,1600]{1,0:T(8,128)(2,1)S(1)}, bf16[40,1600]{1,0:T(8,128)(2,1)S(1)}, u32[]{:S(2)}, u32[]{:S(2)}) collective-permute-start(bf16[40,1600]{1,0:T(8,128)(2,1)S(1)} %get-tuple-element.104), channel_id=1, source_target_pairs={{0,8},{1,9},{2,10},{3,11},{4,12},{5,13},{6,14},{7,15},{8,0},{9,1},... | collective-permute-start | bytes 384008 | tf_op jit(solution)/shard_map/ppermute | solution.py:42
  99.1 5.3 %conv_forward.3 = bf16[14,2,32,640]{3,2,1,0:T(8,128)(2,1)} custom-call(bf16[3,1792,640]{2,1,0:T(8,128)(2,1)S(1)} %own.1, bf16[9,640,640]{2,1,0:T(8,128)(2,1)S(1)} %get-tuple-element.91.w, bf16[14,2,32,640]{3,2,1,0:T(8,128)(2,1)S(1)} %copy-done, bf16[14,32,640]{2,1,0:T(8,128)(2,1)S(1)} %conv_forward.2.first), custom_call_target="tpu_custom_call" | custom-call | tf_op jit(solution)/shard_map/conv_forward/pallas_call | solution.py:537
  104.3 0.0 collective-permute-done.22
  104.3 0.0 collective-permute-done.21.got_a
  104.4 0.6 slice_bitcast_fusion
  105.0 0.6 collective-permute-done.23.got_b
  105.5 0.9 last.1
  (40 shorter events, 0.2 us)
Async XLA Ops:
  0.7 5.3 %copy-start.1 = (bf16[14,2,32,640]{3,2,1,0:T(8,128)(2,1)S(1)}, bf16[14,2,32,640]{3,2,1,0:T(8,128)(2,1)}, u32[]{:S(2)}) copy-start(bf16[14,2,32,640]{3,2,1,0:T(8,128)(2,1)} %u.5) | copy-start | bytes 3440644
  0.7 5.3 %copy-start = (bf16[14,2,32,640]{3,2,1,0:T(8,128)(2,1)S(1)}, bf16[14,2,32,640]{3,2,1,0:T(8,128)(2,1)}, u32[]{:S(2)}) copy-start(bf16[14,2,32,640]{3,2,1,0:T(8,128)(2,1)} %x.9) | copy-start | bytes 3440644
  2.9 13.0 %copy-start.2 = (bf16[14,2,32,640]{3,2,1,0:T(8,128)(2,1)S(1)}, bf16[14,2,32,640]{3,2,1,0:T(8,128)(2,1)}, u32[]{:S(2)}) copy-start(bf16[14,2,32,640]{3,2,1,0:T(8,128)(2,1)} %u.5) | copy-start | bytes 3440644
  3.0 43.3 %collective-permute-start.9 = (bf16[9,160,640]{2,1,0:T(8,128)(2,1)S(1)}, bf16[9,160,640]{2,1,0:T(8,128)(2,1)}, u32[]{:S(2)}, u32[]{:S(2)}) collective-permute-start(bf16[9,160,640]{2,1,0:T(8,128)(2,1)S(1)} %slice.20), channel_id=1, source_target_pairs={{0,16},{16,0},{1,17},{17,1},{2,18},{18,2},{3,19},{19,3},{4,20},{20... | collective-permute-start | bytes 5529608 | tf_op jit(solution)/shard_map/ppermute | solution.py:42
  6.0 10.0 %collective-permute-start.2 = (bf16[14,2,32,640]{3,2,1,0:T(8,128)(2,1)S(1)}, bf16[14,2,32,640]{3,2,1,0:T(8,128)(2,1)S(1)}, u32[]{:S(2)}, u32[]{:S(2)}) collective-permute-start(bf16[14,2,32,640]{3,2,1,0:T(8,128)(2,1)S(1)} %copy-done.1), channel_id=1, source_target_pairs={{0,1},{1,0},{2,3},{3,2},{4,5},{5,4},{6,7},{7,6},{8,9},{9,8},{10,11... | collective-permute-start | bytes 3440648 | tf_op jit(solution)/shard_map/ppermute | solution.py:42
  8.0 17.7 %collective-permute-start.4 = (bf16[14,32,640]{2,1,0:T(8,128)(2,1)S(1)}, bf16[14,32,640]{2,1,0:T(8,128)(2,1)S(1)}, u32[]{:S(2)}, u32[]{:S(2)}) collective-permute-start(bf16[14,32,640]{2,1,0:T(8,128)(2,1)S(1)} %get-tuple-element.62), channel_id=1, source_target_pairs={{1,2},{2,1},{3,4},{4,3},{5,6},{6,5},{7,8},{8,7},{9,10},{10,9},{11,... | collective-permute-start | bytes 1720328 | tf_op jit(solution)/shard_map/ppermute | solution.py:419
  8.7 21.7 %collective-permute-start.6 = (bf16[14,2,32,640]{3,2,1,0:T(8,128)(2,1)S(1)}, bf16[14,2,32,640]{3,2,1,0:T(8,128)(2,1)S(1)}, u32[]{:S(2)}, u32[]{:S(2)}) collective-permute-start(bf16[14,2,32,640]{3,2,1,0:T(8,128)(2,1)S(1)} %copy-done), channel_id=1, source_target_pairs={{0,1},{1,0},{2,3},{3,2},{4,5},{5,4},{6,7},{7,6},{8,9},{9,8},{10,11... | collective-permute-start | bytes 3440648 | tf_op jit(solution)/shard_map/ppermute | solution.py:42
  11.6 2.5 %collective-permute-start = (f32[28,16]{1,0:T(8,128)S(1)}, f32[28,16]{1,0:T(8,128)S(1)}, u32[]{:S(2)}, u32[]{:S(2)}) collective-permute-start(f32[28,16]{1,0:T(8,128)S(1)} %get-tuple-element.59), channel_id=1, source_target_pairs={{0,1},{1,0},{2,3},{3,2},{4,5},{5,4},{6,7},{7,6},{8,9},{9,8},{10,11... | collective-permute-start | bytes 5384 | tf_op jit(solution)/shard_map/ppermute | solution.py:42
  14.1 16.3 %copy-start.10 = (f32[640]{0:T(1024)S(1)}, f32[640]{0:T(1024)}, u32[]{:S(2)}) copy-start(f32[640]{0:T(1024)} %param.6) | copy-start | bytes 7684
  14.1 16.4 %copy-start.11 = (f32[640]{0:T(1024)S(1)}, f32[640]{0:T(1024)}, u32[]{:S(2)}) copy-start(f32[640]{0:T(1024)} %param.7) | copy-start | bytes 7684
  14.1 7.0 %collective-permute-start.1 = (f32[28,16]{1,0:T(8,128)S(1)}, f32[28,16]{1,0:T(8,128)S(1)}, u32[]{:S(2)}, u32[]{:S(2)}) collective-permute-start(f32[28,16]{1,0:T(8,128)S(1)} %add.33), channel_id=1, source_target_pairs={{0,4},{1,5},{2,6},{3,7},{4,0},{5,1},{6,2},{7,3},{8,12},{9,13},{10,... | collective-permute-start | bytes 5384 | tf_op jit(solution)/shard_map/ppermute | solution.py:42
  16.0 1.9 %copy-start.5 = (bf16[14,2,32,640]{3,2,1,0:T(8,128)(2,1)}, bf16[14,2,32,640]{3,2,1,0:T(8,128)(2,1)S(1)}, u32[]{:S(2)}) copy-start(bf16[14,2,32,640]{3,2,1,0:T(8,128)(2,1)S(1)} %collective-permute-done.2.u_mate.refs_4_) | copy-start | bytes 3440644
  21.1 4.6 %collective-permute-start.3 = (f32[28,16]{1,0:T(8,128)S(1)}, f32[28,16]{1,0:T(8,128)S(1)}, u32[]{:S(2)}, u32[]{:S(2)}) collective-permute-start(f32[28,16]{1,0:T(8,128)S(1)} %add.34), channel_id=1, source_target_pairs={{0,8},{1,9},{2,10},{3,11},{4,12},{5,13},{6,14},{7,15},{8,0},{9,1},... | collective-permute-start | bytes 5384 | tf_op jit(solution)/shard_map/ppermute | solution.py:42
  25.7 3.8 %collective-permute-start.5 = (f32[28,16]{1,0:T(8,128)S(1)}, f32[28,16]{1,0:T(8,128)S(1)}, u32[]{:S(2)}, u32[]{:S(2)}) collective-permute-start(f32[28,16]{1,0:T(8,128)S(1)} %add.35), channel_id=1, source_target_pairs={{0,2},{1,3},{2,0},{3,1},{4,6},{5,7},{6,4},{7,5},{8,10},{9,11},{10,... | collective-permute-start | bytes 5384 | tf_op jit(solution)/shard_map/ppermute | solution.py:42
  26.7 3.8 %collective-permute-start.7 = (bf16[14,32,640]{2,1,0:T(8,128)(2,1)S(1)}, bf16[14,32,640]{2,1,0:T(8,128)(2,1)S(1)}, u32[]{:S(2)}, u32[]{:S(2)}) collective-permute-start(bf16[14,32,640]{2,1,0:T(8,128)(2,1)S(1)} %collective-permute-done.4.rim), channel_id=1, source_target_pairs={{0,1},{1,0},{2,3},{3,2},{4,5},{5,4},{6,7},{7,6},{8,9},{9,8},{10,11... | collective-permute-start | bytes 1720328 | tf_op jit(solution)/shard_map/ppermute | solution.py:42
  29.5 15.2 %collective-permute-start.8 = (bf16[14,32,640]{2,1,0:T(8,128)(2,1)S(1)}, bf16[14,32,640]{2,1,0:T(8,128)(2,1)S(1)}, u32[]{:S(2)}, u32[]{:S(2)}) collective-permute-start(bf16[14,32,640]{2,1,0:T(8,128)(2,1)S(1)} %get-tuple-element.70), channel_id=1, source_target_pairs={{1,2},{2,1},{3,4},{4,3},{5,6},{6,5},{7,8},{8,7},{9,10},{10,9},{11,... | collective-permute-start | bytes 1720328 | tf_op jit(solution)/shard_map/ppermute | solution.py:432
  35.7 9.1 %copy-start.3 = (bf16[2688,640]{1,0:T(8,128)(2,1)}, bf16[2688,640]{1,0:T(8,128)(2,1)S(1)}, u32[]{:S(2)}) copy-start(bf16[2688,640]{1,0:T(8,128)(2,1)S(1)} %get-tuple-element.65.mid) | copy-start | bytes 10321924
  35.7 15.9 %copy-start.6 = (bf16[14,2,32,640]{3,2,1,0:T(8,128)(2,1)S(1)}, bf16[14,2,32,640]{3,2,1,0:T(8,128)(2,1)}, u32[]{:S(2)}) copy-start(bf16[14,2,32,640]{3,2,1,0:T(8,128)(2,1)} %copy-done.5) | copy-start | bytes 3440644
  44.8 1.5 %copy-start.9 = (bf16[14,32,640]{2,1,0:T(8,128)(2,1)}, bf16[14,32,640]{2,1,0:T(8,128)(2,1)S(1)}, u32[]{:S(2)}) copy-start(bf16[14,32,640]{2,1,0:T(8,128)(2,1)S(1)} %collective-permute-done.8.refs_5_) | copy-start | bytes 1720324
  46.3 5.3 %collective-permute-start.10 = (bf16[9,160,640]{2,1,0:T(8,128)(2,1)}, bf16[9,160,640]{2,1,0:T(8,128)(2,1)}, u32[]{:S(2)}, u32[]{:S(2)}) collective-permute-start(bf16[9,160,640]{2,1,0:T(8,128)(2,1)} %collective-permute-done.9.refs_1_), channel_id=1, source_target_pairs={{0,1},{1,0},{2,3},{3,2},{4,5},{5,4},{6,7},{7,6},{8,9},{9,8},{10,11... | collective-permute-start | bytes 5529608 | tf_op jit(solution)/shard_map/ppermute | solution.py:42
  47.8 25.7 %collective-permute-start.14 = (bf16[320,1600]{1,0:T(8,128)(2,1)}, bf16[320,1600]{1,0:T(8,128)(2,1)}, u32[]{:S(2)}, u32[]{:S(2)}) collective-permute-start(bf16[320,1600]{1,0:T(8,128)(2,1)} %get-tuple-element.71), channel_id=1, source_target_pairs={{0,16},{16,0},{1,17},{17,1},{2,18},{18,2},{3,19},{19,3},{4,20},{20... | collective-permute-start | bytes 3072008 | tf_op jit(solution)/shard_map/ppermute | solution.py:42
  48.3 22.4 %collective-permute-start.15 = (bf16[160,2560]{1,0:T(8,128)(2,1)}, bf16[160,2560]{1,0:T(8,128)(2,1)}, u32[]{:S(2)}, u32[]{:S(2)}) collective-permute-start(bf16[160,2560]{1,0:T(8,128)(2,1)} %get-tuple-element.80), channel_id=1, source_target_pairs={{0,4},{1,5},{2,6},{3,7},{4,0},{5,1},{6,2},{7,3},{8,12},{9,13},{10,... | collective-permute-start | bytes 2457608 | tf_op jit(solution)/shard_map/ppermute | solution.py:42
  51.6 19.1 %copy-start.8 = (f32[160,2560]{1,0:T(8,128)S(1)}, f32[160,2560]{1,0:T(8,128)}, u32[]{:S(2)}) copy-start(f32[160,2560]{1,0:T(8,128)} %get-tuple-element.79.kept) | copy-start | bytes 4915204
  65.6 7.9 %copy-start.7 = (f32[320,1600]{1,0:T(8,128)S(1)}, f32[320,1600]{1,0:T(8,128)}, u32[]{:S(2)}) copy-start(f32[320,1600]{1,0:T(8,128)} %get-tuple-element.78.kept) | copy-start | bytes 6144004
  65.6 1.3 %collective-permute-start.11 = (f32[40,128]{1,0:T(8,128)S(1)}, f32[40,128]{1,0:T(8,128)S(1)}, u32[]{:S(2)}, u32[]{:S(2)}) collective-permute-start(f32[40,128]{1,0:T(8,128)S(1)} %get-tuple-element.77), channel_id=1, source_target_pairs={{0,1},{1,0},{2,3},{3,2},{4,5},{5,4},{6,7},{7,6},{8,9},{9,8},{10,11... | collective-permute-start | bytes 61448 | tf_op jit(solution)/shard_map/ppermute | solution.py:42
  66.9 3.8 %collective-permute-start.12 = (f32[40,128]{1,0:T(8,128)S(1)}, f32[40,128]{1,0:T(8,128)S(1)}, u32[]{:S(2)}, u32[]{:S(2)}) collective-permute-start(f32[40,128]{1,0:T(8,128)S(1)} %add.39), channel_id=1, source_target_pairs={{0,2},{1,3},{2,0},{3,1},{4,6},{5,7},{6,4},{7,5},{8,10},{9,11},{10,... | collective-permute-start | bytes 61448 | tf_op jit(solution)/shard_map/ppermute | solution.py:42
  70.7 8.7 %copy-start.4 = (bf16[2688,640]{1,0:T(8,128)(2,1)S(1)}, bf16[2688,640]{1,0:T(8,128)(2,1)}, u32[]{:S(2)}) copy-start(bf16[2688,640]{1,0:T(8,128)(2,1)} %copy-done.3) | copy-start | bytes 10321924
  75.0 13.7 %collective-permute-start.16 = (bf16[160,1600]{1,0:T(8,128)(2,1)S(1)}, bf16[160,1600]{1,0:T(8,128)(2,1)S(1)}, u32[]{:S(2)}, u32[]{:S(2)}) collective-permute-start(bf16[160,1600]{1,0:T(8,128)(2,1)S(1)} %get-tuple-element.84), channel_id=1, source_target_pairs={{0,2},{1,3},{2,0},{3,1},{4,6},{5,7},{6,4},{7,5},{8,10},{9,11},{10,... | collective-permute-start | bytes 1536008 | tf_op jit(solution)/shard_map/ppermute | solution.py:42
  76.1 11.9 %collective-permute-start.17 = (bf16[160,1280]{1,0:T(8,128)(2,1)S(1)}, bf16[160,1280]{1,0:T(8,128)(2,1)S(1)}, u32[]{:S(2)}, u32[]{:S(2)}) collective-permute-start(bf16[160,1280]{1,0:T(8,128)(2,1)S(1)} %get-tuple-element.82), channel_id=1, source_target_pairs={{0,16},{16,0},{1,17},{17,1},{2,18},{18,2},{3,19},{19,3},{4,20},{20... | collective-permute-start | bytes 1228808 | tf_op jit(solution)/shard_map/ppermute | solution.py:42
  77.3 4.2 %collective-permute-start.13 = (f32[40,128]{1,0:T(8,128)S(1)}, f32[40,128]{1,0:T(8,128)S(1)}, u32[]{:S(2)}, u32[]{:S(2)}) collective-permute-start(f32[40,128]{1,0:T(8,128)S(1)} %add.40), channel_id=1, source_target_pairs={{0,4},{1,5},{2,6},{3,7},{4,0},{5,1},{6,2},{7,3},{8,12},{9,13},{10,... | collective-permute-start | bytes 61448 | tf_op jit(solution)/shard_map/ppermute | solution.py:42
  81.5 6.4 %collective-permute-start.18 = (f32[40,128]{1,0:T(8,128)S(1)}, f32[40,128]{1,0:T(8,128)S(1)}, u32[]{:S(2)}, u32[]{:S(2)}) collective-permute-start(f32[40,128]{1,0:T(8,128)S(1)} %add.41), channel_id=1, source_target_pairs={{0,8},{1,9},{2,10},{3,11},{4,12},{5,13},{6,14},{7,15},{8,0},{9,1},... | collective-permute-start | bytes 61448 | tf_op jit(solution)/shard_map/ppermute | solution.py:42
  88.0 5.8 %collective-permute-start.20 = (bf16[80,1280]{1,0:T(8,128)(2,1)S(1)}, bf16[80,1280]{1,0:T(8,128)(2,1)S(1)}, u32[]{:S(2)}, u32[]{:S(2)}) collective-permute-start(bf16[80,1280]{1,0:T(8,128)(2,1)S(1)} %get-tuple-element.94), channel_id=1, source_target_pairs={{0,2},{1,3},{2,0},{3,1},{4,6},{5,7},{6,4},{7,5},{8,10},{9,11},{10,... | collective-permute-start | bytes 614408 | tf_op jit(solution)/shard_map/ppermute | solution.py:42
  88.7 7.9 %collective-permute-start.19 = (bf16[80,1600]{1,0:T(8,128)(2,1)S(1)}, bf16[80,1600]{1,0:T(8,128)(2,1)S(1)}, u32[]{:S(2)}, u32[]{:S(2)}) collective-permute-start(bf16[80,1600]{1,0:T(8,128)(2,1)S(1)} %get-tuple-element.97), channel_id=1, source_target_pairs={{0,4},{1,5},{2,6},{3,7},{4,0},{5,1},{6,2},{7,3},{8,12},{9,13},{10,... | collective-permute-start | bytes 768008 | tf_op jit(solution)/shard_map/ppermute | solution.py:42
  93.9 10.5 %collective-permute-start.21 = (bf16[40,1280]{1,0:T(8,128)(2,1)S(1)}, bf16[40,1280]{1,0:T(8,128)(2,1)S(1)}, u32[]{:S(2)}, u32[]{:S(2)}) collective-permute-start(bf16[40,1280]{1,0:T(8,128)(2,1)S(1)} %get-tuple-element.102), channel_id=1, source_target_pairs={{0,8},{1,9},{2,10},{3,11},{4,12},{5,13},{6,14},{7,15},{8,0},{9,1},... | collective-permute-start | bytes 307208 | tf_op jit(solution)/shard_map/ppermute | solution.py:42
  95.6 8.8 %collective-permute-start.22 = (f32[10,128]{1,0:T(8,128)S(1)}, f32[10,128]{1,0:T(8,128)S(1)}, u32[]{:S(2)}, u32[]{:S(2)}) collective-permute-start(f32[10,128]{1,0:T(8,128)S(1)} %slice.12), channel_id=1, source_target_pairs={{0,16},{16,0},{1,17},{17,1},{2,18},{18,2},{3,19},{19,3},{4,20},{20... | collective-permute-start | bytes 15368 | tf_op jit(solution)/shard_map/ppermute | solution.py:42
  96.7 8.8 %collective-permute-start.23 = (bf16[40,1600]{1,0:T(8,128)(2,1)S(1)}, bf16[40,1600]{1,0:T(8,128)(2,1)S(1)}, u32[]{:S(2)}, u32[]{:S(2)}) collective-permute-start(bf16[40,1600]{1,0:T(8,128)(2,1)S(1)} %get-tuple-element.104), channel_id=1, source_target_pairs={{0,8},{1,9},{2,10},{3,11},{4,12},{5,13},{6,14},{7,15},{8,0},{9,1},... | collective-permute-start | bytes 384008 | tf_op jit(solution)/shard_map/ppermute | solution.py:42

commit v7 on v6

--- a/solution.py
+++ b/solution.py
@@ -337,7 +337,7 @@
         for r in range(2):
             centred = (x[img, r].astype(F32) - mean[pl.ds(img, 1), :]) * rstd[pl.ds(img, 1), :]
             normed = centred * gain[...] + bias[...]
-            s = 1.0 / (1.0 + jnp.exp(-normed))
+            s = 0.5 + 0.5 * jnp.tanh(0.5 * normed)
             grad = out[img, r] * s * (1.0 + normed * (1.0 - s))
             out[img, r] = grad
             first = first + jnp.sum(grad, axis=0, keepdims=True)

time: 107 us -> 107 us (level)
  no operation moved by 1% of the time
where the time goes in v7:
time: 107 us; the launch traced here: 106 us
  Pallas kernels  52.2 us (49%)
  starting transfers between devices  32.8 us (31%)
  waiting for transfers between devices  19.7 us (18%)
    ppermute x22, starting transfers between devices, swap(): return lax.ppermute(value, axis, [(i, i ^ bit) for i in range(count)])  31.2 us
    ppermute x22, waiting for transfers between devices, swap(): return lax.ppermute(value, axis, [(i, i ^ bit) for i in range(count)])  19.7 us
    pallas_call x1, Pallas kernels, body(): kernel_call(back_kernel, 32, (struct(inputs.shape, F32), struct((40, LANE...  14 us
    pallas_call x1, Pallas kernels, body(): kernel_call(functools.partial(grad_kernel, block, two), 28, tuple((pltpu....  9.04 us
    pallas_call x1, Pallas kernels, body(): kernel_call(conv_kernel, 32, struct(inputs.shape, BF16), [V] * 4, 'conv_f...  5.26 us
    pallas_call x1, Pallas kernels, body(): kernel_call(functools.partial(act_kernel, size), 24, (struct((6 * block,...  5.2 us
    pallas_call x1, Pallas kernels, body(): kernel_call(conv_first_kernel, 32, struct(row_shape, BF16), [V] * 3, 'con...  4.26 us
    pallas_call x1, Pallas kernels, body(): kernel_call(slice_kernel, 8, struct((taps, part, channels), BF16), [S, H]...  2.2 us
  transfers between devices with their start and end apart: 24, of which 11 were waited for; matrix products, arithmetic and copies ran while one was open for 1% of the time, Pallas kernels for 45%

profile of v7, /device:TPU:0, one launch (start us, length us, event | category | flops | bytes accessed | tf_op | source)
XLA Modules:
  0.0 106.5 jit_solution(16174251424661144832)
XLA Ops:
  0.7 0.1 stack.35.info
  0.7 2.2 %slice.20 = bf16[9,160,640]{2,1,0:T(8,128)(2,1)S(1)} custom-call(s32[5]{0:T(128)S(1)} %stack.35.info, bf16[9,320,640]{2,1,0:T(8,128)(2,1)} %refs_0_.1), custom_call_target="tpu_custom_call" | custom-call | tf_op jit(solution)/shard_map/slice/pallas_call | solution.py:408
  2.9 0.0 copy-start.2
  3.0 3.0 %collective-permute-start.9 = (bf16[9,160,640]{2,1,0:T(8,128)(2,1)S(1)}, bf16[9,160,640]{2,1,0:T(8,128)(2,1)}, u32[]{:S(2)}, u32[]{:S(2)}) collective-permute-start(bf16[9,160,640]{2,1,0:T(8,128)(2,1)S(1)} %slice.20), channel_id=1, source_target_pairs={{0,16},{16,0},{1,17},{17,1},{2,18},{18,2},{3,19},{19,3},{4,20},{20... | collective-permute-start | bytes 5529608 | tf_op jit(solution)/shard_map/ppermute | solution.py:42
  6.0 0.0 collective-permute-start.2
  6.0 2.0 %stats.1 = (f32[28,16]{1,0:T(8,128)S(1)}, bf16[14,32,640]{2,1,0:T(8,128)(2,1)S(1)}, bf16[14,32,640]{2,1,0:T(8,128)(2,1)S(1)}) custom-call(s32[5]{0:T(128)S(1)} %stack.35.info, bf16[14,2,32,640]{3,2,1,0:T(8,128)(2,1)S(1)} %copy-done, bf16[14,2,32,640]{3,2,1,0:T(8,128)(2,1)} %u.5), custom_call_target="tpu_custom_call" | custom-call | tf_op jit(solution)/shard_map/stats/pallas_call | solution.py:414
  8.0 0.7 collective-permute-start.4
  8.7 2.9 %collective-permute-start.6 = (bf16[14,2,32,640]{3,2,1,0:T(8,128)(2,1)S(1)}, bf16[14,2,32,640]{3,2,1,0:T(8,128)(2,1)S(1)}, u32[]{:S(2)}, u32[]{:S(2)}) collective-permute-start(bf16[14,2,32,640]{3,2,1,0:T(8,128)(2,1)S(1)} %copy-done), channel_id=1, source_target_pairs={{0,1},{1,0},{2,3},{3,2},{4,5},{5,4},{6,7},{7,6},{8,9},{9,8},{10,11... | collective-permute-start | bytes 3440648 | tf_op jit(solution)/shard_map/ppermute | solution.py:42
  11.6 0.1 collective-permute-start
  11.7 2.4 %collective-permute-done = f32[28,16]{1,0:T(8,128)S(1)} collective-permute-done((f32[28,16]{1,0:T(8,128)S(1)}, f32[28,16]{1,0:T(8,128)S(1)}, u32[]{:S(2)}, u32[]{:S(2)}) %collective-permute-start) | collective-permute-done | bytes 1824 | tf_op jit(solution)/shard_map/ppermute | solution.py:42
  14.1 1.9 %collective-permute-start.1 = (f32[28,16]{1,0:T(8,128)S(1)}, f32[28,16]{1,0:T(8,128)S(1)}, u32[]{:S(2)}, u32[]{:S(2)}) collective-permute-start(f32[28,16]{1,0:T(8,128)S(1)} %add.33), channel_id=1, source_target_pairs={{0,4},{1,5},{2,6},{3,7},{4,0},{5,1},{6,2},{7,3},{8,12},{9,13},{10,... | collective-permute-start | bytes 5384 | tf_op jit(solution)/shard_map/ppermute | solution.py:42
  16.0 0.0 collective-permute-done.2.u_mate.refs_4_
  16.0 1.9 %turn.1.lhs = bf16[320,1792]{1,0:T(8,128)(2,1)S(1)} custom-call(s32[5]{0:T(128)S(1)} %stack.35.info, bf16[14,2,32,640]{3,2,1,0:T(8,128)(2,1)S(1)} %copy-done.2, bf16[14,2,32,640]{3,2,1,0:T(8,128)(2,1)S(1)} %collective-permute-done.2.u_mate.refs_4_), custom_call_target="tpu_custom_call" | custom-call | tf_op jit(solution)/shard_map/turn/pallas_call | solution.py:420
  17.9 3.1 %collective-permute-done.1 = f32[28,16]{1,0:T(8,128)S(1)} collective-permute-done((f32[28,16]{1,0:T(8,128)S(1)}, f32[28,16]{1,0:T(8,128)S(1)}, u32[]{:S(2)}, u32[]{:S(2)}) %collective-permute-start.1) | collective-permute-done | bytes 1824 | tf_op jit(solution)/shard_map/ppermute | solution.py:42
  21.1 2.8 %collective-permute-start.3 = (f32[28,16]{1,0:T(8,128)S(1)}, f32[28,16]{1,0:T(8,128)S(1)}, u32[]{:S(2)}, u32[]{:S(2)}) collective-permute-start(f32[28,16]{1,0:T(8,128)S(1)} %add.34), channel_id=1, source_target_pairs={{0,8},{1,9},{2,10},{3,11},{4,12},{5,13},{6,14},{7,15},{8,0},{9,1},... | collective-permute-start | bytes 5384 | tf_op jit(solution)/shard_map/ppermute | solution.py:42
  23.8 1.9 %collective-permute-done.3 = f32[28,16]{1,0:T(8,128)S(1)} collective-permute-done((f32[28,16]{1,0:T(8,128)S(1)}, f32[28,16]{1,0:T(8,128)S(1)}, u32[]{:S(2)}, u32[]{:S(2)}) %collective-permute-start.3) | collective-permute-done | bytes 1824 | tf_op jit(solution)/shard_map/ppermute | solution.py:42
  25.7 0.0 collective-permute-done.4.rim
  25.7 1.0 collective-permute-start.5
  26.7 0.0 collective-permute-start.7
  26.7 2.8 %collective-permute-done.5 = f32[28,16]{1,0:T(8,128)S(1)} collective-permute-done((f32[28,16]{1,0:T(8,128)S(1)}, f32[28,16]{1,0:T(8,128)S(1)}, u32[]{:S(2)}, u32[]{:S(2)}) %collective-permute-start.5) | collective-permute-done | bytes 1824 | tf_op jit(solution)/shard_map/ppermute | solution.py:42
  29.5 0.9 collective-permute-start.8
  30.4 0.0 collective-permute-done.6.x_mate
  30.5 0.0 collective-permute-done.7.rim_mate
  30.5 5.2 %activate.1 = (bf16[2688,640]{1,0:T(8,128)(2,1)S(1)}, bf16[2,2688,640]{2,1,0:T(8,128)(2,1)S(1)}, f32[14,640]{1,0:T(8,128)S(1)}, f32[14,640]{1,0:T(8,128)S(1)}) custom-call(s32[5]{0:T(128)S(1)} %stack.35.info, f32[28,16]{1,0:T(8,128)S(1)} %add.36.stats, bf16[14,2,32,640]{3,2,1,0:T(8,128)(2,1)S(1)} %copy-done, ...), custom_call_target="tpu_custom_call" | custom-call | tf_op jit(solution)/shard_map/activate/pallas_call | solution.py:434
  35.7 0.0 copy-start.6
  35.7 9.0 %weight_terms.1 = (bf16[160,2560]{1,0:T(8,128)(2,1)}, f32[160,2560]{1,0:T(8,128)}, bf16[320,1600]{1,0:T(8,128)(2,1)}, f32[320,1600]{1,0:T(8,128)}) custom-call(s32[5]{0:T(128)S(1)} %stack.35.info, bf16[320,1792]{1,0:T(8,128)(2,1)S(1)} %turn.1.lhs, bf16[2688,640]{1,0:T(8,128)(2,1)S(1)} %get-tuple-element.65.mid, bf16[2,2688,640]{2,1,0:T(8,128)(2,1)S(1)} %get-tuple-element.66.side), custom_call_target="tpu_custom_call" | custom-call | tf_op jit(solution)/shard_map/weight_terms/pallas_call | solution.py:462
  44.8 1.5 %collective-permute-done.9.refs_1_ = bf16[9,160,640]{2,1,0:T(8,128)(2,1)} collective-permute-done((bf16[9,160,640]{2,1,0:T(8,128)(2,1)S(1)}, bf16[9,160,640]{2,1,0:T(8,128)(2,1)}, u32[]{:S(2)}, u32[]{:S(2)}) %collective-permute-start.9) | collective-permute-done | bytes 1843232 | tf_op jit(solution)/shard_map/ppermute | solution.py:42
  46.3 1.5 %collective-permute-start.10 = (bf16[9,160,640]{2,1,0:T(8,128)(2,1)}, bf16[9,160,640]{2,1,0:T(8,128)(2,1)}, u32[]{:S(2)}, u32[]{:S(2)}) collective-permute-start(bf16[9,160,640]{2,1,0:T(8,128)(2,1)} %collective-permute-done.9.refs_1_), channel_id=1, source_target_pairs={{0,1},{1,0},{2,3},{3,2},{4,5},{5,4},{6,7},{7,6},{8,9},{9,8},{10,11... | collective-permute-start | bytes 5529608 | tf_op jit(solution)/shard_map/ppermute | solution.py:42
  47.8 0.5 collective-permute-start.14
  48.3 1.6 %collective-permute-start.15 = (bf16[160,2560]{1,0:T(8,128)(2,1)}, bf16[160,2560]{1,0:T(8,128)(2,1)}, u32[]{:S(2)}, u32[]{:S(2)}) collective-permute-start(bf16[160,2560]{1,0:T(8,128)(2,1)} %get-tuple-element.80), channel_id=1, source_target_pairs={{0,4},{1,5},{2,6},{3,7},{4,0},{5,1},{6,2},{7,3},{8,12},{9,13},{10,... | collective-permute-start | bytes 2457608 | tf_op jit(solution)/shard_map/ppermute | solution.py:42
  49.9 0.1 pad_add_fusion.places
  50.0 1.6 %collective-permute-done.10.refs_2_ = bf16[9,160,640]{2,1,0:T(8,128)(2,1)} collective-permute-done((bf16[9,160,640]{2,1,0:T(8,128)(2,1)}, bf16[9,160,640]{2,1,0:T(8,128)(2,1)}, u32[]{:S(2)}, u32[]{:S(2)}) %collective-permute-start.10) | collective-permute-done | bytes 1843232 | tf_op jit(solution)/shard_map/ppermute | solution.py:42
  51.6 14.0 %conv_backward.1 = (f32[14,2,32,640]{3,2,1,0:T(8,128)S(1)}, f32[40,128]{1,0:T(8,128)S(1)}, bf16[9,640,640]{2,1,0:T(8,128)(2,1)S(1)}) custom-call(s32[5]{0:T(128)S(1)} %stack.35.info, s32[3]{0:T(128)S(1)} %pad_add_fusion.places, bf16[9,320,640]{2,1,0:T(8,128)(2,1)} %refs_0_.1, bf16[9,160,640]{2,1,0:T(8,128)(2,1)} %collective-permute-done.9.refs_1_, ...), custom_call_target="tpu_custom_call" | custom-call | tf_op jit(solution)/shard_map/conv_backward/pallas_call | solution.py:479
  65.5 0.4 collective-permute-start.11
  66.0 0.8 collective-permute-done.11
  66.8 1.0 collective-permute-start.12
  67.8 2.8 %collective-permute-done.12 = f32[40,128]{1,0:T(8,128)S(1)} collective-permute-done((f32[40,128]{1,0:T(8,128)S(1)}, f32[40,128]{1,0:T(8,128)S(1)}, u32[]{:S(2)}, u32[]{:S(2)}) %collective-permute-start.12) | collective-permute-done | bytes 20512 | tf_op jit(solution)/shard_map/ppermute | solution.py:42
  70.6 0.0 collective-permute-done.15.got
  70.6 1.6 %split.1 = (bf16[160,1280]{1,0:T(8,128)(2,1)S(1)}, f32[160,1280]{1,0:T(8,128)S(1)}) custom-call(s32[5]{0:T(128)S(1)} %stack.35.info, f32[160,2560]{1,0:T(8,128)S(1)} %copy-done.8, bf16[160,2560]{1,0:T(8,128)(2,1)} %collective-permute-done.15.got), custom_call_target="tpu_custom_call" | custom-call | tf_op jit(solution)/shard_map/split/pallas_call | solution.py:453
  72.3 1.3 %collective-permute-done.14.got = bf16[320,1600]{1,0:T(8,128)(2,1)} collective-permute-done((bf16[320,1600]{1,0:T(8,128)(2,1)}, bf16[320,1600]{1,0:T(8,128)(2,1)}, u32[]{:S(2)}, u32[]{:S(2)}) %collective-permute-start.14) | collective-permute-done | bytes 1024032 | tf_op jit(solution)/shard_map/ppermute | solution.py:42
  73.5 1.4 %fold.5 = (bf16[160,1600]{1,0:T(8,128)(2,1)S(1)}, f32[160,1600]{1,0:T(8,128)S(1)}) custom-call(f32[320,1600]{1,0:T(8,128)S(1)} %copy-done.7, bf16[320,1600]{1,0:T(8,128)(2,1)} %collective-permute-done.14.got), custom_call_target="tpu_custom_call" | custom-call | tf_op jit(solution)/shard_map/fold/pallas_call | solution.py:447
  75.0 1.1 %collective-permute-start.16 = (bf16[160,1600]{1,0:T(8,128)(2,1)S(1)}, bf16[160,1600]{1,0:T(8,128)(2,1)S(1)}, u32[]{:S(2)}, u32[]{:S(2)}) collective-permute-start(bf16[160,1600]{1,0:T(8,128)(2,1)S(1)} %get-tuple-element.84), channel_id=1, source_target_pairs={{0,2},{1,3},{2,0},{3,1},{4,6},{5,7},{6,4},{7,5},{8,10},{9,11},{10,... | collective-permute-start | bytes 1536008 | tf_op jit(solution)/shard_map/ppermute | solution.py:42
  76.1 1.2 %collective-permute-start.17 = (bf16[160,1280]{1,0:T(8,128)(2,1)S(1)}, bf16[160,1280]{1,0:T(8,128)(2,1)S(1)}, u32[]{:S(2)}, u32[]{:S(2)}) collective-permute-start(bf16[160,1280]{1,0:T(8,128)(2,1)S(1)} %get-tuple-element.82), channel_id=1, source_target_pairs={{0,16},{16,0},{1,17},{17,1},{2,18},{18,2},{3,19},{19,3},{4,20},{20... | collective-permute-start | bytes 1228808 | tf_op jit(solution)/shard_map/ppermute | solution.py:42
  77.3 2.2 %collective-permute-start.13 = (f32[40,128]{1,0:T(8,128)S(1)}, f32[40,128]{1,0:T(8,128)S(1)}, u32[]{:S(2)}, u32[]{:S(2)}) collective-permute-start(f32[40,128]{1,0:T(8,128)S(1)} %add.40), channel_id=1, source_target_pairs={{0,4},{1,5},{2,6},{3,7},{4,0},{5,1},{6,2},{7,3},{8,12},{9,13},{10,... | collective-permute-start | bytes 61448 | tf_op jit(solution)/shard_map/ppermute | solution.py:42
  79.4 2.0 %own.1 = bf16[3,1792,640]{2,1,0:T(8,128)(2,1)S(1)} custom-call(s32[5]{0:T(128)S(1)} %stack.35.info, bf16[2688,640]{1,0:T(8,128)(2,1)S(1)} %copy-done.4), custom_call_target="tpu_custom_call" | custom-call | tf_op jit(solution)/shard_map/own/pallas_call | solution.py:509
  81.5 2.1 %collective-permute-start.18 = (f32[40,128]{1,0:T(8,128)S(1)}, f32[40,128]{1,0:T(8,128)S(1)}, u32[]{:S(2)}, u32[]{:S(2)}) collective-permute-start(f32[40,128]{1,0:T(8,128)S(1)} %add.41), channel_id=1, source_target_pairs={{0,8},{1,9},{2,10},{3,11},{4,12},{5,13},{6,14},{7,15},{8,0},{9,1},... | collective-permute-start | bytes 61448 | tf_op jit(solution)/shard_map/ppermute | solution.py:42
  83.6 4.3 %conv_forward.2.first = bf16[14,32,640]{2,1,0:T(8,128)(2,1)S(1)} custom-call(bf16[3,1792,640]{2,1,0:T(8,128)(2,1)S(1)} %own.1, bf16[9,640,640]{2,1,0:T(8,128)(2,1)S(1)} %get-tuple-element.91.w, bf16[14,2,32,640]{3,2,1,0:T(8,128)(2,1)S(1)} %copy-done), custom_call_target="tpu_custom_call" | custom-call | tf_op jit(solution)/shard_map/conv_forward/pallas_call | solution.py:518
  87.9 0.0 collective-permute-done.17.got
  87.9 0.1 fold.6
  88.0 0.6 collective-permute-start.20
  88.6 0.1 fold.7
  88.7 2.2 %collective-permute-start.19 = (bf16[80,1600]{1,0:T(8,128)(2,1)S(1)}, bf16[80,1600]{1,0:T(8,128)(2,1)S(1)}, u32[]{:S(2)}, u32[]{:S(2)}) collective-permute-start(bf16[80,1600]{1,0:T(8,128)(2,1)S(1)} %get-tuple-element.97), channel_id=1, source_target_pairs={{0,4},{1,5},{2,6},{3,7},{4,0},{5,1},{6,2},{7,3},{8,12},{9,13},{10,... | collective-permute-start | bytes 768008 | tf_op jit(solution)/shard_map/ppermute | solution.py:42
  91.0 2.0 %input_grad.1 = bf16[14,2,32,640]{3,2,1,0:T(8,128)(2,1)} custom-call(f32[40,128]{1,0:T(8,128)S(1)} %add.42.sums, f32[14,2,32,640]{3,2,1,0:T(8,128)S(1)} %get-tuple-element.100.grad, bf16[14,2,32,640]{3,2,1,0:T(8,128)(2,1)S(1)} %copy-done, bf16[14,2,32,640]{3,2,1,0:T(8,128)(2,1)S(1)} %copy-done.2, f32[14,640]{1,0:T(8,128)S(1)} %get-tuple-element.75.refs_7_.mean, ...), custom_call_target="tpu_custom_call" | custom-call | tf_op jit(solution)/shard_map/input_grad/pallas_call | solution.py:528
  93.0 0.8 collective-permute-done.20.got
  93.9 1.7 %collective-permute-start.21 = (bf16[40,1280]{1,0:T(8,128)(2,1)S(1)}, bf16[40,1280]{1,0:T(8,128)(2,1)S(1)}, u32[]{:S(2)}, u32[]{:S(2)}) collective-permute-start(bf16[40,1280]{1,0:T(8,128)(2,1)S(1)} %get-tuple-element.102), channel_id=1, source_target_pairs={{0,8},{1,9},{2,10},{3,11},{4,12},{5,13},{6,14},{7,15},{8,0},{9,1},... | collective-permute-start | bytes 307208 | tf_op jit(solution)/shard_map/ppermute | solution.py:42
  95.6 1.1 %collective-permute-start.22 = (f32[10,128]{1,0:T(8,128)S(1)}, f32[10,128]{1,0:T(8,128)S(1)}, u32[]{:S(2)}, u32[]{:S(2)}) collective-permute-start(f32[10,128]{1,0:T(8,128)S(1)} %slice.12), channel_id=1, source_target_pairs={{0,16},{16,0},{1,17},{17,1},{2,18},{18,2},{3,19},{19,3},{4,20},{20... | collective-permute-start | bytes 15368 | tf_op jit(solution)/shard_map/ppermute | solution.py:42
  96.7 0.1 fold.9
  96.7 2.3 %collective-permute-start.23 = (bf16[40,1600]{1,0:T(8,128)(2,1)S(1)}, bf16[40,1600]{1,0:T(8,128)(2,1)S(1)}, u32[]{:S(2)}, u32[]{:S(2)}) collective-permute-start(bf16[40,1600]{1,0:T(8,128)(2,1)S(1)} %get-tuple-element.104), channel_id=1, source_target_pairs={{0,8},{1,9},{2,10},{3,11},{4,12},{5,13},{6,14},{7,15},{8,0},{9,1},... | collective-permute-start | bytes 384008 | tf_op jit(solution)/shard_map/ppermute | solution.py:42
  99.1 5.3 %conv_forward.3 = bf16[14,2,32,640]{3,2,1,0:T(8,128)(2,1)} custom-call(bf16[3,1792,640]{2,1,0:T(8,128)(2,1)S(1)} %own.1, bf16[9,640,640]{2,1,0:T(8,128)(2,1)S(1)} %get-tuple-element.91.w, bf16[14,2,32,640]{3,2,1,0:T(8,128)(2,1)S(1)} %copy-done, bf16[14,32,640]{2,1,0:T(8,128)(2,1)S(1)} %conv_forward.2.first), custom_call_target="tpu_custom_call" | custom-call | tf_op jit(solution)/shard_map/conv_forward/pallas_call | solution.py:537
  104.3 0.0 collective-permute-done.22
  104.3 0.0 collective-permute-done.21.got_a
  104.4 0.6 slice_bitcast_fusion
  105.0 0.6 collective-permute-done.23.got_b
  105.5 0.9 last.1
  (40 shorter events, 0.2 us)
Async XLA Ops:
  0.7 5.3 %copy-start.1 = (bf16[14,2,32,640]{3,2,1,0:T(8,128)(2,1)S(1)}, bf16[14,2,32,640]{3,2,1,0:T(8,128)(2,1)}, u32[]{:S(2)}) copy-start(bf16[14,2,32,640]{3,2,1,0:T(8,128)(2,1)} %u.5) | copy-start | bytes 3440644
  0.7 5.3 %copy-start = (bf16[14,2,32,640]{3,2,1,0:T(8,128)(2,1)S(1)}, bf16[14,2,32,640]{3,2,1,0:T(8,128)(2,1)}, u32[]{:S(2)}) copy-start(bf16[14,2,32,640]{3,2,1,0:T(8,128)(2,1)} %x.9) | copy-start | bytes 3440644
  2.9 13.0 %copy-start.2 = (bf16[14,2,32,640]{3,2,1,0:T(8,128)(2,1)S(1)}, bf16[14,2,32,640]{3,2,1,0:T(8,128)(2,1)}, u32[]{:S(2)}) copy-start(bf16[14,2,32,640]{3,2,1,0:T(8,128)(2,1)} %u.5) | copy-start | bytes 3440644
  3.0 43.3 %collective-permute-start.9 = (bf16[9,160,640]{2,1,0:T(8,128)(2,1)S(1)}, bf16[9,160,640]{2,1,0:T(8,128)(2,1)}, u32[]{:S(2)}, u32[]{:S(2)}) collective-permute-start(bf16[9,160,640]{2,1,0:T(8,128)(2,1)S(1)} %slice.20), channel_id=1, source_target_pairs={{0,16},{16,0},{1,17},{17,1},{2,18},{18,2},{3,19},{19,3},{4,20},{20... | collective-permute-start | bytes 5529608 | tf_op jit(solution)/shard_map/ppermute | solution.py:42
  6.0 10.0 %collective-permute-start.2 = (bf16[14,2,32,640]{3,2,1,0:T(8,128)(2,1)S(1)}, bf16[14,2,32,640]{3,2,1,0:T(8,128)(2,1)S(1)}, u32[]{:S(2)}, u32[]{:S(2)}) collective-permute-start(bf16[14,2,32,640]{3,2,1,0:T(8,128)(2,1)S(1)} %copy-done.1), channel_id=1, source_target_pairs={{0,1},{1,0},{2,3},{3,2},{4,5},{5,4},{6,7},{7,6},{8,9},{9,8},{10,11... | collective-permute-start | bytes 3440648 | tf_op jit(solution)/shard_map/ppermute | solution.py:42
  8.0 17.7 %collective-permute-start.4 = (bf16[14,32,640]{2,1,0:T(8,128)(2,1)S(1)}, bf16[14,32,640]{2,1,0:T(8,128)(2,1)S(1)}, u32[]{:S(2)}, u32[]{:S(2)}) collective-permute-start(bf16[14,32,640]{2,1,0:T(8,128)(2,1)S(1)} %get-tuple-element.62), channel_id=1, source_target_pairs={{1,2},{2,1},{3,4},{4,3},{5,6},{6,5},{7,8},{8,7},{9,10},{10,9},{11,... | collective-permute-start | bytes 1720328 | tf_op jit(solution)/shard_map/ppermute | solution.py:419
  8.7 21.7 %collective-permute-start.6 = (bf16[14,2,32,640]{3,2,1,0:T(8,128)(2,1)S(1)}, bf16[14,2,32,640]{3,2,1,0:T(8,128)(2,1)S(1)}, u32[]{:S(2)}, u32[]{:S(2)}) collective-permute-start(bf16[14,2,32,640]{3,2,1,0:T(8,128)(2,1)S(1)} %copy-done), channel_id=1, source_target_pairs={{0,1},{1,0},{2,3},{3,2},{4,5},{5,4},{6,7},{7,6},{8,9},{9,8},{10,11... | collective-permute-start | bytes 3440648 | tf_op jit(solution)/shard_map/ppermute | solution.py:42
  11.6 2.5 %collective-permute-start = (f32[28,16]{1,0:T(8,128)S(1)}, f32[28,16]{1,0:T(8,128)S(1)}, u32[]{:S(2)}, u32[]{:S(2)}) collective-permute-start(f32[28,16]{1,0:T(8,128)S(1)} %get-tuple-element.59), channel_id=1, source_target_pairs={{0,1},{1,0},{2,3},{3,2},{4,5},{5,4},{6,7},{7,6},{8,9},{9,8},{10,11... | collective-permute-start | bytes 5384 | tf_op jit(solution)/shard_map/ppermute | solution.py:42
  14.1 16.3 %copy-start.10 = (f32[640]{0:T(1024)S(1)}, f32[640]{0:T(1024)}, u32[]{:S(2)}) copy-start(f32[640]{0:T(1024)} %param.6) | copy-start | bytes 7684
  14.1 16.4 %copy-start.11 = (f32[640]{0:T(1024)S(1)}, f32[640]{0:T(1024)}, u32[]{:S(2)}) copy-start(f32[640]{0:T(1024)} %param.7) | copy-start | bytes 7684
  14.1 7.0 %collective-permute-start.1 = (f32[28,16]{1,0:T(8,128)S(1)}, f32[28,16]{1,0:T(8,128)S(1)}, u32[]{:S(2)}, u32[]{:S(2)}) collective-permute-start(f32[28,16]{1,0:T(8,128)S(1)} %add.33), channel_id=1, source_target_pairs={{0,4},{1,5},{2,6},{3,7},{4,0},{5,1},{6,2},{7,3},{8,12},{9,13},{10,... | collective-permute-start | bytes 5384 | tf_op jit(solution)/shard_map/ppermute | solution.py:42
  16.0 1.9 %copy-start.5 = (bf16[14,2,32,640]{3,2,1,0:T(8,128)(2,1)}, bf16[14,2,32,640]{3,2,1,0:T(8,128)(2,1)S(1)}, u32[]{:S(2)}) copy-start(bf16[14,2,32,640]{3,2,1,0:T(8,128)(2,1)S(1)} %collective-permute-done.2.u_mate.refs_4_) | copy-start | bytes 3440644
  21.1 4.6 %collective-permute-start.3 = (f32[28,16]{1,0:T(8,128)S(1)}, f32[28,16]{1,0:T(8,128)S(1)}, u32[]{:S(2)}, u32[]{:S(2)}) collective-permute-start(f32[28,16]{1,0:T(8,128)S(1)} %add.34), channel_id=1, source_target_pairs={{0,8},{1,9},{2,10},{3,11},{4,12},{5,13},{6,14},{7,15},{8,0},{9,1},... | collective-permute-start | bytes 5384 | tf_op jit(solution)/shard_map/ppermute | solution.py:42
  25.7 3.8 %collective-permute-start.5 = (f32[28,16]{1,0:T(8,128)S(1)}, f32[28,16]{1,0:T(8,128)S(1)}, u32[]{:S(2)}, u32[]{:S(2)}) collective-permute-start(f32[28,16]{1,0:T(8,128)S(1)} %add.35), channel_id=1, source_target_pairs={{0,2},{1,3},{2,0},{3,1},{4,6},{5,7},{6,4},{7,5},{8,10},{9,11},{10,... | collective-permute-start | bytes 5384 | tf_op jit(solution)/shard_map/ppermute | solution.py:42
  26.7 3.8 %collective-permute-start.7 = (bf16[14,32,640]{2,1,0:T(8,128)(2,1)S(1)}, bf16[14,32,640]{2,1,0:T(8,128)(2,1)S(1)}, u32[]{:S(2)}, u32[]{:S(2)}) collective-permute-start(bf16[14,32,640]{2,1,0:T(8,128)(2,1)S(1)} %collective-permute-done.4.rim), channel_id=1, source_target_pairs={{0,1},{1,0},{2,3},{3,2},{4,5},{5,4},{6,7},{7,6},{8,9},{9,8},{10,11... | collective-permute-start | bytes 1720328 | tf_op jit(solution)/shard_map/ppermute | solution.py:42
  29.5 15.2 %collective-permute-start.8 = (bf16[14,32,640]{2,1,0:T(8,128)(2,1)S(1)}, bf16[14,32,640]{2,1,0:T(8,128)(2,1)S(1)}, u32[]{:S(2)}, u32[]{:S(2)}) collective-permute-start(bf16[14,32,640]{2,1,0:T(8,128)(2,1)S(1)} %get-tuple-element.70), channel_id=1, source_target_pairs={{1,2},{2,1},{3,4},{4,3},{5,6},{6,5},{7,8},{8,7},{9,10},{10,9},{11,... | collective-permute-start | bytes 1720328 | tf_op jit(solution)/shard_map/ppermute | solution.py:432
  35.7 9.1 %copy-start.3 = (bf16[2688,640]{1,0:T(8,128)(2,1)}, bf16[2688,640]{1,0:T(8,128)(2,1)S(1)}, u32[]{:S(2)}) copy-start(bf16[2688,640]{1,0:T(8,128)(2,1)S(1)} %get-tuple-element.65.mid) | copy-start | bytes 10321924
  35.7 15.9 %copy-start.6 = (bf16[14,2,32,640]{3,2,1,0:T(8,128)(2,1)S(1)}, bf16[14,2,32,640]{3,2,1,0:T(8,128)(2,1)}, u32[]{:S(2)}) copy-start(bf16[14,2,32,640]{3,2,1,0:T(8,128)(2,1)} %copy-done.5) | copy-start | bytes 3440644
  44.8 1.5 %copy-start.9 = (bf16[14,32,640]{2,1,0:T(8,128)(2,1)}, bf16[14,32,640]{2,1,0:T(8,128)(2,1)S(1)}, u32[]{:S(2)}) copy-start(bf16[14,32,640]{2,1,0:T(8,128)(2,1)S(1)} %collective-permute-done.8.refs_5_) | copy-start | bytes 1720324
  46.3 5.3 %collective-permute-start.10 = (bf16[9,160,640]{2,1,0:T(8,128)(2,1)}, bf16[9,160,640]{2,1,0:T(8,128)(2,1)}, u32[]{:S(2)}, u32[]{:S(2)}) collective-permute-start(bf16[9,160,640]{2,1,0:T(8,128)(2,1)} %collective-permute-done.9.refs_1_), channel_id=1, source_target_pairs={{0,1},{1,0},{2,3},{3,2},{4,5},{5,4},{6,7},{7,6},{8,9},{9,8},{10,11... | collective-permute-start | bytes 5529608 | tf_op jit(solution)/shard_map/ppermute | solution.py:42
  47.8 25.7 %collective-permute-start.14 = (bf16[320,1600]{1,0:T(8,128)(2,1)}, bf16[320,1600]{1,0:T(8,128)(2,1)}, u32[]{:S(2)}, u32[]{:S(2)}) collective-permute-start(bf16[320,1600]{1,0:T(8,128)(2,1)} %get-tuple-element.71), channel_id=1, source_target_pairs={{0,16},{16,0},{1,17},{17,1},{2,18},{18,2},{3,19},{19,3},{4,20},{20... | collective-permute-start | bytes 3072008 | tf_op jit(solution)/shard_map/ppermute | solution.py:42
  48.3 22.3 %collective-permute-start.15 = (bf16[160,2560]{1,0:T(8,128)(2,1)}, bf16[160,2560]{1,0:T(8,128)(2,1)}, u32[]{:S(2)}, u32[]{:S(2)}) collective-permute-start(bf16[160,2560]{1,0:T(8,128)(2,1)} %get-tuple-element.80), channel_id=1, source_target_pairs={{0,4},{1,5},{2,6},{3,7},{4,0},{5,1},{6,2},{7,3},{8,12},{9,13},{10,... | collective-permute-start | bytes 2457608 | tf_op jit(solution)/shard_map/ppermute | solution.py:42
  51.6 19.1 %copy-start.8 = (f32[160,2560]{1,0:T(8,128)S(1)}, f32[160,2560]{1,0:T(8,128)}, u32[]{:S(2)}) copy-start(f32[160,2560]{1,0:T(8,128)} %get-tuple-element.79.kept) | copy-start | bytes 4915204
  65.5 8.0 %copy-start.7 = (f32[320,1600]{1,0:T(8,128)S(1)}, f32[320,1600]{1,0:T(8,128)}, u32[]{:S(2)}) copy-start(f32[320,1600]{1,0:T(8,128)} %get-tuple-element.78.kept) | copy-start | bytes 6144004
  65.5 1.3 %collective-permute-start.11 = (f32[40,128]{1,0:T(8,128)S(1)}, f32[40,128]{1,0:T(8,128)S(1)}, u32[]{:S(2)}, u32[]{:S(2)}) collective-permute-start(f32[40,128]{1,0:T(8,128)S(1)} %get-tuple-element.77), channel_id=1, source_target_pairs={{0,1},{1,0},{2,3},{3,2},{4,5},{5,4},{6,7},{7,6},{8,9},{9,8},{10,11... | collective-permute-start | bytes 61448 | tf_op jit(solution)/shard_map/ppermute | solution.py:42
  66.8 3.8 %collective-permute-start.12 = (f32[40,128]{1,0:T(8,128)S(1)}, f32[40,128]{1,0:T(8,128)S(1)}, u32[]{:S(2)}, u32[]{:S(2)}) collective-permute-start(f32[40,128]{1,0:T(8,128)S(1)} %add.39), channel_id=1, source_target_pairs={{0,2},{1,3},{2,0},{3,1},{4,6},{5,7},{6,4},{7,5},{8,10},{9,11},{10,... | collective-permute-start | bytes 61448 | tf_op jit(solution)/shard_map/ppermute | solution.py:42
  70.6 8.8 %copy-start.4 = (bf16[2688,640]{1,0:T(8,128)(2,1)S(1)}, bf16[2688,640]{1,0:T(8,128)(2,1)}, u32[]{:S(2)}) copy-start(bf16[2688,640]{1,0:T(8,128)(2,1)} %copy-done.3) | copy-start | bytes 10321924
  75.0 13.7 %collective-permute-start.16 = (bf16[160,1600]{1,0:T(8,128)(2,1)S(1)}, bf16[160,1600]{1,0:T(8,128)(2,1)S(1)}, u32[]{:S(2)}, u32[]{:S(2)}) collective-permute-start(bf16[160,1600]{1,0:T(8,128)(2,1)S(1)} %get-tuple-element.84), channel_id=1, source_target_pairs={{0,2},{1,3},{2,0},{3,1},{4,6},{5,7},{6,4},{7,5},{8,10},{9,11},{10,... | collective-permute-start | bytes 1536008 | tf_op jit(solution)/shard_map/ppermute | solution.py:42
  76.1 11.9 %collective-permute-start.17 = (bf16[160,1280]{1,0:T(8,128)(2,1)S(1)}, bf16[160,1280]{1,0:T(8,128)(2,1)S(1)}, u32[]{:S(2)}, u32[]{:S(2)}) collective-permute-start(bf16[160,1280]{1,0:T(8,128)(2,1)S(1)} %get-tuple-element.82), channel_id=1, source_target_pairs={{0,16},{16,0},{1,17},{17,1},{2,18},{18,2},{3,19},{19,3},{4,20},{20... | collective-permute-start | bytes 1228808 | tf_op jit(solution)/shard_map/ppermute | solution.py:42
  77.3 4.2 %collective-permute-start.13 = (f32[40,128]{1,0:T(8,128)S(1)}, f32[40,128]{1,0:T(8,128)S(1)}, u32[]{:S(2)}, u32[]{:S(2)}) collective-permute-start(f32[40,128]{1,0:T(8,128)S(1)} %add.40), channel_id=1, source_target_pairs={{0,4},{1,5},{2,6},{3,7},{4,0},{5,1},{6,2},{7,3},{8,12},{9,13},{10,... | collective-permute-start | bytes 61448 | tf_op jit(solution)/shard_map/ppermute | solution.py:42
  81.5 6.4 %collective-permute-start.18 = (f32[40,128]{1,0:T(8,128)S(1)}, f32[40,128]{1,0:T(8,128)S(1)}, u32[]{:S(2)}, u32[]{:S(2)}) collective-permute-start(f32[40,128]{1,0:T(8,128)S(1)} %add.41), channel_id=1, source_target_pairs={{0,8},{1,9},{2,10},{3,11},{4,12},{5,13},{6,14},{7,15},{8,0},{9,1},... | collective-permute-start | bytes 61448 | tf_op jit(solution)/shard_map/ppermute | solution.py:42
  88.0 5.8 %collective-permute-start.20 = (bf16[80,1280]{1,0:T(8,128)(2,1)S(1)}, bf16[80,1280]{1,0:T(8,128)(2,1)S(1)}, u32[]{:S(2)}, u32[]{:S(2)}) collective-permute-start(bf16[80,1280]{1,0:T(8,128)(2,1)S(1)} %get-tuple-element.94), channel_id=1, source_target_pairs={{0,2},{1,3},{2,0},{3,1},{4,6},{5,7},{6,4},{7,5},{8,10},{9,11},{10,... | collective-permute-start | bytes 614408 | tf_op jit(solution)/shard_map/ppermute | solution.py:42
  88.7 7.9 %collective-permute-start.19 = (bf16[80,1600]{1,0:T(8,128)(2,1)S(1)}, bf16[80,1600]{1,0:T(8,128)(2,1)S(1)}, u32[]{:S(2)}, u32[]{:S(2)}) collective-permute-start(bf16[80,1600]{1,0:T(8,128)(2,1)S(1)} %get-tuple-element.97), channel_id=1, source_target_pairs={{0,4},{1,5},{2,6},{3,7},{4,0},{5,1},{6,2},{7,3},{8,12},{9,13},{10,... | collective-permute-start | bytes 768008 | tf_op jit(solution)/shard_map/ppermute | solution.py:42
  93.9 10.5 %collective-permute-start.21 = (bf16[40,1280]{1,0:T(8,128)(2,1)S(1)}, bf16[40,1280]{1,0:T(8,128)(2,1)S(1)}, u32[]{:S(2)}, u32[]{:S(2)}) collective-permute-start(bf16[40,1280]{1,0:T(8,128)(2,1)S(1)} %get-tuple-element.102), channel_id=1, source_target_pairs={{0,8},{1,9},{2,10},{3,11},{4,12},{5,13},{6,14},{7,15},{8,0},{9,1},... | collective-permute-start | bytes 307208 | tf_op jit(solution)/shard_map/ppermute | solution.py:42
  95.6 8.8 %collective-permute-start.22 = (f32[10,128]{1,0:T(8,128)S(1)}, f32[10,128]{1,0:T(8,128)S(1)}, u32[]{:S(2)}, u32[]{:S(2)}) collective-permute-start(f32[10,128]{1,0:T(8,128)S(1)} %slice.12), channel_id=1, source_target_pairs={{0,16},{16,0},{1,17},{17,1},{2,18},{18,2},{3,19},{19,3},{4,20},{20... | collective-permute-start | bytes 15368 | tf_op jit(solution)/shard_map/ppermute | solution.py:42
  96.7 8.8 %collective-permute-start.23 = (bf16[40,1600]{1,0:T(8,128)(2,1)S(1)}, bf16[40,1600]{1,0:T(8,128)(2,1)S(1)}, u32[]{:S(2)}, u32[]{:S(2)}) collective-permute-start(bf16[40,1600]{1,0:T(8,128)(2,1)S(1)} %get-tuple-element.104), channel_id=1, source_target_pairs={{0,8},{1,9},{2,10},{3,11},{4,12},{5,13},{6,14},{7,15},{8,0},{9,1},... | collective-permute-start | bytes 384008 | tf_op jit(solution)/shard_map/ppermute | solution.py:42

commit v8 on v7

--- a/solution.py
+++ b/solution.py
@@ -115,7 +115,8 @@
             value = load(img).astype(F32)
             scale = rstd[pl.ds(img, 1), :] * gain[...]
             normed = (value - mean[pl.ds(img, 1), :]) * scale + bias[...]
-            act = normed / (1.0 + jnp.exp(-normed))
+            turned = 0.5 * normed
+            act = turned + turned * jnp.tanh(turned)
             if keep is not None:
                 act = jnp.where(keep > 0, act, 0.0)
             down, up = shifted(act)

time: 107 us -> 107 us (level)
  transfers between devices with their start and end apart: 24 -> 24, of which waited for: 11 -> 12; matrix products, arithmetic and copies ran while one was open for 1% -> 1% of each run, Pallas kernels for 45% -> 44%
where the time goes in v8:
time: 107 us; the launch traced here: 106 us
  Pallas kernels  51.7 us (48%)
  starting transfers between devices  32.4 us (30%)
  waiting for transfers between devices  20.5 us (19%)
    ppermute x22, starting transfers between devices, swap(): return lax.ppermute(value, axis, [(i, i ^ bit) for i in range(count)])  30.9 us
    ppermute x22, waiting for transfers between devices, swap(): return lax.ppermute(value, axis, [(i, i ^ bit) for i in range(count)])  20.5 us
    pallas_call x1, Pallas kernels, body(): kernel_call(back_kernel, 32, (struct(inputs.shape, F32), struct((40, LANE...  14 us
    pallas_call x1, Pallas kernels, body(): kernel_call(functools.partial(grad_kernel, block, two), 28, tuple((pltpu....  9.04 us
    pallas_call x1, Pallas kernels, body(): kernel_call(conv_kernel, 32, struct(inputs.shape, BF16), [V] * 4, 'conv_f...  5.26 us
    pallas_call x1, Pallas kernels, body(): kernel_call(functools.partial(act_kernel, size), 24, (struct((6 * block,...  4.65 us
    pallas_call x1, Pallas kernels, body(): kernel_call(conv_first_kernel, 32, struct(row_shape, BF16), [V] * 3, 'con...  4.26 us
    pallas_call x1, Pallas kernels, body(): kernel_call(slice_kernel, 8, struct((taps, part, channels), BF16), [S, H]...  2.2 us
  transfers between devices with their start and end apart: 24, of which 12 were waited for; matrix products, arithmetic and copies ran while one was open for 1% of the time, Pallas kernels for 44%

profile of v8, /device:TPU:0, one launch (start us, length us, event | category | flops | bytes accessed | tf_op | source)
XLA Modules:
  0.0 106.5 jit_solution(12572765410242562042)
XLA Ops:
  0.7 0.1 stack.35.info
  0.7 2.2 %slice.20 = bf16[9,160,640]{2,1,0:T(8,128)(2,1)S(1)} custom-call(s32[5]{0:T(128)S(1)} %stack.35.info, bf16[9,320,640]{2,1,0:T(8,128)(2,1)} %refs_0_.1), custom_call_target="tpu_custom_call" | custom-call | tf_op jit(solution)/shard_map/slice/pallas_call | solution.py:409
  2.9 0.0 copy-start.2
  3.0 3.0 %collective-permute-start.9 = (bf16[9,160,640]{2,1,0:T(8,128)(2,1)S(1)}, bf16[9,160,640]{2,1,0:T(8,128)(2,1)}, u32[]{:S(2)}, u32[]{:S(2)}) collective-permute-start(bf16[9,160,640]{2,1,0:T(8,128)(2,1)S(1)} %slice.20), channel_id=1, source_target_pairs={{0,16},{16,0},{1,17},{17,1},{2,18},{18,2},{3,19},{19,3},{4,20},{20... | collective-permute-start | bytes 5529608 | tf_op jit(solution)/shard_map/ppermute | solution.py:42
  6.0 0.0 collective-permute-start.2
  6.0 2.0 %stats.1 = (f32[28,16]{1,0:T(8,128)S(1)}, bf16[14,32,640]{2,1,0:T(8,128)(2,1)S(1)}, bf16[14,32,640]{2,1,0:T(8,128)(2,1)S(1)}) custom-call(s32[5]{0:T(128)S(1)} %stack.35.info, bf16[14,2,32,640]{3,2,1,0:T(8,128)(2,1)S(1)} %copy-done, bf16[14,2,32,640]{3,2,1,0:T(8,128)(2,1)} %u.5), custom_call_target="tpu_custom_call" | custom-call | tf_op jit(solution)/shard_map/stats/pallas_call | solution.py:415
  8.0 0.7 collective-permute-start.4
  8.7 2.9 %collective-permute-start.6 = (bf16[14,2,32,640]{3,2,1,0:T(8,128)(2,1)S(1)}, bf16[14,2,32,640]{3,2,1,0:T(8,128)(2,1)S(1)}, u32[]{:S(2)}, u32[]{:S(2)}) collective-permute-start(bf16[14,2,32,640]{3,2,1,0:T(8,128)(2,1)S(1)} %copy-done), channel_id=1, source_target_pairs={{0,1},{1,0},{2,3},{3,2},{4,5},{5,4},{6,7},{7,6},{8,9},{9,8},{10,11... | collective-permute-start | bytes 3440648 | tf_op jit(solution)/shard_map/ppermute | solution.py:42
  11.6 0.1 collective-permute-start
  11.7 2.4 %collective-permute-done = f32[28,16]{1,0:T(8,128)S(1)} collective-permute-done((f32[28,16]{1,0:T(8,128)S(1)}, f32[28,16]{1,0:T(8,128)S(1)}, u32[]{:S(2)}, u32[]{:S(2)}) %collective-permute-start) | collective-permute-done | bytes 1824 | tf_op jit(solution)/shard_map/ppermute | solution.py:42
  14.1 1.9 %collective-permute-start.1 = (f32[28,16]{1,0:T(8,128)S(1)}, f32[28,16]{1,0:T(8,128)S(1)}, u32[]{:S(2)}, u32[]{:S(2)}) collective-permute-start(f32[28,16]{1,0:T(8,128)S(1)} %add.33), channel_id=1, source_target_pairs={{0,4},{1,5},{2,6},{3,7},{4,0},{5,1},{6,2},{7,3},{8,12},{9,13},{10,... | collective-permute-start | bytes 5384 | tf_op jit(solution)/shard_map/ppermute | solution.py:42
  16.0 0.0 collective-permute-done.2.u_mate.refs_4_
  16.0 1.9 %turn.1.lhs = bf16[320,1792]{1,0:T(8,128)(2,1)S(1)} custom-call(s32[5]{0:T(128)S(1)} %stack.35.info, bf16[14,2,32,640]{3,2,1,0:T(8,128)(2,1)S(1)} %copy-done.2, bf16[14,2,32,640]{3,2,1,0:T(8,128)(2,1)S(1)} %collective-permute-done.2.u_mate.refs_4_), custom_call_target="tpu_custom_call" | custom-call | tf_op jit(solution)/shard_map/turn/pallas_call | solution.py:421
  17.9 3.1 %collective-permute-done.1 = f32[28,16]{1,0:T(8,128)S(1)} collective-permute-done((f32[28,16]{1,0:T(8,128)S(1)}, f32[28,16]{1,0:T(8,128)S(1)}, u32[]{:S(2)}, u32[]{:S(2)}) %collective-permute-start.1) | collective-permute-done | bytes 1824 | tf_op jit(solution)/shard_map/ppermute | solution.py:42
  21.1 2.8 %collective-permute-start.3 = (f32[28,16]{1,0:T(8,128)S(1)}, f32[28,16]{1,0:T(8,128)S(1)}, u32[]{:S(2)}, u32[]{:S(2)}) collective-permute-start(f32[28,16]{1,0:T(8,128)S(1)} %add.34), channel_id=1, source_target_pairs={{0,8},{1,9},{2,10},{3,11},{4,12},{5,13},{6,14},{7,15},{8,0},{9,1},... | collective-permute-start | bytes 5384 | tf_op jit(solution)/shard_map/ppermute | solution.py:42
  23.8 1.9 %collective-permute-done.3 = f32[28,16]{1,0:T(8,128)S(1)} collective-permute-done((f32[28,16]{1,0:T(8,128)S(1)}, f32[28,16]{1,0:T(8,128)S(1)}, u32[]{:S(2)}, u32[]{:S(2)}) %collective-permute-start.3) | collective-permute-done | bytes 1824 | tf_op jit(solution)/shard_map/ppermute | solution.py:42
  25.7 0.0 collective-permute-done.4.rim
  25.7 1.0 collective-permute-start.5
  26.7 0.0 collective-permute-start.7
  26.7 2.8 %collective-permute-done.5 = f32[28,16]{1,0:T(8,128)S(1)} collective-permute-done((f32[28,16]{1,0:T(8,128)S(1)}, f32[28,16]{1,0:T(8,128)S(1)}, u32[]{:S(2)}, u32[]{:S(2)}) %collective-permute-start.5) | collective-permute-done | bytes 1824 | tf_op jit(solution)/shard_map/ppermute | solution.py:42
  29.5 0.9 collective-permute-start.8
  30.4 0.0 collective-permute-done.6.x_mate
  30.5 4.7 %activate.1 = (bf16[2688,640]{1,0:T(8,128)(2,1)S(1)}, bf16[2,2688,640]{2,1,0:T(8,128)(2,1)S(1)}, f32[14,640]{1,0:T(8,128)S(1)}, f32[14,640]{1,0:T(8,128)S(1)}) custom-call(s32[5]{0:T(128)S(1)} %stack.35.info, f32[28,16]{1,0:T(8,128)S(1)} %add.36.stats, bf16[14,2,32,640]{3,2,1,0:T(8,128)(2,1)S(1)} %copy-done, ...), custom_call_target="tpu_custom_call" | custom-call | tf_op jit(solution)/shard_map/activate/pallas_call | solution.py:435
  35.1 0.0 copy-start.6
  35.1 9.0 %weight_terms.1 = (bf16[160,2560]{1,0:T(8,128)(2,1)}, f32[160,2560]{1,0:T(8,128)}, bf16[320,1600]{1,0:T(8,128)(2,1)}, f32[320,1600]{1,0:T(8,128)}) custom-call(s32[5]{0:T(128)S(1)} %stack.35.info, bf16[320,1792]{1,0:T(8,128)(2,1)S(1)} %turn.1.lhs, bf16[2688,640]{1,0:T(8,128)(2,1)S(1)} %get-tuple-element.65.mid, bf16[2,2688,640]{2,1,0:T(8,128)(2,1)S(1)} %get-tuple-element.66.side), custom_call_target="tpu_custom_call" | custom-call | tf_op jit(solution)/shard_map/weight_terms/pallas_call | solution.py:463
  44.2 0.0 collective-permute-done.8.refs_5_
  44.2 2.1 %collective-permute-done.9.refs_1_ = bf16[9,160,640]{2,1,0:T(8,128)(2,1)} collective-permute-done((bf16[9,160,640]{2,1,0:T(8,128)(2,1)S(1)}, bf16[9,160,640]{2,1,0:T(8,128)(2,1)}, u32[]{:S(2)}, u32[]{:S(2)}) %collective-permute-start.9) | collective-permute-done | bytes 1843232 | tf_op jit(solution)/shard_map/ppermute | solution.py:42
  46.3 1.0 collective-permute-start.10
  47.3 0.8 collective-permute-start.14
  48.0 1.6 %collective-permute-start.15 = (bf16[160,2560]{1,0:T(8,128)(2,1)}, bf16[160,2560]{1,0:T(8,128)(2,1)}, u32[]{:S(2)}, u32[]{:S(2)}) collective-permute-start(bf16[160,2560]{1,0:T(8,128)(2,1)} %get-tuple-element.80), channel_id=1, source_target_pairs={{0,4},{1,5},{2,6},{3,7},{4,0},{5,1},{6,2},{7,3},{8,12},{9,13},{10,... | collective-permute-start | bytes 2457608 | tf_op jit(solution)/shard_map/ppermute | solution.py:42
  49.6 0.1 pad_add_fusion.places
  49.7 1.3 %collective-permute-done.10.refs_2_ = bf16[9,160,640]{2,1,0:T(8,128)(2,1)} collective-permute-done((bf16[9,160,640]{2,1,0:T(8,128)(2,1)}, bf16[9,160,640]{2,1,0:T(8,128)(2,1)}, u32[]{:S(2)}, u32[]{:S(2)}) %collective-permute-start.10) | collective-permute-done | bytes 1843232 | tf_op jit(solution)/shard_map/ppermute | solution.py:42
  51.0 14.0 %conv_backward.1 = (f32[14,2,32,640]{3,2,1,0:T(8,128)S(1)}, f32[40,128]{1,0:T(8,128)S(1)}, bf16[9,640,640]{2,1,0:T(8,128)(2,1)S(1)}) custom-call(s32[5]{0:T(128)S(1)} %stack.35.info, s32[3]{0:T(128)S(1)} %pad_add_fusion.places, bf16[9,320,640]{2,1,0:T(8,128)(2,1)} %refs_0_.1, bf16[9,160,640]{2,1,0:T(8,128)(2,1)} %collective-permute-done.9.refs_1_, ...), custom_call_target="tpu_custom_call" | custom-call | tf_op jit(solution)/shard_map/conv_backward/pallas_call | solution.py:480
  65.0 0.4 collective-permute-start.11
  65.4 0.8 collective-permute-done.11
  66.3 1.1 %collective-permute-start.12 = (f32[40,128]{1,0:T(8,128)S(1)}, f32[40,128]{1,0:T(8,128)S(1)}, u32[]{:S(2)}, u32[]{:S(2)}) collective-permute-start(f32[40,128]{1,0:T(8,128)S(1)} %add.39), channel_id=1, source_target_pairs={{0,2},{1,3},{2,0},{3,1},{4,6},{5,7},{6,4},{7,5},{8,10},{9,11},{10,... | collective-permute-start | bytes 61448 | tf_op jit(solution)/shard_map/ppermute | solution.py:42
  67.4 2.7 %collective-permute-done.12 = f32[40,128]{1,0:T(8,128)S(1)} collective-permute-done((f32[40,128]{1,0:T(8,128)S(1)}, f32[40,128]{1,0:T(8,128)S(1)}, u32[]{:S(2)}, u32[]{:S(2)}) %collective-permute-start.12) | collective-permute-done | bytes 20512 | tf_op jit(solution)/shard_map/ppermute | solution.py:42
  70.1 1.6 %split.1 = (bf16[160,1280]{1,0:T(8,128)(2,1)S(1)}, f32[160,1280]{1,0:T(8,128)S(1)}) custom-call(s32[5]{0:T(128)S(1)} %stack.35.info, f32[160,2560]{1,0:T(8,128)S(1)} %copy-done.8, bf16[160,2560]{1,0:T(8,128)(2,1)} %collective-permute-done.15.got), custom_call_target="tpu_custom_call" | custom-call | tf_op jit(solution)/shard_map/split/pallas_call | solution.py:454
  71.7 1.3 %collective-permute-done.14.got = bf16[320,1600]{1,0:T(8,128)(2,1)} collective-permute-done((bf16[320,1600]{1,0:T(8,128)(2,1)}, bf16[320,1600]{1,0:T(8,128)(2,1)}, u32[]{:S(2)}, u32[]{:S(2)}) %collective-permute-start.14) | collective-permute-done | bytes 1024032 | tf_op jit(solution)/shard_map/ppermute | solution.py:42
  73.0 1.4 %fold.5 = (bf16[160,1600]{1,0:T(8,128)(2,1)S(1)}, f32[160,1600]{1,0:T(8,128)S(1)}) custom-call(f32[320,1600]{1,0:T(8,128)S(1)} %copy-done.7, bf16[320,1600]{1,0:T(8,128)(2,1)} %collective-permute-done.14.got), custom_call_target="tpu_custom_call" | custom-call | tf_op jit(solution)/shard_map/fold/pallas_call | solution.py:448
  74.4 1.3 %collective-permute-start.16 = (bf16[160,1600]{1,0:T(8,128)(2,1)S(1)}, bf16[160,1600]{1,0:T(8,128)(2,1)S(1)}, u32[]{:S(2)}, u32[]{:S(2)}) collective-permute-start(bf16[160,1600]{1,0:T(8,128)(2,1)S(1)} %get-tuple-element.84), channel_id=1, source_target_pairs={{0,2},{1,3},{2,0},{3,1},{4,6},{5,7},{6,4},{7,5},{8,10},{9,11},{10,... | collective-permute-start | bytes 1536008 | tf_op jit(solution)/shard_map/ppermute | solution.py:42
  75.8 1.5 %collective-permute-start.17 = (bf16[160,1280]{1,0:T(8,128)(2,1)S(1)}, bf16[160,1280]{1,0:T(8,128)(2,1)S(1)}, u32[]{:S(2)}, u32[]{:S(2)}) collective-permute-start(bf16[160,1280]{1,0:T(8,128)(2,1)S(1)} %get-tuple-element.82), channel_id=1, source_target_pairs={{0,16},{16,0},{1,17},{17,1},{2,18},{18,2},{3,19},{19,3},{4,20},{20... | collective-permute-start | bytes 1228808 | tf_op jit(solution)/shard_map/ppermute | solution.py:42
  77.3 1.6 %collective-permute-start.13 = (f32[40,128]{1,0:T(8,128)S(1)}, f32[40,128]{1,0:T(8,128)S(1)}, u32[]{:S(2)}, u32[]{:S(2)}) collective-permute-start(f32[40,128]{1,0:T(8,128)S(1)} %add.40), channel_id=1, source_target_pairs={{0,4},{1,5},{2,6},{3,7},{4,0},{5,1},{6,2},{7,3},{8,12},{9,13},{10,... | collective-permute-start | bytes 61448 | tf_op jit(solution)/shard_map/ppermute | solution.py:42
  78.9 2.0 %own.1 = bf16[3,1792,640]{2,1,0:T(8,128)(2,1)S(1)} custom-call(s32[5]{0:T(128)S(1)} %stack.35.info, bf16[2688,640]{1,0:T(8,128)(2,1)S(1)} %copy-done.4), custom_call_target="tpu_custom_call" | custom-call | tf_op jit(solution)/shard_map/own/pallas_call | solution.py:510
  80.9 0.1 collective-permute-done.13
  81.1 2.6 %collective-permute-start.18 = (f32[40,128]{1,0:T(8,128)S(1)}, f32[40,128]{1,0:T(8,128)S(1)}, u32[]{:S(2)}, u32[]{:S(2)}) collective-permute-start(f32[40,128]{1,0:T(8,128)S(1)} %add.41), channel_id=1, source_target_pairs={{0,8},{1,9},{2,10},{3,11},{4,12},{5,13},{6,14},{7,15},{8,0},{9,1},... | collective-permute-start | bytes 61448 | tf_op jit(solution)/shard_map/ppermute | solution.py:42
  83.6 4.3 %conv_forward.2.first = bf16[14,32,640]{2,1,0:T(8,128)(2,1)S(1)} custom-call(bf16[3,1792,640]{2,1,0:T(8,128)(2,1)S(1)} %own.1, bf16[9,640,640]{2,1,0:T(8,128)(2,1)S(1)} %get-tuple-element.91.w, bf16[14,2,32,640]{3,2,1,0:T(8,128)(2,1)S(1)} %copy-done), custom_call_target="tpu_custom_call" | custom-call | tf_op jit(solution)/shard_map/conv_forward/pallas_call | solution.py:519
  87.9 0.0 collective-permute-done.17.got
  87.9 0.1 fold.6
  88.0 0.6 collective-permute-start.20
  88.6 0.1 fold.7
  88.7 1.6 %collective-permute-start.19 = (bf16[80,1600]{1,0:T(8,128)(2,1)S(1)}, bf16[80,1600]{1,0:T(8,128)(2,1)S(1)}, u32[]{:S(2)}, u32[]{:S(2)}) collective-permute-start(bf16[80,1600]{1,0:T(8,128)(2,1)S(1)} %get-tuple-element.97), channel_id=1, source_target_pairs={{0,4},{1,5},{2,6},{3,7},{4,0},{5,1},{6,2},{7,3},{8,12},{9,13},{10,... | collective-permute-start | bytes 768008 | tf_op jit(solution)/shard_map/ppermute | solution.py:42
  90.4 2.0 %input_grad.1 = bf16[14,2,32,640]{3,2,1,0:T(8,128)(2,1)} custom-call(f32[40,128]{1,0:T(8,128)S(1)} %add.42.sums, f32[14,2,32,640]{3,2,1,0:T(8,128)S(1)} %get-tuple-element.100.grad, bf16[14,2,32,640]{3,2,1,0:T(8,128)(2,1)S(1)} %copy-done, bf16[14,2,32,640]{3,2,1,0:T(8,128)(2,1)S(1)} %copy-done.2, f32[14,640]{1,0:T(8,128)S(1)} %get-tuple-element.75.refs_7_.mean, ...), custom_call_target="tpu_custom_call" | custom-call | tf_op jit(solution)/shard_map/input_grad/pallas_call | solution.py:529
  92.4 1.4 %collective-permute-done.20.got = bf16[80,1280]{1,0:T(8,128)(2,1)S(1)} collective-permute-done((bf16[80,1280]{1,0:T(8,128)(2,1)S(1)}, bf16[80,1280]{1,0:T(8,128)(2,1)S(1)}, u32[]{:S(2)}, u32[]{:S(2)}) %collective-permute-start.20) | collective-permute-done | bytes 204832 | tf_op jit(solution)/shard_map/ppermute | solution.py:42
  93.9 1.7 %collective-permute-start.21 = (bf16[40,1280]{1,0:T(8,128)(2,1)S(1)}, bf16[40,1280]{1,0:T(8,128)(2,1)S(1)}, u32[]{:S(2)}, u32[]{:S(2)}) collective-permute-start(bf16[40,1280]{1,0:T(8,128)(2,1)S(1)} %get-tuple-element.102), channel_id=1, source_target_pairs={{0,8},{1,9},{2,10},{3,11},{4,12},{5,13},{6,14},{7,15},{8,0},{9,1},... | collective-permute-start | bytes 307208 | tf_op jit(solution)/shard_map/ppermute | solution.py:42
  95.6 1.1 %collective-permute-start.22 = (f32[10,128]{1,0:T(8,128)S(1)}, f32[10,128]{1,0:T(8,128)S(1)}, u32[]{:S(2)}, u32[]{:S(2)}) collective-permute-start(f32[10,128]{1,0:T(8,128)S(1)} %slice.12), channel_id=1, source_target_pairs={{0,16},{16,0},{1,17},{17,1},{2,18},{18,2},{3,19},{19,3},{4,20},{20... | collective-permute-start | bytes 15368 | tf_op jit(solution)/shard_map/ppermute | solution.py:42
  96.7 0.0 collective-permute-done.19.got
  96.7 0.1 fold.9
  96.7 2.3 %collective-permute-start.23 = (bf16[40,1600]{1,0:T(8,128)(2,1)S(1)}, bf16[40,1600]{1,0:T(8,128)(2,1)S(1)}, u32[]{:S(2)}, u32[]{:S(2)}) collective-permute-start(bf16[40,1600]{1,0:T(8,128)(2,1)S(1)} %get-tuple-element.104), channel_id=1, source_target_pairs={{0,8},{1,9},{2,10},{3,11},{4,12},{5,13},{6,14},{7,15},{8,0},{9,1},... | collective-permute-start | bytes 384008 | tf_op jit(solution)/shard_map/ppermute | solution.py:42
  99.1 5.3 %conv_forward.3 = bf16[14,2,32,640]{3,2,1,0:T(8,128)(2,1)} custom-call(bf16[3,1792,640]{2,1,0:T(8,128)(2,1)S(1)} %own.1, bf16[9,640,640]{2,1,0:T(8,128)(2,1)S(1)} %get-tuple-element.91.w, bf16[14,2,32,640]{3,2,1,0:T(8,128)(2,1)S(1)} %copy-done, bf16[14,32,640]{2,1,0:T(8,128)(2,1)S(1)} %conv_forward.2.first), custom_call_target="tpu_custom_call" | custom-call | tf_op jit(solution)/shard_map/conv_forward/pallas_call | solution.py:538
  104.3 0.0 collective-permute-done.22
  104.4 0.6 slice_bitcast_fusion
  105.0 0.6 collective-permute-done.23.got_b
  105.5 0.9 last.1
  (40 shorter events, 0.1 us)
Async XLA Ops:
  0.7 5.3 %copy-start.1 = (bf16[14,2,32,640]{3,2,1,0:T(8,128)(2,1)S(1)}, bf16[14,2,32,640]{3,2,1,0:T(8,128)(2,1)}, u32[]{:S(2)}) copy-start(bf16[14,2,32,640]{3,2,1,0:T(8,128)(2,1)} %u.5) | copy-start | bytes 3440644
  0.7 5.3 %copy-start = (bf16[14,2,32,640]{3,2,1,0:T(8,128)(2,1)S(1)}, bf16[14,2,32,640]{3,2,1,0:T(8,128)(2,1)}, u32[]{:S(2)}) copy-start(bf16[14,2,32,640]{3,2,1,0:T(8,128)(2,1)} %x.9) | copy-start | bytes 3440644
  2.9 13.0 %copy-start.2 = (bf16[14,2,32,640]{3,2,1,0:T(8,128)(2,1)S(1)}, bf16[14,2,32,640]{3,2,1,0:T(8,128)(2,1)}, u32[]{:S(2)}) copy-start(bf16[14,2,32,640]{3,2,1,0:T(8,128)(2,1)} %u.5) | copy-start | bytes 3440644
  3.0 43.3 %collective-permute-start.9 = (bf16[9,160,640]{2,1,0:T(8,128)(2,1)S(1)}, bf16[9,160,640]{2,1,0:T(8,128)(2,1)}, u32[]{:S(2)}, u32[]{:S(2)}) collective-permute-start(bf16[9,160,640]{2,1,0:T(8,128)(2,1)S(1)} %slice.20), channel_id=1, source_target_pairs={{0,16},{16,0},{1,17},{17,1},{2,18},{18,2},{3,19},{19,3},{4,20},{20... | collective-permute-start | bytes 5529608 | tf_op jit(solution)/shard_map/ppermute | solution.py:42
  6.0 10.0 %collective-permute-start.2 = (bf16[14,2,32,640]{3,2,1,0:T(8,128)(2,1)S(1)}, bf16[14,2,32,640]{3,2,1,0:T(8,128)(2,1)S(1)}, u32[]{:S(2)}, u32[]{:S(2)}) collective-permute-start(bf16[14,2,32,640]{3,2,1,0:T(8,128)(2,1)S(1)} %copy-done.1), channel_id=1, source_target_pairs={{0,1},{1,0},{2,3},{3,2},{4,5},{5,4},{6,7},{7,6},{8,9},{9,8},{10,11... | collective-permute-start | bytes 3440648 | tf_op jit(solution)/shard_map/ppermute | solution.py:42
  8.0 17.7 %collective-permute-start.4 = (bf16[14,32,640]{2,1,0:T(8,128)(2,1)S(1)}, bf16[14,32,640]{2,1,0:T(8,128)(2,1)S(1)}, u32[]{:S(2)}, u32[]{:S(2)}) collective-permute-start(bf16[14,32,640]{2,1,0:T(8,128)(2,1)S(1)} %get-tuple-element.62), channel_id=1, source_target_pairs={{1,2},{2,1},{3,4},{4,3},{5,6},{6,5},{7,8},{8,7},{9,10},{10,9},{11,... | collective-permute-start | bytes 1720328 | tf_op jit(solution)/shard_map/ppermute | solution.py:420
  8.7 21.7 %collective-permute-start.6 = (bf16[14,2,32,640]{3,2,1,0:T(8,128)(2,1)S(1)}, bf16[14,2,32,640]{3,2,1,0:T(8,128)(2,1)S(1)}, u32[]{:S(2)}, u32[]{:S(2)}) collective-permute-start(bf16[14,2,32,640]{3,2,1,0:T(8,128)(2,1)S(1)} %copy-done), channel_id=1, source_target_pairs={{0,1},{1,0},{2,3},{3,2},{4,5},{5,4},{6,7},{7,6},{8,9},{9,8},{10,11... | collective-permute-start | bytes 3440648 | tf_op jit(solution)/shard_map/ppermute | solution.py:42
  11.6 2.5 %collective-permute-start = (f32[28,16]{1,0:T(8,128)S(1)}, f32[28,16]{1,0:T(8,128)S(1)}, u32[]{:S(2)}, u32[]{:S(2)}) collective-permute-start(f32[28,16]{1,0:T(8,128)S(1)} %get-tuple-element.59), channel_id=1, source_target_pairs={{0,1},{1,0},{2,3},{3,2},{4,5},{5,4},{6,7},{7,6},{8,9},{9,8},{10,11... | collective-permute-start | bytes 5384 | tf_op jit(solution)/shard_map/ppermute | solution.py:42
  14.1 16.3 %copy-start.10 = (f32[640]{0:T(1024)S(1)}, f32[640]{0:T(1024)}, u32[]{:S(2)}) copy-start(f32[640]{0:T(1024)} %param.6) | copy-start | bytes 7684
  14.1 16.4 %copy-start.11 = (f32[640]{0:T(1024)S(1)}, f32[640]{0:T(1024)}, u32[]{:S(2)}) copy-start(f32[640]{0:T(1024)} %param.7) | copy-start | bytes 7684
  14.1 7.0 %collective-permute-start.1 = (f32[28,16]{1,0:T(8,128)S(1)}, f32[28,16]{1,0:T(8,128)S(1)}, u32[]{:S(2)}, u32[]{:S(2)}) collective-permute-start(f32[28,16]{1,0:T(8,128)S(1)} %add.33), channel_id=1, source_target_pairs={{0,4},{1,5},{2,6},{3,7},{4,0},{5,1},{6,2},{7,3},{8,12},{9,13},{10,... | collective-permute-start | bytes 5384 | tf_op jit(solution)/shard_map/ppermute | solution.py:42
  16.0 1.9 %copy-start.5 = (bf16[14,2,32,640]{3,2,1,0:T(8,128)(2,1)}, bf16[14,2,32,640]{3,2,1,0:T(8,128)(2,1)S(1)}, u32[]{:S(2)}) copy-start(bf16[14,2,32,640]{3,2,1,0:T(8,128)(2,1)S(1)} %collective-permute-done.2.u_mate.refs_4_) | copy-start | bytes 3440644
  21.1 4.6 %collective-permute-start.3 = (f32[28,16]{1,0:T(8,128)S(1)}, f32[28,16]{1,0:T(8,128)S(1)}, u32[]{:S(2)}, u32[]{:S(2)}) collective-permute-start(f32[28,16]{1,0:T(8,128)S(1)} %add.34), channel_id=1, source_target_pairs={{0,8},{1,9},{2,10},{3,11},{4,12},{5,13},{6,14},{7,15},{8,0},{9,1},... | collective-permute-start | bytes 5384 | tf_op jit(solution)/shard_map/ppermute | solution.py:42
  25.7 3.8 %collective-permute-start.5 = (f32[28,16]{1,0:T(8,128)S(1)}, f32[28,16]{1,0:T(8,128)S(1)}, u32[]{:S(2)}, u32[]{:S(2)}) collective-permute-start(f32[28,16]{1,0:T(8,128)S(1)} %add.35), channel_id=1, source_target_pairs={{0,2},{1,3},{2,0},{3,1},{4,6},{5,7},{6,4},{7,5},{8,10},{9,11},{10,... | collective-permute-start | bytes 5384 | tf_op jit(solution)/shard_map/ppermute | solution.py:42
  26.7 3.8 %collective-permute-start.7 = (bf16[14,32,640]{2,1,0:T(8,128)(2,1)S(1)}, bf16[14,32,640]{2,1,0:T(8,128)(2,1)S(1)}, u32[]{:S(2)}, u32[]{:S(2)}) collective-permute-start(bf16[14,32,640]{2,1,0:T(8,128)(2,1)S(1)} %collective-permute-done.4.rim), channel_id=1, source_target_pairs={{0,1},{1,0},{2,3},{3,2},{4,5},{5,4},{6,7},{7,6},{8,9},{9,8},{10,11... | collective-permute-start | bytes 1720328 | tf_op jit(solution)/shard_map/ppermute | solution.py:42
  29.5 14.7 %collective-permute-start.8 = (bf16[14,32,640]{2,1,0:T(8,128)(2,1)S(1)}, bf16[14,32,640]{2,1,0:T(8,128)(2,1)S(1)}, u32[]{:S(2)}, u32[]{:S(2)}) collective-permute-start(bf16[14,32,640]{2,1,0:T(8,128)(2,1)S(1)} %get-tuple-element.70), channel_id=1, source_target_pairs={{1,2},{2,1},{3,4},{4,3},{5,6},{6,5},{7,8},{8,7},{9,10},{10,9},{11,... | collective-permute-start | bytes 1720328 | tf_op jit(solution)/shard_map/ppermute | solution.py:433
  35.1 9.1 %copy-start.3 = (bf16[2688,640]{1,0:T(8,128)(2,1)}, bf16[2688,640]{1,0:T(8,128)(2,1)S(1)}, u32[]{:S(2)}) copy-start(bf16[2688,640]{1,0:T(8,128)(2,1)S(1)} %get-tuple-element.65.mid) | copy-start | bytes 10321924
  35.1 15.9 %copy-start.6 = (bf16[14,2,32,640]{3,2,1,0:T(8,128)(2,1)S(1)}, bf16[14,2,32,640]{3,2,1,0:T(8,128)(2,1)}, u32[]{:S(2)}) copy-start(bf16[14,2,32,640]{3,2,1,0:T(8,128)(2,1)} %copy-done.5) | copy-start | bytes 3440644
  44.2 2.1 %copy-start.9 = (bf16[14,32,640]{2,1,0:T(8,128)(2,1)}, bf16[14,32,640]{2,1,0:T(8,128)(2,1)S(1)}, u32[]{:S(2)}) copy-start(bf16[14,32,640]{2,1,0:T(8,128)(2,1)S(1)} %collective-permute-done.8.refs_5_) | copy-start | bytes 1720324
  46.3 4.7 %collective-permute-start.10 = (bf16[9,160,640]{2,1,0:T(8,128)(2,1)}, bf16[9,160,640]{2,1,0:T(8,128)(2,1)}, u32[]{:S(2)}, u32[]{:S(2)}) collective-permute-start(bf16[9,160,640]{2,1,0:T(8,128)(2,1)} %collective-permute-done.9.refs_1_), channel_id=1, source_target_pairs={{0,1},{1,0},{2,3},{3,2},{4,5},{5,4},{6,7},{7,6},{8,9},{9,8},{10,11... | collective-permute-start | bytes 5529608 | tf_op jit(solution)/shard_map/ppermute | solution.py:42
  47.3 25.7 %collective-permute-start.14 = (bf16[320,1600]{1,0:T(8,128)(2,1)}, bf16[320,1600]{1,0:T(8,128)(2,1)}, u32[]{:S(2)}, u32[]{:S(2)}) collective-permute-start(bf16[320,1600]{1,0:T(8,128)(2,1)} %get-tuple-element.71), channel_id=1, source_target_pairs={{0,16},{16,0},{1,17},{17,1},{2,18},{18,2},{3,19},{19,3},{4,20},{20... | collective-permute-start | bytes 3072008 | tf_op jit(solution)/shard_map/ppermute | solution.py:42
  48.0 22.0 %collective-permute-start.15 = (bf16[160,2560]{1,0:T(8,128)(2,1)}, bf16[160,2560]{1,0:T(8,128)(2,1)}, u32[]{:S(2)}, u32[]{:S(2)}) collective-permute-start(bf16[160,2560]{1,0:T(8,128)(2,1)} %get-tuple-element.80), channel_id=1, source_target_pairs={{0,4},{1,5},{2,6},{3,7},{4,0},{5,1},{6,2},{7,3},{8,12},{9,13},{10,... | collective-permute-start | bytes 2457608 | tf_op jit(solution)/shard_map/ppermute | solution.py:42
  51.0 19.1 %copy-start.8 = (f32[160,2560]{1,0:T(8,128)S(1)}, f32[160,2560]{1,0:T(8,128)}, u32[]{:S(2)}) copy-start(f32[160,2560]{1,0:T(8,128)} %get-tuple-element.79.kept) | copy-start | bytes 4915204
  65.0 8.0 %copy-start.7 = (f32[320,1600]{1,0:T(8,128)S(1)}, f32[320,1600]{1,0:T(8,128)}, u32[]{:S(2)}) copy-start(f32[320,1600]{1,0:T(8,128)} %get-tuple-element.78.kept) | copy-start | bytes 6144004
  65.0 1.3 %collective-permute-start.11 = (f32[40,128]{1,0:T(8,128)S(1)}, f32[40,128]{1,0:T(8,128)S(1)}, u32[]{:S(2)}, u32[]{:S(2)}) collective-permute-start(f32[40,128]{1,0:T(8,128)S(1)} %get-tuple-element.77), channel_id=1, source_target_pairs={{0,1},{1,0},{2,3},{3,2},{4,5},{5,4},{6,7},{7,6},{8,9},{9,8},{10,11... | collective-permute-start | bytes 61448 | tf_op jit(solution)/shard_map/ppermute | solution.py:42
  66.3 3.8 %collective-permute-start.12 = (f32[40,128]{1,0:T(8,128)S(1)}, f32[40,128]{1,0:T(8,128)S(1)}, u32[]{:S(2)}, u32[]{:S(2)}) collective-permute-start(f32[40,128]{1,0:T(8,128)S(1)} %add.39), channel_id=1, source_target_pairs={{0,2},{1,3},{2,0},{3,1},{4,6},{5,7},{6,4},{7,5},{8,10},{9,11},{10,... | collective-permute-start | bytes 61448 | tf_op jit(solution)/shard_map/ppermute | solution.py:42
  70.1 8.8 %copy-start.4 = (bf16[2688,640]{1,0:T(8,128)(2,1)S(1)}, bf16[2688,640]{1,0:T(8,128)(2,1)}, u32[]{:S(2)}) copy-start(bf16[2688,640]{1,0:T(8,128)(2,1)} %copy-done.3) | copy-start | bytes 10321924
  74.4 14.2 %collective-permute-start.16 = (bf16[160,1600]{1,0:T(8,128)(2,1)S(1)}, bf16[160,1600]{1,0:T(8,128)(2,1)S(1)}, u32[]{:S(2)}, u32[]{:S(2)}) collective-permute-start(bf16[160,1600]{1,0:T(8,128)(2,1)S(1)} %get-tuple-element.84), channel_id=1, source_target_pairs={{0,2},{1,3},{2,0},{3,1},{4,6},{5,7},{6,4},{7,5},{8,10},{9,11},{10,... | collective-permute-start | bytes 1536008 | tf_op jit(solution)/shard_map/ppermute | solution.py:42
  75.8 12.2 %collective-permute-start.17 = (bf16[160,1280]{1,0:T(8,128)(2,1)S(1)}, bf16[160,1280]{1,0:T(8,128)(2,1)S(1)}, u32[]{:S(2)}, u32[]{:S(2)}) collective-permute-start(bf16[160,1280]{1,0:T(8,128)(2,1)S(1)} %get-tuple-element.82), channel_id=1, source_target_pairs={{0,16},{16,0},{1,17},{17,1},{2,18},{18,2},{3,19},{19,3},{4,20},{20... | collective-permute-start | bytes 1228808 | tf_op jit(solution)/shard_map/ppermute | solution.py:42
  77.3 3.8 %collective-permute-start.13 = (f32[40,128]{1,0:T(8,128)S(1)}, f32[40,128]{1,0:T(8,128)S(1)}, u32[]{:S(2)}, u32[]{:S(2)}) collective-permute-start(f32[40,128]{1,0:T(8,128)S(1)} %add.40), channel_id=1, source_target_pairs={{0,4},{1,5},{2,6},{3,7},{4,0},{5,1},{6,2},{7,3},{8,12},{9,13},{10,... | collective-permute-start | bytes 61448 | tf_op jit(solution)/shard_map/ppermute | solution.py:42
  81.1 6.9 %collective-permute-start.18 = (f32[40,128]{1,0:T(8,128)S(1)}, f32[40,128]{1,0:T(8,128)S(1)}, u32[]{:S(2)}, u32[]{:S(2)}) collective-permute-start(f32[40,128]{1,0:T(8,128)S(1)} %add.41), channel_id=1, source_target_pairs={{0,8},{1,9},{2,10},{3,11},{4,12},{5,13},{6,14},{7,15},{8,0},{9,1},... | collective-permute-start | bytes 61448 | tf_op jit(solution)/shard_map/ppermute | solution.py:42
  88.0 5.8 %collective-permute-start.20 = (bf16[80,1280]{1,0:T(8,128)(2,1)S(1)}, bf16[80,1280]{1,0:T(8,128)(2,1)S(1)}, u32[]{:S(2)}, u32[]{:S(2)}) collective-permute-start(bf16[80,1280]{1,0:T(8,128)(2,1)S(1)} %get-tuple-element.94), channel_id=1, source_target_pairs={{0,2},{1,3},{2,0},{3,1},{4,6},{5,7},{6,4},{7,5},{8,10},{9,11},{10,... | collective-permute-start | bytes 614408 | tf_op jit(solution)/shard_map/ppermute | solution.py:42
  88.7 7.9 %collective-permute-start.19 = (bf16[80,1600]{1,0:T(8,128)(2,1)S(1)}, bf16[80,1600]{1,0:T(8,128)(2,1)S(1)}, u32[]{:S(2)}, u32[]{:S(2)}) collective-permute-start(bf16[80,1600]{1,0:T(8,128)(2,1)S(1)} %get-tuple-element.97), channel_id=1, source_target_pairs={{0,4},{1,5},{2,6},{3,7},{4,0},{5,1},{6,2},{7,3},{8,12},{9,13},{10,... | collective-permute-start | bytes 768008 | tf_op jit(solution)/shard_map/ppermute | solution.py:42
  93.9 10.5 %collective-permute-start.21 = (bf16[40,1280]{1,0:T(8,128)(2,1)S(1)}, bf16[40,1280]{1,0:T(8,128)(2,1)S(1)}, u32[]{:S(2)}, u32[]{:S(2)}) collective-permute-start(bf16[40,1280]{1,0:T(8,128)(2,1)S(1)} %get-tuple-element.102), channel_id=1, source_target_pairs={{0,8},{1,9},{2,10},{3,11},{4,12},{5,13},{6,14},{7,15},{8,0},{9,1},... | collective-permute-start | bytes 307208 | tf_op jit(solution)/shard_map/ppermute | solution.py:42
  95.6 8.8 %collective-permute-start.22 = (f32[10,128]{1,0:T(8,128)S(1)}, f32[10,128]{1,0:T(8,128)S(1)}, u32[]{:S(2)}, u32[]{:S(2)}) collective-permute-start(f32[10,128]{1,0:T(8,128)S(1)} %slice.12), channel_id=1, source_target_pairs={{0,16},{16,0},{1,17},{17,1},{2,18},{18,2},{3,19},{19,3},{4,20},{20... | collective-permute-start | bytes 15368 | tf_op jit(solution)/shard_map/ppermute | solution.py:42
  96.7 8.8 %collective-permute-start.23 = (bf16[40,1600]{1,0:T(8,128)(2,1)S(1)}, bf16[40,1600]{1,0:T(8,128)(2,1)S(1)}, u32[]{:S(2)}, u32[]{:S(2)}) collective-permute-start(bf16[40,1600]{1,0:T(8,128)(2,1)S(1)} %get-tuple-element.104), channel_id=1, source_target_pairs={{0,8},{1,9},{2,10},{3,11},{4,12},{5,13},{6,14},{7,15},{8,0},{9,1},... | collective-permute-start | bytes 384008 | tf_op jit(solution)/shard_map/ppermute | solution.py:42
